TPU v7x, 32 devices: a whole 2x2x4 slice. The times are simulated.
32 devices in a mesh: dp: 16 (over z, y, x), tensor: 2 (over core).
Axes of the slice: x: 2, y: 2, z: 4, core: 2. Of those that a mesh axis runs over, the one named last changes fastest.
Arguments:
- tokens: bfloat16 [8192, 2048], P('dp'), may hold values from -8 to 8
- segments: int32 [8192], P('dp'), may hold values from 0 to 31, never falling along the last dimension, each value on 1 to 512 neighbouring positions
- ln_gain: bfloat16 [2048], replicated, may hold values from 0.099609375 to 1.8984375
- ln_shift: bfloat16 [2048], replicated, may hold values from -1.75 to 1.75
- qkv_weight: bfloat16 [2048, 3, 2048], P('dp', None, 'tensor'), may hold values from -0.125 to 0.125
- qkv_bias: bfloat16 [3, 2048], P(None, 'tensor'), may hold values from -3 to 3
- out_weight: bfloat16 [2048, 2048], P('tensor', 'dp'), may hold values from -1 to 1
- up_weight: bfloat16 [2048, 8192], P('dp', 'tensor'), may hold values from -0.125 to 0.125
- up_bias: bfloat16 [8192], P('tensor'), may hold values from -3 to 3
- down_weight: bfloat16 [8192, 2048], P('tensor', 'dp'), may hold values from -0.0625 to 0.0625
- branch_bias: bfloat16 [2048], replicated, may hold values from -3 to 3
- cotangent: bfloat16 [8192, 2048], P('dp'), may hold values from -8 to 8
Outputs:
- result: bfloat16 [8192, 2048], P('dp')
- input_grad: float32 [8192, 2048], P('dp')
- ln_gain_grad: float32 [2048], replicated
- ln_shift_grad: float32 [2048], replicated
- qkv_weight_grad: float32 [2048, 3, 2048], P('dp', None, 'tensor')
- qkv_bias_grad: float32 [3, 2048], P(None, 'tensor')
- out_weight_grad: float32 [2048, 2048], P('tensor', 'dp')
- up_weight_grad: float32 [2048, 8192], P('dp', 'tensor')
- up_bias_grad: float32 [8192], P('tensor')
- down_weight_grad: float32 [8192, 2048], P('tensor', 'dp')
- branch_bias_grad: float32 [2048], replicated
Inputs may be any that keep to these rules, and one draw needn't show every extreme that they name: `segments`: document numbers never fall along the array; each document has 1 to 512 tokens and one has exactly 512.
All inputs are finite; a program needn't handle non-finite values.
Results may differ from a plain program's by a relative error of at most 0.012.
Values may be sent and summed in bfloat16 or wider, within the bound.
No kernel may reach another device: no remote copies, remote signals or barrier semaphores. Data moves between devices by JAX's collectives and lax.ppermute only.
A program may use at most 384 MiB of HBM per device.

v0:
```python
from functools import partial

import jax
import jax.numpy as jnp
from jax import lax
from jax.sharding import PartitionSpec as P

HEAD_DIM = 64
ROT_DIM = 32


NEGATIVE = -1e30
EPSILON = 1e-05


def layer_stats(inputs):
    average = jnp.mean(inputs, axis=-1, keepdims=True)
    centered = inputs - average
    variance = jnp.mean(centered * centered, axis=-1, keepdims=True)
    inv_std = lax.rsqrt(variance + EPSILON)
    return (centered * inv_std, inv_std)


def doc_positions(segment_ids):
    places = jnp.arange(segment_ids.shape[0], dtype=jnp.int32)
    begins = jnp.concatenate([jnp.ones((1,), dtype=bool), segment_ids[1:] != segment_ids[:-1]])
    opening = lax.cummax(jnp.where(begins, places, 0), axis=0)
    return places - opening


def rotary_tables(places):
    halfway = ROT_DIM // 2
    freqs = 10000.0 ** (-jnp.arange(halfway, dtype=jnp.float32) * 2.0 / ROT_DIM)
    angles = places.astype(jnp.float32)[:, None] * freqs[None, :]
    return (jnp.cos(angles), jnp.sin(angles))


def rotate(vectors, cosine, sine):
    halfway = ROT_DIM // 2
    first_half = vectors[..., :halfway]
    second_half = vectors[..., halfway:ROT_DIM]
    cos_b = cosine[:, None, :]
    sin_b = sine[:, None, :]
    return jnp.concatenate(
        [
            first_half * cos_b - second_half * sin_b,
            second_half * cos_b + first_half * sin_b,
            vectors[..., ROT_DIM:],
        ],
        axis=-1,
    )


def block_allowed(segment_ids, first_row, block_rows):
    query_pos = first_row + jnp.arange(block_rows, dtype=jnp.int32)
    key_pos = jnp.arange(segment_ids.shape[0], dtype=jnp.int32)
    return (segment_ids[:, None] == segment_ids[None, :]) & (query_pos[:, None] >= key_pos[None, :])


def block_scores(q_block, key_rows, allowed):
    scores = jnp.einsum(
        "qhd,khd->hqk", q_block, key_rows, preferred_element_type=jnp.float32
    ) * HEAD_DIM ** (-0.5)
    return jnp.where(allowed[None], scores, NEGATIVE)


def local(
    tokens,
    segments,
    ln_gain,
    ln_shift,
    qkv_weight,
    qkv_bias,
    out_weight,
    up_weight,
    up_bias,
    down_weight,
    branch_bias,
    cotangent,
):
    row_count, model_width = tokens.shape
    inner_width = qkv_weight.shape[2]
    head_count = inner_width // HEAD_DIM
    block_rows = min(512, row_count)
    starts = jnp.arange(row_count // block_rows, dtype=jnp.int32) * block_rows
    contract_last = (((1,), (1,)), ((), ()))
    contract_first = (((0,), (0,)), ((), ()))
    weight_pieces = 4
    inputs = tokens.astype(jnp.float32)
    normal_x, inv_std = layer_stats(inputs)
    gain_f = ln_gain.astype(jnp.float32)
    normed = (normal_x * gain_f + ln_shift.astype(jnp.float32)).astype(jnp.bfloat16)
    joined_in = jnp.concatenate(
        [qkv_weight.reshape(qkv_weight.shape[0], 3 * inner_width), up_weight], axis=1
    )
    joined_out = jnp.concatenate([out_weight, down_weight], axis=0)
    in_step = joined_in.shape[1] // weight_pieces
    out_step = joined_out.shape[0] // weight_pieces
    pieces_made = []
    for number in range(weight_pieces):
        block_w = lax.all_gather(
            joined_in[:, number * in_step : (number + 1) * in_step], "dp", axis=0, tiled=True
        )
        pieces_made.append(jnp.dot(normed, block_w, preferred_element_type=jnp.float32))
    projected = jnp.concatenate(pieces_made, axis=1)
    qkv_pre = projected[:, : 3 * inner_width] + qkv_bias.astype(jnp.float32).reshape(
        3 * inner_width
    )
    qkv_pre = qkv_pre.reshape(row_count, 3, head_count, HEAD_DIM)
    places = doc_positions(segments)
    cosine, sine = rotary_tables(places)
    queries = rotate(qkv_pre[:, 0], cosine, sine).astype(jnp.bfloat16)
    key_rows = rotate(qkv_pre[:, 1], cosine, sine).astype(jnp.bfloat16)
    value_rows = qkv_pre[:, 2].astype(jnp.bfloat16)

    def attend_block(first_row):
        scores = block_scores(queries, key_rows, block_allowed(segments, first_row, block_rows))
        row_max = jnp.max(scores, axis=-1, keepdims=True)
        exponent = jnp.exp(scores - row_max)
        summed = jnp.sum(exponent, axis=-1, keepdims=True)
        prob_low = (exponent / summed).astype(jnp.bfloat16)
        attn_out = jnp.einsum(
            "hqk,khd->qhd", prob_low, value_rows, preferred_element_type=jnp.float32
        )
        return (attn_out.astype(jnp.bfloat16), (row_max + jnp.log(summed))[..., 0])

    attn_blocks, log_totals = lax.map(attend_block, starts)
    attended = attn_blocks.reshape(row_count, inner_width)
    up_pre = projected[:, 3 * inner_width :] + up_bias.astype(jnp.float32)
    activated, gelu_pull = jax.vjp(partial(jax.nn.gelu, approximate=True), up_pre)
    mixed_act = jnp.concatenate([attended, activated.astype(jnp.bfloat16)], axis=1)
    branch_part = jnp.zeros((row_count, model_width), jnp.float32)
    for number in range(weight_pieces):
        block_w = lax.all_gather(
            joined_out[number * out_step : (number + 1) * out_step], "dp", axis=1, tiled=True
        )
        branch_part = branch_part + jnp.dot(
            mixed_act[:, number * out_step : (number + 1) * out_step],
            block_w,
            preferred_element_type=jnp.float32,
        )
    branches = lax.psum(branch_part, "tensor")
    result = (inputs + branches + branch_bias.astype(jnp.float32)).astype(jnp.bfloat16)
    grad_out = cotangent.astype(jnp.float32)
    grad_pieces = []
    for number in range(weight_pieces):
        block_w = lax.all_gather(
            joined_out[number * out_step : (number + 1) * out_step], "dp", axis=1, tiled=True
        )
        grad_pieces.append(
            lax.dot_general(cotangent, block_w, contract_last, preferred_element_type=jnp.float32)
        )
    mix_grad = jnp.concatenate(grad_pieces, axis=1)
    up_grad = gelu_pull(mix_grad[:, inner_width:])[0].astype(jnp.bfloat16)
    attn_grad = (
        mix_grad[:, :inner_width].astype(jnp.bfloat16).reshape(row_count, head_count, HEAD_DIM)
    )

    def back_block(running, block_in):
        key_grad, value_grad = running
        first_row, log_total = block_in
        scores = block_scores(queries, key_rows, block_allowed(segments, first_row, block_rows))
        probs = jnp.exp(scores - log_total[..., None])
        prob_low = probs.astype(jnp.bfloat16)
        value_grad = value_grad + jnp.einsum(
            "hqk,qhd->khd", prob_low, attn_grad, preferred_element_type=jnp.float32
        )
        prob_grad = jnp.einsum(
            "qhd,khd->hqk", attn_grad, value_rows, preferred_element_type=jnp.float32
        )
        inner_dot = jnp.sum(probs * prob_grad, axis=-1, keepdims=True)
        score_grad = (probs * (prob_grad - inner_dot)).astype(jnp.bfloat16)
        scaling = HEAD_DIM ** (-0.5)
        query_grad = (
            jnp.einsum("hqk,khd->qhd", score_grad, key_rows, preferred_element_type=jnp.float32)
            * scaling
        )
        key_grad = (
            key_grad
            + jnp.einsum("hqk,qhd->khd", score_grad, queries, preferred_element_type=jnp.float32)
            * scaling
        )
        return ((key_grad, value_grad), query_grad)

    zero_heads = jnp.zeros((row_count, head_count, HEAD_DIM), jnp.float32)
    (key_grad, value_grad), query_blocks = lax.scan(
        back_block, (zero_heads, zero_heads), (starts, log_totals)
    )
    query_grad = query_blocks.reshape(row_count, head_count, HEAD_DIM)
    qkv_grad = jnp.stack(
        [rotate(query_grad, cosine, -sine), rotate(key_grad, cosine, -sine), value_grad], axis=1
    )
    qkv_grad = qkv_grad.astype(jnp.bfloat16).reshape(row_count, 3 * inner_width)
    in_grad = jnp.concatenate([qkv_grad, up_grad], axis=1)
    normed_grad = jnp.zeros((row_count, model_width), jnp.float32)
    for number in range(weight_pieces):
        block_w = lax.all_gather(
            joined_in[:, number * in_step : (number + 1) * in_step], "dp", axis=0, tiled=True
        )
        normed_grad = normed_grad + lax.dot_general(
            in_grad[:, number * in_step : (number + 1) * in_step],
            block_w,
            contract_last,
            preferred_element_type=jnp.float32,
        )
    normed_grad = lax.psum(normed_grad, "tensor")
    scaled = normed_grad * gain_f
    input_grad = grad_out + inv_std * (
        scaled
        - jnp.mean(scaled, axis=-1, keepdims=True)
        - normal_x * jnp.mean(scaled * normal_x, axis=-1, keepdims=True)
    )
    gain_local = jnp.sum(normed_grad * normal_x, axis=0)
    shift_local = jnp.sum(normed_grad, axis=0)
    in_cols = in_grad.shape[1]
    shares = lax.psum_scatter(
        jnp.concatenate(
            [
                lax.dot_general(
                    normed, in_grad, contract_first, preferred_element_type=jnp.float32
                ),
                lax.dot_general(
                    cotangent, mixed_act, contract_first, preferred_element_type=jnp.float32
                ),
            ],
            axis=1,
        ),
        "dp",
        scatter_dimension=0,
        tiled=True,
    )
    in_shares = shares[:, :in_cols]
    out_shares = shares[:, in_cols:]
    small = lax.psum(
        (
            gain_local,
            shift_local,
            jnp.sum(qkv_grad.astype(jnp.float32), axis=0).reshape(3, inner_width),
            jnp.sum(up_grad.astype(jnp.float32), axis=0),
            jnp.sum(grad_out, axis=0),
        ),
        "dp",
    )
    qkv_weight_grad = in_shares[:, : 3 * inner_width].reshape(in_shares.shape[0], 3, inner_width)
    up_weight_grad = in_shares[:, 3 * inner_width :]
    out_weight_grad = out_shares[:, :inner_width].T
    down_weight_grad = out_shares[:, inner_width:].T
    return (
        result,
        input_grad,
        small[0],
        small[1],
        qkv_weight_grad,
        small[2],
        out_weight_grad,
        up_weight_grad,
        small[3],
        down_weight_grad,
        small[4],
    )


def solution(mesh):
    return jax.shard_map(
        local,
        mesh=mesh,
        in_specs=(
            P("dp", None),
            P("dp"),
            P(),
            P(),
            P("dp", None, "tensor"),
            P(None, "tensor"),
            P("tensor", "dp"),
            P("dp", "tensor"),
            P("tensor"),
            P("tensor", "dp"),
            P(),
            P("dp", None),
        ),
        out_specs=(
            P("dp", None),
            P("dp", None),
            P(),
            P(),
            P("dp", None, "tensor"),
            P(None, "tensor"),
            P("tensor", "dp"),
            P("dp", "tensor"),
            P("tensor"),
            P("tensor", "dp"),
            P(),
        ),
        check_vma=False,
    )
```

profile of v0, /device:TPU:0, one launch (start us, length us, event | category | flops | bytes accessed | tf_op | source)
XLA Modules:
  0.0 3629.2 jit_solution(4571264481491976837)
XLA Ops:
  21.8 93.8 %all-gather.17.cloned.1.call-done = bf16[1280,2048]{1,0:T(8,128)(2,1)} async-done(((bf16[1280,128]{1,0:T(8,128)(2,1)}), bf16[1280,2048]{1,0:T(8,128)(2,1)}) %all-gather.17.cloned.1.call-update) | async-done | bytes 5242896 | tf_op jit(solution)/shard_map/all_gather | solution.py:134
  126.1 93.1 %all-gather.23.cloned.1.call-done = bf16[1280,2048]{1,0:T(8,128)(2,1)} async-done(((bf16[1280,128]{1,0:T(8,128)(2,1)}), bf16[1280,2048]{1,0:T(8,128)(2,1)}) %all-gather.23.cloned.1.call-update) | async-done | bytes 5242896 | tf_op jit(solution)/shard_map/all_gather | solution.py:134
  219.2 7.5 fusion.87
  226.7 95.5 %all-gather.21.cloned.1.call-done = bf16[1280,2048]{1,0:T(8,128)(2,1)} async-done(((bf16[1280,128]{1,0:T(8,128)(2,1)}), bf16[1280,2048]{1,0:T(8,128)(2,1)}) %all-gather.21.cloned.1.call-update) | async-done | bytes 5242896 | tf_op jit(solution)/shard_map/all_gather | solution.py:134
  322.3 7.5 fusion.86
  329.8 95.9 %all-gather.19.cloned.1.call-done = bf16[1280,2048]{1,0:T(8,128)(2,1)} async-done(((bf16[1280,128]{1,0:T(8,128)(2,1)}), bf16[1280,2048]{1,0:T(8,128)(2,1)}) %all-gather.19.cloned.1.call-update) | async-done | bytes 5242896 | tf_op jit(solution)/shard_map/all_gather | solution.py:134
  425.7 7.5 fusion.85
  433.3 97.2 %all-gather.11.cloned.1.call-done = bf16[2048,1792]{1,0:T(8,128)(2,1)} async-done(((bf16[128,1792]{1,0:T(8,128)(2,1)}), bf16[2048,1792]{1,0:T(8,128)(2,1)}) %all-gather.11.cloned.1.call-update) | async-done | bytes 7340048 | tf_op jit(solution)/shard_map/all_gather | solution.py:101
  530.5 9.1 fusion.78
  539.7 121.2 %all-gather.9.cloned.1.call-done = bf16[2048,1792]{0,1:T(8,128)(2,1)} async-done(((bf16[128,1792]{0,1:T(8,128)(2,1)}), bf16[2048,1792]{0,1:T(8,128)(2,1)}) %all-gather.9.cloned.1.call-update) | async-done | bytes 7340048 | tf_op jit(solution)/shard_map/all_gather | solution.py:101
  660.8 8.0 fusion.80
  682.3 7.3 fusion.84
  689.6 8.7 fusion
  698.3 9.3 fusion.49
  708.9 11.9 multiply_reduce_fusion
  720.8 12.0 multiply_convert_fusion
  737.9 7.1 multiply_bitcast_fusion
  765.8 9.1 fusion.74
  774.9 95.2 %all-gather.13.cloned.1.call-done = bf16[2048,1792]{1,0:T(8,128)(2,1)} async-done(((bf16[128,1792]{1,0:T(8,128)(2,1)}), bf16[2048,1792]{1,0:T(8,128)(2,1)}) %all-gather.13.cloned.1.call-update) | async-done | bytes 7340048 | tf_op jit(solution)/shard_map/all_gather | solution.py:101
  870.2 7.4 fusion.76
  877.7 8.9 convert_reduce_fusion
  886.6 10.2 fusion.51
  896.7 7.1 fusion.53
  913.9 8.9 fusion.38
  922.8 8.7 fusion.40
  931.5 7.7 add_add_fusion.1
  939.2 10.1 add_add_fusion
  949.4 31.7 fusion.14
  981.1 22.2 convolution_bitcast_fusion
  1003.3 65.5 %pad_maximum_fusion = f32[2048,12288]{1,0:T(8,128)} fusion(f32[2048,5120]{1,0:T(8,128)} %convolution_bitcast_fusion, f32[2048,7168]{1,0:T(8,128)} %fusion.14), kind=kLoop, calls=%fused_computation | loop fusion | flops 25165824 | bytes 201326592 | tf_op jit(solution)/shard_map/concatenate | solution.py:217
  1082.5 79.0 %all-reduce.1 = (f32[2048]{0:T(1024)}, f32[2048]{0:T(1024)}, f32[3,1024]{1,0:T(4,128)}, f32[4096]{0:T(1024)}, f32[2048]{0:T(1024)}) all-reduce(f32[2048]{0:T(1024)S(1)} %get-tuple-element.95, f32[2048]{0:T(1024)S(1)} %get-tuple-element.98, f32[3,1024]{1,0:T(4,128)S(1)} %reshape.246, ...), channel_id=1, replica_groups=mesh['dp'=16,'tensor'=2] {'dp'}, use_global_device_ids=true, to_apply=%region_12.13 | all-reduce | flops 13312 | bytes 106496 | tf_op jit(solution)/shard_map/psum | solution.py:234
  1161.5 2448.3 %all-reduce.6.cloned.1.call-done = f32[2048,12288]{1,0:T(8,128)} async-done(((f32[2048,12288]{1,0:T(8,128)}), f32[2048,12288]{1,0:T(8,128)}) %all-reduce.6.cloned.1.call-update) | async-done | bytes 100663312
  (186 shorter events, 100.8 us)
Async XLA Ops:
  7.2 108.4 %all-gather.17.cloned.1.call-start = ((), (), s32[]{:S(2)}) async-start(), calls=%async_computation.4 | async-start | bytes 5570560 | tf_op jit(solution)/shard_map/all_gather | solution.py:134
  9.7 209.6 %all-gather.23.cloned.1.call-start = ((), (), s32[]{:S(2)}) async-start(), calls=%async_computation.7 | async-start | bytes 5570560 | tf_op jit(solution)/shard_map/all_gather | solution.py:134
  10.4 311.9 %all-gather.21.cloned.1.call-start = ((), (), s32[]{:S(2)}) async-start(), calls=%async_computation.6 | async-start | bytes 5570560 | tf_op jit(solution)/shard_map/all_gather | solution.py:134
  11.2 414.6 %all-gather.19.cloned.1.call-start = ((), (), s32[]{:S(2)}) async-start(), calls=%async_computation.5 | async-start | bytes 5570560 | tf_op jit(solution)/shard_map/all_gather | solution.py:134
  11.7 518.8 %all-gather.11.cloned.1.call-start = ((), (), s32[]{:S(2)}) async-start(), calls=%async_computation.1 | async-start | bytes 7798784 | tf_op jit(solution)/shard_map/all_gather | solution.py:101
  15.8 645.0 %all-gather.9.cloned.1.call-start = ((), (), s32[]{:S(2)}) async-start(), calls=%async_computation | async-start | bytes 7798784 | tf_op jit(solution)/shard_map/all_gather | solution.py:101
  16.7 749.1 %all-gather.15.cloned.1.call-start = ((), (), s32[]{:S(2)}) async-start(), calls=%async_computation.3 | async-start | bytes 7798784 | tf_op jit(solution)/shard_map/all_gather | solution.py:101
  17.5 852.7 %all-gather.13.cloned.1.call-start = ((), (), s32[]{:S(2)}) async-start(), calls=%async_computation.2 | async-start | bytes 7798784 | tf_op jit(solution)/shard_map/all_gather | solution.py:101
  18.2 1052.6 %all-reduce.8.cloned.1.call-start = ((), (), s32[]{:S(2)}) async-start(), calls=%async_computation.9 | async-start | bytes 16777216 | tf_op jit(solution)/shard_map/psum | solution.py:142
  19.2 641.6 %copy-start.24 = (f32[2048]{0:T(1024)}, f32[2048]{0:T(1024)S(1)}, u32[]{:S(2)}) copy-start(f32[2048]{0:T(1024)S(1)} %convert_element_type.81) | copy-start | bytes 24580
  20.3 640.6 %copy-start.22 = (f32[512]{0:T(512)}, f32[512]{0:T(512)S(1)}, u32[]{:S(2)}) copy-start(f32[512]{0:T(512)S(1)} %add_rsqrt_fusion) | copy-start | bytes 6148
  21.8 660.1 %copy-start.27 = (f32[512,16]{0,1:T(8,128)}, f32[512,16]{0,1:T(8,128)S(1)}, u32[]{:S(2)}) copy-start(f32[512,16]{0,1:T(8,128)S(1)} %get-tuple-element.139) | copy-start | bytes 98308
  660.8 8.0 copy-start.5
  681.9 7.7 copy-start.16
  708.9 11.9 copy-start.26
  732.8 14.8 slice-start
  732.8 14.8 slice-start.1
  737.0 10.5 slice-start.2
  737.9 9.7 slice-start.3
  755.8 9.9 copy-start.2
  755.8 10.0 copy-start.23
  755.8 10.0 copy-start.25
  774.9 102.7 %copy-start.32 = (f32[4096]{0:T(1024)S(1)}, f32[4096]{0:T(1024)}, u32[]{:S(2)}) copy-start(f32[4096]{0:T(1024)} %convert_element_type.88) | copy-start | bytes 49156
  886.5 44.9 %copy-start.11 = (bf16[512,4096]{1,0:T(8,128)(2,1)}, bf16[512,4096]{1,0:T(8,128)(2,1)S(1)}, u32[]{:S(2)}) copy-start(bf16[512,4096]{1,0:T(8,128)(2,1)S(1)} %get-tuple-element.112) | copy-start | bytes 12582916
  886.6 52.7 %copy-start.3 = (bf16[512,4096]{1,0:T(8,128)(2,1)}, bf16[512,4096]{1,0:T(8,128)(2,1)S(1)}, u32[]{:S(2)}) copy-start(bf16[512,4096]{1,0:T(8,128)(2,1)S(1)} %get-tuple-element.107) | copy-start | bytes 12582916
  886.6 17.3 slice-start.4
  886.6 22.9 slice-start.6
  896.7 12.7 slice-start.7
  913.9 8.9 copy-start.7
  913.9 17.6 slice-start.8
  922.8 8.7 slice-start.9
  949.4 2660.5 %all-reduce.6.cloned.1.call-start = ((), (), s32[]{:S(2)}) async-start(), calls=%async_computation.8 | async-start | bytes 201326592
  (29 other events, 163.2 us)
Sparse Core Ops, SparseCore 0:
  10.7 104.8 all-gather.16
  118.9 100.2 all-gather.22
  221.9 100.2 all-gather.20
  325.4 100.2 all-gather.18
  428.9 101.6 all-gather.10
  533.7 127.1 all-gather.8
  664.1 101.6 all-gather.14
  768.5 101.6 all-gather.12
  949.5 37.0 all-reduce.7
  1069.0 2540.7 all-reduce.5
where the time goes:
time: 3630 us
  waiting for transfers between devices  3150 us (87%)
  matrix products  220 us (6%)
  other arithmetic  123 us (3%)
  blocking collectives  79 us (2%)
  local copies, waits for them, and re-layouts  42.2 us (1%)
    unnamed x11, waiting for transfers between devices  2450 us
    all_gather x4, waiting for transfers between devices, local(): lax.all_gather(joined_out[number * out_step:(number + 1) * out_step], 'dp...  378 us
    all_gather x4, waiting for transfers between devices, local(): lax.all_gather(joined_in[:, number * in_step:(number + 1) * in_step], 'dp...  319 us
    psum x1, blocking collectives, local(): lax.psum((gain_local, shift_local, jnp.sum(qkv_grad.astype(jnp.float32),...  79 us
  transfers between devices with their start and end apart: 10, of which 9 were waited for; matrix products, arithmetic and copies ran while one was open for 8% of the time, Pallas kernels for 0%

commit v1 on v0

v1 whole, which is shorter than its diff:
```python
import jax
import jax.numpy as jnp
from jax import lax
from jax.sharding import PartitionSpec as P

HEAD_DIM = 64
ROT_DIM = 32
NEGATIVE = -1e30
EPSILON = 1e-05
GELU_A = 0.7978845608028654
GELU_B = 0.044715
X_BIT, Y_BIT, ZL_BIT = 0, 1, 2
BF = jnp.bfloat16
F32 = jnp.float32


def doc_positions(segment_ids):
    places = jnp.arange(segment_ids.shape[-1], dtype=jnp.int32)
    begins = jnp.concatenate(
        [jnp.ones(segment_ids.shape[:-1] + (1,), bool), segment_ids[:, 1:] != segment_ids[:, :-1]],
        axis=1,
    )
    opening = lax.cummax(jnp.where(begins, places, 0), axis=1)
    return places - opening


def rotary_tables(places):
    halfway = ROT_DIM // 2
    freqs = 10000.0 ** (-jnp.arange(halfway, dtype=F32) * 2.0 / ROT_DIM)
    angles = places.astype(F32)[..., None] * freqs
    return (jnp.cos(angles), jnp.sin(angles))


def rotate(vectors, cosine, sine):
    halfway = ROT_DIM // 2
    first_half = vectors[..., :halfway]
    second_half = vectors[..., halfway:ROT_DIM]
    cos_b = cosine[:, :, None, :]
    sin_b = sine[:, :, None, :]
    return jnp.concatenate(
        [
            first_half * cos_b - second_half * sin_b,
            second_half * cos_b + first_half * sin_b,
            vectors[..., ROT_DIM:],
        ],
        axis=-1,
    )


def local_part(dp_size):
    top_bits = [b for b in range(3, dp_size.bit_length() - 1)]
    gather_bits = top_bits + [Y_BIT]

    def swap(value, bit):
        return lax.ppermute(value, "dp", [(i, i ^ (1 << bit)) for i in range(dp_size)])

    def swap_core(value):
        return lax.ppermute(value, "tensor", [(0, 1), (1, 0)])

    def ordered(bit, own, other):
        return jnp.where(bit == 0, jnp.stack([own, other]), jnp.stack([other, own]))

    def pick(value, index):
        return lax.dynamic_index_in_dim(value, index, 0, keepdims=False)

    def local(
        tokens,
        segments,
        ln_gain,
        ln_shift,
        qkv_weight,
        qkv_bias,
        out_weight,
        up_weight,
        up_bias,
        down_weight,
        branch_bias,
        cotangent,
    ):
        rows, width = tokens.shape
        half = rows // 2
        share = qkv_weight.shape[0]
        me = lax.axis_index("dp")
        core = lax.axis_index("tensor")

        def my(bit):
            return (me >> bit) & 1

        x_mine, zl_mine = my(X_BIT), my(ZL_BIT)
        block = x_mine + 2 * zl_mine
        att = qkv_weight.shape[2] // 4
        hid = up_weight.shape[1] // 4
        heads = att // HEAD_DIM

        def to_mixed(value):
            lead = value.shape[:-1]
            split = value.reshape(lead + (width // (4 * share), 2, 2 * share))
            return jnp.swapaxes(split, -3, -2).reshape(lead + (width,))

        def from_mixed(value):
            lead = value.shape[:-1]
            split = value.reshape(lead + (2, width // (4 * share), 2 * share))
            return jnp.swapaxes(split, -3, -2).reshape(lead + (width,))

        def gather_weight(piece):
            cols = piece.shape[2]
            w = piece.reshape(share, 2, 2, cols).transpose(2, 1, 0, 3)
            w = ordered(x_mine, pick(w, x_mine), swap(pick(w, 1 - x_mine), X_BIT))
            w = jnp.swapaxes(w, 0, 1)
            w = ordered(zl_mine, pick(w, zl_mine), swap(pick(w, 1 - zl_mine), ZL_BIT))
            for bit in gather_bits:
                w = ordered(my(bit), w, swap(w, bit))
            return w.reshape(width, cols)

        def scatter_grad(grad):
            cols = grad.shape[1]
            for bit in reversed(gather_bits):
                grad = grad.reshape((2, -1, cols))
                got = swap(pick(grad, 1 - my(bit)), bit)
                grad = (pick(grad, my(bit)).astype(F32) + got.astype(F32)).astype(BF)
            g = grad.reshape(2, 2, share, cols)
            g = ordered(zl_mine, pick(g, zl_mine), swap(pick(g, 1 - zl_mine), ZL_BIT))
            g = jnp.swapaxes(g, 0, 1)
            g = ordered(x_mine, pick(g, x_mine), swap(pick(g, 1 - x_mine), X_BIT))
            return g.transpose(2, 1, 0, 3).reshape(share, 4, cols).astype(F32)

        def gather_act(piece):
            a = jnp.stack([piece, swap(piece, ZL_BIT)])
            a = jnp.stack([a, swap(a, X_BIT)])
            a = a.reshape(4, half, width)
            a = ordered(core, a, swap_core(a))
            return jnp.swapaxes(a, 0, 1).reshape(4 * rows, width)

        def scatter_act(part):
            p = part.reshape(4, 2, half, width).swapaxes(0, 1)
            got = swap_core(pick(p, 1 - core).astype(BF))
            p = pick(p, core) + got.astype(F32)
            p = p.reshape(2, 2, half, width)
            p = p[0] + swap(p[1].astype(BF), X_BIT).astype(F32)
            return p[0] + swap(p[1].astype(BF), ZL_BIT).astype(F32)

        def both_cores(value):
            return ordered(core, value, swap_core(value)).reshape((rows,) + value.shape[1:])

        my_tokens = pick(tokens.reshape(2, half, width), core).astype(F32)
        my_cot = pick(cotangent.reshape(2, half, width), core)
        average = jnp.mean(my_tokens, axis=-1, keepdims=True)
        centered = my_tokens - average
        inv_std = lax.rsqrt(jnp.mean(centered * centered, axis=-1, keepdims=True) + EPSILON)
        normal_x = centered * inv_std
        gain_f = ln_gain.astype(F32)
        my_normed = (normal_x * gain_f + ln_shift.astype(F32)).astype(BF)

        qkv_full = gather_weight(
            qkv_weight.reshape(share, 3, 4, att).swapaxes(1, 2).reshape(share, 4, 3 * att)
        )
        normed = gather_act(to_mixed(my_normed))
        up_full = gather_weight(up_weight.reshape(share, 4, hid))
        cot = gather_act(to_mixed(my_cot))
        out_full = gather_weight(out_weight.T.reshape(share, 4, att))
        down_full = gather_weight(down_weight.T.reshape(share, 4, hid))

        seg = jnp.stack([segments, swap(segments, ZL_BIT)])
        seg = jnp.stack([seg, swap(seg, X_BIT)]).reshape(4, rows)
        places = doc_positions(seg)
        cosine, sine = rotary_tables(places)
        order = jnp.arange(rows, dtype=jnp.int32)
        allowed = (seg[:, :, None] == seg[:, None, :]) & (order[:, None] >= order[None, :])[None]

        my_qkv_bias = lax.dynamic_slice_in_dim(qkv_bias, block * att, att, 1).astype(F32)
        my_up_bias = lax.dynamic_slice_in_dim(up_bias, block * hid, hid, 0).astype(F32)

        qkv_pre = jnp.dot(normed, qkv_full, preferred_element_type=F32) + my_qkv_bias.reshape(-1)
        qkv_pre = qkv_pre.reshape(4, rows, 3, heads, HEAD_DIM)
        queries = rotate(qkv_pre[:, :, 0], cosine, sine).astype(BF)
        key_rows = rotate(qkv_pre[:, :, 1], cosine, sine).astype(BF)
        value_rows = qkv_pre[:, :, 2].astype(BF)
        scaling = HEAD_DIM ** (-0.5)
        scores = (
            jnp.einsum("sqhd,skhd->shqk", queries, key_rows, preferred_element_type=F32) * scaling
        )
        scores = jnp.where(allowed[:, None], scores, NEGATIVE)
        row_max = jnp.max(scores, axis=-1, keepdims=True)
        exponent = jnp.exp(scores - row_max)
        summed = jnp.sum(exponent, axis=-1, keepdims=True)
        probs = exponent / summed
        prob_low = probs.astype(BF)
        attended = (
            jnp.einsum("shqk,skhd->sqhd", prob_low, value_rows, preferred_element_type=F32)
            .astype(BF)
            .reshape(4 * rows, att)
        )

        up_pre = jnp.dot(normed, up_full, preferred_element_type=F32) + my_up_bias
        squared = up_pre * up_pre
        th = jnp.tanh(GELU_A * (up_pre + GELU_B * up_pre * squared))
        act = (0.5 * up_pre * (1.0 + th)).astype(BF)
        slope = 0.5 * (1.0 + th) + 0.5 * up_pre * (1.0 - th * th) * (
            GELU_A * (1.0 + 3.0 * GELU_B * squared)
        )

        first = (((0,), (0,)), ((), ()))
        last = (((1,), (1,)), ((), ()))
        out_grad = scatter_grad(lax.dot_general(cot, attended, first, preferred_element_type=BF))
        down_grad = scatter_grad(lax.dot_general(cot, act, first, preferred_element_type=BF))

        branches = lax.dot_general(
            attended, out_full, last, preferred_element_type=F32
        ) + lax.dot_general(act, down_full, last, preferred_element_type=F32)
        branches = from_mixed(scatter_act(branches))
        result = both_cores((my_tokens + branches + branch_bias.astype(F32)).astype(BF))

        act_grad = jnp.dot(cot, down_full, preferred_element_type=F32)
        up_g = (act_grad * slope).astype(BF)
        up_grad = scatter_grad(lax.dot_general(normed, up_g, first, preferred_element_type=BF))
        attn_grad = (
            jnp.dot(cot, out_full, preferred_element_type=F32)
            .astype(BF)
            .reshape(4, rows, heads, HEAD_DIM)
        )
        value_grad = jnp.einsum("shqk,sqhd->skhd", prob_low, attn_grad, preferred_element_type=F32)
        prob_grad = jnp.einsum("sqhd,skhd->shqk", attn_grad, value_rows, preferred_element_type=F32)
        inner = jnp.sum(probs * prob_grad, axis=-1, keepdims=True)
        score_grad = (probs * (prob_grad - inner)).astype(BF)
        query_grad = (
            jnp.einsum("shqk,skhd->sqhd", score_grad, key_rows, preferred_element_type=F32)
            * scaling
        )
        key_grad = (
            jnp.einsum("shqk,sqhd->skhd", score_grad, queries, preferred_element_type=F32) * scaling
        )
        qkv_g = (
            jnp.stack(
                [rotate(query_grad, cosine, -sine), rotate(key_grad, cosine, -sine), value_grad],
                axis=2,
            )
            .astype(BF)
            .reshape(4 * rows, 3 * att)
        )
        qkv_grad = scatter_grad(lax.dot_general(normed, qkv_g, first, preferred_element_type=BF))

        normed_grad = lax.dot_general(
            qkv_g, qkv_full, last, preferred_element_type=F32
        ) + lax.dot_general(up_g, up_full, last, preferred_element_type=F32)
        normed_grad = from_mixed(scatter_act(normed_grad))
        scaled = normed_grad * gain_f
        input_grad = my_cot.astype(F32) + inv_std * (
            scaled
            - jnp.mean(scaled, axis=-1, keepdims=True)
            - normal_x * jnp.mean(scaled * normal_x, axis=-1, keepdims=True)
        )
        input_grad = both_cores(input_grad)

        def placed(value, wide):
            full = jnp.zeros(value.shape[:-1] + (wide,), F32)
            return lax.dynamic_update_slice_in_dim(
                full, value, block * value.shape[-1], value.ndim - 1
            )

        qkv_b, up_b = lax.psum(
            (
                placed(jnp.sum(qkv_g.astype(F32), axis=0).reshape(3, att), 4 * att),
                placed(jnp.sum(up_g.astype(F32), axis=0), 4 * hid),
            ),
            "dp",
        )
        gain_g, shift_g, branch_g = lax.psum(
            (
                jnp.sum(normed_grad * normal_x, axis=0),
                jnp.sum(normed_grad, axis=0),
                jnp.sum(my_cot.astype(F32), axis=0),
            ),
            ("dp", "tensor"),
        )
        return (
            result,
            input_grad,
            gain_g,
            shift_g,
            qkv_grad.reshape(share, 4, 3, att).swapaxes(1, 2).reshape(share, 3, 4 * att),
            qkv_b,
            out_grad.reshape(share, 4 * att).T,
            up_grad.reshape(share, 4 * hid),
            up_b,
            down_grad.reshape(share, 4 * hid).T,
            branch_g,
        )

    return local


def solution(mesh):
    return jax.shard_map(
        local_part(mesh.shape["dp"]),
        mesh=mesh,
        in_specs=(
            P("dp", None),
            P("dp"),
            P(),
            P(),
            P("dp", None, "tensor"),
            P(None, "tensor"),
            P("tensor", "dp"),
            P("dp", "tensor"),
            P("tensor"),
            P("tensor", "dp"),
            P(),
            P("dp", None),
        ),
        out_specs=(
            P("dp", None),
            P("dp", None),
            P(),
            P(),
            P("dp", None, "tensor"),
            P(None, "tensor"),
            P("tensor", "dp"),
            P("dp", "tensor"),
            P("tensor"),
            P("tensor", "dp"),
            P(),
        ),
        check_vma=False,
    )
```

time: 3630 us -> 1120 us (0.31)
  waiting for transfers between devices: 3150 us -> 341 us
  local copies, waits for them, and re-layouts: 42.2 us -> 248 us
  other arithmetic: 123 us -> 173 us
  matrix products: 220 us -> 171 us
  starting transfers between devices: 0.39 us -> 47.1 us
  blocking collectives: 79 us -> 122 us
    unnamed x11 -> x0, waiting for transfers between devices: 2450 us -> none
    all_gather x8 -> x0, waiting for transfers between devices: 697 us -> none  [the longest x4 378 us: local(): lax.all_gather(joined_out[number * out_step:(number + 1) * out_step], 'dp...]
    ppermute x0 -> x48, waiting for transfers between devices: none -> 341 us  [the longest x42 341 us: swap(): lax.ppermute(value, 'dp', [(i, i ^ 1 << bit) for i in range(dp_size)])]
    concatenate x2 -> x0, other arithmetic: 67.9 us -> none  [the longest x1 65.5 us: local(): jnp.concatenate([lax.dot_general(normed, in_grad, contract_first, preferr...]
    another operation x1 -> x30, local copies, waits for them, and re-layouts: 0.12 us -> 65.1 us
    dot_general x24 -> x17, matrix products: 220 us -> 159 us  [the longest x1 17.2 us: local(): act_grad = jnp.dot(cot, down_full, preferred_element_type=F32)]
    select_n x1 -> x31, other arithmetic: 0.08 us -> 54.9 us  [the longest x30 54.8 us: ordered(): return jnp.where(bit == 0, jnp.stack([own, other]), jnp.stack([other, own]))]
    ppermute x0 -> x48, starting transfers between devices: none -> 47.1 us  [the longest x42 46.3 us: swap(): lax.ppermute(value, 'dp', [(i, i ^ 1 << bit) for i in range(dp_size)])]
  transfers between devices with their start and end apart: 10 -> 48, of which waited for: 9 -> 21; matrix products, arithmetic and copies ran while one was open for 8% -> 35% of each run, Pallas kernels for 0% -> 0%
where the time goes in v1:
time: 1120 us; the launch traced here: 1100 us
  waiting for transfers between devices  341 us (30%)
  local copies, waits for them, and re-layouts  248 us (22%)
  other arithmetic  173 us (15%)
  matrix products  171 us (15%)
  blocking collectives  122 us (11%)
  starting transfers between devices  47.1 us (4%)
    ppermute x42, waiting for transfers between devices, swap(): lax.ppermute(value, 'dp', [(i, i ^ 1 << bit) for i in range(dp_size)])  341 us
    psum x1, blocking collectives, local(): lax.psum((placed(jnp.sum(qkv_g.astype(F32), axis=0).reshape(3, att), 4 *...  84.8 us
    select_n x30, other arithmetic, ordered(): return jnp.where(bit == 0, jnp.stack([own, other]), jnp.stack([other, own]))  54.8 us
    another operation x27, local copies, waits for them, and re-layouts  50.1 us
    ppermute x42, starting transfers between devices, swap(): lax.ppermute(value, 'dp', [(i, i ^ 1 << bit) for i in range(dp_size)])  46.3 us
    unnamed x188, local copies, waits for them, and re-layouts  40.5 us
    psum x1, blocking collectives, local(): lax.psum((jnp.sum(normed_grad * normal_x, axis=0), jnp.sum(normed_grad, a...  37.4 us
  transfers between devices with their start and end apart: 48, of which 21 were waited for; matrix products, arithmetic and copies ran while one was open for 35% of the time, Pallas kernels for 0%

profile of v1, /device:TPU:0, one launch (start us, length us, event | category | flops | bytes accessed | tf_op | source)
XLA Modules:
  0.0 1104.9 jit_solution(5990343281462090086)
XLA Ops:
  48.1 17.8 %collective-permute-done = bf16[256,2048]{0,1:T(8,128)(2,1)S(1)} collective-permute-done((bf16[256,2048]{0,1:T(8,128)(2,1)S(1)}, bf16[256,2048]{0,1:T(8,128)(2,1)S(1)}, u32[]{:S(2)}, u32[]{:S(2)}) %collective-permute-start) | collective-permute-done | bytes 1048608 | tf_op jit(solution)/shard_map/ppermute | solution.py:55
  115.3 16.8 %collective-permute-done.14 = bf16[2,128,1024]{2,1,0:T(8,128)(2,1)S(1)} collective-permute-done((bf16[2,128,1024]{2,1,0:T(8,128)(2,1)}, bf16[2,128,1024]{2,1,0:T(8,128)(2,1)S(1)}, u32[]{:S(2)}, u32[]{:S(2)}) %collective-permute-start.14) | collective-permute-done | bytes 524320 | tf_op jit(solution)/shard_map/ppermute | solution.py:55
  160.3 57.4 %collective-permute-done.15 = bf16[2,2,128,1024]{3,2,1,0:T(8,128)(2,1)} collective-permute-done((bf16[2,2,128,1024]{3,2,1,0:T(8,128)(2,1)}, bf16[2,2,128,1024]{3,2,1,0:T(8,128)(2,1)}, u32[]{:S(2)}, u32[]{:S(2)}) %collective-permute-start.15) | collective-permute-done | bytes 1048608 | tf_op jit(solution)/shard_map/ppermute | solution.py:55
  221.5 12.9 %collective-permute-done.5 = bf16[2,2,128,768]{3,2,1,0:T(8,128)(2,1)S(1)} collective-permute-done((bf16[2,2,128,768]{3,2,1,0:T(8,128)(2,1)S(1)}, bf16[2,2,128,768]{3,2,1,0:T(8,128)(2,1)S(1)}, u32[]{:S(2)}, u32[]{:S(2)}) %collective-permute-start.5) | collective-permute-done | bytes 786464 | tf_op jit(solution)/shard_map/ppermute | solution.py:55
  236.5 12.1 %collective-permute-done.19 = bf16[2,2,128,1024]{3,2,1,0:T(8,128)(2,1)S(1)} collective-permute-done((bf16[2,2,128,1024]{3,2,1,0:T(8,128)(2,1)S(1)}, bf16[2,2,128,1024]{3,2,1,0:T(8,128)(2,1)S(1)}, u32[]{:S(2)}, u32[]{:S(2)}) %collective-permute-start.19) | collective-permute-done | bytes 1048608 | tf_op jit(solution)/shard_map/ppermute | solution.py:55
  285.5 31.6 %collective-permute-done.6 = bf16[2,2,2,128,768]{4,3,2,1,0:T(8,128)(2,1)} collective-permute-done((bf16[2,2,2,128,768]{4,3,2,1,0:T(8,128)(2,1)}, bf16[2,2,2,128,768]{4,3,2,1,0:T(8,128)(2,1)}, u32[]{:S(2)}, u32[]{:S(2)}) %collective-permute-start.6) | collective-permute-done | bytes 1572896 | tf_op jit(solution)/shard_map/ppermute | solution.py:55
  324.5 25.5 %collective-permute-done.20 = bf16[2,2,2,128,1024]{4,3,2,1,0:T(8,128)(2,1)} collective-permute-done((bf16[2,2,2,128,1024]{4,3,2,1,0:T(8,128)(2,1)}, bf16[2,2,2,128,1024]{4,3,2,1,0:T(8,128)(2,1)}, u32[]{:S(2)}, u32[]{:S(2)}) %collective-permute-start.20) | collective-permute-done | bytes 2097184 | tf_op jit(solution)/shard_map/ppermute | solution.py:55
  371.0 10.7 broadcast_add_fusion
  381.7 11.9 %reshape.1286 = f32[4,512,3,4,64]{4,3,2,1,0:T(4,128)} reshape(f32[2048,768]{1,0:T(8,128)} %broadcast_add_fusion) | data formatting | bytes 12582912 | tf_op jit(solution)/shard_map/reshape | solution.py:174
  413.3 8.5 copy.181
  421.9 13.4 %fusion.80 = f32[2048,1024]{1,0:T(8,128)} fusion(bf16[2048,2048]{1,0:T(8,128)(2,1)} %bitcast.386, bf16[2048,1024]{1,0:T(8,128)(2,1)S(1)} %bitcast.447), kind=kOutput, calls=%fused_computation.246 | convolution fusion | flops 8589934592 | bytes 20971520 | tf_op jit(solution)/shard_map/dot_general | solution.py:194
  435.3 15.6 %fusion.77 = f32[2048,2048]{1,0:T(8,128)} fusion(bf16[2048,1024]{1,0:T(8,128)(2,1)S(1)} %bitcast.450, f32[2048,1024]{1,0:T(8,128)} %fusion.80, f32[1024]{0:T(1024)S(1)} %copy-done.76), kind=kOutput, calls=%fused_computation.243 | convolution fusion | flops 8610906112 | bytes 29364224 | tf_op jit(solution)/shard_map/dot_general | solution.py:209
  450.8 17.2 %convert_reduce_fusion = (f32[1024]{0:T(1024)}, bf16[2048,1024]{1,0:T(8,128)(2,1)}) fusion(f32[2048,1024]{1,0:T(8,128)} %fusion.80, f32[1024]{0:T(1024)S(1)} %copy-done.76, bf16[2048,2048]{1,0:T(8,128)(2,1)S(1)} %bitcast.383, bf16[2048,1024]{1,0:T(8,128)(2,1)S(1)} %bitcast.451), kind=kOutput, calls=%fused_computation.13 | convolution fusion | flops 8633973760 | bytes 25174016 | tf_op jit(solution)/shard_map/dot_general | solution.py:213
  490.0 12.0 %fusion.79 = (f32[4,4,512]{2,1,0:T(4,128)}, f32[4,4,512,512]{2,3,1,0:T(8,128)}) fusion(pred[4,512,512]{1,2,0:T(8,128)(4,1)} %compare_and_fusion, bf16[4,512,4,32]{1,3,2,0:T(8,128)(2,1)S(1)} %slice.190, bf16[4,512,4,16]{1,3,2,0:T(8,128)(2,1)} %get-tuple-element.98, bf16[4,512,4,16]{1,3,2,0:T(8,128)(2,1)} %get-tuple-element.99, ...), kind=kOutput, calls=%fused_computation.245 | convolution fusion | flops 559940096 | bytes 19955712 | tf_op jit(solution)/shard_map/sub | solution.py:184
  502.0 9.8 fusion.51
  517.0 9.5 multiply_reduce_fusion
  526.5 12.2 %multiply_convert_fusion = bf16[4,4,512,512]{2,3,1,0:T(8,128)(2,1)S(1)} fusion(f32[4,4,512,512]{2,3,1,0:T(8,128)} %get-tuple-element.108, f32[4,4,512]{2,1,0:T(4,128)} %get-tuple-element.107, f32[4,4,512,512]{2,3,1,0:T(8,128)} %get-tuple-element.106, f32[4,4,512]{2,1,0:T(4,128)} %get-tuple-element.105), kind=kLoop, calls=%fused_computation.1 | loop fusion | flops 16777216 | bytes 42008576 | tf_op jit(solution)/shard_map/convert_element_type | solution.py:224
  544.2 12.3 %copy.228 = bf16[2048,2048]{1,0:T(8,128)(2,1)} copy(bf16[2048,2048]{0,1:T(8,128)(2,1)} %bitcast.387) | data formatting | bytes 16777216 | tf_op jit(solution)/shard_map/dot_general | solution.py:240
  564.3 10.4 fusion.81
  582.8 9.4 fusion.12
  596.9 12.3 %copy.229 = bf16[2048,2048]{1,0:T(8,128)(2,1)} copy(bf16[2048,2048]{0,1:T(8,128)(2,1)} %bitcast.380) | data formatting | bytes 16777216 | tf_op jit(solution)/shard_map/dot_general | solution.py:204
  609.2 15.7 %fusion.10 = bf16[2,1024,1024]{2,1,0:T(8,128)(2,1)} fusion(bf16[2,1024,2048]{2,1,0:T(8,128)(2,1)} %bitcast.424, f32[2048,1024]{1,0:T(8,128)} %fusion.80, f32[1024]{0:T(1024)S(1)} %copy-done.77), kind=kOutput, calls=%fused_computation.38 | convolution fusion | flops 8610906112 | bytes 20975616 | tf_op jit(solution)/shard_map/dot_general | solution.py:205
  630.2 17.1 %convolution_add_fusion.1 = f32[2048,2048]{1,0:T(8,128)} fusion(f32[2048,2048]{1,0:T(8,128)} %fusion.81, bf16[2048,1024]{1,0:T(8,128)(2,1)} %get-tuple-element.110, bf16[2048,1024]{1,0:T(8,128)(2,1)S(1)} %bitcast.448), kind=kOutput, calls=%fused_computation.22 | convolution fusion | flops 8594128896 | bytes 41943040 | tf_op jit(solution)/shard_map/dot_general | solution.py:244
  698.2 8.8 copy.189
  721.8 35.6 %collective-permute-done.44 = bf16[1024,1024]{1,0:T(8,128)(2,1)} collective-permute-done((bf16[1024,1024]{1,0:T(8,128)(2,1)}, bf16[1024,1024]{1,0:T(8,128)(2,1)}, u32[]{:S(2)}, u32[]{:S(2)}) %collective-permute-start.44) | collective-permute-done | bytes 2097184 | tf_op jit(solution)/shard_map/ppermute | solution.py:55
  789.0 24.0 %collective-permute-done.34 = bf16[2,128,768]{2,1,0:T(8,128)(2,1)S(1)} collective-permute-done((bf16[2,128,768]{2,1,0:T(8,128)(2,1)S(1)}, bf16[2,128,768]{2,1,0:T(8,128)(2,1)S(1)}, u32[]{:S(2)}, u32[]{:S(2)}) %collective-permute-start.34) | collective-permute-done | bytes 393248 | tf_op jit(solution)/shard_map/ppermute | solution.py:55
  815.5 12.7 %collective-permute-done.41 = bf16[512,1024]{1,0:T(8,128)(2,1)} collective-permute-done((bf16[512,1024]{1,0:T(8,128)(2,1)S(1)}, bf16[512,1024]{1,0:T(8,128)(2,1)}, u32[]{:S(2)}, u32[]{:S(2)}) %collective-permute-start.41) | collective-permute-done | bytes 1048608 | tf_op jit(solution)/shard_map/ppermute | solution.py:55
  831.9 18.7 %collective-permute-done.45 = bf16[512,1024]{1,0:T(8,128)(2,1)} collective-permute-done((bf16[512,1024]{1,0:T(8,128)(2,1)}, bf16[512,1024]{1,0:T(8,128)(2,1)}, u32[]{:S(2)}, u32[]{:S(2)}) %collective-permute-start.45) | collective-permute-done | bytes 1048608 | tf_op jit(solution)/shard_map/ppermute | solution.py:55
  870.3 17.7 %collective-permute-done.30 = bf16[256,2048]{0,1:T(8,128)(2,1)S(1)} collective-permute-done((bf16[256,2048]{0,1:T(8,128)(2,1)S(1)}, bf16[256,2048]{0,1:T(8,128)(2,1)S(1)}, u32[]{:S(2)}, u32[]{:S(2)}) %collective-permute-start.30) | collective-permute-done | bytes 1048608 | tf_op jit(solution)/shard_map/ppermute | solution.py:55
  891.6 18.9 %collective-permute-done.23 = bf16[256,2048]{1,0:T(8,128)(2,1)S(1)} collective-permute-done((bf16[256,2048]{1,0:T(8,128)(2,1)S(1)}, bf16[256,2048]{1,0:T(8,128)(2,1)S(1)}, u32[]{:S(2)}, u32[]{:S(2)}) %collective-permute-start.23) | collective-permute-done | bytes 1048608 | tf_op jit(solution)/shard_map/ppermute | solution.py:55
  942.6 84.8 %all-reduce.2 = (f32[3,1024]{1,0:T(4,128)}, f32[4096]{0:T(1024)}) all-reduce(f32[3,1024]{1,0:T(4,128)S(1)} %constant_dynamic-update-slice_fusion, f32[4096]{0:T(1024)S(1)} %copy-done.56), channel_id=1, replica_groups=mesh['dp'=16,'tensor'=2] {'dp'}, use_global_device_ids=true, to_apply=%region_14.15 | all-reduce | flops 7168 | bytes 57344 | tf_op jit(solution)/shard_map/psum | solution.py:260
  1055.5 37.4 %all-reduce.1 = (f32[2048]{0:T(1024)}, f32[2048]{0:T(1024)}, f32[2048]{0:T(1024)}) all-reduce(f32[2048]{0:T(1024)S(1)} %bitcast.502, f32[2048]{0:T(1024)S(1)} %bitcast.503, f32[2048]{0:T(1024)S(1)} %copy-done.60), channel_id=1, replica_groups=mesh['dp'=16,'tensor'=2] {'dp','tensor'}, use_global_device_ids=true, to_apply=%region_10.11 | all-reduce | flops 6144 | bytes 49152 | tf_op jit(solution)/shard_map/psum | solution.py:267
  (462 shorter events, 472.1 us)
Async XLA Ops:
  5.4 65.5 %collective-permute-start.9 = (bf16[2,128,256]{1,2,0:T(8,128)(2,1)}, bf16[2,128,256]{1,2,0:T(8,128)(2,1)}, u32[]{:S(2)}, u32[]{:S(2)}) collective-permute-start(bf16[2,128,256]{1,2,0:T(8,128)(2,1)} %get-tuple-element.97), channel_id=1, source_target_pairs={{0,2},{2,0},{4,6},{6,4},{8,10},{10,8},{12,14},{14,12},{16,18},{18,... | collective-permute-start | bytes 393224 | tf_op jit(solution)/shard_map/ppermute | solution.py:55
  9.3 71.9 %collective-permute-start.3 = (bf16[2,128,768]{1,2,0:T(8,128)(2,1)}, bf16[2,128,768]{1,2,0:T(8,128)(2,1)}, u32[]{:S(2)}, u32[]{:S(2)}) collective-permute-start(bf16[2,128,768]{1,2,0:T(8,128)(2,1)} %get-tuple-element.87), channel_id=1, source_target_pairs={{0,2},{2,0},{4,6},{6,4},{8,10},{10,8},{12,14},{14,12},{16,18},{18,... | collective-permute-start | bytes 1179656 | tf_op jit(solution)/shard_map/ppermute | solution.py:55
  12.6 73.3 %collective-permute-start.13 = (bf16[2,128,1024]{1,2,0:T(8,128)(2,1)}, bf16[2,128,1024]{1,2,0:T(8,128)(2,1)}, u32[]{:S(2)}, u32[]{:S(2)}) collective-permute-start(bf16[2,128,1024]{1,2,0:T(8,128)(2,1)} %get-tuple-element.75), channel_id=1, source_target_pairs={{0,2},{2,0},{4,6},{6,4},{8,10},{10,8},{12,14},{14,12},{16,18},{18,... | collective-permute-start | bytes 1572872 | tf_op jit(solution)/shard_map/ppermute | solution.py:55
  16.3 79.7 %collective-permute-start.17 = (bf16[2,128,1024]{1,2,0:T(8,128)(2,1)}, bf16[2,128,1024]{1,2,0:T(8,128)(2,1)}, u32[]{:S(2)}, u32[]{:S(2)}) collective-permute-start(bf16[2,128,1024]{1,2,0:T(8,128)(2,1)} %get-tuple-element.79), channel_id=1, source_target_pairs={{0,2},{2,0},{4,6},{6,4},{8,10},{10,8},{12,14},{14,12},{16,18},{18,... | collective-permute-start | bytes 1572872 | tf_op jit(solution)/shard_map/ppermute | solution.py:55
  70.0 64.2 %collective-permute-start.1 = (bf16[2,256,2048]{1,2,0:T(8,128)(2,1)}, bf16[2,256,2048]{1,2,0:T(8,128)(2,1)}, u32[]{:S(2)}, u32[]{:S(2)}) collective-permute-start(bf16[2,256,2048]{1,2,0:T(8,128)(2,1)} %get-tuple-element.63), channel_id=1, source_target_pairs={{0,2},{2,0},{4,6},{6,4},{8,10},{10,8},{12,14},{14,12},{16,18},{18,... | collective-permute-start | bytes 6291464 | tf_op jit(solution)/shard_map/ppermute | solution.py:55
  78.6 74.1 %collective-permute-start.25 = (bf16[256,2048]{0,1:T(8,128)(2,1)}, bf16[256,2048]{0,1:T(8,128)(2,1)}, u32[]{:S(2)}, u32[]{:S(2)}) collective-permute-start(bf16[256,2048]{0,1:T(8,128)(2,1)} %bitcast.458), channel_id=1, source_target_pairs={{0,8},{2,10},{4,12},{6,14},{8,0},{10,2},{12,4},{14,6},{16,24},{18,... | collective-permute-start | bytes 3145736 | tf_op jit(solution)/shard_map/ppermute | solution.py:55
  95.9 51.1 %collective-permute-start.4 = (bf16[2,128,768]{2,1,0:T(8,128)(2,1)}, bf16[2,128,768]{2,1,0:T(8,128)(2,1)}, u32[]{:S(2)}, u32[]{:S(2)}) collective-permute-start(bf16[2,128,768]{2,1,0:T(8,128)(2,1)} %bitcast.496), channel_id=1, source_target_pairs={{0,8},{2,10},{4,12},{6,14},{8,0},{10,2},{12,4},{14,6},{16,24},{18,... | collective-permute-start | bytes 1179656 | tf_op jit(solution)/shard_map/ppermute | solution.py:55
  133.3 84.4 %collective-permute-start.15 = (bf16[2,2,128,1024]{3,2,1,0:T(8,128)(2,1)}, bf16[2,2,128,1024]{3,2,1,0:T(8,128)(2,1)}, u32[]{:S(2)}, u32[]{:S(2)}) collective-permute-start(bf16[2,2,128,1024]{3,2,1,0:T(8,128)(2,1)} %maximum_select_fusion.16), channel_id=1, source_target_pairs={{0,16},{2,18},{4,20},{6,22},{8,24},{10,26},{12,28},{14,30},{16,0},... | collective-permute-start | bytes 3145736 | tf_op jit(solution)/shard_map/ppermute | solution.py:55
  144.8 209.9 %collective-permute-start.2 = (bf16[4,256,2048]{2,1,0:T(8,128)(2,1)}, bf16[4,256,2048]{2,1,0:T(8,128)(2,1)}, u32[]{:S(2)}, u32[]{:S(2)}) collective-permute-start(bf16[4,256,2048]{2,1,0:T(8,128)(2,1)} %copy.145), channel_id=1, source_target_pairs={{0,1},{1,0},{2,3},{3,2},{4,5},{5,4},{6,7},{7,6},{8,9},{9,8},{10,11... | collective-permute-start | bytes 12582920 | tf_op jit(solution)/shard_map/ppermute | solution.py:58
  148.3 86.2 %collective-permute-start.5 = (bf16[2,2,128,768]{3,2,1,0:T(8,128)(2,1)S(1)}, bf16[2,2,128,768]{3,2,1,0:T(8,128)(2,1)S(1)}, u32[]{:S(2)}, u32[]{:S(2)}) collective-permute-start(bf16[2,2,128,768]{3,2,1,0:T(8,128)(2,1)S(1)} %maximum_select_fusion.26), channel_id=1, source_target_pairs={{0,16},{2,18},{4,20},{6,22},{8,24},{10,26},{12,28},{14,30},{16,0},... | collective-permute-start | bytes 2359304 | tf_op jit(solution)/shard_map/ppermute | solution.py:55
  152.5 96.1 %collective-permute-start.19 = (bf16[2,2,128,1024]{3,2,1,0:T(8,128)(2,1)S(1)}, bf16[2,2,128,1024]{3,2,1,0:T(8,128)(2,1)S(1)}, u32[]{:S(2)}, u32[]{:S(2)}) collective-permute-start(bf16[2,2,128,1024]{3,2,1,0:T(8,128)(2,1)S(1)} %maximum_select_fusion.19), channel_id=1, source_target_pairs={{0,16},{2,18},{4,20},{6,22},{8,24},{10,26},{12,28},{14,30},{16,0},... | collective-permute-start | bytes 3145736 | tf_op jit(solution)/shard_map/ppermute | solution.py:55
  155.9 112.8 %collective-permute-start.26 = (bf16[2,256,2048]{1,2,0:T(8,128)(2,1)}, bf16[2,256,2048]{1,2,0:T(8,128)(2,1)}, u32[]{:S(2)}, u32[]{:S(2)}) collective-permute-start(bf16[2,256,2048]{1,2,0:T(8,128)(2,1)} %get-tuple-element.61), channel_id=1, source_target_pairs={{0,2},{2,0},{4,6},{6,4},{8,10},{10,8},{12,14},{14,12},{16,18},{18,... | collective-permute-start | bytes 6291464 | tf_op jit(solution)/shard_map/ppermute | solution.py:55
  234.4 85.0 %collective-permute-start.16 = (bf16[2,2,2,128,1024]{4,3,2,1,0:T(8,128)(2,1)}, bf16[2,2,2,128,1024]{4,3,2,1,0:T(8,128)(2,1)}, u32[]{:S(2)}, u32[]{:S(2)}) collective-permute-start(bf16[2,2,2,128,1024]{4,3,2,1,0:T(8,128)(2,1)} %maximum_select_fusion.7), channel_id=1, source_target_pairs={{0,4},{2,6},{4,0},{6,2},{8,12},{10,14},{12,8},{14,10},{16,20},{18,... | collective-permute-start | bytes 6291464 | tf_op jit(solution)/shard_map/ppermute | solution.py:55
  248.6 68.5 %collective-permute-start.6 = (bf16[2,2,2,128,768]{4,3,2,1,0:T(8,128)(2,1)}, bf16[2,2,2,128,768]{4,3,2,1,0:T(8,128)(2,1)}, u32[]{:S(2)}, u32[]{:S(2)}) collective-permute-start(bf16[2,2,2,128,768]{4,3,2,1,0:T(8,128)(2,1)} %maximum_select_fusion.12), channel_id=1, source_target_pairs={{0,4},{2,6},{4,0},{6,2},{8,12},{10,14},{12,8},{14,10},{16,20},{18,... | collective-permute-start | bytes 4718600 | tf_op jit(solution)/shard_map/ppermute | solution.py:55
  251.3 98.6 %collective-permute-start.20 = (bf16[2,2,2,128,1024]{4,3,2,1,0:T(8,128)(2,1)}, bf16[2,2,2,128,1024]{4,3,2,1,0:T(8,128)(2,1)}, u32[]{:S(2)}, u32[]{:S(2)}) collective-permute-start(bf16[2,2,2,128,1024]{4,3,2,1,0:T(8,128)(2,1)} %maximum_select_fusion.9), channel_id=1, source_target_pairs={{0,4},{2,6},{4,0},{6,2},{8,12},{10,14},{12,8},{14,10},{16,20},{18,... | collective-permute-start | bytes 6291464 | tf_op jit(solution)/shard_map/ppermute | solution.py:55
  285.4 120.0 %collective-permute-start.27 = (bf16[4,256,2048]{2,1,0:T(8,128)(2,1)}, bf16[4,256,2048]{2,1,0:T(8,128)(2,1)}, u32[]{:S(2)}, u32[]{:S(2)}) collective-permute-start(bf16[4,256,2048]{2,1,0:T(8,128)(2,1)} %copy.180), channel_id=1, source_target_pairs={{0,1},{1,0},{2,3},{3,2},{4,5},{5,4},{6,7},{7,6},{8,9},{9,8},{10,11... | collective-permute-start | bytes 12582920 | tf_op jit(solution)/shard_map/ppermute | solution.py:58
  595.7 121.0 %collective-permute-start.40 = (bf16[1024,1024]{1,0:T(8,128)(2,1)}, bf16[1024,1024]{1,0:T(8,128)(2,1)}, u32[]{:S(2)}, u32[]{:S(2)}) collective-permute-start(bf16[1024,1024]{1,0:T(8,128)(2,1)} %dynamic-slice_bitcast_fusion.1), channel_id=1, source_target_pairs={{0,4},{2,6},{4,0},{6,2},{8,12},{10,14},{12,8},{14,10},{16,20},{18,... | collective-permute-start | bytes 6291464 | tf_op jit(solution)/shard_map/ppermute | solution.py:55
  659.7 102.7 %collective-permute-start.28 = (bf16[4,256,2048]{1,2,0:T(8,128)(2,1)}, bf16[4,256,2048]{1,2,0:T(8,128)(2,1)}, u32[]{:S(2)}, u32[]{:S(2)}) collective-permute-start(bf16[4,256,2048]{1,2,0:T(8,128)(2,1)} %bitcast.449), channel_id=1, source_target_pairs={{0,1},{1,0},{2,3},{3,2},{4,5},{5,4},{6,7},{7,6},{8,9},{9,8},{10,11... | collective-permute-start | bytes 12582920 | tf_op jit(solution)/shard_map/ppermute | solution.py:58
  672.4 104.9 %collective-permute-start.21 = (bf16[4,256,2048]{2,1,0:T(8,128)(2,1)}, bf16[4,256,2048]{2,1,0:T(8,128)(2,1)}, u32[]{:S(2)}, u32[]{:S(2)}) collective-permute-start(bf16[4,256,2048]{2,1,0:T(8,128)(2,1)} %fusion.7), channel_id=1, source_target_pairs={{0,1},{1,0},{2,3},{3,2},{4,5},{5,4},{6,7},{7,6},{8,9},{9,8},{10,11... | collective-permute-start | bytes 12582920 | tf_op jit(solution)/shard_map/ppermute | solution.py:58
  688.6 68.8 %collective-permute-start.44 = (bf16[1024,1024]{1,0:T(8,128)(2,1)}, bf16[1024,1024]{1,0:T(8,128)(2,1)}, u32[]{:S(2)}, u32[]{:S(2)}) collective-permute-start(bf16[1024,1024]{1,0:T(8,128)(2,1)} %dynamic-slice_bitcast_fusion), channel_id=1, source_target_pairs={{0,4},{2,6},{4,0},{6,2},{8,12},{10,14},{12,8},{14,10},{16,20},{18,... | collective-permute-start | bytes 6291464 | tf_op jit(solution)/shard_map/ppermute | solution.py:55
  712.8 314.6 %collective-permute-start.39 = (bf16[2,128,256]{1,2,0:T(8,128)(2,1)}, bf16[2,128,256]{1,2,0:T(8,128)(2,1)}, u32[]{:S(2)}, u32[]{:S(2)}) collective-permute-start(bf16[2,128,256]{1,2,0:T(8,128)(2,1)} %bitcast.156), channel_id=1, source_target_pairs={{0,2},{2,0},{4,6},{6,4},{8,10},{10,8},{12,14},{14,12},{16,18},{18,... | collective-permute-start | bytes 393224 | tf_op jit(solution)/shard_map/ppermute | solution.py:55
  716.6 57.7 %collective-permute-start.33 = (bf16[512,768]{1,0:T(8,128)(2,1)}, bf16[512,768]{1,0:T(8,128)(2,1)S(1)}, u32[]{:S(2)}, u32[]{:S(2)}) collective-permute-start(bf16[512,768]{1,0:T(8,128)(2,1)} %dynamic-slice_bitcast_fusion.5), channel_id=1, source_target_pairs={{0,16},{2,18},{4,20},{6,22},{8,24},{10,26},{12,28},{14,30},{16,0},... | collective-permute-start | bytes 2359304 | tf_op jit(solution)/shard_map/ppermute | solution.py:55
  757.4 70.9 %collective-permute-start.41 = (bf16[512,1024]{1,0:T(8,128)(2,1)S(1)}, bf16[512,1024]{1,0:T(8,128)(2,1)}, u32[]{:S(2)}, u32[]{:S(2)}) collective-permute-start(bf16[512,1024]{1,0:T(8,128)(2,1)S(1)} %dynamic-slice_bitcast_fusion.4), channel_id=1, source_target_pairs={{0,16},{2,18},{4,20},{6,22},{8,24},{10,26},{12,28},{14,30},{16,0},... | collective-permute-start | bytes 3145736 | tf_op jit(solution)/shard_map/ppermute | solution.py:55
  772.7 79.7 %collective-permute-start.29 = (bf16[2,256,2048]{1,2,0:T(8,128)(2,1)}, bf16[2,256,2048]{1,2,0:T(8,128)(2,1)}, u32[]{:S(2)}, u32[]{:S(2)}) collective-permute-start(bf16[2,256,2048]{1,2,0:T(8,128)(2,1)} %slice.186), channel_id=1, source_target_pairs={{0,2},{2,0},{4,6},{6,4},{8,10},{10,8},{12,14},{14,12},{16,18},{18,... | collective-permute-start | bytes 6291464 | tf_op jit(solution)/shard_map/ppermute | solution.py:55
  775.3 75.3 %collective-permute-start.45 = (bf16[512,1024]{1,0:T(8,128)(2,1)}, bf16[512,1024]{1,0:T(8,128)(2,1)}, u32[]{:S(2)}, u32[]{:S(2)}) collective-permute-start(bf16[512,1024]{1,0:T(8,128)(2,1)} %dynamic-slice_bitcast_fusion.3), channel_id=1, source_target_pairs={{0,16},{2,18},{4,20},{6,22},{8,24},{10,26},{12,28},{14,30},{16,0},... | collective-permute-start | bytes 3145736 | tf_op jit(solution)/shard_map/ppermute | solution.py:55
  813.0 53.5 %collective-permute-start.22 = (bf16[2,256,2048]{2,1,0:T(8,128)(2,1)}, bf16[2,256,2048]{2,1,0:T(8,128)(2,1)}, u32[]{:S(2)}, u32[]{:S(2)}) collective-permute-start(bf16[2,256,2048]{2,1,0:T(8,128)(2,1)} %slice.187), channel_id=1, source_target_pairs={{0,2},{2,0},{4,6},{6,4},{8,10},{10,8},{12,14},{14,12},{16,18},{18,... | collective-permute-start | bytes 6291464 | tf_op jit(solution)/shard_map/ppermute | solution.py:55
  828.3 202.4 %collective-permute-start.35 = (bf16[2,128,768]{1,2,0:T(8,128)(2,1)}, bf16[2,128,768]{1,2,0:T(8,128)(2,1)}, u32[]{:S(2)}, u32[]{:S(2)}) collective-permute-start(bf16[2,128,768]{1,2,0:T(8,128)(2,1)} %bitcast.495), channel_id=1, source_target_pairs={{0,2},{2,0},{4,6},{6,4},{8,10},{10,8},{12,14},{14,12},{16,18},{18,... | collective-permute-start | bytes 1179656 | tf_op jit(solution)/shard_map/ppermute | solution.py:55
  850.6 80.5 %collective-permute-start.42 = (bf16[2,128,1024]{2,1,0:T(8,128)(2,1)}, bf16[2,128,1024]{2,1,0:T(8,128)(2,1)}, u32[]{:S(2)}, u32[]{:S(2)}) collective-permute-start(bf16[2,128,1024]{2,1,0:T(8,128)(2,1)} %get-tuple-element.71), channel_id=1, source_target_pairs={{0,8},{2,10},{4,12},{6,14},{8,0},{10,2},{12,4},{14,6},{16,24},{18,... | collective-permute-start | bytes 1572872 | tf_op jit(solution)/shard_map/ppermute | solution.py:55
  931.0 168.8 %collective-permute-start.31 = (f32[256,2048]{1,0:T(8,128)}, f32[256,2048]{1,0:T(8,128)}, u32[]{:S(2)}, u32[]{:S(2)}) collective-permute-start(f32[256,2048]{1,0:T(8,128)} %get-tuple-element.58), channel_id=1, source_target_pairs={{0,1},{1,0},{2,3},{3,2},{4,5},{5,4},{6,7},{7,6},{8,9},{9,8},{10,11... | collective-permute-start | bytes 6291464 | tf_op jit(solution)/shard_map/ppermute | solution.py:58
  935.7 104.7 %collective-permute-start.43 = (bf16[2,128,1024]{1,2,0:T(8,128)(2,1)}, bf16[2,128,1024]{1,2,0:T(8,128)(2,1)}, u32[]{:S(2)}, u32[]{:S(2)}) collective-permute-start(bf16[2,128,1024]{1,2,0:T(8,128)(2,1)} %bitcast.490), channel_id=1, source_target_pairs={{0,2},{2,0},{4,6},{6,4},{8,10},{10,8},{12,14},{14,12},{16,18},{18,... | collective-permute-start | bytes 1572872 | tf_op jit(solution)/shard_map/ppermute | solution.py:55
  941.3 105.3 %collective-permute-start.47 = (bf16[2,128,1024]{1,2,0:T(8,128)(2,1)}, bf16[2,128,1024]{1,2,0:T(8,128)(2,1)}, u32[]{:S(2)}, u32[]{:S(2)}) collective-permute-start(bf16[2,128,1024]{1,2,0:T(8,128)(2,1)} %bitcast.491), channel_id=1, source_target_pairs={{0,2},{2,0},{4,6},{6,4},{8,10},{10,8},{12,14},{14,12},{16,18},{18,... | collective-permute-start | bytes 1572872 | tf_op jit(solution)/shard_map/ppermute | solution.py:55
  1030.6 66.1 %collective-permute-start.24 = (bf16[256,2048]{1,0:T(8,128)(2,1)}, bf16[256,2048]{1,0:T(8,128)(2,1)}, u32[]{:S(2)}, u32[]{:S(2)}) collective-permute-start(bf16[256,2048]{1,0:T(8,128)(2,1)} %get-tuple-element.59), channel_id=1, source_target_pairs={{0,1},{1,0},{2,3},{3,2},{4,5},{5,4},{6,7},{7,6},{8,9},{9,8},{10,11... | collective-permute-start | bytes 3145736 | tf_op jit(solution)/shard_map/ppermute | solution.py:58
  (104 other events, 1725.2 us)

commit v2 on v1

v2 whole, which is shorter than its diff:
```python
import functools

import jax
import jax.numpy as jnp
from jax import lax
from jax.experimental import pallas as pl
from jax.experimental.pallas import tpu as pltpu
from jax.sharding import PartitionSpec as P

HEAD_DIM = 64
ROT_DIM = 32
LANES = 128
NEGATIVE = -1e30
EPSILON = 1e-05
GELU_A = 0.7978845608028654
GELU_B = 0.044715
X_BIT, Y_BIT, ZL_BIT = 0, 1, 2
BF = jnp.bfloat16
F32 = jnp.float32


def doc_positions(segment_ids):
    places = jnp.arange(segment_ids.shape[-1], dtype=jnp.int32)
    begins = jnp.concatenate(
        [jnp.ones(segment_ids.shape[:-1] + (1,), bool), segment_ids[:, 1:] != segment_ids[:, :-1]],
        axis=1,
    )
    opening = lax.cummax(jnp.where(begins, places, 0), axis=1)
    return places - opening


def dot_nt(a, b):
    return lax.dot_general(a, b, (((1,), (1,)), ((), ())), preferred_element_type=F32)


def dot_tn(a, b):
    return lax.dot_general(a, b, (((0,), (0,)), ((), ())), preferred_element_type=F32)


def attention_kernel(step, pre_ref, grad_ref, cos_ref, left_ref, right_ref, seg_q_ref, seg_k_ref, out_ref, dpre_ref):
    rows, width = grad_ref.shape
    scaling = HEAD_DIM ** (-0.5)
    cos, left, right = cos_ref[...], left_ref[...], right_ref[...]
    head_of = lax.broadcasted_iota(jnp.int32, (rows, LANES), 1) // HEAD_DIM

    def turn(v, sign):
        ahead = pltpu.roll(v, LANES - ROT_DIM // 2, 1)
        behind = pltpu.roll(v, ROT_DIM // 2, 1)
        return v * cos + sign * (ahead * left + behind * right)

    for pair in range(width // LANES):
        cols = slice(pair * LANES, (pair + 1) * LANES)
        q = turn(pre_ref[:, pair * LANES : (pair + 1) * LANES], 1.0).astype(BF)
        k = turn(pre_ref[:, width + pair * LANES : width + (pair + 1) * LANES], 1.0).astype(BF)
        v = pre_ref[:, 2 * width + pair * LANES : 2 * width + (pair + 1) * LANES].astype(BF)
        g = grad_ref[:, cols]
        dk = [None] * (rows // step)
        dv = [None] * (rows // step)
        for first in range(0, rows, step):
            seen = first + step
            allowed = seg_q_ref[0, first:seen, :] == seg_k_ref[0, :, :seen]
            allowed = allowed & (
                lax.broadcasted_iota(jnp.int32, (step, seen), 0) + first
                >= lax.broadcasted_iota(jnp.int32, (step, seen), 1)
            )
            att_both = dq_both = None
            for h in range(LANES // HEAD_DIM):
                mine = head_of[first:seen] == h
                qh = jnp.where(mine, q[first:seen], 0).astype(BF)
                gh = jnp.where(mine, g[first:seen], 0).astype(BF)
                s = jnp.where(allowed, dot_nt(qh, k[:seen]) * scaling, NEGATIVE)
                e = jnp.exp(s - jnp.max(s, axis=-1, keepdims=True))
                p = e * (1.0 / jnp.sum(e, axis=-1, keepdims=True))
                low = p.astype(BF)
                att = jnp.dot(low, v[:seen], preferred_element_type=F32)
                dp = dot_nt(gh, v[:seen])
                inner = jnp.sum(p * dp, axis=-1, keepdims=True)
                ds = (p * (dp - inner)).astype(BF)
                dq = jnp.dot(ds, k[:seen], preferred_element_type=F32)
                att_both = att if h == 0 else jnp.where(mine, att, att_both)
                dq_both = dq if h == 0 else jnp.where(mine, dq, dq_both)
                dkh = dot_tn(ds, qh)
                dvh = dot_tn(low, gh)
                for part in range(seen // step):
                    sl = slice(part * step, (part + 1) * step)
                    dk[part] = dkh[sl] if dk[part] is None else dk[part] + dkh[sl]
                    dv[part] = dvh[sl] if dv[part] is None else dv[part] + dvh[sl]
            out_ref[first:seen, cols] = att_both.astype(BF)
            dpre_ref[first:seen, cols] = turn_rows(dq_both * scaling, cos, left, right, first, seen)
        dk = jnp.concatenate(dk, axis=0) * scaling
        dpre_ref[:, width + pair * LANES : width + (pair + 1) * LANES] = turn(dk, -1.0).astype(BF)
        dpre_ref[:, 2 * width + pair * LANES : 2 * width + (pair + 1) * LANES] = jnp.concatenate(dv, axis=0).astype(BF)


def turn_rows(v, cos, left, right, first, seen):
    ahead = pltpu.roll(v, LANES - ROT_DIM // 2, 1)
    behind = pltpu.roll(v, ROT_DIM // 2, 1)
    return (v * cos[first:seen] - (ahead * left[first:seen] + behind * right[first:seen])).astype(BF)


def attention(pre, grad, cos, left, right, seg, step=512):
    count, rows = seg.shape
    width = grad.shape[1]
    row_block = lambda cols: pl.BlockSpec((rows, cols), lambda s: (s, 0))
    return pl.pallas_call(
        functools.partial(attention_kernel, step),
        grid=(count,),
        out_shape=[
            jax.ShapeDtypeStruct((count * rows, width), BF),
            jax.ShapeDtypeStruct((count * rows, 3 * width), BF),
        ],
        in_specs=[
            row_block(3 * width),
            row_block(width),
            row_block(LANES),
            row_block(LANES),
            row_block(LANES),
            pl.BlockSpec((1, rows, 1), lambda s: (s, 0, 0)),
            pl.BlockSpec((1, 1, rows), lambda s: (s, 0, 0)),
        ],
        out_specs=[row_block(width), row_block(3 * width)],
        compiler_params=pltpu.CompilerParams(vmem_limit_bytes=48 * 1024 * 1024),
        cost_estimate=pl.CostEstimate(flops=40 * 10**9, bytes_accessed=16 * 10**6, transcendentals=0),
    )(pre, grad, cos, left, right, seg[:, :, None], seg[:, None, :])


def rotary_lanes(places):
    halfway = ROT_DIM // 2
    lane = jnp.arange(LANES, dtype=jnp.int32) % HEAD_DIM
    freqs = 10000.0 ** (-(lane % halfway).astype(F32) * 2.0 / ROT_DIM)
    angles = places.astype(F32)[:, None] * freqs[None, :]
    turned = lane < ROT_DIM
    cos = jnp.where(turned, jnp.cos(angles), 1.0)
    sin = jnp.where(turned, jnp.sin(angles), 0.0)
    return cos, jnp.where(lane < halfway, -sin, 0.0), jnp.where(lane >= halfway, sin, 0.0)


def local_part(dp_size):
    top_bits = [b for b in range(3, dp_size.bit_length() - 1)]
    first = (((0,), (0,)), ((), ()))
    last = (((1,), (1,)), ((), ()))

    def swap(value, bit):
        return lax.ppermute(value, "dp", [(i, i ^ (1 << bit)) for i in range(dp_size)])

    def swap_core(value):
        return lax.ppermute(value, "tensor", [(0, 1), (1, 0)])

    def ordered(bit, own, other, axis=0):
        return jnp.where(
            bit == 0, jnp.stack([own, other], axis), jnp.stack([other, own], axis)
        )

    def pick(value, index, axis=0):
        return lax.dynamic_index_in_dim(value, index, axis, keepdims=False)

    def sync(*values):
        return lax.optimization_barrier(values)

    def local(
        tokens,
        segments,
        ln_gain,
        ln_shift,
        qkv_weight,
        qkv_bias,
        out_weight,
        up_weight,
        up_bias,
        down_weight,
        branch_bias,
        cotangent,
    ):
        rows, width = tokens.shape
        half = rows // 2
        wide = width // 2
        share = qkv_weight.shape[0]
        me = lax.axis_index("dp")
        core = lax.axis_index("tensor")
        x_mine, y_mine, zl_mine = (me >> X_BIT) & 1, (me >> Y_BIT) & 1, (me >> ZL_BIT) & 1
        block = x_mine + 2 * zl_mine
        att = qkv_weight.shape[2] // 4
        hid = up_weight.shape[1] // 4

        def to_mixed(value):
            lead = value.shape[:-1]
            split = value.reshape(lead + (width // (4 * share), 2, 2 * share))
            return jnp.swapaxes(split, -3, -2).reshape(lead + (width,))

        def from_mixed(value):
            lead = value.shape[:-1]
            split = value.reshape(lead + (2, width // (4 * share), 2 * share))
            return jnp.swapaxes(split, -3, -2).reshape(lead + (width,))

        def w_parts(piece):
            return piece.reshape(share, 2, 2, piece.shape[2]).transpose(2, 1, 0, 3)

        def w_x(w):
            return ordered(x_mine, pick(w, x_mine), swap(pick(w, 1 - x_mine), X_BIT), 1)

        def w_zl(w):
            return ordered(zl_mine, pick(w, zl_mine), swap(pick(w, 1 - zl_mine), ZL_BIT))

        def w_top(w):
            for bit in top_bits:
                w = ordered((me >> bit) & 1, w, swap(w, bit))
            return w.reshape((-1,) + w.shape[-1:])

        def w_y(w):
            return ordered(y_mine, w, swap(w, Y_BIT)).reshape(width, -1)

        def fold(grad, bit):
            grad = grad.reshape((2, -1) + grad.shape[-1:])
            mine = (me >> bit) & 1
            got = swap(pick(grad, 1 - mine), bit)
            return (pick(grad, mine).astype(F32) + got.astype(F32)).astype(BF)

        def g_y(grad):
            return fold(grad, Y_BIT)

        def g_top(grad):
            for bit in reversed(top_bits):
                grad = fold(grad, bit)
            return grad.reshape(2, 2, share, -1)

        def g_zl(grad):
            return ordered(zl_mine, pick(grad, zl_mine), swap(pick(grad, 1 - zl_mine), ZL_BIT), 1)

        def g_x(grad):
            got = swap(pick(grad, 1 - x_mine), X_BIT)
            grad = ordered(x_mine, pick(grad, x_mine), got)
            return grad.transpose(2, 1, 0, 3).reshape(share, 4, -1)

        def a_first(piece):
            return (
                jnp.stack([piece[:, :wide], swap(piece[:, :wide], ZL_BIT)]),
                jnp.stack([piece[:, wide:], swap(piece[:, wide:], X_BIT)]),
            )

        def a_second(pair):
            return (
                jnp.stack([pair[0], swap(pair[0], X_BIT)]).reshape(4, half, wide),
                jnp.stack([pair[1], swap(pair[1], ZL_BIT)], 1).reshape(4, half, wide),
            )

        def a_core(pair):
            mine = jnp.concatenate(pair, axis=-1)
            return ordered(core, mine, swap_core(mine), 1).reshape(4 * rows, width)

        def s_core(part):
            part = part.reshape(4, 2, half, width)
            got = swap_core(pick(part, 1 - core, 1).astype(BF))
            return (pick(part, core, 1) + got.astype(F32)).reshape(2, 2, half, width)

        def s_first(part):
            a, b = part[..., :wide], part[..., wide:]
            return (
                a[0] + swap(a[1].astype(BF), X_BIT).astype(F32),
                b[:, 0] + swap(b[:, 1].astype(BF), ZL_BIT).astype(F32),
            )

        def s_second(pair):
            a, b = pair
            a = a[0] + swap(a[1].astype(BF), ZL_BIT).astype(F32)
            b = b[0] + swap(b[1].astype(BF), X_BIT).astype(F32)
            return from_mixed(jnp.concatenate([a, b], axis=-1))

        def both_cores(value):
            return ordered(core, value, swap_core(value)).reshape((rows,) + value.shape[1:])

        step = hid // 2
        up_p = w_parts(up_weight.reshape(share, 4, hid))
        down_p = w_parts(down_weight.T.reshape(share, 4, hid))
        qkv_p = qkv_weight.reshape(share, 3, 4, att).swapaxes(1, 2).reshape(share, 4, 3 * att)
        att_p = w_parts(
            jnp.concatenate([qkv_p, out_weight.T.reshape(share, 4, att)], axis=2)
        )

        u0 = w_x(up_p[..., :step])
        seg = jnp.stack([segments, swap(segments, ZL_BIT)])
        seg = jnp.stack([seg, swap(seg, X_BIT)]).reshape(4, rows)
        my_tokens = pick(tokens.reshape(2, half, width), core).astype(F32)
        my_cot = pick(cotangent.reshape(2, half, width), core)
        average = jnp.mean(my_tokens, axis=-1, keepdims=True)
        centered = my_tokens - average
        inv_std = lax.rsqrt(jnp.mean(centered * centered, axis=-1, keepdims=True) + EPSILON)
        normal_x = centered * inv_std
        gain_f = ln_gain.astype(F32)
        my_normed = to_mixed((normal_x * gain_f + ln_shift.astype(F32)).astype(BF))
        u0, my_normed, up_p = sync(u0, my_normed, up_p)
        u0 = w_zl(u0)
        nh = a_first(my_normed)
        u1 = w_x(up_p[..., step:])
        cot_mixed = to_mixed(my_cot)
        u0, nh, u1, down_p, att_p, cot_mixed = sync(u0, nh, u1, down_p, att_p, cot_mixed)
        u0 = w_top(u0)
        u1 = w_zl(u1)
        nh = a_second(nh)
        dd = w_x(down_p)
        places = doc_positions(seg)
        tables = rotary_lanes(places.reshape(-1))
        u0, u1, nh, dd, att_p, cot_mixed, tables = sync(
            u0, u1, nh, dd, att_p, cot_mixed, tables
        )
        u0 = w_y(u0)
        u1 = w_top(u1)
        dd = w_zl(dd)
        aa = w_x(att_p)
        ch = a_first(cot_mixed)
        normed = a_core(nh)
        u0, u1, dd, aa, ch, normed = sync(u0, u1, dd, aa, ch, normed)
        u1 = w_y(u1)
        d0 = w_top(dd[..., :step])
        ch = a_second(ch)
        u0, u1, d0, dd, aa, ch, normed = sync(u0, u1, d0, dd, aa, ch, normed)
        d0 = w_y(d0)
        d1 = w_top(dd[..., step:])
        aa = w_zl(aa)
        cot = a_core(ch)
        my_up_bias = lax.dynamic_slice_in_dim(up_bias, block * hid, hid, 0).astype(F32)
        up_full = jnp.concatenate([u0, u1], axis=1)
        up_pre = jnp.dot(normed, up_full, preferred_element_type=F32) + my_up_bias
        squared = up_pre * up_pre
        th = jnp.tanh(GELU_A * (up_pre + GELU_B * up_pre * squared))
        act = (0.5 * up_pre * (1.0 + th)).astype(BF)
        slope = (
            0.5 * (1.0 + th)
            + 0.5 * up_pre * (1.0 - th * th) * (GELU_A * (1.0 + 3.0 * GELU_B * squared))
        ).astype(BF)
        up_full, d0, d1, aa, cot, act, slope, normed = sync(
            up_full, d0, d1, aa, cot, act, slope, normed
        )
        d1 = w_y(d1)
        a0 = w_top(aa[..., : 2 * att])
        gd = lax.dot_general(cot, act, first, preferred_element_type=BF)
        d0, d1, a0, aa, gd, cot, act, slope, normed = sync(
            d0, d1, a0, aa, gd, cot, act, slope, normed
        )
        a0 = w_y(a0)
        a1 = w_top(aa[..., 2 * att :])
        down_full = jnp.concatenate([d0, d1], axis=1)
        up_g = (jnp.dot(cot, down_full, preferred_element_type=F32) * slope.astype(F32)).astype(BF)
        gu = lax.dot_general(normed, up_g, first, preferred_element_type=BF)
        a0, a1, gd, gu, up_g, normed, cot, down_full, act = sync(
            a0, a1, gd, gu, up_g, normed, cot, down_full, act
        )
        a1 = w_y(a1)
        my_qkv_bias = lax.dynamic_slice_in_dim(qkv_bias, block * att, att, 1).astype(F32)
        part_qk = jnp.dot(normed, a0, preferred_element_type=F32) + my_qkv_bias[:2].reshape(-1)
        branches = lax.dot_general(act, down_full, last, preferred_element_type=F32)
        a1, part_qk, gd, gu, normed, cot, branches = sync(
            a1, part_qk, gd, gu, normed, cot, branches
        )
        gd0 = g_y(gd[:, :step])
        part_v = jnp.dot(normed, a1[:, :att], preferred_element_type=F32) + my_qkv_bias[2]
        attn_grad = jnp.dot(cot, a1[:, att:], preferred_element_type=BF)
        attended, qkv_g = attention(
            jnp.concatenate([part_qk, part_v], axis=1), attn_grad, *tables, seg
        )
        gd0, gd, gu, attended, qkv_g, normed, cot, branches = sync(
            gd0, gd, gu, attended, qkv_g, normed, cot, branches
        )
        gd1 = g_y(gd[:, step:])
        gd0 = g_top(gd0)
        qkv_full = jnp.concatenate([a0, a1[:, :att]], axis=1)
        normed_grad = lax.dot_general(
            qkv_g, qkv_full, last, preferred_element_type=F32
        ) + lax.dot_general(up_g, up_full, last, preferred_element_type=F32)
        gq = lax.dot_general(normed, qkv_g, first, preferred_element_type=BF)
        gd0, gd1, gu, gq, normed_grad, attended, branches, cot = sync(
            gd0, gd1, gu, gq, normed_grad, attended, branches, cot
        )
        gu0 = g_y(gu[:, :step])
        gd1 = g_top(gd1)
        gd0 = g_zl(gd0)
        normed_grad = s_core(normed_grad)
        branches = branches + lax.dot_general(
            attended, a1[:, att:], last, preferred_element_type=F32
        )
        go = lax.dot_general(cot, attended, first, preferred_element_type=BF)
        gu0, gd1, gd0, normed_grad, branches, gu, gq, go = sync(
            gu0, gd1, gd0, normed_grad, branches, gu, gq, go
        )
        gu1 = g_y(gu[:, step:])
        gu0 = g_top(gu0)
        gd1 = g_zl(gd1)
        gd0 = g_x(gd0)
        normed_grad = s_first(normed_grad)
        branches = s_core(branches)
        gu1, gu0, gd1, gd0, normed_grad, branches, gq, go = sync(
            gu1, gu0, gd1, gd0, normed_grad, branches, gq, go
        )
        ga0 = g_y(gq[:, : 2 * att])
        gu1 = g_top(gu1)
        gu0 = g_zl(gu0)
        gd1 = g_x(gd1)
        normed_grad = s_second(normed_grad)
        ga0, gu1, gu0, gd1, normed_grad, branches, gq, go = sync(
            ga0, gu1, gu0, gd1, normed_grad, branches, gq, go
        )
        ga1 = g_y(jnp.concatenate([gq[:, 2 * att :], go], axis=1))
        ga0 = g_top(ga0)
        gu1 = g_zl(gu1)
        gu0 = g_x(gu0)
        branches = s_first(branches)
        scaled = normed_grad * gain_f
        input_grad = my_cot.astype(F32) + inv_std * (
            scaled
            - jnp.mean(scaled, axis=-1, keepdims=True)
            - normal_x * jnp.mean(scaled * normal_x, axis=-1, keepdims=True)
        )
        input_grad = both_cores(input_grad)
        lines = jnp.stack(
            [
                jnp.sum(normed_grad * normal_x, axis=0),
                jnp.sum(normed_grad, axis=0),
                jnp.sum(my_cot.astype(F32), axis=0),
            ]
        )
        lines = lines + swap_core(lines)
        ga1, ga0, gu1, gu0, branches, lines = sync(ga1, ga0, gu1, gu0, branches, lines)
        ga1 = g_top(ga1)
        ga0 = g_zl(ga0)
        gu1 = g_x(gu1)
        branches = s_second(branches)
        biases = jnp.concatenate(
            [jnp.sum(qkv_g.astype(F32), axis=0), jnp.sum(up_g.astype(F32), axis=0)]
        )
        for bit in top_bits + [Y_BIT]:
            lines = lines + swap(lines, bit)
            biases = biases + swap(biases, bit)
        ga1, ga0, gu1, branches, lines, biases = sync(ga1, ga0, gu1, branches, lines, biases)
        ga1 = g_zl(ga1)
        ga0 = g_x(ga0)
        result = both_cores((my_tokens + branches + branch_bias.astype(F32)).astype(BF))
        for bit in (X_BIT, ZL_BIT):
            lines = lines + swap(lines, bit)
        biases = ordered(x_mine, biases, swap(biases, X_BIT))
        ga1, ga0, result, lines, biases = sync(ga1, ga0, result, lines, biases)
        ga1 = g_x(ga1)
        biases = ordered(zl_mine, biases, swap(biases, ZL_BIT)).reshape(4, 3 * att + hid)

        gdown = jnp.concatenate([gd0, gd1], axis=2).astype(F32).reshape(share, 4 * hid).T
        gup = jnp.concatenate([gu0, gu1], axis=2).astype(F32).reshape(share, 4 * hid)
        gqkv = jnp.concatenate([ga0, ga1[..., :att]], axis=2).astype(F32)
        gqkv = gqkv.reshape(share, 4, 3, att).swapaxes(1, 2).reshape(share, 3, 4 * att)
        gout = ga1[..., att:].astype(F32).reshape(share, 4 * att).T
        qkv_b = biases[:, : 3 * att].reshape(4, 3, att).swapaxes(0, 1).reshape(3, 4 * att)
        up_b = biases[:, 3 * att :].reshape(4 * hid)
        return (
            result,
            input_grad,
            lines[0],
            lines[1],
            gqkv,
            qkv_b,
            gout,
            gup,
            up_b,
            gdown,
            lines[2],
        )

    return local


def solution(mesh):
    return jax.shard_map(
        local_part(mesh.shape["dp"]),
        mesh=mesh,
        in_specs=(
            P("dp", None),
            P("dp"),
            P(),
            P(),
            P("dp", None, "tensor"),
            P(None, "tensor"),
            P("tensor", "dp"),
            P("dp", "tensor"),
            P("tensor"),
            P("tensor", "dp"),
            P(),
            P("dp", None),
        ),
        out_specs=(
            P("dp", None),
            P("dp", None),
            P(),
            P(),
            P("dp", None, "tensor"),
            P(None, "tensor"),
            P("tensor", "dp"),
            P("dp", "tensor"),
            P("tensor"),
            P("tensor", "dp"),
            P(),
        ),
        check_vma=False,
    )
```

time: 1120 us -> 753 us (0.67)
  waiting for transfers between devices: 341 us -> 218 us
  blocking collectives: 122 us -> 0 us
  local copies, waits for them, and re-layouts: 248 us -> 141 us
  other arithmetic: 173 us -> 138 us
  starting transfers between devices: 47.1 us -> 82.1 us
  matrix products: 171 us -> 139 us
  Pallas kernels: 0 us -> 22.3 us
    ppermute x42 -> x70, waiting for transfers between devices: 341 us -> 218 us  [swap(): lax.ppermute(value, 'dp', [(i, i ^ 1 << bit) for i in range(dp_size)])]
    psum x2 -> x0, blocking collectives: 122 us -> none  [the longest x1 84.8 us: local(): lax.psum((placed(jnp.sum(qkv_g.astype(F32), axis=0).reshape(3, att), 4 *...]
    another operation x30 -> x20, local copies, waits for them, and re-layouts: 65.1 us -> 17.2 us  [the longest x2 7.87 us: a_second(): jnp.stack([pair[1], swap(pair[1], ZL_BIT)], 1).reshape(4, half, wide)]
    reshape x12 -> x3, local copies, waits for them, and re-layouts: 37.9 us -> 1.29 us  [the longest x1 1.25 us: local(): gqkv.reshape(share, 4, 3, att).swapaxes(1, 2).reshape(share, 3, 4 * att)]
    ppermute x42 -> x70, starting transfers between devices: 46.3 us -> 81.8 us  [swap(): lax.ppermute(value, 'dp', [(i, i ^ 1 << bit) for i in range(dp_size)])]
    dot_general x14 -> x10, matrix products: 118 us -> 92.5 us  [the longest x1 15.4 us: local(): branches = lax.dot_general(act, down_full, last, preferred_element_type=F32)]
    dot_general x2 -> x0, local copies, waits for them, and re-layouts: 24.7 us -> none  [the longest x1 12.3 us: local(): lax.dot_general(normed, qkv_g, first, preferred_element_type=BF)]
    unnamed x188 -> x155, local copies, waits for them, and re-layouts: 40.5 us -> 17 us
  transfers between devices with their start and end apart: 48 -> 77, of which waited for: 21 -> 36; matrix products, arithmetic and copies ran while one was open for 35% -> 38% of each run, Pallas kernels for 0% -> 3%
where the time goes in v2:
time: 753 us; the launch traced here: 742 us
  waiting for transfers between devices  218 us (29%)
  local copies, waits for them, and re-layouts  141 us (19%)
  matrix products  139 us (18%)
  other arithmetic  138 us (18%)
  starting transfers between devices  82.1 us (11%)
  Pallas kernels  22.3 us (3%)
    ppermute x70, waiting for transfers between devices, swap(): lax.ppermute(value, 'dp', [(i, i ^ 1 << bit) for i in range(dp_size)])  218 us
    ppermute x70, starting transfers between devices, swap(): lax.ppermute(value, 'dp', [(i, i ^ 1 << bit) for i in range(dp_size)])  81.8 us
    select_n x38, other arithmetic, ordered(): jnp.where(bit == 0, jnp.stack([own, other], axis), jnp.stack([other, own]...  49.9 us
    pallas_call x1, Pallas kernels, attention(): pl.pallas_call(functools.partial(attention_kernel, step), grid=(count,),...  22.3 us
    select_n x9, local copies, waits for them, and re-layouts, ordered(): jnp.where(bit == 0, jnp.stack([own, other], axis), jnp.stack([other, own]...  21.1 us
    add x2, other arithmetic, s_core(): return (pick(part, core, 1) + got.astype(F32)).reshape(2, 2, half, width)  20.2 us
    dot_general x1, matrix products, local(): up_pre = jnp.dot(normed, up_full, preferred_element_type=F32) + my_up_bias  19 us
    dot_general x1, matrix products, local(): lax.dot_general(up_g, up_full, last, preferred_element_type=F32)  17.8 us
  transfers between devices with their start and end apart: 77, of which 36 were waited for; matrix products, arithmetic and copies ran while one was open for 38% of the time, Pallas kernels for 3%

profile of v2, /device:TPU:0, one launch (start us, length us, event | category | flops | bytes accessed | tf_op | source)
XLA Modules:
  0.0 742.4 jit_solution(4469149276277486204)
XLA Ops:
  43.1 6.3 collective-permute-done.3
  68.3 9.6 %collective-permute-done.5 = bf16[2,2,128,512]{3,2,0,1:T(8,128)(2,1)S(1)} collective-permute-done((bf16[2,2,128,512]{3,2,0,1:T(8,128)(2,1)S(1)}, bf16[2,2,128,512]{3,2,0,1:T(8,128)(2,1)S(1)}, u32[]{:S(2)}, u32[]{:S(2)}) %collective-permute-start.5) | collective-permute-done | bytes 524320 | tf_op jit(solution)/shard_map/ppermute | solution.py:144
  80.3 13.1 %collective-permute-done.8 = bf16[2,256,1024]{1,2,0:T(8,128)(2,1)S(1)} collective-permute-done((bf16[2,256,1024]{1,2,0:T(8,128)(2,1)S(1)}, bf16[2,256,1024]{1,2,0:T(8,128)(2,1)S(1)}, u32[]{:S(2)}, u32[]{:S(2)}) %collective-permute-start.8) | collective-permute-done | bytes 1048608 | tf_op jit(solution)/shard_map/ppermute | solution.py:144
  124.4 14.1 %collective-permute-done.14 = bf16[2,128,1024]{2,1,0:T(8,128)(2,1)} collective-permute-done((bf16[2,128,1024]{2,1,0:T(8,128)(2,1)}, bf16[2,128,1024]{2,1,0:T(8,128)(2,1)}, u32[]{:S(2)}, u32[]{:S(2)}) %collective-permute-start.14) | collective-permute-done | bytes 524320 | tf_op jit(solution)/shard_map/ppermute | solution.py:144
  160.0 7.9 %maximum_select_fusion = bf16[4,2,256,2048]{3,2,0,1:T(8,128)(2,1)} fusion(bf16[4,1,256,2048]{3,2,0,1:T(8,128)(2,1)} %bitcast.67, bf16[4,1,256,2048]{3,2,0,1:T(8,128)(2,1)S(1)} %copy-done, pred[]{:T(512)S(6)} %eq.17), kind=kLoop, calls=%fused_computation.1 | loop fusion | flops 12582912 | bytes 16777216 | tf_op jit(solution)/shard_map/jit(_where)/select_n | solution.py:150
  167.9 8.4 %copy.116 = bf16[4,2,256,2048]{3,2,1,0:T(8,128)(2,1)} copy(bf16[4,2,256,2048]{3,2,0,1:T(8,128)(2,1)} %maximum_select_fusion) | data formatting | bytes 16777216 | tf_op jit(solution)/shard_map/jit(_where)/select_n | solution.py:150
  185.4 24.1 %collective-permute-done.20 = bf16[2,2,128,512]{3,2,0,1:T(8,128)(2,1)} collective-permute-done((bf16[2,2,128,512]{3,2,0,1:T(8,128)(2,1)}, bf16[2,2,128,512]{3,2,0,1:T(8,128)(2,1)}, u32[]{:S(2)}, u32[]{:S(2)}) %collective-permute-start.20) | collective-permute-done | bytes 524320 | tf_op jit(solution)/shard_map/ppermute | solution.py:144
  239.2 19.0 %add_convert_fusion = (bf16[2048,1024]{1,0:T(8,128)(2,1)}, bf16[2048,1024]{1,0:T(8,128)(2,1)}) fusion(f32[1024]{0:T(1024)S(1)} %dynamic-slice_convert_fusion.3, bf16[2048,2048]{1,0:T(8,128)(2,1)} %bitcast.436, bf16[2048,1024]{1,0:T(8,128)(2,1)S(1)} %constant_dynamic-update-slice_fusion), kind=kOutput, calls=%fused_computation.11 | convolution fusion | flops 8631877632 | bytes 20975616 | tf_op jit(solution)/shard_map/dot_general | solution.py:322
  266.9 8.4 %copy.121 = bf16[4,2,256,2048]{3,2,1,0:T(8,128)(2,1)} copy(bf16[4,2,256,2048]{3,2,0,1:T(8,128)(2,1)} %maximum_select_fusion.1) | data formatting | bytes 16777216 | tf_op jit(solution)/shard_map/jit(_where)/select_n | solution.py:150
  278.3 14.3 %fusion.49 = bf16[2048,1024]{1,0:T(8,128)(2,1)} fusion(bf16[2048,2048]{1,0:T(8,128)(2,1)} %bitcast.443, bf16[2048,1024]{1,0:T(8,128)(2,1)} %get-tuple-element.194), kind=kOutput, calls=%fused_computation.255 | convolution fusion | flops 8589934592 | bytes 16777216 | tf_op jit(solution)/shard_map/dot_general | solution.py:335
  292.5 8.5 %collective-permute-done.28 = bf16[2,2,128,512]{3,2,0,1:T(8,128)(2,1)S(1)} collective-permute-done((bf16[2,2,128,512]{3,2,0,1:T(8,128)(2,1)S(1)}, bf16[2,2,128,512]{3,2,0,1:T(8,128)(2,1)S(1)}, u32[]{:S(2)}, u32[]{:S(2)}) %collective-permute-start.28) | collective-permute-done | bytes 524320 | tf_op jit(solution)/shard_map/ppermute | solution.py:144
  308.2 11.7 %multiply_convert_fusion = bf16[2048,1024]{1,0:T(8,128)(2,1)S(1)} fusion(bf16[2048,1024]{1,0:T(8,128)(2,1)} %get-tuple-element.186, bf16[2048,2048]{1,0:T(8,128)(2,1)S(1)} %bitcast.446, bf16[2048,1024]{1,0:T(8,128)(2,1)} %constant_dynamic-update-slice_fusion.2), kind=kOutput, calls=%fused_computation.10 | convolution fusion | flops 8596226048 | bytes 20971520 | tf_op jit(solution)/shard_map/dot_general | solution.py:342
  320.0 11.0 %fusion.50 = bf16[2048,1024]{1,0:T(8,128)(2,1)} fusion(bf16[2048,2048]{1,0:T(8,128)(2,1)S(1)} %bitcast.440, bf16[2048,1024]{1,0:T(8,128)(2,1)S(1)} %multiply_convert_fusion), kind=kOutput, calls=%fused_computation.256 | convolution fusion | flops 8589934592 | bytes 16777216 | tf_op jit(solution)/shard_map/dot_general | solution.py:343
  332.2 15.4 %fusion.51 = f32[2048,2048]{1,0:T(8,128)} fusion(bf16[2048,1024]{1,0:T(8,128)(2,1)} %get-tuple-element.194, bf16[2048,1024]{1,0:T(8,128)(2,1)} %constant_dynamic-update-slice_fusion.2), kind=kOutput, calls=%fused_computation.257 | convolution fusion | flops 8589934592 | bytes 25165824 | tf_op jit(solution)/shard_map/dot_general | solution.py:350
  367.2 22.3 %shard_map.203 = (bf16[2048,256]{1,0:T(8,128)(2,1)S(1)}, bf16[2048,768]{1,0:T(8,128)(2,1)}) custom-call(f32[2048,768]{1,0:T(8,128)} %pad_maximum_fusion.pre_ref, bf16[2048,256]{1,0:T(8,128)(2,1)S(1)} %fusion.29.grad_ref, f32[2048,128]{1,0:T(8,128)S(1)} %get-tuple-element.202.cos_ref, f32[2048,128]{1,0:T(8,128)S(1)} %get-tuple-element.203.left_ref, ...), custom_call_target="tpu_custom_call" | custom-call | flops 40000000000 | bytes 16000000 | tf_op jit(solution)/shard_map/pallas_call | solution.py:105
  397.7 9.7 %fusion.2 = f32[2048,2048]{1,0:T(8,128)} fusion(bf16[2048,768]{1,0:T(8,128)(2,1)S(1)} %copy-done.31, bf16[2048,256]{1,0:T(8,128)(2,1)S(1)} %slice.183, bf16[2048,512]{1,0:T(8,128)(2,1)S(1)} %bitcast.522), kind=kOutput, calls=%fused_computation.22 | convolution fusion | flops 6448742400 | bytes 23068672 | tf_op jit(solution)/shard_map/dot_general | solution.py:366
  407.4 17.8 %convolution_add_fusion.1 = f32[2048,2048]{1,0:T(8,128)} fusion(f32[2048,2048]{1,0:T(8,128)} %fusion.2, bf16[2048,1024]{1,0:T(8,128)(2,1)} %copy-done.16, bf16[2048,1024]{1,0:T(8,128)(2,1)} %copy-done.47), kind=kOutput, calls=%fused_computation.14 | convolution fusion | flops 8594128896 | bytes 41943040 | tf_op jit(solution)/shard_map/dot_general | solution.py:368
  425.2 10.9 %fusion.52 = bf16[2048,768]{1,0:T(8,128)(2,1)} fusion(bf16[2048,2048]{1,0:T(8,128)(2,1)} %bitcast.437, bf16[2048,768]{1,0:T(8,128)(2,1)S(1)} %copy-done.31), kind=kOutput, calls=%fused_computation.258 | convolution fusion | flops 6442450944 | bytes 14680064 | tf_op jit(solution)/shard_map/dot_general | solution.py:369
  449.0 14.8 %convolution_add_fusion = f32[2048,2048]{1,0:T(8,128)} fusion(f32[2048,2048]{1,0:T(8,128)} %fusion.51, bf16[2048,256]{1,0:T(8,128)(2,1)S(1)} %get-tuple-element.223, bf16[2048,512]{1,0:T(8,128)(2,1)S(1)} %bitcast.435), kind=kOutput, calls=%fused_computation | convolution fusion | flops 2151677952 | bytes 35651584 | tf_op jit(solution)/shard_map/dot_general | solution.py:377
  472.8 10.1 %bitcast_add_fusion.1 = f32[4,256,2048]{2,1,0:T(8,128)} fusion(bf16[4,256,2048]{2,1,0:T(8,128)(2,1)} %collective-permute-done.38, f32[4,2,256,2048]{3,2,1,0:T(8,128)} %bitcast.431, s32[]{:T(128)S(6)} %select_n.411), kind=kLoop, calls=%fused_computation.4 | loop fusion | flops 4194304 | bytes 20971524 | tf_op jit(solution)/shard_map/add | solution.py:253
  482.9 8.9 %copy.126 = f32[4,256,2048]{1,2,0:T(8,128)} copy(f32[4,256,2048]{2,1,0:T(8,128)} %bitcast_add_fusion.1) | data formatting | bytes 16777216 | tf_op jit(solution)/shard_map/add | solution.py:253
  511.6 7.3 collective-permute-done.41
  520.8 12.2 %collective-permute-done.40 = bf16[512,512]{1,0:T(8,128)(2,1)S(1)} collective-permute-done((bf16[512,512]{1,0:T(8,128)(2,1)S(1)}, bf16[512,512]{1,0:T(8,128)(2,1)S(1)}, u32[]{:S(2)}, u32[]{:S(2)}) %collective-permute-start.40) | collective-permute-done | bytes 524320 | tf_op jit(solution)/shard_map/ppermute | solution.py:144
  534.2 13.3 %collective-permute-done.44 = bf16[2,256,1024]{1,2,0:T(8,128)(2,1)S(1)} collective-permute-done((bf16[2,256,1024]{1,2,0:T(8,128)(2,1)S(1)}, bf16[2,256,1024]{1,2,0:T(8,128)(2,1)S(1)}, u32[]{:S(2)}, u32[]{:S(2)}) %collective-permute-start.44) | collective-permute-done | bytes 1048608 | tf_op jit(solution)/shard_map/ppermute | solution.py:144
  549.2 10.1 %bitcast_add_fusion = f32[4,256,2048]{2,1,0:T(8,128)} fusion(bf16[4,256,2048]{2,1,0:T(8,128)(2,1)} %collective-permute-done.45, f32[4,2,256,2048]{3,2,1,0:T(8,128)} %bitcast.414, s32[]{:T(128)S(6)} %select_n.411), kind=kLoop, calls=%fused_computation.3 | loop fusion | flops 4194304 | bytes 20971524 | tf_op jit(solution)/shard_map/add | solution.py:253
  559.4 8.7 %copy.128 = f32[4,256,2048]{1,2,0:T(8,128)} copy(f32[4,256,2048]{2,1,0:T(8,128)} %bitcast_add_fusion) | data formatting | bytes 16777216 | tf_op jit(solution)/shard_map/add | solution.py:253
  578.4 11.7 %collective-permute-done.48 = bf16[2,128,512]{2,1,0:T(8,128)(2,1)S(1)} collective-permute-done((bf16[2,128,512]{2,1,0:T(8,128)(2,1)S(1)}, bf16[2,128,512]{2,1,0:T(8,128)(2,1)S(1)}, u32[]{:S(2)}, u32[]{:S(2)}) %collective-permute-start.48) | collective-permute-done | bytes 262176 | tf_op jit(solution)/shard_map/ppermute | solution.py:144
  618.4 6.9 collective-permute-done.54
  626.3 15.5 %collective-permute-done.53 = bf16[512,512]{1,0:T(8,128)(2,1)S(1)} collective-permute-done((bf16[512,512]{1,0:T(8,128)(2,1)S(1)}, bf16[512,512]{1,0:T(8,128)(2,1)S(1)}, u32[]{:S(2)}, u32[]{:S(2)}) %collective-permute-start.53) | collective-permute-done | bytes 524320 | tf_op jit(solution)/shard_map/ppermute | solution.py:144
  642.3 12.4 %collective-permute-done.57 = bf16[2,256,1024]{1,2,0:T(8,128)(2,1)S(1)} collective-permute-done((bf16[2,256,1024]{1,2,0:T(8,128)(2,1)S(1)}, bf16[2,256,1024]{1,2,0:T(8,128)(2,1)S(1)}, u32[]{:S(2)}, u32[]{:S(2)}) %collective-permute-start.57) | collective-permute-done | bytes 1048608 | tf_op jit(solution)/shard_map/ppermute | solution.py:144
  669.8 8.5 %collective-permute-done.63 = bf16[256,1024]{0,1:T(8,128)(2,1)S(1)} collective-permute-done((bf16[256,1024]{0,1:T(8,128)(2,1)S(1)}, bf16[256,1024]{0,1:T(8,128)(2,1)S(1)}, u32[]{:S(2)}, u32[]{:S(2)}) %collective-permute-start.63) | collective-permute-done | bytes 524320 | tf_op jit(solution)/shard_map/ppermute | solution.py:144
  678.5 8.5 %collective-permute-done.62 = bf16[256,1024]{0,1:T(8,128)(2,1)S(1)} collective-permute-done((bf16[256,1024]{0,1:T(8,128)(2,1)S(1)}, bf16[256,1024]{0,1:T(8,128)(2,1)S(1)}, u32[]{:S(2)}, u32[]{:S(2)}) %collective-permute-start.62) | collective-permute-done | bytes 524320 | tf_op jit(solution)/shard_map/ppermute | solution.py:144
  (519 shorter events, 358.5 us)
Async XLA Ops:
  57.0 36.4 %collective-permute-start.8 = (bf16[2,256,1024]{1,2,0:T(8,128)(2,1)S(1)}, bf16[2,256,1024]{1,2,0:T(8,128)(2,1)S(1)}, u32[]{:S(2)}, u32[]{:S(2)}) collective-permute-start(bf16[2,256,1024]{1,2,0:T(8,128)(2,1)S(1)} %pad_maximum_fusion.11), channel_id=1, source_target_pairs={{0,8},{2,10},{4,12},{6,14},{8,0},{10,2},{12,4},{14,6},{16,24},{18,... | collective-permute-start | bytes 3145736 | tf_op jit(solution)/shard_map/ppermute | solution.py:144
  60.2 38.6 %collective-permute-start.7 = (bf16[2,256,1024]{1,2,0:T(8,128)(2,1)}, bf16[2,256,1024]{1,2,0:T(8,128)(2,1)}, u32[]{:S(2)}, u32[]{:S(2)}) collective-permute-start(bf16[2,256,1024]{1,2,0:T(8,128)(2,1)} %pad_maximum_fusion.10), channel_id=1, source_target_pairs={{0,2},{2,0},{4,6},{6,4},{8,10},{10,8},{12,14},{14,12},{16,18},{18,... | collective-permute-start | bytes 3145736 | tf_op jit(solution)/shard_map/ppermute | solution.py:144
  111.5 48.5 %collective-permute-start.18 = (bf16[4,256,2048]{2,1,0:T(8,128)(2,1)}, bf16[4,256,2048]{2,1,0:T(8,128)(2,1)}, u32[]{:S(2)}, u32[]{:S(2)}) collective-permute-start(bf16[4,256,2048]{2,1,0:T(8,128)(2,1)} %get-tuple-element.306), channel_id=1, source_target_pairs={{0,1},{1,0},{2,3},{3,2},{4,5},{5,4},{6,7},{7,6},{8,9},{9,8},{10,11... | collective-permute-start | bytes 12582920 | tf_op jit(solution)/shard_map/ppermute | solution.py:147
  112.7 25.9 %collective-permute-start.14 = (bf16[2,128,1024]{2,1,0:T(8,128)(2,1)}, bf16[2,128,1024]{2,1,0:T(8,128)(2,1)}, u32[]{:S(2)}, u32[]{:S(2)}) collective-permute-start(bf16[2,128,1024]{2,1,0:T(8,128)(2,1)} %get-tuple-element.326), channel_id=1, source_target_pairs={{0,8},{2,10},{4,12},{6,14},{8,0},{10,2},{12,4},{14,6},{16,24},{18,... | collective-permute-start | bytes 1572872 | tf_op jit(solution)/shard_map/ppermute | solution.py:144
  113.3 28.8 %collective-permute-start.13 = (bf16[2,2,128,512]{3,2,0,1:T(8,128)(2,1)}, bf16[2,2,128,512]{3,2,0,1:T(8,128)(2,1)}, u32[]{:S(2)}, u32[]{:S(2)}) collective-permute-start(bf16[2,2,128,512]{3,2,0,1:T(8,128)(2,1)} %maximum_select_fusion.23), channel_id=1, source_target_pairs={{0,16},{2,18},{4,20},{6,22},{8,24},{10,26},{12,28},{14,30},{16,0},... | collective-permute-start | bytes 1572872 | tf_op jit(solution)/shard_map/ppermute | solution.py:144
  118.8 27.6 %collective-permute-start.15 = (bf16[2,128,1024]{2,1,0:T(8,128)(2,1)}, bf16[2,128,1024]{2,1,0:T(8,128)(2,1)}, u32[]{:S(2)}, u32[]{:S(2)}) collective-permute-start(bf16[2,128,1024]{2,1,0:T(8,128)(2,1)} %bitcast.544), channel_id=1, source_target_pairs={{0,2},{2,0},{4,6},{6,4},{8,10},{10,8},{12,14},{14,12},{16,18},{18,... | collective-permute-start | bytes 1572872 | tf_op jit(solution)/shard_map/ppermute | solution.py:144
  120.3 36.3 %collective-permute-start.12 = (bf16[1024,512]{1,0:T(8,128)(2,1)}, bf16[1024,512]{1,0:T(8,128)(2,1)}, u32[]{:S(2)}, u32[]{:S(2)}) collective-permute-start(bf16[1024,512]{1,0:T(8,128)(2,1)} %bitcast.478), channel_id=1, source_target_pairs={{0,4},{2,6},{4,0},{6,2},{8,12},{10,14},{12,8},{14,10},{16,20},{18,... | collective-permute-start | bytes 3145736 | tf_op jit(solution)/shard_map/ppermute | solution.py:144
  176.2 36.0 %collective-permute-start.22 = (bf16[2,256,1024]{1,2,0:T(8,128)(2,1)}, bf16[2,256,1024]{1,2,0:T(8,128)(2,1)}, u32[]{:S(2)}, u32[]{:S(2)}) collective-permute-start(bf16[2,256,1024]{1,2,0:T(8,128)(2,1)} %pad_maximum_fusion.13), channel_id=1, source_target_pairs={{0,8},{2,10},{4,12},{6,14},{8,0},{10,2},{12,4},{14,6},{16,24},{18,... | collective-permute-start | bytes 3145736 | tf_op jit(solution)/shard_map/ppermute | solution.py:144
  176.5 42.8 %collective-permute-start.19 = (bf16[1024,512]{1,0:T(8,128)(2,1)}, bf16[1024,512]{1,0:T(8,128)(2,1)}, u32[]{:S(2)}, u32[]{:S(2)}) collective-permute-start(bf16[1024,512]{1,0:T(8,128)(2,1)} %bitcast.56), channel_id=1, source_target_pairs={{0,4},{2,6},{4,0},{6,2},{8,12},{10,14},{12,8},{14,10},{16,20},{18,... | collective-permute-start | bytes 3145736 | tf_op jit(solution)/shard_map/ppermute | solution.py:144
  178.1 45.3 %collective-permute-start.21 = (bf16[2,256,1024]{1,2,0:T(8,128)(2,1)}, bf16[2,256,1024]{1,2,0:T(8,128)(2,1)}, u32[]{:S(2)}, u32[]{:S(2)}) collective-permute-start(bf16[2,256,1024]{1,2,0:T(8,128)(2,1)} %pad_maximum_fusion.12), channel_id=1, source_target_pairs={{0,2},{2,0},{4,6},{6,4},{8,10},{10,8},{12,14},{14,12},{16,18},{18,... | collective-permute-start | bytes 3145736 | tf_op jit(solution)/shard_map/ppermute | solution.py:144
  179.7 29.8 %collective-permute-start.20 = (bf16[2,2,128,512]{3,2,0,1:T(8,128)(2,1)}, bf16[2,2,128,512]{3,2,0,1:T(8,128)(2,1)}, u32[]{:S(2)}, u32[]{:S(2)}) collective-permute-start(bf16[2,2,128,512]{3,2,0,1:T(8,128)(2,1)} %get-tuple-element.318), channel_id=1, source_target_pairs={{0,16},{2,18},{4,20},{6,22},{8,24},{10,26},{12,28},{14,30},{16,0},... | collective-permute-start | bytes 1572872 | tf_op jit(solution)/shard_map/ppermute | solution.py:144
  233.3 29.5 %collective-permute-start.26 = (bf16[4,256,2048]{2,1,0:T(8,128)(2,1)S(1)}, bf16[4,256,2048]{2,1,0:T(8,128)(2,1)S(1)}, u32[]{:S(2)}, u32[]{:S(2)}) collective-permute-start(bf16[4,256,2048]{2,1,0:T(8,128)(2,1)S(1)} %get-tuple-element.304), channel_id=1, source_target_pairs={{0,1},{1,0},{2,3},{3,2},{4,5},{5,4},{6,7},{7,6},{8,9},{9,8},{10,11... | collective-permute-start | bytes 12582920 | tf_op jit(solution)/shard_map/ppermute | solution.py:147
  233.5 27.4 %collective-permute-start.24 = (bf16[2,2,128,512]{3,2,0,1:T(8,128)(2,1)S(1)}, bf16[2,2,128,512]{3,2,0,1:T(8,128)(2,1)S(1)}, u32[]{:S(2)}, u32[]{:S(2)}) collective-permute-start(bf16[2,2,128,512]{3,2,0,1:T(8,128)(2,1)S(1)} %get-tuple-element.316), channel_id=1, source_target_pairs={{0,16},{2,18},{4,20},{6,22},{8,24},{10,26},{12,28},{14,30},{16,0},... | collective-permute-start | bytes 1572872 | tf_op jit(solution)/shard_map/ppermute | solution.py:144
  237.1 25.3 %collective-permute-start.23 = (bf16[1024,512]{1,0:T(8,128)(2,1)S(1)}, bf16[1024,512]{1,0:T(8,128)(2,1)S(1)}, u32[]{:S(2)}, u32[]{:S(2)}) collective-permute-start(bf16[1024,512]{1,0:T(8,128)(2,1)S(1)} %bitcast.480), channel_id=1, source_target_pairs={{0,4},{2,6},{4,0},{6,2},{8,12},{10,14},{12,8},{14,10},{16,20},{18,... | collective-permute-start | bytes 3145736 | tf_op jit(solution)/shard_map/ppermute | solution.py:144
  275.4 25.7 %collective-permute-start.28 = (bf16[2,2,128,512]{3,2,0,1:T(8,128)(2,1)S(1)}, bf16[2,2,128,512]{3,2,0,1:T(8,128)(2,1)S(1)}, u32[]{:S(2)}, u32[]{:S(2)}) collective-permute-start(bf16[2,2,128,512]{3,2,0,1:T(8,128)(2,1)S(1)} %get-tuple-element.312), channel_id=1, source_target_pairs={{0,16},{2,18},{4,20},{6,22},{8,24},{10,26},{12,28},{14,30},{16,0},... | collective-permute-start | bytes 1572872 | tf_op jit(solution)/shard_map/ppermute | solution.py:144
  302.7 28.3 %collective-permute-start.30 = (bf16[2,2,128,512]{3,2,0,1:T(8,128)(2,1)S(1)}, bf16[2,2,128,512]{3,2,0,1:T(8,128)(2,1)S(1)}, u32[]{:S(2)}, u32[]{:S(2)}) collective-permute-start(bf16[2,2,128,512]{3,2,0,1:T(8,128)(2,1)S(1)} %get-tuple-element.310), channel_id=1, source_target_pairs={{0,16},{2,18},{4,20},{6,22},{8,24},{10,26},{12,28},{14,30},{16,0},... | collective-permute-start | bytes 1572872 | tf_op jit(solution)/shard_map/ppermute | solution.py:144
  303.5 27.7 %collective-permute-start.29 = (bf16[1024,512]{1,0:T(8,128)(2,1)S(1)}, bf16[1024,512]{1,0:T(8,128)(2,1)S(1)}, u32[]{:S(2)}, u32[]{:S(2)}) collective-permute-start(bf16[1024,512]{1,0:T(8,128)(2,1)S(1)} %bitcast.485), channel_id=1, source_target_pairs={{0,4},{2,6},{4,0},{6,2},{8,12},{10,14},{12,8},{14,10},{16,20},{18,... | collective-permute-start | bytes 3145736 | tf_op jit(solution)/shard_map/ppermute | solution.py:144
  358.7 30.9 %collective-permute-start.32 = (bf16[1024,512]{1,0:T(8,128)(2,1)}, bf16[1024,512]{1,0:T(8,128)(2,1)}, u32[]{:S(2)}, u32[]{:S(2)}) collective-permute-start(bf16[1024,512]{1,0:T(8,128)(2,1)} %dynamic-slice_bitcast_fusion.5), channel_id=1, source_target_pairs={{0,4},{2,6},{4,0},{6,2},{8,12},{10,14},{12,8},{14,10},{16,20},{18,... | collective-permute-start | bytes 3145736 | tf_op jit(solution)/shard_map/ppermute | solution.py:144
  392.1 44.0 %collective-permute-start.33 = (bf16[512,512]{1,0:T(8,128)(2,1)}, bf16[512,512]{1,0:T(8,128)(2,1)}, u32[]{:S(2)}, u32[]{:S(2)}) collective-permute-start(bf16[512,512]{1,0:T(8,128)(2,1)} %dynamic-slice_bitcast_fusion.11), channel_id=1, source_target_pairs={{0,16},{2,18},{4,20},{6,22},{8,24},{10,26},{12,28},{14,30},{16,0},... | collective-permute-start | bytes 1572872 | tf_op jit(solution)/shard_map/ppermute | solution.py:144
  396.1 41.3 %collective-permute-start.34 = (bf16[1024,512]{1,0:T(8,128)(2,1)}, bf16[1024,512]{1,0:T(8,128)(2,1)}, u32[]{:S(2)}, u32[]{:S(2)}) collective-permute-start(bf16[1024,512]{1,0:T(8,128)(2,1)} %dynamic-slice_bitcast_fusion.4), channel_id=1, source_target_pairs={{0,4},{2,6},{4,0},{6,2},{8,12},{10,14},{12,8},{14,10},{16,20},{18,... | collective-permute-start | bytes 3145736 | tf_op jit(solution)/shard_map/ppermute | solution.py:144
  445.1 27.7 %collective-permute-start.38 = (bf16[4,256,2048]{2,1,0:T(8,128)(2,1)}, bf16[4,256,2048]{2,1,0:T(8,128)(2,1)}, u32[]{:S(2)}, u32[]{:S(2)}) collective-permute-start(bf16[4,256,2048]{2,1,0:T(8,128)(2,1)} %fusion), channel_id=1, source_target_pairs={{0,1},{1,0},{2,3},{3,2},{4,5},{5,4},{6,7},{7,6},{8,9},{9,8},{10,11... | collective-permute-start | bytes 12582920 | tf_op jit(solution)/shard_map/ppermute | solution.py:147
  445.3 26.6 %collective-permute-start.36 = (bf16[512,512]{1,0:T(8,128)(2,1)S(1)}, bf16[512,512]{1,0:T(8,128)(2,1)S(1)}, u32[]{:S(2)}, u32[]{:S(2)}) collective-permute-start(bf16[512,512]{1,0:T(8,128)(2,1)S(1)} %dynamic-slice_bitcast_fusion.10), channel_id=1, source_target_pairs={{0,16},{2,18},{4,20},{6,22},{8,24},{10,26},{12,28},{14,30},{16,0},... | collective-permute-start | bytes 1572872 | tf_op jit(solution)/shard_map/ppermute | solution.py:144
  496.0 53.2 %collective-permute-start.45 = (bf16[4,256,2048]{2,1,0:T(8,128)(2,1)S(1)}, bf16[4,256,2048]{2,1,0:T(8,128)(2,1)}, u32[]{:S(2)}, u32[]{:S(2)}) collective-permute-start(bf16[4,256,2048]{2,1,0:T(8,128)(2,1)S(1)} %fusion.1), channel_id=1, source_target_pairs={{0,1},{1,0},{2,3},{3,2},{4,5},{5,4},{6,7},{7,6},{8,9},{9,8},{10,11... | collective-permute-start | bytes 12582920 | tf_op jit(solution)/shard_map/ppermute | solution.py:147
  518.9 28.6 %collective-permute-start.44 = (bf16[2,256,1024]{1,2,0:T(8,128)(2,1)S(1)}, bf16[2,256,1024]{1,2,0:T(8,128)(2,1)S(1)}, u32[]{:S(2)}, u32[]{:S(2)}) collective-permute-start(bf16[2,256,1024]{1,2,0:T(8,128)(2,1)S(1)} %slice_bitcast_fusion.2), channel_id=1, source_target_pairs={{0,8},{2,10},{4,12},{6,14},{8,0},{10,2},{12,4},{14,6},{16,24},{18,... | collective-permute-start | bytes 3145736 | tf_op jit(solution)/shard_map/ppermute | solution.py:144
  518.9 28.6 %collective-permute-start.43 = (bf16[2,256,1024]{1,2,0:T(8,128)(2,1)S(1)}, bf16[2,256,1024]{1,2,0:T(8,128)(2,1)S(1)}, u32[]{:S(2)}, u32[]{:S(2)}) collective-permute-start(bf16[2,256,1024]{1,2,0:T(8,128)(2,1)S(1)} %slice_bitcast_fusion.3), channel_id=1, source_target_pairs={{0,2},{2,0},{4,6},{6,4},{8,10},{10,8},{12,14},{14,12},{16,18},{18,... | collective-permute-start | bytes 3145736 | tf_op jit(solution)/shard_map/ppermute | solution.py:144
  574.7 28.4 %collective-permute-start.47 = (bf16[512,512]{1,0:T(8,128)(2,1)}, bf16[512,512]{1,0:T(8,128)(2,1)}, u32[]{:S(2)}, u32[]{:S(2)}) collective-permute-start(bf16[512,512]{1,0:T(8,128)(2,1)} %dynamic-slice_bitcast_fusion.8), channel_id=1, source_target_pairs={{0,16},{2,18},{4,20},{6,22},{8,24},{10,26},{12,28},{14,30},{16,0},... | collective-permute-start | bytes 1572872 | tf_op jit(solution)/shard_map/ppermute | solution.py:144
  612.9 29.1 %collective-permute-start.52 = (bf16[1024,512]{1,0:T(8,128)(2,1)S(1)}, bf16[1024,512]{1,0:T(8,128)(2,1)S(1)}, u32[]{:S(2)}, u32[]{:S(2)}) collective-permute-start(bf16[1024,512]{1,0:T(8,128)(2,1)S(1)} %dynamic-slice_bitcast_fusion), channel_id=1, source_target_pairs={{0,4},{2,6},{4,0},{6,2},{8,12},{10,14},{12,8},{14,10},{16,20},{18,... | collective-permute-start | bytes 3145736 | tf_op jit(solution)/shard_map/ppermute | solution.py:144
  615.4 26.4 %collective-permute-start.53 = (bf16[512,512]{1,0:T(8,128)(2,1)S(1)}, bf16[512,512]{1,0:T(8,128)(2,1)S(1)}, u32[]{:S(2)}, u32[]{:S(2)}) collective-permute-start(bf16[512,512]{1,0:T(8,128)(2,1)S(1)} %dynamic-slice_bitcast_fusion.7), channel_id=1, source_target_pairs={{0,16},{2,18},{4,20},{6,22},{8,24},{10,26},{12,28},{14,30},{16,0},... | collective-permute-start | bytes 1572872 | tf_op jit(solution)/shard_map/ppermute | solution.py:144
  618.1 36.6 %collective-permute-start.57 = (bf16[2,256,1024]{1,2,0:T(8,128)(2,1)S(1)}, bf16[2,256,1024]{1,2,0:T(8,128)(2,1)S(1)}, u32[]{:S(2)}, u32[]{:S(2)}) collective-permute-start(bf16[2,256,1024]{1,2,0:T(8,128)(2,1)S(1)} %slice_bitcast_fusion), channel_id=1, source_target_pairs={{0,8},{2,10},{4,12},{6,14},{8,0},{10,2},{12,4},{14,6},{16,24},{18,... | collective-permute-start | bytes 3145736 | tf_op jit(solution)/shard_map/ppermute | solution.py:144
  625.3 29.5 %collective-permute-start.56 = (bf16[2,256,1024]{1,2,0:T(8,128)(2,1)S(1)}, bf16[2,256,1024]{1,2,0:T(8,128)(2,1)S(1)}, u32[]{:S(2)}, u32[]{:S(2)}) collective-permute-start(bf16[2,256,1024]{1,2,0:T(8,128)(2,1)S(1)} %slice_bitcast_fusion.1), channel_id=1, source_target_pairs={{0,2},{2,0},{4,6},{6,4},{8,10},{10,8},{12,14},{14,12},{16,18},{18,... | collective-permute-start | bytes 3145736 | tf_op jit(solution)/shard_map/ppermute | solution.py:144
  665.9 30.8 %collective-permute-start.59 = (bf16[512,512]{1,0:T(8,128)(2,1)}, bf16[512,512]{1,0:T(8,128)(2,1)}, u32[]{:S(2)}, u32[]{:S(2)}) collective-permute-start(bf16[512,512]{1,0:T(8,128)(2,1)} %dynamic-slice_bitcast_fusion.6), channel_id=1, source_target_pairs={{0,16},{2,18},{4,20},{6,22},{8,24},{10,26},{12,28},{14,30},{16,0},... | collective-permute-start | bytes 1572872 | tf_op jit(solution)/shard_map/ppermute | solution.py:144
  711.0 26.2 %collective-permute-start.74 = (f32[256,2048]{1,0:T(8,128)S(1)}, f32[256,2048]{1,0:T(8,128)}, u32[]{:S(2)}, u32[]{:S(2)}) collective-permute-start(f32[256,2048]{1,0:T(8,128)S(1)} %copy-done.8), channel_id=1, source_target_pairs={{0,1},{1,0},{2,3},{3,2},{4,5},{5,4},{6,7},{7,6},{8,9},{9,8},{10,11... | collective-permute-start | bytes 6291464 | tf_op jit(solution)/shard_map/ppermute | solution.py:147
  (117 other events, 1198.7 us)

commit v3 on v1

v3 whole, which is shorter than its diff:
```python
import functools

import jax
import jax.numpy as jnp
from jax import lax
from jax.experimental import pallas as pl
from jax.experimental.pallas import tpu as pltpu
from jax.sharding import PartitionSpec as P

HEAD_DIM = 64
ROT_DIM = 32
LANES = 128
NEGATIVE = -1e30
EPSILON = 1e-05
GELU_A = 0.7978845608028654
GELU_B = 0.044715
X_BIT, Y_BIT, ZL_BIT = 0, 1, 2
BF = jnp.bfloat16
F32 = jnp.float32


def dot_nt(a, b):
    return lax.dot_general(a, b, (((1,), (1,)), ((), ())), preferred_element_type=F32)


def dot_tn(a, b):
    return lax.dot_general(a, b, (((0,), (0,)), ((), ())), preferred_element_type=F32)


def attention_kernel(
    pre_ref, grad_ref, cos_ref, left_ref, right_ref, line_ref, column_ref, out_ref, dpre_ref
):
    half, width = grad_ref.shape[2:]
    rows = 2 * half
    scaling = HEAD_DIM ** (-0.5)

    def both(ref, cols=slice(None)):
        block = ref[:, 0, :, cols]
        return block.reshape(rows, block.shape[-1])

    cos, left, right = both(cos_ref), both(left_ref), both(right_ref)
    head_of = lax.broadcasted_iota(jnp.int32, (rows, LANES), 1) // HEAD_DIM

    def turn(v, sign):
        ahead = pltpu.roll(v, LANES - ROT_DIM // 2, 1)
        behind = pltpu.roll(v, ROT_DIM // 2, 1)
        return v * cos + sign * (ahead * left + behind * right)

    line, column = line_ref[0], column_ref[0]
    allowed = (line[:, 0:1] >= column[0:1]) & (line[:, 1:2] <= column[0:1])
    for pair in range(width // LANES):
        parts = [slice(b + pair * LANES, b + (pair + 1) * LANES) for b in (0, width, 2 * width)]
        q = turn(both(pre_ref, parts[0]), 1.0).astype(BF)
        k = turn(both(pre_ref, parts[1]), 1.0).astype(BF)
        v = both(pre_ref, parts[2]).astype(BF)
        g = both(grad_ref, parts[0])
        att = dq = dk = dv = None
        for h in range(LANES // HEAD_DIM):
            mine = head_of == h
            qh = jnp.where(mine, q, 0).astype(BF)
            gh = jnp.where(mine, g, 0).astype(BF)
            s = jnp.where(allowed, dot_nt(qh, k) * scaling, NEGATIVE)
            e = jnp.exp(s - jnp.max(s, axis=-1, keepdims=True))
            p = e * (1.0 / jnp.sum(e, axis=-1, keepdims=True))
            low = p.astype(BF)
            att_h = jnp.dot(low, v, preferred_element_type=F32)
            dp = dot_nt(gh, v)
            inner = jnp.sum(p * dp, axis=-1, keepdims=True)
            ds = (p * (dp - inner)).astype(BF)
            dq_h = jnp.dot(ds, k, preferred_element_type=F32)
            dk_h = dot_tn(ds, qh)
            dv_h = dot_tn(low, gh)
            att = att_h if h == 0 else jnp.where(mine, att_h, att)
            dq = dq_h if h == 0 else jnp.where(mine, dq_h, dq)
            dk = dk_h if h == 0 else dk + dk_h
            dv = dv_h if h == 0 else dv + dv_h
        for ref, cols, value in (
            (out_ref, parts[0], att),
            (dpre_ref, parts[0], turn(dq * scaling, -1.0)),
            (dpre_ref, parts[1], turn(dk * scaling, -1.0)),
            (dpre_ref, parts[2], dv),
        ):
            ref[:, 0, :, cols] = value.astype(BF).reshape(2, half, LANES)


def attention(pre, grad, tables, line, column):
    count, rows = column.shape[0], column.shape[2]
    half, width = rows // 2, grad.shape[1]

    def split(value):
        return value.reshape(2, count, half, value.shape[1])

    def block(cols):
        return pl.BlockSpec((2, 1, half, cols), lambda s: (0, s, 0, 0))

    attended, dpre = pl.pallas_call(
        attention_kernel,
        grid=(count,),
        out_shape=[
            jax.ShapeDtypeStruct((2, count, half, width), BF),
            jax.ShapeDtypeStruct((2, count, half, 3 * width), BF),
        ],
        in_specs=[
            block(3 * width),
            block(width),
            block(LANES),
            block(LANES),
            block(LANES),
            pl.BlockSpec((1, rows, LANES), lambda s: (s, 0, 0)),
            pl.BlockSpec((1, 8, rows), lambda s: (s, 0, 0)),
        ],
        out_specs=[block(width), block(3 * width)],
        compiler_params=pltpu.CompilerParams(vmem_limit_bytes=48 * 1024 * 1024),
        cost_estimate=pl.CostEstimate(
            flops=20 * 10**9, bytes_accessed=16 * 10**6, transcendentals=4 * 10**6
        ),
    )(split(pre), split(grad), *[split(t) for t in tables], line, column)
    return attended.reshape(2 * count * half, width), dpre.reshape(2 * count * half, 3 * width)


def rotary_lanes(places):
    halfway = ROT_DIM // 2
    lane = jnp.arange(LANES, dtype=jnp.int32) % HEAD_DIM
    freqs = 10000.0 ** (-(lane % halfway).astype(F32) * 2.0 / ROT_DIM)
    angles = places.astype(F32)[:, None] * freqs[None, :]
    turned = lane < ROT_DIM
    cos = jnp.where(turned, jnp.cos(angles), 1.0)
    sin = jnp.where(turned, jnp.sin(angles), 0.0)
    return cos, jnp.where(lane < halfway, -sin, 0.0), jnp.where(lane >= halfway, sin, 0.0)


def join_kernel(plan, *refs):
    count = len(plan)
    out_ref, sems = refs[-2], refs[-1]
    copies = [
        pltpu.make_async_copy(
            refs[which].at[pl.ds(source, size)], out_ref.at[pl.ds(target, size)], sems.at[i]
        )
        for i, (which, source, size, target) in enumerate(plan)
    ]
    for copy in copies:
        copy.start()
    for copy in copies:
        copy.wait()


def join_rows(arrays, plan):
    rows = sum(size for _, _, size, _ in plan)
    first = arrays[0]
    anywhere = pl.BlockSpec(memory_space=pl.ANY)
    return pl.pallas_call(
        functools.partial(join_kernel, plan),
        out_shape=jax.ShapeDtypeStruct((rows,) + first.shape[1:], first.dtype),
        in_specs=[anywhere] * len(arrays),
        out_specs=anywhere,
        scratch_shapes=[pltpu.SemaphoreType.DMA((len(plan),))],
        cost_estimate=pl.CostEstimate(
            flops=0, bytes_accessed=2 * rows * first.shape[1] * first.dtype.itemsize, transcendentals=0
        ),
    )(*arrays)


def place_kernel(core_ref, own_ref, other_ref, out_ref, sems):
    half = own_ref.shape[0]
    core = core_ref[0]
    copies = [
        pltpu.make_async_copy(
            ref, out_ref.at[pl.ds(pl.multiple_of(which * half, half), half)], sems.at[i]
        )
        for i, (ref, which) in enumerate(((own_ref, core), (other_ref, 1 - core)))
    ]
    for copy in copies:
        copy.start()
    for copy in copies:
        copy.wait()


def place_halves(core, own, other):
    anywhere = pl.BlockSpec(memory_space=pl.ANY)
    return pl.pallas_call(
        place_kernel,
        out_shape=jax.ShapeDtypeStruct((2 * own.shape[0],) + own.shape[1:], own.dtype),
        grid_spec=pltpu.PrefetchScalarGridSpec(
            num_scalar_prefetch=1,
            grid=(1,),
            in_specs=[anywhere] * 2,
            out_specs=anywhere,
            scratch_shapes=[pltpu.SemaphoreType.DMA((2,))],
        ),
        cost_estimate=pl.CostEstimate(
            flops=0, bytes_accessed=4 * own.size * own.dtype.itemsize, transcendentals=0
        ),
    )(core.reshape(1).astype(jnp.int32), own, other)


def pair_kernel(a_ref, b_ref, c_ref, d_ref, out_ref):
    total = dot_nt(a_ref[...], b_ref[...]) + dot_nt(c_ref[...], d_ref[...])
    out_ref[...] = total.astype(out_ref.dtype)


def pair_dot(part, parts, a, b, c, d, tile=256):
    rows, width = a.shape[0] // parts, b.shape[0]
    return pl.pallas_call(
        pair_kernel,
        grid=(width // tile,),
        out_shape=jax.ShapeDtypeStruct((rows, width), BF),
        in_specs=[
            pl.BlockSpec((rows, a.shape[1]), lambda i: (part, 0)),
            pl.BlockSpec((tile, b.shape[1]), lambda i: (i, 0)),
            pl.BlockSpec((rows, c.shape[1]), lambda i: (part, 0)),
            pl.BlockSpec((tile, d.shape[1]), lambda i: (i, 0)),
        ],
        out_specs=pl.BlockSpec((rows, tile), lambda i: (0, i)),
        compiler_params=pltpu.CompilerParams(vmem_limit_bytes=48 * 1024 * 1024),
        cost_estimate=pl.CostEstimate(
            flops=2 * rows * width * (a.shape[1] + c.shape[1]),
            bytes_accessed=2 * (rows + width) * (a.shape[1] + c.shape[1]) + 2 * rows * width,
            transcendentals=0,
        ),
    )(a, b, c, d)


def standardize(inputs):
    average = jnp.mean(inputs, axis=-1, keepdims=True)
    centered = inputs - average
    inv_std = lax.rsqrt(jnp.mean(centered * centered, axis=-1, keepdims=True) + EPSILON)
    return centered * inv_std, inv_std


def input_gradient(normed_grad, cot, normal_x, inv_std, gain):
    scaled = normed_grad * gain
    return cot + inv_std * (
        scaled
        - jnp.mean(scaled, axis=-1, keepdims=True)
        - normal_x * jnp.mean(scaled * normal_x, axis=-1, keepdims=True)
    )


def norm_kernel(table_ref, tok_ref, cot_ref, gain_ref, shift_ref, normed_ref, mixed_ref, *, cols):
    normal_x, _ = standardize(tok_ref[...].astype(F32))
    normed = (normal_x * gain_ref[...].astype(F32) + shift_ref[...].astype(F32)).astype(BF)
    for n in range(tok_ref.shape[1] // cols):
        target = pl.ds(pl.multiple_of(table_ref[n], cols), cols)
        normed_ref[:, target] = normed[:, n * cols : (n + 1) * cols]
        mixed_ref[:, target] = cot_ref[:, n * cols : (n + 1) * cols]


def natural(table_ref, kept_ref, got_ref, cols):
    parts = []
    for n in range(kept_ref.shape[1] // cols):
        source = pl.ds(pl.multiple_of(table_ref[n], cols), cols)
        parts.append(kept_ref[:, source].astype(F32) + got_ref[:, source].astype(F32))
    return jnp.concatenate(parts, axis=1)


def norm_back_kernel(
    table_ref, tok_ref, cot_ref, gain_ref, kept_ref, got_ref, grad_ref, lines_ref, *, cols
):
    normal_x, inv_std = standardize(tok_ref[...].astype(F32))
    cot = cot_ref[...].astype(F32)
    normed_grad = natural(table_ref, kept_ref, got_ref, cols)
    grad_ref[...] = input_gradient(
        normed_grad, cot, normal_x, inv_std, gain_ref[...].astype(F32)
    )

    @pl.when(pl.program_id(0) == 0)
    def _():
        lines_ref[...] = jnp.zeros_like(lines_ref)

    for row, value in enumerate((normed_grad * normal_x, normed_grad, cot)):
        lines_ref[row : row + 1, :] += jnp.sum(value, axis=0, keepdims=True)


def result_kernel(table_ref, tok_ref, bias_ref, kept_ref, got_ref, out_ref, *, cols):
    branches = natural(table_ref, kept_ref, got_ref, cols)
    out_ref[...] = (tok_ref[...].astype(F32) + branches + bias_ref[...].astype(F32)).astype(BF)


def on_half(kernel, table, cols, whole, lines, mine, outs, tile=64):
    half, width = whole[0].shape[0] // 2, whole[0].shape[1]
    steps = half // tile
    last_entry = table.shape[0] - 1
    block = pl.BlockSpec((tile, width), lambda i, t: (i, 0))
    return pl.pallas_call(
        functools.partial(kernel, cols=cols),
        out_shape=outs,
        grid_spec=pltpu.PrefetchScalarGridSpec(
            num_scalar_prefetch=1,
            grid=(steps,),
            in_specs=[pl.BlockSpec((tile, width), lambda i, t: (t[last_entry] * steps + i, 0))]
            * len(whole)
            + [pl.BlockSpec((1, width), lambda i, t: (0, 0))] * len(lines)
            + [block] * len(mine),
            out_specs=[
                block if out.shape[0] == half else pl.BlockSpec(out.shape, lambda i, t: (0, 0))
                for out in outs
            ],
        ),
        compiler_params=pltpu.CompilerParams(vmem_limit_bytes=32 * 1024 * 1024),
        cost_estimate=pl.CostEstimate(
            flops=20 * half * width, bytes_accessed=12 * half * width, transcendentals=0
        ),
    )(table, *whole, *[line.reshape(1, width) for line in lines], *mine)


def local_part(dp_size):
    top_bits = [b for b in range(3, dp_size.bit_length() - 1)]
    first = (((0,), (0,)), ((), ()))

    def swap(value, bit):
        return lax.ppermute(value, "dp", [(i, i ^ (1 << bit)) for i in range(dp_size)])

    def swap_core(value):
        return lax.ppermute(value, "tensor", [(0, 1), (1, 0)])

    def swap_mixed(value, bits):
        pairs = [(2 * i + c, 2 * (i ^ (1 << bits[c])) + c) for i in range(dp_size) for c in (0, 1)]
        return lax.ppermute(value, ("dp", "tensor"), pairs)

    def swap_first(value):
        return swap_mixed(value, (ZL_BIT, X_BIT))

    def swap_second(value):
        return swap_mixed(value, (X_BIT, ZL_BIT))

    def ordered(bit, own, other, axis):
        return jnp.where(
            bit == 0,
            jnp.concatenate([own, other], axis),
            jnp.concatenate([other, own], axis),
        )

    def part_of(value, index, axis):
        size = value.shape[axis] // 2
        return lax.dynamic_slice_in_dim(value, index * size, size, axis)

    def sync(*values):
        return lax.optimization_barrier(values)

    def local(
        tokens,
        segments,
        ln_gain,
        ln_shift,
        qkv_weight,
        qkv_bias,
        out_weight,
        up_weight,
        up_bias,
        down_weight,
        branch_bias,
        cotangent,
    ):
        rows, width = tokens.shape
        half = rows // 2
        wide = width // 2
        share = qkv_weight.shape[0]
        unit = 4 * share
        cols = 2 * share
        me = lax.axis_index("dp")
        core = lax.axis_index("tensor")
        x_mine, y_mine, zl_mine = (me >> X_BIT) & 1, (me >> Y_BIT) & 1, (me >> ZL_BIT) & 1
        block = 2 * x_mine + zl_mine
        att = qkv_weight.shape[2] // 4
        hid = up_weight.shape[1] // 4
        tops = 2 ** len(top_bits)

        n = jnp.arange(4 * tops, dtype=jnp.int32)
        table = ((((n & 1) ^ y_mine) * tops + ((n >> 2) ^ (me >> 3))) * 2 + ((n >> 1) & 1)) * cols
        table = jnp.concatenate([table, core.reshape(1)]).astype(jnp.int32)
        aligned = cols % LANES == 0

        def relative(split):
            for axis, bit in enumerate([Y_BIT] + top_bits[::-1]):
                split = jnp.where((me >> bit) & 1 == 1, jnp.flip(split, axis + 1), split)
            return split

        def to_mixed(value):
            count = value.shape[0]
            split = value.reshape(count, tops, 2, 2, cols).transpose(0, 3, 1, 2, 4)
            split = relative(split.reshape((count, 2) + (2,) * len(top_bits) + (unit,)))
            return split.reshape(count, width)

        def from_mixed(value):
            count = value.shape[0]
            split = relative(value.reshape((count, 2) + (2,) * len(top_bits) + (unit,)))
            split = split.reshape(count, 2, tops, 2, cols).transpose(0, 2, 3, 1, 4)
            return split.reshape(count, width)

        def my_rows(value):
            return lax.dynamic_slice_in_dim(value, core * half, half, 0)

        def norm_forward():
            shape = jax.ShapeDtypeStruct((half, width), BF)
            if aligned:
                return on_half(
                    norm_kernel,
                    table,
                    cols,
                    [tokens, cotangent],
                    [ln_gain, ln_shift],
                    [],
                    [shape, shape],
                )
            normal_x, _ = standardize(my_rows(tokens).astype(F32))
            normed = normal_x * ln_gain.astype(F32) + ln_shift.astype(F32)
            return to_mixed(normed.astype(BF)), to_mixed(my_rows(cotangent))

        def norm_backward(kept, got):
            if aligned:
                return on_half(
                    norm_back_kernel,
                    table,
                    cols,
                    [tokens, cotangent],
                    [ln_gain],
                    [kept, got],
                    [
                        jax.ShapeDtypeStruct((half, width), F32),
                        jax.ShapeDtypeStruct((8, width), F32),
                    ],
                )
            normal_x, inv_std = standardize(my_rows(tokens).astype(F32))
            cot = my_rows(cotangent).astype(F32)
            grad = from_mixed(add(kept, got))
            lines = jnp.stack(
                [jnp.sum(v, axis=0) for v in (grad * normal_x, grad, cot)]
                + [jnp.zeros((width,), F32)] * 5
            )
            return input_gradient(grad, cot, normal_x, inv_std, ln_gain.astype(F32)), lines

        def finish(kept, got):
            if aligned:
                return on_half(
                    result_kernel,
                    table,
                    cols,
                    [tokens],
                    [branch_bias],
                    [kept, got],
                    [jax.ShapeDtypeStruct((half, width), BF)],
                )[0]
            branches = from_mixed(add(kept, got))
            return (my_rows(tokens).astype(F32) + branches + branch_bias.astype(F32)).astype(BF)

        def w_x(piece):
            got = swap(part_of(piece, 1 - x_mine, 1), X_BIT)
            return ordered(x_mine, part_of(piece, x_mine, 1), got, 0)

        def w_zl(w):
            got = swap(part_of(w, 1 - zl_mine, 1), ZL_BIT)
            return ordered(zl_mine, part_of(w, zl_mine, 1), got, 0)

        def w_top(w):
            rest = None
            for bit in top_bits:
                mine = w if rest is None else jnp.concatenate([w, rest])
                got = swap(mine, bit)
                rest = got if rest is None else jnp.concatenate([rest, got])
            return rest

        def w_join(own, rest, far, far_rest):
            return jnp.concatenate([own, rest, far, far_rest])

        def add(*values):
            total = values[0].astype(F32)
            for value in values[1:]:
                total = total + value.astype(F32)
            return total

        def g_y(grad):
            return add(grad[:wide], swap(grad[wide:], Y_BIT)).astype(BF)

        def g_top(grad):
            for bit in reversed(top_bits):
                cut = grad.shape[0] // 2
                grad = add(grad[:cut], swap(grad[cut:], bit)).astype(BF)
            return grad

        def g_zl(grad):
            got = swap(part_of(grad, 1 - zl_mine, 0), ZL_BIT)
            return ordered(zl_mine, part_of(grad, zl_mine, 0), got, 1)

        def g_x(grad):
            got = swap(part_of(grad, 1 - x_mine, 0), X_BIT)
            return ordered(x_mine, part_of(grad, x_mine, 0), got, 1)

        def a_join(pair, second, got_pair, got_second):
            return join_rows(
                [pair, second, got_pair, got_second],
                (
                    (0, 0, 2 * half, 0),
                    (1, 0, 2 * half, 2 * half),
                    (2, 0, half, 4 * half),
                    (3, 0, half, 5 * half),
                    (2, half, half, 6 * half),
                    (3, half, half, 7 * half),
                ),
            )

        def s_join(kept, got):
            got = got.reshape(4, half, width)
            kept = kept.reshape(4, half, width)
            pair = add(kept[:2], jnp.stack([got[0], got[2]])).reshape(2 * half, width)
            send = add(kept[2:], jnp.stack([got[1], got[3]])).astype(BF).reshape(2 * half, width)
            return pair, send

        uu = w_x(up_weight)
        n_own, c_own = norm_forward()
        seg = segments.reshape(1, rows)
        seg = jnp.concatenate([seg, swap_first(seg)])
        uu, n_own, c_own, seg, qkv_weight, out_weight, down_weight = sync(
            uu, n_own, c_own, seg, qkv_weight, out_weight, down_weight
        )
        uu = w_zl(uu)
        seg = jnp.concatenate([seg, swap_second(seg)])
        n_pair = jnp.concatenate([n_own, swap_first(n_own)])
        qkv_piece = qkv_weight.reshape(share, 3, 4, att).swapaxes(1, 2).reshape(share, 4, 3 * att)
        out_piece = out_weight.T.reshape(share, 4, att)
        aa = w_x(jnp.concatenate([qkv_piece, out_piece], axis=2).reshape(share, 16 * att))
        uu, n_pair, aa, c_own, seg, down_weight = sync(uu, n_pair, aa, c_own, seg, down_weight)
        u_rest = w_top(uu)
        u_far = swap(uu, Y_BIT)
        n_second = swap_second(n_pair)
        n_got_pair = swap_core(n_pair)
        aa = w_zl(aa)
        dd = w_x(down_weight.T)
        uu, u_rest, u_far, n_pair, n_second, n_got_pair, aa, dd, c_own, seg = sync(
            uu, u_rest, u_far, n_pair, n_second, n_got_pair, aa, dd, c_own, seg
        )
        a_rest = w_top(aa)
        a_far = swap(aa, Y_BIT)
        u_far_rest = swap(u_rest, Y_BIT)
        n_got_second = swap_core(n_second)
        dd = w_zl(dd)
        c_pair = jnp.concatenate([c_own, swap_first(c_own)])
        order = jnp.broadcast_to(jnp.arange(rows, dtype=jnp.int32), (4, rows))
        begins = jnp.concatenate([jnp.ones((4, 1), bool), seg[:, 1:] != seg[:, :-1]], axis=1)
        opening = lax.cummax(jnp.where(begins, order, 0), axis=1)

        def halves(value):
            return jnp.where(core == 0, value, jnp.roll(value, half, axis=1))

        order, opening = halves(order), halves(opening)
        tables = rotary_lanes(
            (order - opening).reshape(4, 2, half).swapaxes(0, 1).reshape(4 * rows)
        )
        line = jnp.stack([order, opening], axis=2)
        line = jnp.pad(line, ((0, 0), (0, 0), (0, LANES - 2)))
        column = jnp.broadcast_to(order[:, None, :], (4, 8, rows))
        (
            uu,
            u_rest,
            u_far,
            u_far_rest,
            aa,
            a_rest,
            a_far,
            dd,
            c_pair,
            n_pair,
            n_second,
            n_got_pair,
            n_got_second,
            tables,
            line,
            column,
        ) = sync(
            uu,
            u_rest,
            u_far,
            u_far_rest,
            aa,
            a_rest,
            a_far,
            dd,
            c_pair,
            n_pair,
            n_second,
            n_got_pair,
            n_got_second,
            tables,
            line,
            column,
        )
        d_rest = w_top(dd)
        d_far = swap(dd, Y_BIT)
        a_far_rest = swap(a_rest, Y_BIT)
        c_second = swap_second(c_pair)
        c_got_pair = swap_core(c_pair)
        normed = a_join(n_pair, n_second, n_got_pair, n_got_second)
        my_up_bias = lax.dynamic_slice_in_dim(up_bias, block * hid, hid, 0).astype(F32)
        up_full = w_join(uu, u_rest, u_far, u_far_rest)
        up_pre = jnp.dot(normed, up_full, preferred_element_type=F32) + my_up_bias
        squared = up_pre * up_pre
        gate = 0.5 + 0.5 * jnp.tanh(up_pre * (GELU_A + GELU_A * GELU_B * squared))
        act_f = up_pre * gate
        act = act_f.astype(BF)
        slope = gate + act_f * (1.0 - gate) * (2.0 * GELU_A + 6.0 * GELU_A * GELU_B * squared)
        slope = slope.astype(BF)
        (
            dd,
            d_rest,
            d_far,
            aa,
            a_rest,
            a_far,
            a_far_rest,
            c_pair,
            c_second,
            c_got_pair,
            normed,
            up_full,
            act,
            slope,
        ) = sync(
            dd,
            d_rest,
            d_far,
            aa,
            a_rest,
            a_far,
            a_far_rest,
            c_pair,
            c_second,
            c_got_pair,
            normed,
            up_full,
            act,
            slope,
        )
        d_far_rest = swap(d_rest, Y_BIT)
        c_got_second = swap_core(c_second)
        a_full = w_join(aa, a_rest, a_far, a_far_rest)
        my_qkv_bias = lax.dynamic_slice_in_dim(qkv_bias, block * att, att, 1).astype(F32)
        qkv_full, out_full = a_full[:, : 3 * att], a_full[:, 3 * att :]
        pre = jnp.dot(normed, qkv_full, preferred_element_type=F32) + my_qkv_bias.reshape(-1)
        cot = a_join(c_pair, c_second, c_got_pair, c_got_second)

        def weight_grad(left, right):
            return lax.dot_general(left, right, first, preferred_element_type=F32).astype(BF)

        gd = weight_grad(cot, act)
        d_far_rest, pre, cot, gd, qkv_full, out_full = sync(
            d_far_rest, pre, cot, gd, qkv_full, out_full
        )
        gd = g_y(gd)
        attn_grad = jnp.dot(cot, out_full, preferred_element_type=F32).astype(BF)
        attended, qkv_g = attention(pre, attn_grad, tables, line, column)
        ga = jnp.concatenate([weight_grad(normed, qkv_g), weight_grad(cot, attended)], axis=1)
        gd, attended, qkv_g, ga, d_far_rest = sync(gd, attended, qkv_g, ga, d_far_rest)
        gd = g_top(gd)
        ga = g_y(ga)
        down_full = w_join(dd, d_rest, d_far, d_far_rest)
        up_g = (jnp.dot(cot, down_full, preferred_element_type=F32) * slope.astype(F32)).astype(BF)
        n_send = pair_dot(1, 2, up_g, up_full, qkv_g, qkv_full)
        n_got = swap_core(n_send)
        n_keep = pair_dot(0, 2, up_g, up_full, qkv_g, qkv_full)
        gu = weight_grad(normed, up_g)
        n_pair, n_send = s_join(n_keep, n_got)
        gd, ga, gu, n_pair, n_send, up_g, down_full = sync(
            gd, ga, gu, n_pair, n_send, up_g, down_full
        )
        ga = g_top(ga)
        gu = g_y(gu)
        gd = g_zl(gd)
        n_got = swap_second(n_send)
        b_send = pair_dot(1, 2, act, down_full, attended, out_full)
        b_got = swap_core(b_send)
        b_keep = pair_dot(0, 2, act, down_full, attended, out_full)
        biases = jnp.concatenate(
            [jnp.sum(qkv_g.astype(F32), axis=0), jnp.sum(up_g.astype(F32), axis=0)]
        )
        b_pair, b_send = s_join(b_keep, b_got)
        n_send = add(n_pair[half:], n_got[half:]).astype(BF)
        n_keep = add(n_pair[:half], n_got[:half])
        ga, gd, gu, n_send, n_keep, b_pair, b_send, biases = sync(
            ga, gd, gu, n_send, n_keep, b_pair, b_send, biases
        )
        gu = g_top(gu)
        ga = g_zl(ga)
        gd = g_x(gd)
        n_got = swap_first(n_send)
        b_got = swap_second(b_send)
        input_grad, lines = norm_backward(n_keep, n_got)
        b_send = add(b_pair[half:], b_got[half:]).astype(BF)
        b_keep = add(b_pair[:half], b_got[:half])
        gu, ga, gd, b_send, b_keep, input_grad, lines, biases = sync(
            gu, ga, gd, b_send, b_keep, input_grad, lines, biases
        )
        gu = g_zl(gu)
        ga = g_x(ga)
        b_got = swap_first(b_send)
        input_other = swap_core(input_grad)
        lines = lines[:3].reshape(-1)
        lines = lines + swap_core(lines)
        spread = lax.dynamic_update_slice_in_dim(
            jnp.zeros((4, biases.shape[0]), F32), biases[None], block, 0
        )
        lines = jnp.concatenate([lines, spread.reshape(-1)])
        for bit in top_bits + [Y_BIT]:
            lines = lines + swap(lines, bit)
        result = finish(b_keep, b_got)
        gu, ga, result, lines, input_other = sync(gu, ga, result, lines, input_other)
        gu = g_x(gu)
        result = place_halves(core, result, swap_core(result))
        input_grad = place_halves(core, input_grad, input_other)
        for bit in (X_BIT, ZL_BIT):
            lines = lines + swap(lines, bit)

        gdown = gd.astype(F32).T
        gup = gu.astype(F32)
        ga = ga.reshape(share, 4, 4 * att)
        gqkv = ga[..., : 3 * att].astype(F32)
        gqkv = gqkv.reshape(share, 4, 3, att).swapaxes(1, 2).reshape(share, 3, 4 * att)
        gout = ga[..., 3 * att :].astype(F32).reshape(share, 4 * att).T
        biases = lines[3 * width :].reshape(4, 3 * att + hid)
        qkv_b = biases[:, : 3 * att].reshape(4, 3, att).swapaxes(0, 1).reshape(3, 4 * att)
        up_b = biases[:, 3 * att :].reshape(4 * hid)
        return (
            result,
            input_grad,
            lines[:width],
            lines[width : 2 * width],
            gqkv,
            qkv_b,
            gout,
            gup,
            up_b,
            gdown,
            lines[2 * width : 3 * width],
        )

    return local


def solution(mesh):
    return jax.shard_map(
        local_part(mesh.shape["dp"]),
        mesh=mesh,
        in_specs=(
            P("dp", None),
            P("dp"),
            P(),
            P(),
            P("dp", None, "tensor"),
            P(None, "tensor"),
            P("tensor", "dp"),
            P("dp", "tensor"),
            P("tensor"),
            P("tensor", "dp"),
            P(),
            P("dp", None),
        ),
        out_specs=(
            P("dp", None),
            P("dp", None),
            P(),
            P(),
            P("dp", None, "tensor"),
            P(None, "tensor"),
            P("tensor", "dp"),
            P("dp", "tensor"),
            P("tensor"),
            P("tensor", "dp"),
            P(),
        ),
        check_vma=False,
    )
```

time: 1120 us -> 1330 us (1.19)
  Pallas kernels: 0 us -> 783 us
  waiting for transfers between devices: 341 us -> 153 us
  local copies, waits for them, and re-layouts: 248 us -> 89.3 us
  blocking collectives: 122 us -> 0 us
  other arithmetic: 173 us -> 84.1 us
  matrix products: 171 us -> 84.3 us
  starting transfers between devices: 47.1 us -> 121 us
    pallas_call x0 -> x12, Pallas kernels: none -> 783 us  [the longest x2 511 us: join_rows(): pl.pallas_call(functools.partial(join_kernel, plan), out_shape=jax.ShapeD...]
    ppermute x42 -> x31, waiting for transfers between devices: 341 us -> 123 us  [swap(): lax.ppermute(value, 'dp', [(i, i ^ 1 << bit) for i in range(dp_size)])]
    psum x2 -> x0, blocking collectives: 122 us -> none  [the longest x1 84.8 us: local(): lax.psum((placed(jnp.sum(qkv_g.astype(F32), axis=0).reshape(3, att), 4 *...]
    dot_general x15 -> x6, matrix products: 135 us -> 58 us  [the longest x4 42.7 us: weight_grad(): lax.dot_general(left, right, first, preferred_element_type=F32).astype(BF)]
    ppermute x6 -> x9, starting transfers between devices: 0.72 us -> 75.4 us  [swap_core(): return lax.ppermute(value, 'tensor', [(0, 1), (1, 0)])]
    another operation x30 -> x4, local copies, waits for them, and re-layouts: 65.1 us -> 1.6 us  [the longest x1 1.35 us: local(): line = jnp.stack([order, opening], axis=2)]
    reshape x16 -> x8, local copies, waits for them, and re-layouts: 49.4 us -> 2.72 us  [the longest x3 1.39 us: on_half(): line.reshape(1, width)]
    ppermute x0 -> x10, waiting for transfers between devices: none -> 29.2 us  [swap_mixed(): return lax.ppermute(value, ('dp', 'tensor'), pairs)]
  transfers between devices with their start and end apart: 48 -> 50, of which waited for: 21 -> 15; matrix products, arithmetic and copies ran while one was open for 35% -> 15% of each run, Pallas kernels for 0% -> 53%
where the time goes in v3:
time: 1330 us; the launch traced here: 1320 us
  Pallas kernels  783 us (59%)
  waiting for transfers between devices  153 us (12%)
  starting transfers between devices  121 us (9%)
  local copies, waits for them, and re-layouts  89.3 us (7%)
  matrix products  84.3 us (6%)
  other arithmetic  84.1 us (6%)
    pallas_call x2, Pallas kernels, join_rows(): pl.pallas_call(functools.partial(join_kernel, plan), out_shape=jax.ShapeD...  511 us
    pallas_call x2, Pallas kernels, place_halves(): pl.pallas_call(place_kernel, out_shape=jax.ShapeDtypeStruct((2 * own.shap...  193 us
    ppermute x31, waiting for transfers between devices, swap(): lax.ppermute(value, 'dp', [(i, i ^ 1 << bit) for i in range(dp_size)])  123 us
    ppermute x9, starting transfers between devices, swap_core(): return lax.ppermute(value, 'tensor', [(0, 1), (1, 0)])  75.4 us
    pallas_call x4, Pallas kernels, pair_dot(): pl.pallas_call(pair_kernel, grid=(width // tile,), out_shape=jax.ShapeDty...  47.9 us
    dot_general x4, matrix products, weight_grad(): lax.dot_general(left, right, first, preferred_element_type=F32).astype(BF)  42.7 us
    ppermute x31, starting transfers between devices, swap(): lax.ppermute(value, 'dp', [(i, i ^ 1 << bit) for i in range(dp_size)])  37.7 us
    unnamed x103, local copies, waits for them, and re-layouts  35.9 us
  transfers between devices with their start and end apart: 50, of which 15 were waited for; matrix products, arithmetic and copies ran while one was open for 15% of the time, Pallas kernels for 53%

profile of v3, /device:TPU:0, one launch (start us, length us, event | category | flops | bytes accessed | tf_op | source)
XLA Modules:
  0.0 1316.4 jit_solution(299249855912655193)
XLA Ops:
  13.6 4.7 collective-permute-done
  33.6 11.1 collective-permute-done.5
  66.6 23.9 %collective-permute-done.10 = bf16[256,1024]{1,0:T(8,128)(2,1)} collective-permute-done((bf16[256,1024]{1,0:T(8,128)(2,1)}, bf16[256,1024]{1,0:T(8,128)(2,1)}, u32[]{:S(2)}, u32[]{:S(2)}) %collective-permute-start.10) | collective-permute-done | bytes 524320 | tf_op jit(solution)/shard_map/ppermute | solution.py:311
  94.2 5.7 collective-permute-done.11
  108.8 22.5 %collective-permute-start.17 = (bf16[512,2048]{1,0:T(8,128)(2,1)}, bf16[512,2048]{1,0:T(8,128)(2,1)}, u32[]{:S(2)}, u32[]{:S(2)}) collective-permute-start(bf16[512,2048]{1,0:T(8,128)(2,1)} %collective-permute-done.8.refs_1_), channel_id=1, source_target_pairs={{0,1},{1,0},{2,3},{3,2},{4,5},{5,4},{6,7},{7,6},{8,9},{9,8},{10,11... | collective-permute-start | bytes 6291464 | tf_op jit(solution)/shard_map/ppermute | solution.py:314
  137.3 5.8 fusion.6
  159.7 25.0 %collective-permute-start.22 = (bf16[512,2048]{1,0:T(8,128)(2,1)}, bf16[512,2048]{1,0:T(8,128)(2,1)}, u32[]{:S(2)}, u32[]{:S(2)}) collective-permute-start(bf16[512,2048]{1,0:T(8,128)(2,1)} %pad_maximum_fusion.2.refs_0_), channel_id=1, source_target_pairs={{0,1},{1,0},{2,3},{3,2},{4,5},{5,4},{6,7},{7,6},{8,9},{9,8},{10,11... | collective-permute-start | bytes 6291464 | tf_op jit(solution)/shard_map/ppermute | solution.py:314
  193.2 255.3 %shard_map.204 = bf16[2048,2048]{1,0:T(8,128)(2,1)} custom-call(bf16[512,2048]{1,0:T(8,128)(2,1)} %pad_maximum_fusion.1.refs_0_, bf16[512,2048]{1,0:T(8,128)(2,1)} %collective-permute-done.8.refs_1_, bf16[512,2048]{1,0:T(8,128)(2,1)} %collective-permute-done.9.refs_2_, bf16[512,2048]{1,0:T(8,128)(2,1)} %collective-permute-done.17.refs_3_), custom_call_target="tpu_custom_call" | custom-call | bytes 16777216 | tf_op jit(solution)/shard_map/pallas_call | solution.py:151
  448.4 17.8 %add_convert_fusion = (bf16[2048,1024]{1,0:T(8,128)(2,1)}, bf16[2048,1024]{1,0:T(8,128)(2,1)}) fusion(f32[1024]{0:T(1024)S(1)} %dynamic-slice_convert_fusion, bf16[2048,2048]{1,0:T(8,128)(2,1)} %shard_map.204, bf16[2048,1024]{1,0:T(8,128)(2,1)} %constant_dynamic-update-slice_fusion.b_ref), kind=kOutput, calls=%fused_computation.2 | convolution fusion | flops 8623489024 | bytes 20975616 | tf_op jit(solution)/shard_map/dot_general | solution.py:594
  482.5 8.5 broadcast_add_fusion
  491.1 255.3 %shard_map.205 = bf16[2048,2048]{1,0:T(8,128)(2,1)} custom-call(bf16[512,2048]{1,0:T(8,128)(2,1)} %pad_maximum_fusion.2.refs_0_, bf16[512,2048]{1,0:T(8,128)(2,1)} %collective-permute-done.21.refs_1_, bf16[512,2048]{1,0:T(8,128)(2,1)} %collective-permute-done.22.refs_2_, bf16[512,2048]{1,0:T(8,128)(2,1)} %collective-permute-done.24.refs_3_), custom_call_target="tpu_custom_call" | custom-call | bytes 16777216 | tf_op jit(solution)/shard_map/pallas_call | solution.py:151
  746.3 13.1 convolution_convert_fusion.1
  763.1 24.6 %shard_map.206 = (bf16[2,4,256,256]{3,2,1,0:T(8,128)(2,1)S(1)}, bf16[2,4,256,768]{3,2,1,0:T(8,128)(2,1)}) custom-call(f32[2,4,256,768]{3,2,1,0:T(8,128)} %bitcast.143, bf16[2,4,256,256]{3,2,1,0:T(8,128)(2,1)S(1)} %bitcast.119, f32[2,4,256,128]{3,2,1,0:T(8,128)S(1)} %bitcast.115, f32[2,4,256,128]{3,2,1,0:T(8,128)S(1)} %bitcast.114, ...), custom_call_target="tpu_custom_call" | custom-call | flops 20000000000 | bytes 16000000 | tf_op jit(solution)/shard_map/pallas_call | solution.py:96
  787.6 7.3 convolution_convert_fusion.3
  794.9 9.6 convolution_convert_fusion.2
  812.6 13.0 multiply_convert_fusion.a_ref
  825.6 12.8 shard_map.208
  842.1 12.7 convolution_convert_fusion
  854.8 12.9 shard_map.207
  867.7 20.9 %collective-permute-done.26 = bf16[512,1024]{1,0:T(8,128)(2,1)} collective-permute-done((bf16[512,1024]{1,0:T(8,128)(2,1)}, bf16[512,1024]{1,0:T(8,128)(2,1)}, u32[]{:S(2)}, u32[]{:S(2)}) %collective-permute-start.26) | collective-permute-done | bytes 1048608 | tf_op jit(solution)/shard_map/ppermute | solution.py:311
  898.7 5.0 fusion.3
  903.7 11.1 shard_map.210
  925.6 11.2 shard_map.209
  936.7 21.7 %collective-permute-done.30 = bf16[256,1024]{1,0:T(8,128)(2,1)S(1)} collective-permute-done((bf16[256,1024]{1,0:T(8,128)(2,1)S(1)}, bf16[256,1024]{1,0:T(8,128)(2,1)S(1)}, u32[]{:S(2)}, u32[]{:S(2)}) %collective-permute-start.30) | collective-permute-done | bytes 524320 | tf_op jit(solution)/shard_map/ppermute | solution.py:311
  976.2 5.0 fusion.2
  990.3 21.7 %collective-permute-done.35 = bf16[256,1024]{1,0:T(8,128)(2,1)} collective-permute-done((bf16[256,1024]{1,0:T(8,128)(2,1)}, bf16[256,1024]{1,0:T(8,128)(2,1)}, u32[]{:S(2)}, u32[]{:S(2)}) %collective-permute-start.35) | collective-permute-done | bytes 524320 | tf_op jit(solution)/shard_map/ppermute | solution.py:311
  1014.9 8.6 collective-permute-done.36
  1026.4 12.7 collective-permute-done.38.got_ref
  1048.7 24.4 %collective-permute-start.42 = (f32[6144]{0:T(1024)S(1)}, f32[6144]{0:T(1024)S(1)}, u32[]{:S(2)}, u32[]{:S(2)}) collective-permute-start(f32[6144]{0:T(1024)S(1)} %reshape.316), channel_id=1, source_target_pairs={{0,1},{1,0},{2,3},{3,2},{4,5},{5,4},{6,7},{7,6},{8,9},{9,8},{10,11... | collective-permute-start | bytes 73736 | tf_op jit(solution)/shard_map/ppermute | solution.py:314
  1080.0 7.1 collective-permute-done.43
  1113.1 128.2 %shard_map.214 = f32[512,2048]{1,0:T(8,128)} custom-call(s32[1]{0:T(128)} %bitcast.core_ref, f32[256,2048]{1,0:T(8,128)} %copy-done.7, f32[256,2048]{1,0:T(8,128)} %collective-permute-done.45.other_ref), custom_call_target="tpu_custom_call" | custom-call | bytes 8388608 | tf_op jit(solution)/shard_map/pallas_call | solution.py:180
  1251.3 64.6 %shard_map.213 = bf16[512,2048]{1,0:T(8,128)(2,1)} custom-call(s32[1]{0:T(128)} %bitcast.core_ref, bf16[256,2048]{1,0:T(8,128)(2,1)} %copy-done.5, bf16[256,2048]{1,0:T(8,128)(2,1)} %collective-permute-done.46.other_ref), custom_call_target="tpu_custom_call" | custom-call | bytes 4194304 | tf_op jit(solution)/shard_map/pallas_call | solution.py:180
  (319 shorter events, 230.7 us)
Async XLA Ops:
  52.8 49.1 %collective-permute-start.8 = (bf16[512,2048]{1,0:T(8,128)(2,1)}, bf16[512,2048]{1,0:T(8,128)(2,1)}, u32[]{:S(2)}, u32[]{:S(2)}) collective-permute-start(bf16[512,2048]{1,0:T(8,128)(2,1)} %pad_maximum_fusion.1.refs_0_), channel_id=1, source_target_pairs={{0,2},{1,9},{2,0},{3,11},{4,6},{5,13},{6,4},{7,15},{8,10},{9,1},{1... | collective-permute-start | bytes 6291464 | tf_op jit(solution)/shard_map/ppermute | solution.py:318
  54.6 47.4 %collective-permute-start.9 = (bf16[512,2048]{1,0:T(8,128)(2,1)}, bf16[512,2048]{1,0:T(8,128)(2,1)}, u32[]{:S(2)}, u32[]{:S(2)}) collective-permute-start(bf16[512,2048]{1,0:T(8,128)(2,1)} %pad_maximum_fusion.1.refs_0_), channel_id=1, source_target_pairs={{0,1},{1,0},{2,3},{3,2},{4,5},{5,4},{6,7},{7,6},{8,9},{9,8},{10,11... | collective-permute-start | bytes 6291464 | tf_op jit(solution)/shard_map/ppermute | solution.py:314
  55.6 34.9 %collective-permute-start.10 = (bf16[256,1024]{1,0:T(8,128)(2,1)}, bf16[256,1024]{1,0:T(8,128)(2,1)}, u32[]{:S(2)}, u32[]{:S(2)}) collective-permute-start(bf16[256,1024]{1,0:T(8,128)(2,1)} %get-tuple-element.345), channel_id=1, source_target_pairs={{0,8},{2,10},{4,12},{6,14},{8,0},{10,2},{12,4},{14,6},{16,24},{18,... | collective-permute-start | bytes 1572872 | tf_op jit(solution)/shard_map/ppermute | solution.py:311
  57.9 44.0 %collective-permute-start.6 = (bf16[512,1024]{1,0:T(8,128)(2,1)}, bf16[512,1024]{1,0:T(8,128)(2,1)}, u32[]{:S(2)}, u32[]{:S(2)}) collective-permute-start(bf16[512,1024]{1,0:T(8,128)(2,1)} %maximum_select_fusion.1), channel_id=1, source_target_pairs={{0,16},{2,18},{4,20},{6,22},{8,24},{10,26},{12,28},{14,30},{16,0},... | collective-permute-start | bytes 3145736 | tf_op jit(solution)/shard_map/ppermute | solution.py:311
  60.5 41.4 %collective-permute-start.7 = (bf16[512,1024]{1,0:T(8,128)(2,1)}, bf16[512,1024]{1,0:T(8,128)(2,1)}, u32[]{:S(2)}, u32[]{:S(2)}) collective-permute-start(bf16[512,1024]{1,0:T(8,128)(2,1)} %maximum_select_fusion.1), channel_id=1, source_target_pairs={{0,4},{2,6},{4,0},{6,2},{8,12},{10,14},{12,8},{14,10},{16,20},{18,... | collective-permute-start | bytes 3145736 | tf_op jit(solution)/shard_map/ppermute | solution.py:311
  102.0 53.5 %collective-permute-start.13 = (bf16[512,1024]{1,0:T(8,128)(2,1)}, bf16[512,1024]{1,0:T(8,128)(2,1)}, u32[]{:S(2)}, u32[]{:S(2)}) collective-permute-start(bf16[512,1024]{1,0:T(8,128)(2,1)} %maximum_select_fusion.3), channel_id=1, source_target_pairs={{0,16},{2,18},{4,20},{6,22},{8,24},{10,26},{12,28},{14,30},{16,0},... | collective-permute-start | bytes 3145736 | tf_op jit(solution)/shard_map/ppermute | solution.py:311
  103.2 52.2 %collective-permute-start.14 = (bf16[512,1024]{1,0:T(8,128)(2,1)}, bf16[512,1024]{1,0:T(8,128)(2,1)}, u32[]{:S(2)}, u32[]{:S(2)}) collective-permute-start(bf16[512,1024]{1,0:T(8,128)(2,1)} %maximum_select_fusion.3), channel_id=1, source_target_pairs={{0,4},{2,6},{4,0},{6,2},{8,12},{10,14},{12,8},{14,10},{16,20},{18,... | collective-permute-start | bytes 3145736 | tf_op jit(solution)/shard_map/ppermute | solution.py:311
  105.7 27.6 %collective-permute-start.15 = (bf16[256,1024]{1,0:T(8,128)(2,1)}, bf16[256,1024]{1,0:T(8,128)(2,1)}, u32[]{:S(2)}, u32[]{:S(2)}) collective-permute-start(bf16[256,1024]{1,0:T(8,128)(2,1)} %get-tuple-element.341), channel_id=1, source_target_pairs={{0,8},{2,10},{4,12},{6,14},{8,0},{10,2},{12,4},{14,6},{16,24},{18,... | collective-permute-start | bytes 1572872 | tf_op jit(solution)/shard_map/ppermute | solution.py:311
  108.7 40.3 %collective-permute-start.16 = (bf16[256,2048]{1,0:T(8,128)(2,1)S(1)}, bf16[256,2048]{1,0:T(8,128)(2,1)}, u32[]{:S(2)}, u32[]{:S(2)}) collective-permute-start(bf16[256,2048]{1,0:T(8,128)(2,1)S(1)} %get-tuple-element.131), channel_id=1, source_target_pairs={{0,8},{1,3},{2,10},{3,1},{4,12},{5,7},{6,14},{7,5},{8,0},{9,11},{1... | collective-permute-start | bytes 3145736 | tf_op jit(solution)/shard_map/ppermute | solution.py:318
  108.8 46.7 %collective-permute-start.17 = (bf16[512,2048]{1,0:T(8,128)(2,1)}, bf16[512,2048]{1,0:T(8,128)(2,1)}, u32[]{:S(2)}, u32[]{:S(2)}) collective-permute-start(bf16[512,2048]{1,0:T(8,128)(2,1)} %collective-permute-done.8.refs_1_), channel_id=1, source_target_pairs={{0,1},{1,0},{2,3},{3,2},{4,5},{5,4},{6,7},{7,6},{8,9},{9,8},{10,11... | collective-permute-start | bytes 6291464 | tf_op jit(solution)/shard_map/ppermute | solution.py:314
  155.4 310.8 %collective-permute-start.18 = (bf16[512,1024]{1,0:T(8,128)(2,1)}, bf16[512,1024]{1,0:T(8,128)(2,1)S(1)}, u32[]{:S(2)}, u32[]{:S(2)}) collective-permute-start(bf16[512,1024]{1,0:T(8,128)(2,1)} %maximum_select_fusion.5), channel_id=1, source_target_pairs={{0,16},{2,18},{4,20},{6,22},{8,24},{10,26},{12,28},{14,30},{16,0},... | collective-permute-start | bytes 3145736 | tf_op jit(solution)/shard_map/ppermute | solution.py:311
  158.0 308.3 %collective-permute-start.19 = (bf16[512,1024]{1,0:T(8,128)(2,1)}, bf16[512,1024]{1,0:T(8,128)(2,1)}, u32[]{:S(2)}, u32[]{:S(2)}) collective-permute-start(bf16[512,1024]{1,0:T(8,128)(2,1)} %maximum_select_fusion.5), channel_id=1, source_target_pairs={{0,4},{2,6},{4,0},{6,2},{8,12},{10,14},{12,8},{14,10},{16,20},{18,... | collective-permute-start | bytes 3145736 | tf_op jit(solution)/shard_map/ppermute | solution.py:311
  158.5 307.7 %collective-permute-start.21 = (bf16[512,2048]{1,0:T(8,128)(2,1)}, bf16[512,2048]{1,0:T(8,128)(2,1)}, u32[]{:S(2)}, u32[]{:S(2)}) collective-permute-start(bf16[512,2048]{1,0:T(8,128)(2,1)} %pad_maximum_fusion.2.refs_0_), channel_id=1, source_target_pairs={{0,2},{1,9},{2,0},{3,11},{4,6},{5,13},{6,4},{7,15},{8,10},{9,1},{1... | collective-permute-start | bytes 6291464 | tf_op jit(solution)/shard_map/ppermute | solution.py:318
  159.7 306.5 %collective-permute-start.22 = (bf16[512,2048]{1,0:T(8,128)(2,1)}, bf16[512,2048]{1,0:T(8,128)(2,1)}, u32[]{:S(2)}, u32[]{:S(2)}) collective-permute-start(bf16[512,2048]{1,0:T(8,128)(2,1)} %pad_maximum_fusion.2.refs_0_), channel_id=1, source_target_pairs={{0,1},{1,0},{2,3},{3,2},{4,5},{5,4},{6,7},{7,6},{8,9},{9,8},{10,11... | collective-permute-start | bytes 6291464 | tf_op jit(solution)/shard_map/ppermute | solution.py:314
  184.8 281.4 %collective-permute-start.20 = (bf16[512,1024]{1,0:T(8,128)(2,1)}, bf16[512,1024]{1,0:T(8,128)(2,1)}, u32[]{:S(2)}, u32[]{:S(2)}) collective-permute-start(bf16[512,1024]{1,0:T(8,128)(2,1)} %collective-permute-done.13), channel_id=1, source_target_pairs={{0,4},{2,6},{4,0},{6,2},{8,12},{10,14},{12,8},{14,10},{16,20},{18,... | collective-permute-start | bytes 3145736 | tf_op jit(solution)/shard_map/ppermute | solution.py:311
  474.1 285.3 %collective-permute-start.23 = (bf16[512,1024]{1,0:T(8,128)(2,1)}, bf16[512,1024]{1,0:T(8,128)(2,1)}, u32[]{:S(2)}, u32[]{:S(2)}) collective-permute-start(bf16[512,1024]{1,0:T(8,128)(2,1)} %copy-done.34), channel_id=1, source_target_pairs={{0,4},{2,6},{4,0},{6,2},{8,12},{10,14},{12,8},{14,10},{16,20},{18,... | collective-permute-start | bytes 3145736 | tf_op jit(solution)/shard_map/ppermute | solution.py:311
  759.6 48.1 %collective-permute-start.25 = (bf16[1024,1024]{1,0:T(8,128)(2,1)S(1)}, bf16[1024,1024]{1,0:T(8,128)(2,1)S(1)}, u32[]{:S(2)}, u32[]{:S(2)}) collective-permute-start(bf16[1024,1024]{1,0:T(8,128)(2,1)S(1)} %slice.202), channel_id=1, source_target_pairs={{0,4},{2,6},{4,0},{6,2},{8,12},{10,14},{12,8},{14,10},{16,20},{18,... | collective-permute-start | bytes 6291464 | tf_op jit(solution)/shard_map/ppermute | solution.py:311
  838.3 55.2 %collective-permute-start.28 = (bf16[1024,2048]{1,0:T(8,128)(2,1)}, bf16[1024,2048]{1,0:T(8,128)(2,1)}, u32[]{:S(2)}, u32[]{:S(2)}) collective-permute-start(bf16[1024,2048]{1,0:T(8,128)(2,1)} %shard_map.208), channel_id=1, source_target_pairs={{0,1},{1,0},{2,3},{3,2},{4,5},{5,4},{6,7},{7,6},{8,9},{9,8},{10,11... | collective-permute-start | bytes 12582920 | tf_op jit(solution)/shard_map/ppermute | solution.py:314
  839.4 49.2 %collective-permute-start.26 = (bf16[512,1024]{1,0:T(8,128)(2,1)}, bf16[512,1024]{1,0:T(8,128)(2,1)}, u32[]{:S(2)}, u32[]{:S(2)}) collective-permute-start(bf16[512,1024]{1,0:T(8,128)(2,1)} %slice.204), channel_id=1, source_target_pairs={{0,16},{2,18},{4,20},{6,22},{8,24},{10,26},{12,28},{14,30},{16,0},... | collective-permute-start | bytes 3145736 | tf_op jit(solution)/shard_map/ppermute | solution.py:311
  841.3 50.0 %collective-permute-start.27 = (bf16[1024,1024]{1,0:T(8,128)(2,1)}, bf16[1024,1024]{1,0:T(8,128)(2,1)S(1)}, u32[]{:S(2)}, u32[]{:S(2)}) collective-permute-start(bf16[1024,1024]{1,0:T(8,128)(2,1)} %slice.206), channel_id=1, source_target_pairs={{0,4},{2,6},{4,0},{6,2},{8,12},{10,14},{12,8},{14,10},{16,20},{18,... | collective-permute-start | bytes 6291464 | tf_op jit(solution)/shard_map/ppermute | solution.py:311
  914.8 56.2 %collective-permute-start.33 = (bf16[1024,2048]{1,0:T(8,128)(2,1)}, bf16[1024,2048]{1,0:T(8,128)(2,1)}, u32[]{:S(2)}, u32[]{:S(2)}) collective-permute-start(bf16[1024,2048]{1,0:T(8,128)(2,1)} %shard_map.210), channel_id=1, source_target_pairs={{0,1},{1,0},{2,3},{3,2},{4,5},{5,4},{6,7},{7,6},{8,9},{9,8},{10,11... | collective-permute-start | bytes 12582920 | tf_op jit(solution)/shard_map/ppermute | solution.py:314
  916.3 48.4 %collective-permute-start.31 = (bf16[1024,1024]{1,0:T(8,128)(2,1)}, bf16[1024,1024]{1,0:T(8,128)(2,1)}, u32[]{:S(2)}, u32[]{:S(2)}) collective-permute-start(bf16[1024,1024]{1,0:T(8,128)(2,1)} %slice.220), channel_id=1, source_target_pairs={{0,4},{2,6},{4,0},{6,2},{8,12},{10,14},{12,8},{14,10},{16,20},{18,... | collective-permute-start | bytes 6291464 | tf_op jit(solution)/shard_map/ppermute | solution.py:311
  917.2 51.4 %collective-permute-start.32 = (bf16[512,2048]{1,0:T(8,128)(2,1)}, bf16[512,2048]{1,0:T(8,128)(2,1)S(1)}, u32[]{:S(2)}, u32[]{:S(2)}) collective-permute-start(bf16[512,2048]{1,0:T(8,128)(2,1)} %get-tuple-element.184), channel_id=1, source_target_pairs={{0,2},{1,9},{2,0},{3,11},{4,6},{5,13},{6,4},{7,15},{8,10},{9,1},{1... | collective-permute-start | bytes 6291464 | tf_op jit(solution)/shard_map/ppermute | solution.py:318
  921.4 38.4 %collective-permute-start.29 = (bf16[512,1024]{1,0:T(8,128)(2,1)S(1)}, bf16[512,1024]{1,0:T(8,128)(2,1)S(1)}, u32[]{:S(2)}, u32[]{:S(2)}) collective-permute-start(bf16[512,1024]{1,0:T(8,128)(2,1)S(1)} %slice.218), channel_id=1, source_target_pairs={{0,16},{2,18},{4,20},{6,22},{8,24},{10,26},{12,28},{14,30},{16,0},... | collective-permute-start | bytes 3145736 | tf_op jit(solution)/shard_map/ppermute | solution.py:311
  923.2 35.2 %collective-permute-start.30 = (bf16[256,1024]{1,0:T(8,128)(2,1)S(1)}, bf16[256,1024]{1,0:T(8,128)(2,1)S(1)}, u32[]{:S(2)}, u32[]{:S(2)}) collective-permute-start(bf16[256,1024]{1,0:T(8,128)(2,1)S(1)} %get-tuple-element.339), channel_id=1, source_target_pairs={{0,8},{2,10},{4,12},{6,14},{8,0},{10,2},{12,4},{14,6},{16,24},{18,... | collective-permute-start | bytes 1572872 | tf_op jit(solution)/shard_map/ppermute | solution.py:311
  981.2 63.5 %collective-permute-start.37 = (bf16[512,2048]{1,0:T(8,128)(2,1)}, bf16[512,2048]{1,0:T(8,128)(2,1)}, u32[]{:S(2)}, u32[]{:S(2)}) collective-permute-start(bf16[512,2048]{1,0:T(8,128)(2,1)} %get-tuple-element.192), channel_id=1, source_target_pairs={{0,2},{1,9},{2,0},{3,11},{4,6},{5,13},{6,4},{7,15},{8,10},{9,1},{1... | collective-permute-start | bytes 6291464 | tf_op jit(solution)/shard_map/ppermute | solution.py:318
  984.9 57.3 %collective-permute-start.34 = (bf16[512,1024]{1,0:T(8,128)(2,1)}, bf16[512,1024]{1,0:T(8,128)(2,1)}, u32[]{:S(2)}, u32[]{:S(2)}) collective-permute-start(bf16[512,1024]{1,0:T(8,128)(2,1)} %slice.236), channel_id=1, source_target_pairs={{0,16},{2,18},{4,20},{6,22},{8,24},{10,26},{12,28},{14,30},{16,0},... | collective-permute-start | bytes 3145736 | tf_op jit(solution)/shard_map/ppermute | solution.py:311
  988.2 50.8 %collective-permute-start.38 = (bf16[256,2048]{1,0:T(8,128)(2,1)}, bf16[256,2048]{1,0:T(8,128)(2,1)S(1)}, u32[]{:S(2)}, u32[]{:S(2)}) collective-permute-start(bf16[256,2048]{1,0:T(8,128)(2,1)} %get-tuple-element.194), channel_id=1, source_target_pairs={{0,8},{1,3},{2,10},{3,1},{4,12},{5,7},{6,14},{7,5},{8,0},{9,11},{1... | collective-permute-start | bytes 3145736 | tf_op jit(solution)/shard_map/ppermute | solution.py:318
  989.6 33.9 %collective-permute-start.36 = (bf16[128,2048]{1,0:T(8,128)(2,1)}, bf16[128,2048]{1,0:T(8,128)(2,1)}, u32[]{:S(2)}, u32[]{:S(2)}) collective-permute-start(bf16[128,2048]{1,0:T(8,128)(2,1)} %get-tuple-element.335), channel_id=1, source_target_pairs={{0,2},{2,0},{4,6},{6,4},{8,10},{10,8},{12,14},{14,12},{16,18},{18,... | collective-permute-start | bytes 1572872 | tf_op jit(solution)/shard_map/ppermute | solution.py:311
  1103.8 147.5 %collective-permute-start.46 = (bf16[256,2048]{1,0:T(8,128)(2,1)S(1)}, bf16[256,2048]{1,0:T(8,128)(2,1)}, u32[]{:S(2)}, u32[]{:S(2)}) collective-permute-start(bf16[256,2048]{1,0:T(8,128)(2,1)S(1)} %shard_map.212.own_ref), channel_id=1, source_target_pairs={{0,1},{1,0},{2,3},{3,2},{4,5},{5,4},{6,7},{7,6},{8,9},{9,8},{10,11... | collective-permute-start | bytes 3145736 | tf_op jit(solution)/shard_map/ppermute | solution.py:314
  1110.1 138.4 %collective-permute-start.49 = (bf16[128,2048]{1,0:T(8,128)(2,1)}, bf16[128,2048]{1,0:T(8,128)(2,1)}, u32[]{:S(2)}, u32[]{:S(2)}) collective-permute-start(bf16[128,2048]{1,0:T(8,128)(2,1)} %get-tuple-element.329), channel_id=1, source_target_pairs={{0,2},{2,0},{4,6},{6,4},{8,10},{10,8},{12,14},{14,12},{16,18},{18,... | collective-permute-start | bytes 1572872 | tf_op jit(solution)/shard_map/ppermute | solution.py:311
  1111.6 135.0 %collective-permute-start.48 = (f32[13312]{0:T(1024)S(1)}, f32[13312]{0:T(1024)S(1)}, u32[]{:S(2)}, u32[]{:S(2)}) collective-permute-start(f32[13312]{0:T(1024)S(1)} %add.235), channel_id=1, source_target_pairs={{0,8},{2,10},{4,12},{6,14},{8,0},{10,2},{12,4},{14,6},{16,24},{18,... | collective-permute-start | bytes 159752 | tf_op jit(solution)/shard_map/ppermute | solution.py:311
  (60 other events, 879.6 us)

commit v4 on v3

v4 whole, which is shorter than its diff:
```python
import functools

import jax
import jax.numpy as jnp
from jax import lax
from jax.experimental import pallas as pl
from jax.experimental.pallas import tpu as pltpu
from jax.sharding import PartitionSpec as P

HEAD_DIM = 64
ROT_DIM = 32
LANES = 128
NEGATIVE = -1e30
EPSILON = 1e-05
GELU_A = 0.7978845608028654
GELU_B = 0.044715
X_BIT, Y_BIT, ZL_BIT = 0, 1, 2
BF = jnp.bfloat16
F32 = jnp.float32


def dot_nn(a, b):
    return jnp.dot(a, b, preferred_element_type=F32)


def dot_nt(a, b):
    return lax.dot_general(a, b, (((1,), (1,)), ((), ())), preferred_element_type=F32)


def dot_tn(a, b):
    return lax.dot_general(a, b, (((0,), (0,)), ((), ())), preferred_element_type=F32)


def call(kernel, outs, grid, in_specs, out_specs, *operands, prefetch=0):
    return pl.pallas_call(
        kernel,
        out_shape=outs,
        grid_spec=pltpu.PrefetchScalarGridSpec(
            num_scalar_prefetch=prefetch, grid=grid, in_specs=in_specs, out_specs=out_specs
        ),
        compiler_params=pltpu.CompilerParams(vmem_limit_bytes=54 * 1024 * 1024),
        cost_estimate=pl.CostEstimate(flops=1000, bytes_accessed=1000, transcendentals=0),
    )(*operands)


def resident(value):
    return pl.BlockSpec(value.shape, lambda *_: (0,) * value.ndim)


def wide_dot(rows, refs, cols):
    total, low = None, 0
    for ref in refs:
        high = low + ref.shape[0]
        term = dot_nn(rows[:, low:high], ref[:, cols])
        total = term if total is None else total + term
        low = high
    return total


def join_kernel(flags_ref, pair_ref, second_ref, got_pair_ref, got_second_ref, out_ref):
    i = pl.program_id(0)
    place = lax.rem(i, 4)
    for own, (p_ref, s_ref) in enumerate(
        ((pair_ref, second_ref), (got_pair_ref, got_second_ref))
    ):
        here = (i // 4) == own
        crossed = flags_ref[own] == 1
        from_pair = (place == 0) | ((place == 1) & jnp.logical_not(crossed))
        from_pair = from_pair | ((place == 2) & crossed)

        @pl.when(here & from_pair)
        def _(ref=p_ref):
            out_ref[...] = ref[...]

        @pl.when(here & jnp.logical_not(from_pair))
        def _(ref=s_ref):
            out_ref[...] = ref[...]


def join(flags, pair, second, got_pair, got_second):
    half, width = pair.shape[0] // 2, pair.shape[1]

    def spec(low, edge):
        return pl.BlockSpec((half, width), lambda i, f: (jnp.where(i - low > edge, 1, 0), 0))

    return call(
        join_kernel,
        jax.ShapeDtypeStruct((8 * half, width), pair.dtype),
        (8,),
        [spec(0, 0), spec(0, 2), spec(4, 0), spec(4, 2)],
        pl.BlockSpec((half, width), lambda i, f: (i, 0)),
        flags,
        pair,
        second,
        got_pair,
        got_second,
        prefetch=1,
    )


def place_kernel(core_ref, own_ref, other_ref, out_ref):
    steps = pl.num_programs(0) // 2

    @pl.when(pl.program_id(0) < steps)
    def _():
        out_ref[...] = own_ref[...]

    @pl.when(pl.program_id(0) >= steps)
    def _():
        out_ref[...] = other_ref[...]


def place_halves(core, own, other, steps=2):
    tile, width = own.shape[0] // steps, own.shape[1]
    return call(
        place_kernel,
        jax.ShapeDtypeStruct((2 * own.shape[0], width), own.dtype),
        (2 * steps,),
        [
            pl.BlockSpec((tile, width), lambda i, c: (jnp.minimum(i, steps - 1), 0)),
            pl.BlockSpec((tile, width), lambda i, c: (jnp.maximum(i - steps, 0), 0)),
        ],
        pl.BlockSpec((tile, width), lambda i, c: (lax.rem(i + steps * c[0], 2 * steps), 0)),
        core.reshape(1).astype(jnp.int32),
        own,
        other,
        prefetch=1,
    )


def up_kernel(rows_ref, bias_ref, *refs, chunk):
    weights, act_ref, slope_ref = refs[:-2], refs[-2], refs[-1]
    rows = rows_ref[...]
    for low in range(0, act_ref.shape[1], chunk):
        cols = slice(low, low + chunk)
        u = wide_dot(rows, weights, cols) + bias_ref[:, cols]
        squared = u * u
        gate = 0.5 + 0.5 * jnp.tanh(u * (GELU_A + GELU_A * GELU_B * squared))
        act = u * gate
        act_ref[:, cols] = act.astype(BF)
        slope = gate + act * (1.0 - gate) * (2.0 * GELU_A + 6.0 * GELU_A * GELU_B * squared)
        slope_ref[:, cols] = slope.astype(BF)


def up_project(rows, bias, weights, tile=256):
    count, hid = rows.shape[0], weights[0].shape[1]
    out = jax.ShapeDtypeStruct((count, hid), BF)
    block = pl.BlockSpec((tile, hid), lambda i: (i, 0))
    return call(
        functools.partial(up_kernel, chunk=256),
        [out, out],
        (count // tile,),
        [pl.BlockSpec((tile, rows.shape[1]), lambda i: (i, 0)), pl.BlockSpec((1, hid), lambda i: (0, 0))]
        + [resident(w) for w in weights],
        [block, block],
        rows,
        bias.reshape(1, hid),
        *weights,
    )


def add_row_sum(sum_ref, value):
    @pl.when(pl.program_id(0) == 0)
    def _():
        sum_ref[...] = jnp.zeros_like(sum_ref)

    sum_ref[0:1, :] += jnp.sum(value.astype(F32), axis=0, keepdims=True)


def up_grad_kernel(rows_ref, slope_ref, *refs):
    weights, grad_ref, sum_ref = refs[:-2], refs[-2], refs[-1]
    grad = wide_dot(rows_ref[...], weights, slice(None)) * slope_ref[...].astype(F32)
    grad = grad.astype(BF)
    grad_ref[...] = grad
    add_row_sum(sum_ref, grad)


def up_gradient(rows, slope, weights, tile=256):
    count, hid = slope.shape
    block = pl.BlockSpec((tile, hid), lambda i: (i, 0))
    return call(
        up_grad_kernel,
        [jax.ShapeDtypeStruct((count, hid), BF), jax.ShapeDtypeStruct((8, hid), F32)],
        (count // tile,),
        [pl.BlockSpec((tile, rows.shape[1]), lambda i: (i, 0)), block]
        + [resident(w) for w in weights],
        [block, pl.BlockSpec((8, hid), lambda i: (0, 0))],
        rows,
        slope,
        *weights,
    )


def weight_grad_kernel(terms, starts, *refs):
    outs = refs[2 * terms :]
    for n, out_ref in enumerate(outs):

        @pl.when((pl.program_id(0) >= starts[n]) & (pl.program_id(0) < starts[n + 1]))
        def _(out_ref=out_ref):
            low = 0
            for t in range(terms):
                value = dot_tn(refs[2 * t][...], refs[2 * t + 1][...])
                out_ref[:, low : low + value.shape[1]] = value.astype(BF)
                low = low + value.shape[1]


def weight_grads(unit, *pairs):
    width = pairs[0][0].shape[1]
    cols = sum(right.shape[1] for _, right in pairs)
    steps = width // unit
    rest = steps // 2 - 1
    sizes = [size for size in (rest, 1, rest, 1) if size]
    starts = [sum(sizes[:n]) for n in range(len(sizes) + 1)]

    def left_block(i):
        lower = i <= rest
        place = jnp.where(lower, i, i - rest - 1)
        return 0, jnp.where(place == rest, 0, place + 1) + jnp.where(lower, rest + 1, 0)

    in_specs, operands = [], []
    for left, right in pairs:
        in_specs.append(pl.BlockSpec((left.shape[0], unit), left_block))
        in_specs.append(resident(right))
        operands += [left, right]

    def out_block(n):
        return lambda i: (jnp.clip(i - starts[n], 0, sizes[n] - 1), 0)

    outs = call(
        functools.partial(weight_grad_kernel, len(pairs), starts),
        [jax.ShapeDtypeStruct((size * unit, cols), BF) for size in sizes],
        (steps,),
        in_specs,
        [pl.BlockSpec((unit, cols), out_block(n)) for n in range(len(sizes))],
        *operands,
    )
    return outs if rest else [None, outs[0], None, outs[1]]


def pair_kernel(pieces, cut, _, a_ref, c_ref, *refs):
    out_ref = refs[-1]
    a, c = a_ref[...], c_ref[...]
    low = 0
    for b_ref, d_ref in zip(refs[:pieces], refs[pieces : 2 * pieces]):
        high = low + b_ref.shape[0]
        total = dot_nt(a, b_ref[...]) + dot_nt(c, d_ref[:, cut : cut + c.shape[1]])
        out_ref[:, low:high] = total.astype(BF)
        low = high


def pair_dot(part, crossed, a, b, c, d, cut):
    rows, width = a.shape[0] // 2, sum(piece.shape[0] for piece in b)
    tile = rows // 4

    def out_block(i, f):
        return jnp.where((f[0] == 1) & (i > 0) & (i < 3), 3 - i, i), 0

    return call(
        functools.partial(pair_kernel, len(b), cut),
        jax.ShapeDtypeStruct((rows, width), BF),
        (4,),
        [
            pl.BlockSpec((tile, a.shape[1]), lambda i, f: (part * 4 + i, 0)),
            pl.BlockSpec((tile, c.shape[1]), lambda i, f: (part * 4 + i, 0)),
        ]
        + [resident(w) for w in b]
        + [resident(w) for w in d],
        pl.BlockSpec((tile, width), out_block),
        crossed.reshape(1).astype(jnp.int32),
        a,
        c,
        *b,
        *d,
        prefetch=1,
    )


def attention_kernel(
    rows_ref, cot_ref, bias_ref, cos_ref, left_ref, right_ref, line_ref, column_ref, *refs
):
    weights, (out_ref, dpre_ref, sum_ref) = refs[:-3], refs[-3:]
    half, width = out_ref.shape[2:]
    rows = 2 * half
    scaling = HEAD_DIM ** (-0.5)

    def both(ref):
        return ref[:, 0].reshape(rows, ref.shape[3])

    cos, left, right = both(cos_ref), both(left_ref), both(right_ref)
    normed, cot = both(rows_ref), both(cot_ref)
    head_of = lax.broadcasted_iota(jnp.int32, (rows, LANES), 1) // HEAD_DIM

    def turn(v, sign):
        ahead = pltpu.roll(v, LANES - ROT_DIM // 2, 1)
        behind = pltpu.roll(v, ROT_DIM // 2, 1)
        return v * cos + sign * (ahead * left + behind * right)

    line, column = line_ref[0], column_ref[0]
    allowed = (line[:, 0:1] >= column[0:1]) & (line[:, 1:2] <= column[0:1])
    pre = wide_dot(normed, weights, slice(0, 3 * width)) + bias_ref[...]
    grads = wide_dot(cot, weights, slice(3 * width, 4 * width)).astype(BF)
    dpre_all = [None] * (3 * width // LANES)
    for pair in range(width // LANES):
        parts = [slice(b + pair * LANES, b + (pair + 1) * LANES) for b in (0, width, 2 * width)]
        q = turn(pre[:, parts[0]], 1.0).astype(BF)
        k = turn(pre[:, parts[1]], 1.0).astype(BF)
        v = pre[:, parts[2]].astype(BF)
        g = grads[:, parts[0]]
        att = dq = dk = dv = None
        for h in range(LANES // HEAD_DIM):
            mine = head_of == h
            qh = jnp.where(mine, q, 0).astype(BF)
            gh = jnp.where(mine, g, 0).astype(BF)
            s = jnp.where(allowed, dot_nt(qh, k) * scaling, NEGATIVE)
            e = jnp.exp(s - jnp.max(s, axis=-1, keepdims=True))
            p = e * (1.0 / jnp.sum(e, axis=-1, keepdims=True))
            low = p.astype(BF)
            att_h = dot_nn(low, v)
            dp = dot_nt(gh, v)
            inner = jnp.sum(p * dp, axis=-1, keepdims=True)
            ds = (p * (dp - inner)).astype(BF)
            dq_h = dot_nn(ds, k)
            dk_h = dot_tn(ds, qh)
            dv_h = dot_tn(low, gh)
            att = att_h if h == 0 else jnp.where(mine, att_h, att)
            dq = dq_h if h == 0 else jnp.where(mine, dq_h, dq)
            dk = dk_h if h == 0 else dk + dk_h
            dv = dv_h if h == 0 else dv + dv_h
        out_ref[:, 0, :, parts[0]] = att.astype(BF).reshape(2, half, LANES)
        for n, value in enumerate((turn(dq * scaling, -1.0), turn(dk * scaling, -1.0), dv)):
            value = value.astype(BF)
            dpre_ref[:, 0, :, parts[n]] = value.reshape(2, half, LANES)
            dpre_all[parts[n].start // LANES] = value
    add_row_sum(sum_ref, jnp.concatenate(dpre_all, axis=1))


def attention(normed, cot, bias, tables, line, column, weights):
    count, rows = column.shape[0], column.shape[2]
    half, width = rows // 2, weights[0].shape[1] // 4

    def split(value):
        return value.reshape(2, count, half, value.shape[1])

    def block(cols):
        return pl.BlockSpec((2, 1, half, cols), lambda s: (0, s, 0, 0))

    attended, dpre, sums = call(
        attention_kernel,
        [
            jax.ShapeDtypeStruct((2, count, half, width), BF),
            jax.ShapeDtypeStruct((2, count, half, 3 * width), BF),
            jax.ShapeDtypeStruct((8, 3 * width), F32),
        ],
        (count,),
        [
            block(normed.shape[1]),
            block(cot.shape[1]),
            pl.BlockSpec((1, 3 * width), lambda s: (0, 0)),
            block(LANES),
            block(LANES),
            block(LANES),
            pl.BlockSpec((1, rows, LANES), lambda s: (s, 0, 0)),
            pl.BlockSpec((1, 8, rows), lambda s: (s, 0, 0)),
        ]
        + [resident(w) for w in weights],
        [block(width), block(3 * width), pl.BlockSpec((8, 3 * width), lambda s: (0, 0))],
        split(normed),
        split(cot),
        bias.reshape(1, 3 * width),
        *[split(t) for t in tables],
        line,
        column,
        *weights,
    )
    tokens = 2 * count * half
    return attended.reshape(tokens, width), dpre.reshape(tokens, 3 * width), sums


def rotary_lanes(places):
    halfway = ROT_DIM // 2
    lane = jnp.arange(LANES, dtype=jnp.int32) % HEAD_DIM
    freqs = 10000.0 ** (-(lane % halfway).astype(F32) * 2.0 / ROT_DIM)
    angles = places.astype(F32)[:, None] * freqs[None, :]
    turned = lane < ROT_DIM
    cos = jnp.where(turned, jnp.cos(angles), 1.0)
    sin = jnp.where(turned, jnp.sin(angles), 0.0)
    return cos, jnp.where(lane < halfway, -sin, 0.0), jnp.where(lane >= halfway, sin, 0.0)


def standardize(inputs):
    average = jnp.mean(inputs, axis=-1, keepdims=True)
    centered = inputs - average
    inv_std = lax.rsqrt(jnp.mean(centered * centered, axis=-1, keepdims=True) + EPSILON)
    return centered * inv_std, inv_std


def input_gradient(normed_grad, cot, normal_x, inv_std, gain):
    scaled = normed_grad * gain
    return cot + inv_std * (
        scaled
        - jnp.mean(scaled, axis=-1, keepdims=True)
        - normal_x * jnp.mean(scaled * normal_x, axis=-1, keepdims=True)
    )


def norm_kernel(table_ref, tok_ref, cot_ref, gain_ref, shift_ref, normed_ref, mixed_ref, *, cols):
    normal_x, _ = standardize(tok_ref[...].astype(F32))
    normed = (normal_x * gain_ref[...].astype(F32) + shift_ref[...].astype(F32)).astype(BF)
    for n in range(tok_ref.shape[1] // cols):
        target = pl.ds(pl.multiple_of(table_ref[n], cols), cols)
        normed_ref[:, target] = normed[:, n * cols : (n + 1) * cols]
        mixed_ref[:, target] = cot_ref[:, n * cols : (n + 1) * cols]


def natural(table_ref, kept_ref, got_ref, cols):
    parts = []
    for n in range(kept_ref.shape[1] // cols):
        source = pl.ds(pl.multiple_of(table_ref[n], cols), cols)
        parts.append(kept_ref[:, source].astype(F32) + got_ref[:, source].astype(F32))
    return jnp.concatenate(parts, axis=1)


def norm_back_kernel(
    table_ref, tok_ref, cot_ref, gain_ref, kept_ref, got_ref, grad_ref, lines_ref, *, cols
):
    normal_x, inv_std = standardize(tok_ref[...].astype(F32))
    cot = cot_ref[...].astype(F32)
    normed_grad = natural(table_ref, kept_ref, got_ref, cols)
    grad_ref[...] = input_gradient(
        normed_grad, cot, normal_x, inv_std, gain_ref[...].astype(F32)
    )

    @pl.when(pl.program_id(0) == 0)
    def _():
        lines_ref[...] = jnp.zeros_like(lines_ref)

    for row, value in enumerate((normed_grad * normal_x, normed_grad, cot)):
        lines_ref[row : row + 1, :] += jnp.sum(value, axis=0, keepdims=True)


def result_kernel(table_ref, tok_ref, bias_ref, kept_ref, got_ref, out_ref, *, cols):
    branches = natural(table_ref, kept_ref, got_ref, cols)
    out_ref[...] = (tok_ref[...].astype(F32) + branches + bias_ref[...].astype(F32)).astype(BF)


def on_half(kernel, table, cols, whole, lines, mine, outs, tile=64):
    half, width = whole[0].shape[0] // 2, whole[0].shape[1]
    steps = half // tile
    last_entry = table.shape[0] - 1
    block = pl.BlockSpec((tile, width), lambda i, t: (i, 0))
    return pl.pallas_call(
        functools.partial(kernel, cols=cols),
        out_shape=outs,
        grid_spec=pltpu.PrefetchScalarGridSpec(
            num_scalar_prefetch=1,
            grid=(steps,),
            in_specs=[pl.BlockSpec((tile, width), lambda i, t: (t[last_entry] * steps + i, 0))]
            * len(whole)
            + [pl.BlockSpec((1, width), lambda i, t: (0, 0))] * len(lines)
            + [block] * len(mine),
            out_specs=[
                block if out.shape[0] == half else pl.BlockSpec(out.shape, lambda i, t: (0, 0))
                for out in outs
            ],
        ),
        compiler_params=pltpu.CompilerParams(vmem_limit_bytes=32 * 1024 * 1024),
        cost_estimate=pl.CostEstimate(
            flops=1000, bytes_accessed=1000, transcendentals=0
        ),
    )(table, *whole, *[line.reshape(1, width) for line in lines], *mine)


def local_part(dp_size):
    top_bits = [b for b in range(3, dp_size.bit_length() - 1)]

    def swap(value, bit):
        return lax.ppermute(value, "dp", [(i, i ^ (1 << bit)) for i in range(dp_size)])

    def swap_core(value):
        return lax.ppermute(value, "tensor", [(0, 1), (1, 0)])

    def swap_mixed(value, bits):
        pairs = [(2 * i + c, 2 * (i ^ (1 << bits[c])) + c) for i in range(dp_size) for c in (0, 1)]
        return lax.ppermute(value, ("dp", "tensor"), pairs)

    def ordered(bit, own, other, axis):
        return jnp.where(
            bit == 0,
            jnp.concatenate([own, other], axis),
            jnp.concatenate([other, own], axis),
        )

    def part_of(value, index, axis):
        size = value.shape[axis] // 2
        return lax.dynamic_slice_in_dim(value, index * size, size, axis)

    def sync(*values):
        return lax.optimization_barrier(values)

    def local(
        tokens,
        segments,
        ln_gain,
        ln_shift,
        qkv_weight,
        qkv_bias,
        out_weight,
        up_weight,
        up_bias,
        down_weight,
        branch_bias,
        cotangent,
    ):
        rows, width = tokens.shape
        half = rows // 2
        wide = width // 2
        share = qkv_weight.shape[0]
        unit = 4 * share
        cols = 2 * share
        me = lax.axis_index("dp")
        core = lax.axis_index("tensor")
        x_mine, y_mine, zl_mine = (me >> X_BIT) & 1, (me >> Y_BIT) & 1, (me >> ZL_BIT) & 1
        block = 2 * x_mine + zl_mine
        att = qkv_weight.shape[2] // 4
        hid = up_weight.shape[1] // 4
        tops = 2 ** len(top_bits)

        n = jnp.arange(4 * tops, dtype=jnp.int32)
        table = ((((n & 1) ^ y_mine) * tops + ((n >> 2) ^ (me >> 3))) * 2 + ((n >> 1) & 1)) * cols
        table = jnp.concatenate([table, core.reshape(1)]).astype(jnp.int32)
        aligned = cols % LANES == 0

        def relative(split):
            for axis, bit in enumerate([Y_BIT] + top_bits[::-1]):
                split = jnp.where((me >> bit) & 1 == 1, jnp.flip(split, axis + 1), split)
            return split

        def to_mixed(value):
            count = value.shape[0]
            split = value.reshape(count, tops, 2, 2, cols).transpose(0, 3, 1, 2, 4)
            split = relative(split.reshape((count, 2) + (2,) * len(top_bits) + (unit,)))
            return split.reshape(count, width)

        def from_mixed(value):
            count = value.shape[0]
            split = relative(value.reshape((count, 2) + (2,) * len(top_bits) + (unit,)))
            split = split.reshape(count, 2, tops, 2, cols).transpose(0, 2, 3, 1, 4)
            return split.reshape(count, width)

        def my_rows(value):
            return lax.dynamic_slice_in_dim(value, core * half, half, 0)

        def norm_forward():
            shape = jax.ShapeDtypeStruct((half, width), BF)
            if aligned:
                return on_half(
                    norm_kernel,
                    table,
                    cols,
                    [tokens, cotangent],
                    [ln_gain, ln_shift],
                    [],
                    [shape, shape],
                )
            normal_x, _ = standardize(my_rows(tokens).astype(F32))
            normed = normal_x * ln_gain.astype(F32) + ln_shift.astype(F32)
            return to_mixed(normed.astype(BF)), to_mixed(my_rows(cotangent))

        def norm_backward(kept, got):
            if aligned:
                return on_half(
                    norm_back_kernel,
                    table,
                    cols,
                    [tokens, cotangent],
                    [ln_gain],
                    [kept, got],
                    [
                        jax.ShapeDtypeStruct((half, width), F32),
                        jax.ShapeDtypeStruct((8, width), F32),
                    ],
                )
            normal_x, inv_std = standardize(my_rows(tokens).astype(F32))
            cot = my_rows(cotangent).astype(F32)
            grad = from_mixed(add(kept, got))
            lines = jnp.stack(
                [jnp.sum(v, axis=0) for v in (grad * normal_x, grad, cot)]
                + [jnp.zeros((width,), F32)] * 5
            )
            return input_gradient(grad, cot, normal_x, inv_std, ln_gain.astype(F32)), lines

        def finish(kept, got):
            if aligned:
                return on_half(
                    result_kernel,
                    table,
                    cols,
                    [tokens],
                    [branch_bias],
                    [kept, got],
                    [jax.ShapeDtypeStruct((half, width), BF)],
                )[0]
            branches = from_mixed(add(kept, got))
            return (my_rows(tokens).astype(F32) + branches + branch_bias.astype(F32)).astype(BF)

        def w_x(piece):
            return part_of(piece, x_mine, 1), swap(part_of(piece, 1 - x_mine, 1), X_BIT)

        def w_zl(w):
            return part_of(w, zl_mine, 1), swap(part_of(w, 1 - zl_mine, 1), ZL_BIT)

        def w_top(w):
            rest = None
            for bit in top_bits:
                mine = w if rest is None else jnp.concatenate([w, rest])
                got = swap(mine, bit)
                rest = got if rest is None else jnp.concatenate([rest, got])
            return rest

        def add(*values):
            total = values[0].astype(F32)
            for value in values[1:]:
                total = total + value.astype(F32)
            return total

        def top_send(kept, got):
            if kept is None:
                return None, None
            if tops > 2:
                return add(kept, got).astype(BF), None
            cut = kept.shape[0] // 2
            return add(kept[:cut], got[:cut]).astype(BF), add(kept[cut:], got[cut:]).astype(BF)

        def g_top(rest):
            if rest is None or tops == 2:
                return None if rest is None else swap(rest, top_bits[0])
            own = jnp.zeros((unit,) + rest.shape[1:], rest.dtype)
            grad = jnp.concatenate([own, rest])
            for bit in reversed(top_bits):
                cut = grad.shape[0] // 2
                grad = add(grad[:cut], swap(grad[cut:], bit)).astype(BF)
            return grad

        def g_own(kept, got, *tops_got):
            tops_got = [value for value in tops_got if value is not None]
            if len(tops_got) > 1:
                tops_got = [jnp.concatenate(tops_got)]
            return add(kept, got, *tops_got).astype(BF)

        def g_zl(grad):
            return part_of(grad, zl_mine, 0), swap(part_of(grad, 1 - zl_mine, 0), ZL_BIT)

        def g_x(grad):
            return part_of(grad, x_mine, 0), swap(part_of(grad, 1 - x_mine, 0), X_BIT)

        def g_swap_y(value):
            return None if value is None else swap(value, Y_BIT)

        straight = jnp.zeros((2,), jnp.int32)
        crossed = jnp.stack([core, 1 - core]).astype(jnp.int32)

        u_x = w_x(up_weight)
        n_own, c_own = norm_forward()
        seg = segments.reshape(1, rows)
        u_x, c_own, qkv_weight, out_weight, down_weight = sync(
            u_x, c_own, qkv_weight, out_weight, down_weight
        )
        uu = w_zl(ordered(x_mine, *u_x, 0))
        n_got = swap(n_own, ZL_BIT)
        seg = jnp.concatenate([seg, swap(seg, ZL_BIT)])
        qkv_piece = qkv_weight.reshape(share, 3, 4, att).swapaxes(1, 2).reshape(share, 4, 3 * att)
        out_piece = out_weight.T.reshape(share, 4, att)
        a_x = w_x(jnp.concatenate([qkv_piece, out_piece], axis=2).reshape(share, 16 * att))
        d_x = w_x(down_weight.T)
        uu, n_own, n_got, a_x, d_x, c_own, seg = sync(uu, n_own, n_got, a_x, d_x, c_own, seg)
        uu = ordered(zl_mine, *uu, 0)
        u_rest = w_top(uu)
        u_far = swap(uu, Y_BIT)
        n_pair = jnp.concatenate([n_own, n_got])
        n_second = swap(n_pair, X_BIT)
        n_got_pair = swap_core(n_pair)
        aa = w_zl(ordered(x_mine, *a_x, 0))
        seg = jnp.concatenate([seg, swap(seg, X_BIT)])
        dd = ordered(x_mine, *d_x, 0)
        u_rest, u_far, n_second, n_got_pair, aa, dd, c_own, seg = sync(
            u_rest, u_far, n_second, n_got_pair, aa, dd, c_own, seg
        )
        aa = ordered(zl_mine, *aa, 0)
        a_rest = w_top(aa)
        a_far = swap(aa, Y_BIT)
        u_far_rest = g_swap_y(u_rest)
        n_got_second = swap_core(n_second)
        dd = w_zl(dd)
        c_got = swap_mixed(c_own, (ZL_BIT, X_BIT))
        order = jnp.broadcast_to(jnp.arange(rows, dtype=jnp.int32), (4, rows))
        begins = jnp.concatenate([jnp.ones((4, 1), bool), seg[:, 1:] != seg[:, :-1]], axis=1)
        opening = lax.cummax(jnp.where(begins, order, 0), axis=1)

        def halves(value):
            return jnp.where(core == 0, value, jnp.roll(value, half, axis=1))

        order, opening = halves(order), halves(opening)
        tables = rotary_lanes(
            (order - opening).reshape(4, 2, half).swapaxes(0, 1).reshape(4 * rows)
        )
        line = jnp.stack([order, opening], axis=2)
        line = jnp.pad(line, ((0, 0), (0, 0), (0, LANES - 2)))
        column = jnp.broadcast_to(order[:, None, :], (4, 8, rows))
        u_far_rest, a_rest, a_far, dd, c_own, c_got, n_got_second, tables, line, column = sync(
            u_far_rest, a_rest, a_far, dd, c_own, c_got, n_got_second, tables, line, column
        )
        dd = ordered(zl_mine, *dd, 0)
        d_rest = w_top(dd)
        d_far = swap(dd, Y_BIT)
        a_far_rest = g_swap_y(a_rest)
        c_pair = jnp.concatenate([c_own, c_got])
        c_second = swap_mixed(c_pair, (X_BIT, ZL_BIT))
        c_got_pair = swap_core(c_pair)
        normed = join(straight, n_pair, n_second, n_got_pair, n_got_second)
        my_up_bias = lax.dynamic_slice_in_dim(up_bias, block * hid, hid, 0).astype(F32)
        up_w = [w for w in (uu, u_rest, u_far, u_far_rest) if w is not None]
        act, slope = up_project(normed, my_up_bias, up_w)
        d_rest, d_far, a_far_rest, c_second, c_got_pair, normed, act, slope = sync(
            d_rest, d_far, a_far_rest, c_second, c_got_pair, normed, act, slope
        )
        d_far_rest = g_swap_y(d_rest)
        c_got_second = swap_core(c_second)
        cot = join(crossed, c_pair, c_second, c_got_pair, c_got_second)
        gd = weight_grads(unit, (cot, act))
        d_far_rest, cot, gd = sync(d_far_rest, cot, gd)
        d_a = g_swap_y(gd[0])
        my_qkv_bias = lax.dynamic_slice_in_dim(qkv_bias, block * att, att, 1).astype(F32)
        att_w = [w for w in (aa, a_rest, a_far, a_far_rest) if w is not None]
        attended, qkv_g, qkv_sums = attention(
            normed, cot, my_qkv_bias, tables, line, column, att_w
        )
        d_a, gd, attended, qkv_g, d_far_rest = sync(d_a, gd, attended, qkv_g, d_far_rest)
        d_z1, d_z2 = top_send(gd[2], d_a)
        d_z1 = g_top(d_z1)
        d_b = swap(gd[1], Y_BIT)
        ga = weight_grads(unit, (normed, qkv_g), (cot, attended))
        d_z1, d_z2, d_b, ga, cot, slope = sync(d_z1, d_z2, d_b, ga, cot, slope)
        d_z2 = g_top(d_z2)
        a_a = g_swap_y(ga[0])
        down_w = [w for w in (dd, d_rest, d_far, d_far_rest) if w is not None]
        up_g, up_sums = up_gradient(cot, slope, down_w)
        n_send = pair_dot(1, 1 - core, up_g, up_w, qkv_g, att_w, 0)
        d_z2, a_a, ga, up_g, n_send = sync(d_z2, a_a, ga, up_g, n_send)
        d_l = g_zl(g_own(gd[3], d_b, d_z1, d_z2))
        a_z1, a_z2 = top_send(ga[2], a_a)
        a_z1 = g_top(a_z1)
        a_b = swap(ga[1], Y_BIT)
        n_got = swap_core(n_send)
        gu = weight_grads(unit, (normed, up_g))
        n_kept = pair_dot(0, core, up_g, up_w, qkv_g, att_w, 0)
        d_l, a_z1, a_z2, a_b, gu, n_got, n_kept, act, attended = sync(
            d_l, a_z1, a_z2, a_b, gu, n_got, n_kept, act, attended
        )
        n_second = swap_mixed(add(n_kept[2 * half :], n_got[2 * half :]).astype(BF), (X_BIT, ZL_BIT))
        a_z2 = g_top(a_z2)
        u_a = g_swap_y(gu[0])
        d_x = g_x(ordered(zl_mine, *d_l, 1))
        b_send = pair_dot(1, 1 - core, act, down_w, attended, att_w, 3 * att)
        a_z2, u_a, gu, d_x, n_second, b_send, act, attended = sync(
            a_z2, u_a, gu, d_x, n_second, b_send, act, attended
        )
        n_first = add(n_kept[half : 2 * half], n_got[half : 2 * half], n_second[half:])
        n_first = swap_mixed(n_first.astype(BF), (ZL_BIT, X_BIT))
        u_z1, u_z2 = top_send(gu[2], u_a)
        u_z1 = g_top(u_z1)
        u_b = swap(gu[1], Y_BIT)
        a_l = g_zl(g_own(ga[3], a_b, a_z1, a_z2))
        b_got = swap_core(b_send)
        b_kept = pair_dot(0, core, act, down_w, attended, att_w, 3 * att)
        n_keep = add(n_kept[:half], n_got[:half], n_second[:half])
        u_z1, u_z2, u_b, a_l, n_first, n_keep, b_got, b_kept = sync(
            u_z1, u_z2, u_b, a_l, n_first, n_keep, b_got, b_kept
        )
        b_second = swap_mixed(add(b_kept[2 * half :], b_got[2 * half :]).astype(BF), (X_BIT, ZL_BIT))
        u_z2 = g_top(u_z2)
        a_x = g_x(ordered(zl_mine, *a_l, 1))
        input_grad, lines = norm_backward(n_keep, n_first)
        input_other = swap_core(input_grad)
        lines = lines[:3].reshape(-1)
        lines = lines + swap_core(lines)
        biases = jnp.concatenate([qkv_sums[0], up_sums[0]])
        spread = lax.dynamic_update_slice_in_dim(
            jnp.zeros((4, biases.shape[0]), F32), biases[None], block, 0
        )
        lines = jnp.concatenate([lines, spread.reshape(-1)])
        for bit in top_bits + [Y_BIT]:
            lines = lines + swap(lines, bit)
        u_z2, a_x, b_second, input_grad, input_other, lines = sync(
            u_z2, a_x, b_second, input_grad, input_other, lines
        )
        b_first = add(b_kept[half : 2 * half], b_got[half : 2 * half], b_second[half:])
        b_first = swap_mixed(b_first.astype(BF), (ZL_BIT, X_BIT))
        u_l = g_zl(g_own(gu[3], u_b, u_z1, u_z2))
        b_keep = add(b_kept[:half], b_got[:half], b_second[:half])
        input_grad = place_halves(core, input_grad, input_other)
        lines = lines + swap(lines, X_BIT)
        lines = lines + swap(lines, ZL_BIT)
        ga = ordered(x_mine, *a_x, 1)
        gd = ordered(x_mine, *d_x, 1)
        u_l, b_first, b_keep, lines = sync(u_l, b_first, b_keep, lines)
        gu = g_x(ordered(zl_mine, *u_l, 1))
        result = finish(b_keep, b_first)
        result = place_halves(core, result, swap_core(result))
        gu = ordered(x_mine, *gu, 1)

        gdown = gd.astype(F32).T
        gup = gu.astype(F32)
        ga = ga.reshape(share, 4, 4 * att)
        gqkv = ga[..., : 3 * att].astype(F32)
        gqkv = gqkv.reshape(share, 4, 3, att).swapaxes(1, 2).reshape(share, 3, 4 * att)
        gout = ga[..., 3 * att :].astype(F32).reshape(share, 4 * att).T
        biases = lines[3 * width :].reshape(4, 3 * att + hid)
        qkv_b = biases[:, : 3 * att].reshape(4, 3, att).swapaxes(0, 1).reshape(3, 4 * att)
        up_b = biases[:, 3 * att :].reshape(4 * hid)
        return (
            result,
            input_grad,
            lines[:width],
            lines[width : 2 * width],
            gqkv,
            qkv_b,
            gout,
            gup,
            up_b,
            gdown,
            lines[2 * width : 3 * width],
        )

    return local


def solution(mesh):
    return jax.shard_map(
        local_part(mesh.shape["dp"]),
        mesh=mesh,
        in_specs=(
            P("dp", None),
            P("dp"),
            P(),
            P(),
            P("dp", None, "tensor"),
            P(None, "tensor"),
            P("tensor", "dp"),
            P("dp", "tensor"),
            P("tensor"),
            P("tensor", "dp"),
            P(),
            P("dp", None),
        ),
        out_specs=(
            P("dp", None),
            P("dp", None),
            P(),
            P(),
            P("dp", None, "tensor"),
            P(None, "tensor"),
            P("tensor", "dp"),
            P("dp", "tensor"),
            P("tensor"),
            P("tensor", "dp"),
            P(),
        ),
        check_vma=False,
    )
```

time: 1330 us -> 593 us (0.45)
  Pallas kernels: 783 us -> 198 us
  matrix products: 84.3 us -> 0 us
  starting transfers between devices: 121 us -> 60.6 us
  waiting for transfers between devices: 153 us -> 205 us
  local copies, waits for them, and re-layouts: 89.3 us -> 57.6 us
  other arithmetic: 84.1 us -> 60 us
    pallas_call x9 -> x14, Pallas kernels: 776 us -> 191 us  [call(): pl.pallas_call(kernel, out_shape=outs, grid_spec=pltpu.PrefetchScalarGrid...]
    dot_general x8 -> x0, matrix products: 84.3 us -> none  [the longest x4 42.7 us: weight_grad(): lax.dot_general(left, right, first, preferred_element_type=F32).astype(BF)]
    ppermute x31 -> x41, waiting for transfers between devices: 123 us -> 202 us  [swap(): lax.ppermute(value, 'dp', [(i, i ^ 1 << bit) for i in range(dp_size)])]
    ppermute x9, starting transfers between devices: 75.4 us -> 1.6 us  [swap_core(): return lax.ppermute(value, 'tensor', [(0, 1), (1, 0)])]
    ppermute x10 -> x6, waiting for transfers between devices: 29.2 us -> 0.02 us  [swap_mixed(): return lax.ppermute(value, ('dp', 'tensor'), pairs)]
    unnamed x103 -> x111, local copies, waits for them, and re-layouts: 35.9 us -> 19.6 us
    ppermute x31 -> x41, starting transfers between devices: 37.7 us -> 50.9 us  [swap(): lax.ppermute(value, 'dp', [(i, i ^ 1 << bit) for i in range(dp_size)])]
  transfers between devices with their start and end apart: 50 -> 56, of which waited for: 15 -> 17; matrix products, arithmetic and copies ran while one was open for 15% -> 15% of each run, Pallas kernels for 53% -> 33%
where the time goes in v4:
time: 593 us; the launch traced here: 584 us
  waiting for transfers between devices  205 us (35%)
  Pallas kernels  198 us (33%)
  starting transfers between devices  60.6 us (10%)
  other arithmetic  60 us (10%)
  local copies, waits for them, and re-layouts  57.6 us (10%)
    ppermute x41, waiting for transfers between devices, swap(): lax.ppermute(value, 'dp', [(i, i ^ 1 << bit) for i in range(dp_size)])  202 us
    pallas_call x14, Pallas kernels, call(): pl.pallas_call(kernel, out_shape=outs, grid_spec=pltpu.PrefetchScalarGrid...  191 us
    ppermute x41, starting transfers between devices, swap(): lax.ppermute(value, 'dp', [(i, i ^ 1 << bit) for i in range(dp_size)])  50.9 us
    unnamed x111, local copies, waits for them, and re-layouts  19.6 us
    select_n x10, other arithmetic, ordered(): jnp.where(bit == 0, jnp.concatenate([own, other], axis), jnp.concatenate(...  16.3 us
    dynamic_slice x12, local copies, waits for them, and re-layouts, part_of(): return lax.dynamic_slice_in_dim(value, index * size, size, axis)  13.9 us
  transfers between devices with their start and end apart: 56, of which 17 were waited for; matrix products, arithmetic and copies ran while one was open for 15% of the time, Pallas kernels for 33%

profile of v4, /device:TPU:0, one launch (start us, length us, event | category | flops | bytes accessed | tf_op | source)
XLA Modules:
  0.0 583.6 jit_solution(15516748418423424246)
XLA Ops:
  12.3 6.0 %collective-permute-done = bf16[128,2048]{1,0:T(8,128)(2,1)} collective-permute-done((bf16[128,2048]{1,0:T(8,128)(2,1)}, bf16[128,2048]{1,0:T(8,128)(2,1)}, u32[]{:S(2)}, u32[]{:S(2)}) %collective-permute-start) | collective-permute-done | bytes 524320 | tf_op jit(solution)/shard_map/ppermute | solution.py:477
  36.5 10.4 %collective-permute-done.5 = s32[1,512]{1,0:T(1,128)S(1)} collective-permute-done((s32[1,512]{1,0:T(1,128)S(1)}, s32[1,512]{1,0:T(1,128)S(1)}, u32[]{:S(2)}, u32[]{:S(2)}) %collective-permute-start.5) | collective-permute-done | bytes 2080 | tf_op jit(solution)/shard_map/ppermute | solution.py:477
  49.0 4.9 collective-permute-done.4
  69.1 35.0 %collective-permute-done.11 = s32[2,512]{1,0:T(2,128)S(1)} collective-permute-done((s32[2,512]{1,0:T(2,128)S(1)}, s32[2,512]{1,0:T(2,128)S(1)}, u32[]{:S(2)}, u32[]{:S(2)}) %collective-permute-start.11) | collective-permute-done | bytes 4128 | tf_op jit(solution)/shard_map/ppermute | solution.py:477
  107.5 14.7 %collective-permute-done.10 = bf16[256,1024]{1,0:T(8,128)(2,1)S(1)} collective-permute-done((bf16[256,1024]{1,0:T(8,128)(2,1)S(1)}, bf16[256,1024]{1,0:T(8,128)(2,1)S(1)}, u32[]{:S(2)}, u32[]{:S(2)}) %collective-permute-start.10) | collective-permute-done | bytes 524320 | tf_op jit(solution)/shard_map/ppermute | solution.py:477
  134.2 17.0 %collective-permute-done.15 = bf16[256,1024]{1,0:T(8,128)(2,1)} collective-permute-done((bf16[256,1024]{1,0:T(8,128)(2,1)S(1)}, bf16[256,1024]{1,0:T(8,128)(2,1)}, u32[]{:S(2)}, u32[]{:S(2)}) %collective-permute-start.15) | collective-permute-done | bytes 524320 | tf_op jit(solution)/shard_map/ppermute | solution.py:477
  154.9 5.9 %fusion.2 = (f32[2048,128]{1,0:T(8,128)}, f32[2048,128]{1,0:T(8,128)}, f32[2048,128]{1,0:T(8,128)}) fusion(f32[128]{0:T(128)S(1)} %fusion.15, f32[2048]{0:T(1024)S(1)} %bitcast.96, pred[128]{0:T(512)(128)(4,1)S(1)} %get-tuple-element.418, pred[128]{0:T(512)(128)(4,1)S(1)} %broadcast_compare_fusion.2, pred[128]{0:T(512)(128)(4,1)S(1)} %get-tuple-element.419), kind=kLoop, calls=%fused_computation.15 | loop fusion | flops 1572864 | bytes 3154816 | tf_op jit(solution)/shard_map/jit(_where)/select_n | solution.py:387
  160.8 17.7 %collective-permute-done.13.refs_1_.refs_5_ = bf16[512,1024]{1,0:T(8,128)(2,1)} collective-permute-done((bf16[512,1024]{1,0:T(8,128)(2,1)}, bf16[512,1024]{1,0:T(8,128)(2,1)}, u32[]{:S(2)}, u32[]{:S(2)}) %collective-permute-start.13) | collective-permute-done | bytes 1048608 | tf_op jit(solution)/shard_map/ppermute | solution.py:477
  191.2 10.7 %shard_map.204.rows_ref.refs_0_ = bf16[2048,2048]{1,0:T(8,128)(2,1)} custom-call(s32[2]{0:T(128)} %broadcast_10_flags_ref.2.flags_ref, bf16[512,2048]{1,0:T(8,128)(2,1)} %constant_dynamic-update-slice_fusion.pair_ref, bf16[512,2048]{1,0:T(8,128)(2,1)} %collective-permute-done.8.second_ref, bf16[512,2048]{1,0:T(8,128)(2,1)} %collective-permute-done.9.got_pair_ref, ...), custom_call_target="tpu_custom_call" | custom-call | flops 1000 | bytes 1000 | tf_op jit(solution)/shard_map/pallas_call | solution.py:35
  202.0 17.3 %shard_map.205 = (bf16[2048,1024]{1,0:T(8,128)(2,1)}, bf16[2048,1024]{1,0:T(8,128)(2,1)}) custom-call(bf16[2048,2048]{1,0:T(8,128)(2,1)} %shard_map.204.rows_ref.refs_0_, f32[1,1024]{1,0:T(1,128)} %bitcast.101, bf16[512,1024]{1,0:T(8,128)(2,1)} %copy-done.8, bf16[512,1024]{1,0:T(8,128)(2,1)} %collective-permute-done.6.refs_1_, bf16[512,1024]{1,0:T(8,128)(2,1)} %copy-done.13, ...), custom_call_target="tpu_custom_call" | custom-call | flops 1000 | bytes 1000 | tf_op jit(solution)/shard_map/pallas_call | solution.py:35
  219.3 17.0 %collective-permute-done.18.refs_1_ = bf16[512,1024]{1,0:T(8,128)(2,1)} collective-permute-done((bf16[512,1024]{1,0:T(8,128)(2,1)}, bf16[512,1024]{1,0:T(8,128)(2,1)}, u32[]{:S(2)}, u32[]{:S(2)}) %collective-permute-start.18) | collective-permute-done | bytes 1048608 | tf_op jit(solution)/shard_map/ppermute | solution.py:477
  240.8 10.8 %shard_map.206.refs_0_.refs_2_.rows_ref = bf16[2048,2048]{1,0:T(8,128)(2,1)} custom-call(s32[2]{0:T(128)} %pad_add_fusion.4.flags_ref, bf16[512,2048]{1,0:T(8,128)(2,1)} %constant_dynamic-update-slice_fusion.2.pair_ref, bf16[512,2048]{1,0:T(8,128)(2,1)} %collective-permute-done.21.second_ref, bf16[512,2048]{1,0:T(8,128)(2,1)} %collective-permute-done.22.got_pair_ref, ...), custom_call_target="tpu_custom_call" | custom-call | flops 1000 | bytes 1000 | tf_op jit(solution)/shard_map/pallas_call | solution.py:35
  251.6 14.7 %shard_map.207 = (bf16[512,1024]{1,0:T(8,128)(2,1)}, bf16[512,1024]{1,0:T(8,128)(2,1)}, bf16[512,1024]{1,0:T(8,128)(2,1)}, bf16[512,1024]{1,0:T(8,128)(2,1)}) custom-call(bf16[2048,2048]{1,0:T(8,128)(2,1)} %shard_map.206.refs_0_.refs_2_.rows_ref, bf16[2048,1024]{1,0:T(8,128)(2,1)} %get-tuple-element.268.refs_1_.a_ref), custom_call_target="tpu_custom_call" | custom-call | flops 1000 | bytes 1000 | tf_op jit(solution)/shard_map/pallas_call | solution.py:35
  269.2 34.4 %shard_map.208 = (bf16[2,4,256,256]{3,2,1,0:T(8,128)(2,1)}, bf16[2,4,256,768]{3,2,1,0:T(8,128)(2,1)}, f32[8,768]{1,0:T(8,128)}) custom-call(bf16[2,4,256,2048]{3,2,1,0:T(8,128)(2,1)} %bitcast.76, bf16[2,4,256,2048]{3,2,1,0:T(8,128)(2,1)} %bitcast.77, f32[1,768]{1,0:T(1,128)} %bitcast.105, f32[2,4,256,128]{3,2,1,0:T(8,128)} %bitcast.87, ...), custom_call_target="tpu_custom_call" | custom-call | flops 1000 | bytes 1000 | tf_op jit(solution)/shard_map/pallas_call | solution.py:35
  306.3 15.2 %shard_map.209 = (bf16[512,1024]{1,0:T(8,128)(2,1)}, bf16[512,1024]{1,0:T(8,128)(2,1)}, bf16[512,1024]{1,0:T(8,128)(2,1)}, bf16[512,1024]{1,0:T(8,128)(2,1)}) custom-call(bf16[2048,2048]{1,0:T(8,128)(2,1)} %shard_map.204.rows_ref.refs_0_, bf16[2048,768]{1,0:T(8,128)(2,1)} %bitcast.78, bf16[2048,2048]{1,0:T(8,128)(2,1)} %shard_map.206.refs_0_.refs_2_.rows_ref, ...), custom_call_target="tpu_custom_call" | custom-call | flops 1000 | bytes 1000 | tf_op jit(solution)/shard_map/pallas_call | solution.py:35
  321.5 8.7 %collective-permute-done.26 = bf16[256,1024]{1,0:T(8,128)(2,1)S(1)} collective-permute-done((bf16[256,1024]{1,0:T(8,128)(2,1)S(1)}, bf16[256,1024]{1,0:T(8,128)(2,1)S(1)}, u32[]{:S(2)}, u32[]{:S(2)}) %collective-permute-start.26) | collective-permute-done | bytes 524320 | tf_op jit(solution)/shard_map/ppermute | solution.py:477
  331.8 14.6 %shard_map.210 = (bf16[2048,1024]{1,0:T(8,128)(2,1)}, f32[8,1024]{1,0:T(8,128)}) custom-call(bf16[2048,2048]{1,0:T(8,128)(2,1)} %shard_map.206.refs_0_.refs_2_.rows_ref, bf16[2048,1024]{1,0:T(8,128)(2,1)} %get-tuple-element.233.slope_ref, bf16[512,1024]{1,0:T(8,128)(2,1)} %maximum_select_fusion.5.refs_0_, bf16[512,1024]{1,0:T(8,128)(2,1)} %collective-permute-done.18.refs_1_, ...), custom_call_target="tpu_custom_call" | custom-call | flops 1000 | bytes 1000 | tf_op jit(solution)/shard_map/pallas_call | solution.py:35
  346.4 13.4 %shard_map.211 = bf16[1024,2048]{1,0:T(8,128)(2,1)} custom-call(s32[1]{0:T(128)} %bitcast.18._, bf16[2048,1024]{1,0:T(8,128)(2,1)} %get-tuple-element.241.a_ref.refs_1_, bf16[2048,768]{1,0:T(8,128)(2,1)} %bitcast.79, bf16[512,1024]{1,0:T(8,128)(2,1)} %copy-done.8, bf16[512,1024]{1,0:T(8,128)(2,1)} %collective-permute-done.6.refs_1_, ...), custom_call_target="tpu_custom_call" | custom-call | flops 1000 | bytes 1000 | tf_op jit(solution)/shard_map/pallas_call | solution.py:35
  367.7 13.5 %shard_map.213 = bf16[1024,2048]{1,0:T(8,128)(2,1)} custom-call(s32[1]{0:T(128)} %bitcast._.core_ref, bf16[2048,1024]{1,0:T(8,128)(2,1)} %get-tuple-element.241.a_ref.refs_1_, bf16[2048,768]{1,0:T(8,128)(2,1)} %bitcast.80, bf16[512,1024]{1,0:T(8,128)(2,1)} %copy-done.8, bf16[512,1024]{1,0:T(8,128)(2,1)} %collective-permute-done.6.refs_1_, ...), custom_call_target="tpu_custom_call" | custom-call | flops 1000 | bytes 1000 | tf_op jit(solution)/shard_map/pallas_call | solution.py:35
  381.1 14.6 %shard_map.212 = (bf16[512,1024]{1,0:T(8,128)(2,1)}, bf16[512,1024]{1,0:T(8,128)(2,1)}, bf16[512,1024]{1,0:T(8,128)(2,1)}, bf16[512,1024]{1,0:T(8,128)(2,1)}) custom-call(bf16[2048,2048]{1,0:T(8,128)(2,1)} %shard_map.204.rows_ref.refs_0_, bf16[2048,1024]{1,0:T(8,128)(2,1)} %get-tuple-element.241.a_ref.refs_1_), custom_call_target="tpu_custom_call" | custom-call | flops 1000 | bytes 1000 | tf_op jit(solution)/shard_map/pallas_call | solution.py:35
  395.8 4.2 add_convert_fusion.1
  407.0 11.2 %shard_map.214 = bf16[1024,2048]{1,0:T(8,128)(2,1)} custom-call(s32[1]{0:T(128)} %bitcast.18._, bf16[2048,1024]{1,0:T(8,128)(2,1)} %get-tuple-element.268.refs_1_.a_ref, bf16[2048,256]{1,0:T(8,128)(2,1)} %bitcast.82, bf16[512,1024]{1,0:T(8,128)(2,1)} %maximum_select_fusion.5.refs_0_, bf16[512,1024]{1,0:T(8,128)(2,1)} %collective-permute-done.18.refs_1_, ...), custom_call_target="tpu_custom_call" | custom-call | flops 1000 | bytes 1000 | tf_op jit(solution)/shard_map/pallas_call | solution.py:35
  418.2 19.3 %collective-permute-done.36 = bf16[128,2048]{1,0:T(8,128)(2,1)S(1)} collective-permute-done((bf16[128,2048]{1,0:T(8,128)(2,1)S(1)}, bf16[128,2048]{1,0:T(8,128)(2,1)S(1)}, u32[]{:S(2)}, u32[]{:S(2)}) %collective-permute-start.36) | collective-permute-done | bytes 524320 | tf_op jit(solution)/shard_map/ppermute | solution.py:477
  438.3 4.6 convert_add_fusion.1
  453.1 10.9 %shard_map.215 = bf16[1024,2048]{1,0:T(8,128)(2,1)} custom-call(s32[1]{0:T(128)} %bitcast._.core_ref, bf16[2048,1024]{1,0:T(8,128)(2,1)} %get-tuple-element.268.refs_1_.a_ref, bf16[2048,256]{1,0:T(8,128)(2,1)} %bitcast.83, bf16[512,1024]{1,0:T(8,128)(2,1)} %maximum_select_fusion.5.refs_0_, bf16[512,1024]{1,0:T(8,128)(2,1)} %collective-permute-done.18.refs_1_, ...), custom_call_target="tpu_custom_call" | custom-call | flops 1000 | bytes 1000 | tf_op jit(solution)/shard_map/pallas_call | solution.py:35
  464.1 16.3 %collective-permute-done.40 = bf16[256,1024]{1,0:T(8,128)(2,1)S(1)} collective-permute-done((bf16[256,1024]{1,0:T(8,128)(2,1)S(1)}, bf16[256,1024]{1,0:T(8,128)(2,1)S(1)}, u32[]{:S(2)}, u32[]{:S(2)}) %collective-permute-start.40) | collective-permute-done | bytes 524320 | tf_op jit(solution)/shard_map/ppermute | solution.py:477
  484.2 3.8 add_convert_fusion
  503.0 22.5 %collective-permute-done.44 = bf16[128,2048]{1,0:T(8,128)(2,1)S(1)} collective-permute-done((bf16[128,2048]{1,0:T(8,128)(2,1)S(1)}, bf16[128,2048]{1,0:T(8,128)(2,1)S(1)}, u32[]{:S(2)}, u32[]{:S(2)}) %collective-permute-start.44) | collective-permute-done | bytes 524320 | tf_op jit(solution)/shard_map/ppermute | solution.py:477
  526.3 5.3 convert_add_fusion
  551.0 8.5 %collective-permute-done.53 = f32[13312]{0:T(1024)S(1)} collective-permute-done((f32[13312]{0:T(1024)S(1)}, f32[13312]{0:T(1024)S(1)}, u32[]{:S(2)}, u32[]{:S(2)}) %collective-permute-start.53) | collective-permute-done | bytes 53280 | tf_op jit(solution)/shard_map/ppermute | solution.py:477
  567.4 5.2 shard_map.219
  579.1 4.1 shard_map.218
  (319 shorter events, 169.2 us)
Async XLA Ops:
  10.7 43.1 %collective-permute-start.2 = (bf16[256,2048]{1,0:T(8,128)(2,1)}, bf16[256,2048]{1,0:T(8,128)(2,1)}, u32[]{:S(2)}, u32[]{:S(2)}) collective-permute-start(bf16[256,2048]{1,0:T(8,128)(2,1)} %get-tuple-element.164), channel_id=1, source_target_pairs={{0,8},{2,10},{4,12},{6,14},{8,0},{10,2},{12,4},{14,6},{16,24},{18,... | collective-permute-start | bytes 3145736 | tf_op jit(solution)/shard_map/ppermute | solution.py:477
  58.4 64.7 %collective-permute-start.8 = (bf16[512,2048]{1,0:T(8,128)(2,1)}, bf16[512,2048]{1,0:T(8,128)(2,1)}, u32[]{:S(2)}, u32[]{:S(2)}) collective-permute-start(bf16[512,2048]{1,0:T(8,128)(2,1)} %constant_dynamic-update-slice_fusion.pair_ref), channel_id=1, source_target_pairs={{0,2},{2,0},{4,6},{6,4},{8,10},{10,8},{12,14},{14,12},{16,18},{18,... | collective-permute-start | bytes 6291464 | tf_op jit(solution)/shard_map/ppermute | solution.py:477
  59.9 63.4 %collective-permute-start.9 = (bf16[512,2048]{1,0:T(8,128)(2,1)}, bf16[512,2048]{1,0:T(8,128)(2,1)}, u32[]{:S(2)}, u32[]{:S(2)}) collective-permute-start(bf16[512,2048]{1,0:T(8,128)(2,1)} %constant_dynamic-update-slice_fusion.pair_ref), channel_id=1, source_target_pairs={{0,1},{1,0},{2,3},{3,2},{4,5},{5,4},{6,7},{7,6},{8,9},{9,8},{10,11... | collective-permute-start | bytes 6291464 | tf_op jit(solution)/shard_map/ppermute | solution.py:480
  62.0 60.1 %collective-permute-start.6 = (bf16[512,1024]{1,0:T(8,128)(2,1)S(1)}, bf16[512,1024]{1,0:T(8,128)(2,1)}, u32[]{:S(2)}, u32[]{:S(2)}) collective-permute-start(bf16[512,1024]{1,0:T(8,128)(2,1)S(1)} %maximum_select_fusion.1.refs_0_), channel_id=1, source_target_pairs={{0,16},{2,18},{4,20},{6,22},{8,24},{10,26},{12,28},{14,30},{16,0},... | collective-permute-start | bytes 3145736 | tf_op jit(solution)/shard_map/ppermute | solution.py:477
  64.7 57.5 %collective-permute-start.7 = (bf16[512,1024]{1,0:T(8,128)(2,1)S(1)}, bf16[512,1024]{1,0:T(8,128)(2,1)S(1)}, u32[]{:S(2)}, u32[]{:S(2)}) collective-permute-start(bf16[512,1024]{1,0:T(8,128)(2,1)S(1)} %maximum_select_fusion.1.refs_0_), channel_id=1, source_target_pairs={{0,4},{2,6},{4,0},{6,2},{8,12},{10,14},{12,8},{14,10},{16,20},{18,... | collective-permute-start | bytes 3145736 | tf_op jit(solution)/shard_map/ppermute | solution.py:477
  66.2 37.9 %collective-permute-start.11 = (s32[2,512]{1,0:T(2,128)S(1)}, s32[2,512]{1,0:T(2,128)S(1)}, u32[]{:S(2)}, u32[]{:S(2)}) collective-permute-start(s32[2,512]{1,0:T(2,128)S(1)} %pad_add_fusion.2), channel_id=1, source_target_pairs={{0,2},{2,0},{4,6},{6,4},{8,10},{10,8},{12,14},{14,12},{16,18},{18,... | collective-permute-start | bytes 12296 | tf_op jit(solution)/shard_map/ppermute | solution.py:477
  123.5 56.4 %collective-permute-start.17 = (bf16[512,2048]{1,0:T(8,128)(2,1)}, bf16[512,2048]{1,0:T(8,128)(2,1)}, u32[]{:S(2)}, u32[]{:S(2)}) collective-permute-start(bf16[512,2048]{1,0:T(8,128)(2,1)} %collective-permute-done.8.second_ref), channel_id=1, source_target_pairs={{0,1},{1,0},{2,3},{3,2},{4,5},{5,4},{6,7},{7,6},{8,9},{9,8},{10,11... | collective-permute-start | bytes 6291464 | tf_op jit(solution)/shard_map/ppermute | solution.py:480
  129.0 49.6 %collective-permute-start.13 = (bf16[512,1024]{1,0:T(8,128)(2,1)}, bf16[512,1024]{1,0:T(8,128)(2,1)}, u32[]{:S(2)}, u32[]{:S(2)}) collective-permute-start(bf16[512,1024]{1,0:T(8,128)(2,1)} %maximum_select_fusion.4.refs_0_.refs_4_), channel_id=1, source_target_pairs={{0,16},{2,18},{4,20},{6,22},{8,24},{10,26},{12,28},{14,30},{16,0},... | collective-permute-start | bytes 3145736 | tf_op jit(solution)/shard_map/ppermute | solution.py:477
  132.1 46.5 %collective-permute-start.14 = (bf16[512,1024]{1,0:T(8,128)(2,1)}, bf16[512,1024]{1,0:T(8,128)(2,1)}, u32[]{:S(2)}, u32[]{:S(2)}) collective-permute-start(bf16[512,1024]{1,0:T(8,128)(2,1)} %maximum_select_fusion.4.refs_0_.refs_4_), channel_id=1, source_target_pairs={{0,4},{2,6},{4,0},{6,2},{8,12},{10,14},{12,8},{14,10},{16,20},{18,... | collective-permute-start | bytes 3145736 | tf_op jit(solution)/shard_map/ppermute | solution.py:477
  133.7 46.2 %collective-permute-start.12 = (bf16[512,1024]{1,0:T(8,128)(2,1)}, bf16[512,1024]{1,0:T(8,128)(2,1)}, u32[]{:S(2)}, u32[]{:S(2)}) collective-permute-start(bf16[512,1024]{1,0:T(8,128)(2,1)} %collective-permute-done.6.refs_1_), channel_id=1, source_target_pairs={{0,4},{2,6},{4,0},{6,2},{8,12},{10,14},{12,8},{14,10},{16,20},{18,... | collective-permute-start | bytes 3145736 | tf_op jit(solution)/shard_map/ppermute | solution.py:477
  183.9 52.4 %collective-permute-start.21 = (bf16[512,2048]{1,0:T(8,128)(2,1)}, bf16[512,2048]{1,0:T(8,128)(2,1)}, u32[]{:S(2)}, u32[]{:S(2)}) collective-permute-start(bf16[512,2048]{1,0:T(8,128)(2,1)} %constant_dynamic-update-slice_fusion.2.pair_ref), channel_id=1, source_target_pairs={{0,2},{1,9},{2,0},{3,11},{4,6},{5,13},{6,4},{7,15},{8,10},{9,1},{1... | collective-permute-start | bytes 6291464 | tf_op jit(solution)/shard_map/ppermute | solution.py:484
  184.4 51.9 %collective-permute-start.22 = (bf16[512,2048]{1,0:T(8,128)(2,1)}, bf16[512,2048]{1,0:T(8,128)(2,1)}, u32[]{:S(2)}, u32[]{:S(2)}) collective-permute-start(bf16[512,2048]{1,0:T(8,128)(2,1)} %constant_dynamic-update-slice_fusion.2.pair_ref), channel_id=1, source_target_pairs={{0,1},{1,0},{2,3},{3,2},{4,5},{5,4},{6,7},{7,6},{8,9},{9,8},{10,11... | collective-permute-start | bytes 6291464 | tf_op jit(solution)/shard_map/ppermute | solution.py:480
  187.0 49.3 %collective-permute-start.18 = (bf16[512,1024]{1,0:T(8,128)(2,1)}, bf16[512,1024]{1,0:T(8,128)(2,1)}, u32[]{:S(2)}, u32[]{:S(2)}) collective-permute-start(bf16[512,1024]{1,0:T(8,128)(2,1)} %maximum_select_fusion.5.refs_0_), channel_id=1, source_target_pairs={{0,16},{2,18},{4,20},{6,22},{8,24},{10,26},{12,28},{14,30},{16,0},... | collective-permute-start | bytes 3145736 | tf_op jit(solution)/shard_map/ppermute | solution.py:477
  187.4 48.8 %collective-permute-start.19 = (bf16[512,1024]{1,0:T(8,128)(2,1)}, bf16[512,1024]{1,0:T(8,128)(2,1)}, u32[]{:S(2)}, u32[]{:S(2)}) collective-permute-start(bf16[512,1024]{1,0:T(8,128)(2,1)} %maximum_select_fusion.5.refs_0_), channel_id=1, source_target_pairs={{0,4},{2,6},{4,0},{6,2},{8,12},{10,14},{12,8},{14,10},{16,20},{18,... | collective-permute-start | bytes 3145736 | tf_op jit(solution)/shard_map/ppermute | solution.py:477
  188.9 47.3 %collective-permute-start.20 = (bf16[512,1024]{1,0:T(8,128)(2,1)}, bf16[512,1024]{1,0:T(8,128)(2,1)S(1)}, u32[]{:S(2)}, u32[]{:S(2)}) collective-permute-start(bf16[512,1024]{1,0:T(8,128)(2,1)} %collective-permute-done.13.refs_1_.refs_5_), channel_id=1, source_target_pairs={{0,4},{2,6},{4,0},{6,2},{8,12},{10,14},{12,8},{14,10},{16,20},{18,... | collective-permute-start | bytes 3145736 | tf_op jit(solution)/shard_map/ppermute | solution.py:477
  236.3 30.0 %collective-permute-start.23 = (bf16[512,1024]{1,0:T(8,128)(2,1)}, bf16[512,1024]{1,0:T(8,128)(2,1)}, u32[]{:S(2)}, u32[]{:S(2)}) collective-permute-start(bf16[512,1024]{1,0:T(8,128)(2,1)} %collective-permute-done.18.refs_1_), channel_id=1, source_target_pairs={{0,4},{2,6},{4,0},{6,2},{8,12},{10,14},{12,8},{14,10},{16,20},{18,... | collective-permute-start | bytes 3145736 | tf_op jit(solution)/shard_map/ppermute | solution.py:477
  266.4 37.2 %collective-permute-start.25 = (bf16[512,1024]{1,0:T(8,128)(2,1)}, bf16[512,1024]{1,0:T(8,128)(2,1)S(1)}, u32[]{:S(2)}, u32[]{:S(2)}) collective-permute-start(bf16[512,1024]{1,0:T(8,128)(2,1)} %get-tuple-element.198), channel_id=1, source_target_pairs={{0,4},{2,6},{4,0},{6,2},{8,12},{10,14},{12,8},{14,10},{16,20},{18,... | collective-permute-start | bytes 3145736 | tf_op jit(solution)/shard_map/ppermute | solution.py:477
  330.2 30.4 %collective-permute-start.29 = (bf16[512,1024]{1,0:T(8,128)(2,1)}, bf16[512,1024]{1,0:T(8,128)(2,1)}, u32[]{:S(2)}, u32[]{:S(2)}) collective-permute-start(bf16[512,1024]{1,0:T(8,128)(2,1)} %get-tuple-element.228), channel_id=1, source_target_pairs={{0,4},{2,6},{4,0},{6,2},{8,12},{10,14},{12,8},{14,10},{16,20},{18,... | collective-permute-start | bytes 3145736 | tf_op jit(solution)/shard_map/ppermute | solution.py:477
  360.6 35.2 %collective-permute-start.33 = (bf16[1024,2048]{1,0:T(8,128)(2,1)}, bf16[1024,2048]{1,0:T(8,128)(2,1)}, u32[]{:S(2)}, u32[]{:S(2)}) collective-permute-start(bf16[1024,2048]{1,0:T(8,128)(2,1)} %shard_map.211), channel_id=1, source_target_pairs={{0,1},{1,0},{2,3},{3,2},{4,5},{5,4},{6,7},{7,6},{8,9},{9,8},{10,11... | collective-permute-start | bytes 12582920 | tf_op jit(solution)/shard_map/ppermute | solution.py:480
  360.6 35.1 %collective-permute-start.32 = (bf16[512,1024]{1,0:T(8,128)(2,1)}, bf16[512,1024]{1,0:T(8,128)(2,1)S(1)}, u32[]{:S(2)}, u32[]{:S(2)}) collective-permute-start(bf16[512,1024]{1,0:T(8,128)(2,1)} %get-tuple-element.240), channel_id=1, source_target_pairs={{0,4},{2,6},{4,0},{6,2},{8,12},{10,14},{12,8},{14,10},{16,20},{18,... | collective-permute-start | bytes 3145736 | tf_op jit(solution)/shard_map/ppermute | solution.py:477
  363.9 31.9 %collective-permute-start.31 = (bf16[256,1024]{1,0:T(8,128)(2,1)S(1)}, bf16[256,1024]{1,0:T(8,128)(2,1)}, u32[]{:S(2)}, u32[]{:S(2)}) collective-permute-start(bf16[256,1024]{1,0:T(8,128)(2,1)S(1)} %get-tuple-element.381), channel_id=1, source_target_pairs={{0,16},{2,18},{4,20},{6,22},{8,24},{10,26},{12,28},{14,30},{16,0},... | collective-permute-start | bytes 1572872 | tf_op jit(solution)/shard_map/ppermute | solution.py:477
  400.0 37.5 %collective-permute-start.37 = (bf16[512,2048]{1,0:T(8,128)(2,1)}, bf16[512,2048]{1,0:T(8,128)(2,1)}, u32[]{:S(2)}, u32[]{:S(2)}) collective-permute-start(bf16[512,2048]{1,0:T(8,128)(2,1)} %add_convert_fusion.1), channel_id=1, source_target_pairs={{0,2},{1,9},{2,0},{3,11},{4,6},{5,13},{6,4},{7,15},{8,10},{9,1},{1... | collective-permute-start | bytes 6291464 | tf_op jit(solution)/shard_map/ppermute | solution.py:484
  401.5 36.0 %collective-permute-start.35 = (bf16[512,1024]{1,0:T(8,128)(2,1)}, bf16[512,1024]{1,0:T(8,128)(2,1)}, u32[]{:S(2)}, u32[]{:S(2)}) collective-permute-start(bf16[512,1024]{1,0:T(8,128)(2,1)} %get-tuple-element.248), channel_id=1, source_target_pairs={{0,4},{2,6},{4,0},{6,2},{8,12},{10,14},{12,8},{14,10},{16,20},{18,... | collective-permute-start | bytes 3145736 | tf_op jit(solution)/shard_map/ppermute | solution.py:477
  404.0 33.5 %collective-permute-start.36 = (bf16[128,2048]{1,0:T(8,128)(2,1)S(1)}, bf16[128,2048]{1,0:T(8,128)(2,1)S(1)}, u32[]{:S(2)}, u32[]{:S(2)}) collective-permute-start(bf16[128,2048]{1,0:T(8,128)(2,1)S(1)} %get-tuple-element.392), channel_id=1, source_target_pairs={{0,2},{2,0},{4,6},{6,4},{8,10},{10,8},{12,14},{14,12},{16,18},{18,... | collective-permute-start | bytes 1572872 | tf_op jit(solution)/shard_map/ppermute | solution.py:477
  404.6 32.9 %collective-permute-start.34 = (bf16[256,1024]{1,0:T(8,128)(2,1)S(1)}, bf16[256,1024]{1,0:T(8,128)(2,1)S(1)}, u32[]{:S(2)}, u32[]{:S(2)}) collective-permute-start(bf16[256,1024]{1,0:T(8,128)(2,1)S(1)} %copy-done.39), channel_id=1, source_target_pairs={{0,16},{2,18},{4,20},{6,22},{8,24},{10,26},{12,28},{14,30},{16,0},... | collective-permute-start | bytes 1572872 | tf_op jit(solution)/shard_map/ppermute | solution.py:477
  438.3 42.1 %collective-permute-start.42 = (bf16[1024,2048]{1,0:T(8,128)(2,1)}, bf16[1024,2048]{1,0:T(8,128)(2,1)}, u32[]{:S(2)}, u32[]{:S(2)}) collective-permute-start(bf16[1024,2048]{1,0:T(8,128)(2,1)} %shard_map.214), channel_id=1, source_target_pairs={{0,1},{1,0},{2,3},{3,2},{4,5},{5,4},{6,7},{7,6},{8,9},{9,8},{10,11... | collective-permute-start | bytes 12582920 | tf_op jit(solution)/shard_map/ppermute | solution.py:480
  442.9 37.5 %collective-permute-start.41 = (bf16[256,2048]{1,0:T(8,128)(2,1)}, bf16[256,2048]{1,0:T(8,128)(2,1)S(1)}, u32[]{:S(2)}, u32[]{:S(2)}) collective-permute-start(bf16[256,2048]{1,0:T(8,128)(2,1)} %get-tuple-element.377), channel_id=1, source_target_pairs={{0,8},{1,3},{2,10},{3,1},{4,12},{5,7},{6,14},{7,5},{8,0},{9,11},{1... | collective-permute-start | bytes 3145736 | tf_op jit(solution)/shard_map/ppermute | solution.py:484
  444.9 35.5 %collective-permute-start.39 = (bf16[512,1024]{1,0:T(8,128)(2,1)}, bf16[512,1024]{1,0:T(8,128)(2,1)S(1)}, u32[]{:S(2)}, u32[]{:S(2)}) collective-permute-start(bf16[512,1024]{1,0:T(8,128)(2,1)} %get-tuple-element.261), channel_id=1, source_target_pairs={{0,4},{2,6},{4,0},{6,2},{8,12},{10,14},{12,8},{14,10},{16,20},{18,... | collective-permute-start | bytes 3145736 | tf_op jit(solution)/shard_map/ppermute | solution.py:477
  447.9 32.5 %collective-permute-start.40 = (bf16[256,1024]{1,0:T(8,128)(2,1)S(1)}, bf16[256,1024]{1,0:T(8,128)(2,1)S(1)}, u32[]{:S(2)}, u32[]{:S(2)}) collective-permute-start(bf16[256,1024]{1,0:T(8,128)(2,1)S(1)} %get-tuple-element.390), channel_id=1, source_target_pairs={{0,8},{2,10},{4,12},{6,14},{8,0},{10,2},{12,4},{14,6},{16,24},{18,... | collective-permute-start | bytes 1572872 | tf_op jit(solution)/shard_map/ppermute | solution.py:477
  484.2 41.3 %collective-permute-start.46 = (f32[256,2048]{1,0:T(8,128)}, f32[256,2048]{1,0:T(8,128)}, u32[]{:S(2)}, u32[]{:S(2)}) collective-permute-start(f32[256,2048]{1,0:T(8,128)} %get-tuple-element.288.own_ref), channel_id=1, source_target_pairs={{0,1},{1,0},{2,3},{3,2},{4,5},{5,4},{6,7},{7,6},{8,9},{9,8},{10,11... | collective-permute-start | bytes 6291464 | tf_op jit(solution)/shard_map/ppermute | solution.py:480
  488.1 37.5 %collective-permute-start.45 = (bf16[512,2048]{1,0:T(8,128)(2,1)}, bf16[512,2048]{1,0:T(8,128)(2,1)}, u32[]{:S(2)}, u32[]{:S(2)}) collective-permute-start(bf16[512,2048]{1,0:T(8,128)(2,1)} %add_convert_fusion), channel_id=1, source_target_pairs={{0,2},{1,9},{2,0},{3,11},{4,6},{5,13},{6,4},{7,15},{8,10},{9,1},{1... | collective-permute-start | bytes 6291464 | tf_op jit(solution)/shard_map/ppermute | solution.py:484
  496.5 29.1 %collective-permute-start.44 = (bf16[128,2048]{1,0:T(8,128)(2,1)S(1)}, bf16[128,2048]{1,0:T(8,128)(2,1)S(1)}, u32[]{:S(2)}, u32[]{:S(2)}) collective-permute-start(bf16[128,2048]{1,0:T(8,128)(2,1)S(1)} %get-tuple-element.388), channel_id=1, source_target_pairs={{0,2},{2,0},{4,6},{6,4},{8,10},{10,8},{12,14},{14,12},{16,18},{18,... | collective-permute-start | bytes 1572872 | tf_op jit(solution)/shard_map/ppermute | solution.py:477
  (75 other events, 892.1 us)

commit v5 on v4

--- a/solution.py
+++ b/solution.py
@@ -55,6 +55,91 @@
         total = term if total is None else total + term
         low = high
     return total
+
+
+def sum_kernel(*refs):
+    total = refs[0][...].astype(F32)
+    for ref in refs[1:-1]:
+        total = total + ref[...].astype(F32)
+    refs[-1][...] = total.astype(BF)
+
+
+def sum_rows(rows, *terms, tile=128):
+    width = terms[0][0].shape[1]
+    tile = min(tile, rows)
+
+    def spec(start):
+        return pl.BlockSpec((tile, width), lambda i: (start // tile + i, 0))
+
+    return call(
+        sum_kernel,
+        jax.ShapeDtypeStruct((rows, width), BF),
+        (rows // tile,),
+        [spec(start) for _, start in terms],
+        spec(0),
+        *[value for value, _ in terms],
+    )
+
+
+def split_kernel(flag_ref, kept_ref, got_ref, one_ref, two_ref, send_ref, own_ref):
+    sending = pl.program_id(0) == 0
+    upper = (flag_ref[0] == 1) != sending
+    total = kept_ref[...].astype(F32) + got_ref[...].astype(F32)
+    total = total + jnp.where(upper, two_ref[...], one_ref[...]).astype(F32)
+
+    @pl.when(sending)
+    def _():
+        send_ref[...] = total.astype(BF)
+
+    @pl.when(jnp.logical_not(sending))
+    def _():
+        own_ref[...] = total.astype(BF)
+
+
+def split_sum(flag, kept, got, one, two):
+    rows, cols = one.shape
+    out = jax.ShapeDtypeStruct((rows, cols), BF)
+    picked = pl.BlockSpec((rows, cols), lambda i, f: (jnp.where(i == 0, 1 - f[0], f[0]), 0))
+    return call(
+        split_kernel,
+        [out, out],
+        (2,),
+        [picked, picked, resident(one), resident(two)],
+        [pl.BlockSpec((rows, cols), lambda i, f: (0, 0))] * 2,
+        flag.reshape(1).astype(jnp.int32),
+        kept,
+        got,
+        one,
+        two,
+        prefetch=1,
+    )
+
+
+def cross_kernel(flags_ref, own_ref, got_ref, send_ref, kept_ref):
+    cols = own_ref.shape[1]
+    for n, out_ref in enumerate((send_ref, kept_ref)):
+
+        @pl.when(pl.program_id(0) == n)
+        def _(out_ref=out_ref):
+            for ref, place in ((own_ref, flags_ref[0]), (got_ref, 1 - flags_ref[0])):
+                out_ref[:, pl.ds(pl.multiple_of(place * cols, cols), cols)] = ref[...]
+
+
+def cross(zl, x, own, got):
+    rows, cols = own.shape[0] // 2, own.shape[1]
+    out = jax.ShapeDtypeStruct((rows, 2 * cols), BF)
+    picked = pl.BlockSpec((rows, cols), lambda i, f: (jnp.where(i == 0, 1 - f[1], f[1]), 0))
+    return call(
+        cross_kernel,
+        [out, out],
+        (2,),
+        [picked, picked],
+        [pl.BlockSpec((rows, 2 * cols), lambda i, f: (0, 0))] * 2,
+        jnp.stack([zl, x]).astype(jnp.int32),
+        own,
+        got,
+        prefetch=1,
+    )
 
 
 def join_kernel(flags_ref, pair_ref, second_ref, got_pair_ref, got_second_ref, out_ref):
@@ -110,11 +195,12 @@
         out_ref[...] = other_ref[...]
 
 
-def place_halves(core, own, other, steps=2):
-    tile, width = own.shape[0] // steps, own.shape[1]
+def place_halves(core, own, other, steps=2, rows=None):
+    rows, width = rows or own.shape[0], own.shape[1]
+    tile = rows // steps
     return call(
         place_kernel,
-        jax.ShapeDtypeStruct((2 * own.shape[0], width), own.dtype),
+        jax.ShapeDtypeStruct((2 * rows, width), own.dtype),
         (2 * steps,),
         [
             pl.BlockSpec((tile, width), lambda i, c: (jnp.minimum(i, steps - 1), 0)),
@@ -204,18 +290,19 @@
                 low = low + value.shape[1]
 
 
-def weight_grads(unit, *pairs):
+def weight_grads(unit, parts, *pairs):
     width = pairs[0][0].shape[1]
     cols = sum(right.shape[1] for _, right in pairs)
-    steps = width // unit
-    rest = steps // 2 - 1
-    sizes = [size for size in (rest, 1, rest, 1) if size]
+    tops = width // unit // 2
+    every = ((tops + 1, tops - 1), (tops, 1), (1, tops - 1), (0, 1))
+    sizes = [every[part][1] for part in parts]
     starts = [sum(sizes[:n]) for n in range(len(sizes) + 1)]
 
     def left_block(i):
-        lower = i <= rest
-        place = jnp.where(lower, i, i - rest - 1)
-        return 0, jnp.where(place == rest, 0, place + 1) + jnp.where(lower, rest + 1, 0)
+        place = i
+        for n, part in enumerate(parts):
+            place = jnp.where(i >= starts[n], i - starts[n] + every[part][0], place)
+        return 0, place
 
     in_specs, operands = [], []
     for left, right in pairs:
@@ -226,53 +313,67 @@
     def out_block(n):
         return lambda i: (jnp.clip(i - starts[n], 0, sizes[n] - 1), 0)
 
-    outs = call(
+    return call(
         functools.partial(weight_grad_kernel, len(pairs), starts),
         [jax.ShapeDtypeStruct((size * unit, cols), BF) for size in sizes],
-        (steps,),
+        (starts[-1],),
         in_specs,
         [pl.BlockSpec((unit, cols), out_block(n)) for n in range(len(sizes))],
         *operands,
     )
-    return outs if rest else [None, outs[0], None, outs[1]]
-
-
-def pair_kernel(pieces, cut, _, a_ref, c_ref, *refs):
-    out_ref = refs[-1]
+
+
+def pair_kernel(pieces, adding, _, a_ref, c_ref, *refs):
     a, c = a_ref[...], c_ref[...]
-    low = 0
-    for b_ref, d_ref in zip(refs[:pieces], refs[pieces : 2 * pieces]):
-        high = low + b_ref.shape[0]
-        total = dot_nt(a, b_ref[...]) + dot_nt(c, d_ref[:, cut : cut + c.shape[1]])
-        out_ref[:, low:high] = total.astype(BF)
-        low = high
-
-
-def pair_dot(part, crossed, a, b, c, d, cut):
+    outs = refs[2 * pieces + adding :]
+
+    def into(out_ref):
+        low = 0
+        for b_ref, d_ref in zip(refs[:pieces], refs[pieces : 2 * pieces]):
+            high = low + b_ref.shape[0]
+            total = dot_nt(a, b_ref[...]) + dot_nt(c, d_ref[...])
+            if adding:
+                total = total + refs[2 * pieces][:, low:high].astype(F32)
+            out_ref[:, low:high] = total.astype(BF)
+            low = high
+
+    steps = 4 // len(outs)
+    for n, out_ref in enumerate(outs):
+        pl.when(pl.program_id(0) // steps == n)(functools.partial(into, out_ref))
+
+
+def pair_dot(part, crossed, a, b, c, d, cut, got=None):
     rows, width = a.shape[0] // 2, sum(piece.shape[0] for piece in b)
     tile = rows // 4
-
-    def out_block(i, f):
-        return jnp.where((f[0] == 1) & (i > 0) & (i < 3), 3 - i, i), 0
-
-    return call(
-        functools.partial(pair_kernel, len(b), cut),
-        jax.ShapeDtypeStruct((rows, width), BF),
+    adding = got is not None
+
+    def row_block(i, f):
+        return part * 4 + jnp.where((f[0] == 1) & (i > 0) & (i < 3), 3 - i, i), 0
+
+    count = 2 if adding else 1
+    steps = 4 // count
+
+    def out_block(n):
+        return lambda i, f: (jnp.clip(i - n * steps, 0, steps - 1), 0)
+
+    outs = call(
+        functools.partial(pair_kernel, len(b), int(adding)),
+        [jax.ShapeDtypeStruct((rows // count, width), BF)] * count,
         (4,),
-        [
-            pl.BlockSpec((tile, a.shape[1]), lambda i, f: (part * 4 + i, 0)),
-            pl.BlockSpec((tile, c.shape[1]), lambda i, f: (part * 4 + i, 0)),
-        ]
+        [pl.BlockSpec((tile, a.shape[1]), row_block), pl.BlockSpec((tile, c.shape[1]), row_block)]
         + [resident(w) for w in b]
-        + [resident(w) for w in d],
-        pl.BlockSpec((tile, width), out_block),
+        + [pl.BlockSpec((w.shape[0], c.shape[1]), lambda i, f: (0, cut // c.shape[1])) for w in d]
+        + [pl.BlockSpec((tile, width), lambda i, f: (i, 0))] * int(adding),
+        [pl.BlockSpec((tile, width), out_block(n)) for n in range(count)],
         crossed.reshape(1).astype(jnp.int32),
         a,
         c,
         *b,
         *d,
+        *([got] if adding else []),
         prefetch=1,
     )
+    return outs if adding else outs[0]
 
 
 def attention_kernel(
@@ -412,69 +513,80 @@
         mixed_ref[:, target] = cot_ref[:, n * cols : (n + 1) * cols]
 
 
-def natural(table_ref, kept_ref, got_ref, cols):
+def natural(table_ref, refs, cols):
     parts = []
-    for n in range(kept_ref.shape[1] // cols):
+    for n in range(refs[0].shape[1] // cols):
         source = pl.ds(pl.multiple_of(table_ref[n], cols), cols)
-        parts.append(kept_ref[:, source].astype(F32) + got_ref[:, source].astype(F32))
+        total = refs[0][:, source].astype(F32)
+        for ref in refs[1:]:
+            total = total + ref[:, source].astype(F32)
+        parts.append(total)
     return jnp.concatenate(parts, axis=1)
 
 
-def norm_back_kernel(
-    table_ref, tok_ref, cot_ref, gain_ref, kept_ref, got_ref, grad_ref, lines_ref, *, cols
-):
-    normal_x, inv_std = standardize(tok_ref[...].astype(F32))
-    cot = cot_ref[...].astype(F32)
-    normed_grad = natural(table_ref, kept_ref, got_ref, cols)
-    grad_ref[...] = input_gradient(
-        normed_grad, cot, normal_x, inv_std, gain_ref[...].astype(F32)
-    )
-
-    @pl.when(pl.program_id(0) == 0)
+def norm_back_kernel(table_ref, tok_ref, cot_ref, gain_ref, *refs, cols):
+    pieces, (grad_ref, lines_ref) = refs[:-2], refs[-2:]
+    i, last_tile = pl.program_id(0), pl.num_programs(0) - 1
+
+    @pl.when(i == 0)
     def _():
         lines_ref[...] = jnp.zeros_like(lines_ref)
 
-    for row, value in enumerate((normed_grad * normal_x, normed_grad, cot)):
-        lines_ref[row : row + 1, :] += jnp.sum(value, axis=0, keepdims=True)
-
-
-def result_kernel(table_ref, tok_ref, bias_ref, kept_ref, got_ref, out_ref, *, cols):
-    branches = natural(table_ref, kept_ref, got_ref, cols)
+    @pl.when(i == last_tile)
+    def _():
+        grad_ref[...] = jnp.zeros_like(grad_ref)
+        grad_ref[0:8, :] = lines_ref[...]
+
+    @pl.when(i < last_tile)
+    def _():
+        normal_x, inv_std = standardize(tok_ref[...].astype(F32))
+        cot = cot_ref[...].astype(F32)
+        normed_grad = natural(table_ref, pieces, cols)
+        grad_ref[...] = input_gradient(
+            normed_grad, cot, normal_x, inv_std, gain_ref[...].astype(F32)
+        )
+        for row, value in enumerate((normed_grad * normal_x, normed_grad, cot)):
+            lines_ref[row : row + 1, :] += jnp.sum(value, axis=0, keepdims=True)
+
+
+def result_kernel(table_ref, tok_ref, bias_ref, *refs, cols):
+    pieces, out_ref = refs[:-1], refs[-1]
+    branches = natural(table_ref, pieces, cols)
     out_ref[...] = (tok_ref[...].astype(F32) + branches + bias_ref[...].astype(F32)).astype(BF)
 
 
-def on_half(kernel, table, cols, whole, lines, mine, outs, tile=64):
+def on_half(kernel, table, cols, whole, lines, mine, outs, extra=0, scratch=(), tile=64):
     half, width = whole[0].shape[0] // 2, whole[0].shape[1]
     steps = half // tile
     last_entry = table.shape[0] - 1
-    block = pl.BlockSpec((tile, width), lambda i, t: (i, 0))
+
+    def row(i):
+        return jnp.minimum(i, steps - 1)
+
     return pl.pallas_call(
         functools.partial(kernel, cols=cols),
         out_shape=outs,
         grid_spec=pltpu.PrefetchScalarGridSpec(
             num_scalar_prefetch=1,
-            grid=(steps,),
-            in_specs=[pl.BlockSpec((tile, width), lambda i, t: (t[last_entry] * steps + i, 0))]
+            grid=(steps + extra,),
+            in_specs=[pl.BlockSpec((tile, width), lambda i, t: (t[last_entry] * steps + row(i), 0))]
             * len(whole)
             + [pl.BlockSpec((1, width), lambda i, t: (0, 0))] * len(lines)
-            + [block] * len(mine),
-            out_specs=[
-                block if out.shape[0] == half else pl.BlockSpec(out.shape, lambda i, t: (0, 0))
-                for out in outs
-            ],
+            + [pl.BlockSpec((tile, width), lambda i, t: (row(i), 0))] * len(mine),
+            out_specs=[pl.BlockSpec((tile, width), lambda i, t: (i, 0))] * len(outs),
+            scratch_shapes=list(scratch),
         ),
         compiler_params=pltpu.CompilerParams(vmem_limit_bytes=32 * 1024 * 1024),
-        cost_estimate=pl.CostEstimate(
-            flops=1000, bytes_accessed=1000, transcendentals=0
-        ),
+        cost_estimate=pl.CostEstimate(flops=1000, bytes_accessed=1000, transcendentals=0),
     )(table, *whole, *[line.reshape(1, width) for line in lines], *mine)
 
 
 def local_part(dp_size):
     top_bits = [b for b in range(3, dp_size.bit_length() - 1)]
 
-    def swap(value, bit):
-        return lax.ppermute(value, "dp", [(i, i ^ (1 << bit)) for i in range(dp_size)])
+    def swap(value, *bits):
+        flip = sum(1 << bit for bit in bits)
+        return lax.ppermute(value, "dp", [(i, i ^ flip) for i in range(dp_size)])
 
     def swap_core(value):
         return lax.ppermute(value, "tensor", [(0, 1), (1, 0)])
@@ -566,7 +678,7 @@
             normed = normal_x * ln_gain.astype(F32) + ln_shift.astype(F32)
             return to_mixed(normed.astype(BF)), to_mixed(my_rows(cotangent))
 
-        def norm_backward(kept, got):
+        def norm_backward(*pieces):
             if aligned:
                 return on_half(
                     norm_back_kernel,
@@ -574,22 +686,19 @@
                     cols,
                     [tokens, cotangent],
                     [ln_gain],
-                    [kept, got],
-                    [
-                        jax.ShapeDtypeStruct((half, width), F32),
-                        jax.ShapeDtypeStruct((8, width), F32),
-                    ],
-                )
+                    list(pieces),
+                    [jax.ShapeDtypeStruct((half + 64, width), F32)],
+                    extra=1,
+                    scratch=[pltpu.VMEM((8, width), F32)],
+                )[0]
             normal_x, inv_std = standardize(my_rows(tokens).astype(F32))
             cot = my_rows(cotangent).astype(F32)
-            grad = from_mixed(add(kept, got))
-            lines = jnp.stack(
-                [jnp.sum(v, axis=0) for v in (grad * normal_x, grad, cot)]
-                + [jnp.zeros((width,), F32)] * 5
-            )
-            return input_gradient(grad, cot, normal_x, inv_std, ln_gain.astype(F32)), lines
-
-        def finish(kept, got):
+            grad = from_mixed(add(*[piece[:half] for piece in pieces]))
+            lines = [jnp.sum(v, axis=0, keepdims=True) for v in (grad * normal_x, grad, cot)]
+            result = input_gradient(grad, cot, normal_x, inv_std, ln_gain.astype(F32))
+            return jnp.concatenate([result] + lines + [jnp.zeros((61, width), F32)])
+
+        def finish(*pieces):
             if aligned:
                 return on_half(
                     result_kernel,
@@ -597,10 +706,10 @@
                     cols,
                     [tokens],
                     [branch_bias],
-                    [kept, got],
+                    list(pieces),
                     [jax.ShapeDtypeStruct((half, width), BF)],
                 )[0]
-            branches = from_mixed(add(kept, got))
+            branches = from_mixed(add(*[piece[:half] for piece in pieces]))
             return (my_rows(tokens).astype(F32) + branches + branch_bias.astype(F32)).astype(BF)
 
         def w_x(piece):
@@ -608,6 +717,9 @@
 
         def w_zl(w):
             return part_of(w, zl_mine, 1), swap(part_of(w, 1 - zl_mine, 1), ZL_BIT)
+
+        def w_place(pair):
+            return place_halves(zl_mine, *pair, steps=1)
 
         def w_top(w):
             rest = None
@@ -629,7 +741,7 @@
             if tops > 2:
                 return add(kept, got).astype(BF), None
             cut = kept.shape[0] // 2
-            return add(kept[:cut], got[:cut]).astype(BF), add(kept[cut:], got[cut:]).astype(BF)
+            return sum_rows(cut, (kept, 0), (got, 0)), sum_rows(cut, (kept, cut), (got, cut))
 
         def g_top(rest):
             if rest is None or tops == 2:
@@ -641,17 +753,20 @@
                 grad = add(grad[:cut], swap(grad[cut:], bit)).astype(BF)
             return grad
 
-        def g_own(kept, got, *tops_got):
-            tops_got = [value for value in tops_got if value is not None]
-            if len(tops_got) > 1:
-                tops_got = [jnp.concatenate(tops_got)]
-            return add(kept, got, *tops_got).astype(BF)
-
-        def g_zl(grad):
-            return part_of(grad, zl_mine, 0), swap(part_of(grad, 1 - zl_mine, 0), ZL_BIT)
-
-        def g_x(grad):
-            return part_of(grad, x_mine, 0), swap(part_of(grad, 1 - x_mine, 0), X_BIT)
+        def g_split(kept, got, one, two):
+            if two is not None:
+                return split_sum(zl_mine, kept, got, one, two)
+            total = add(kept, got, one[:unit]).astype(BF)
+            return part_of(total, 1 - zl_mine, 0), part_of(total, zl_mine, 0)
+
+        def g_zl(split):
+            return split[1], swap(split[0], ZL_BIT)
+
+        def g_cross(pair):
+            return cross(zl_mine, x_mine, *pair)
+
+        def g_x(split):
+            return split[1], swap(split[0], X_BIT)
 
         def g_swap_y(value):
             return None if value is None else swap(value, Y_BIT)
@@ -659,38 +774,42 @@
         straight = jnp.zeros((2,), jnp.int32)
         crossed = jnp.stack([core, 1 - core]).astype(jnp.int32)
 
+        def far_side(far):
+            return swap_mixed(far, (X_BIT, ZL_BIT))
+
+        def near_side(near, second):
+            return swap_mixed(sum_rows(half, (near, half), (second, half)), (ZL_BIT, X_BIT))
+
         u_x = w_x(up_weight)
         n_own, c_own = norm_forward()
-        seg = segments.reshape(1, rows)
-        u_x, c_own, qkv_weight, out_weight, down_weight = sync(
-            u_x, c_own, qkv_weight, out_weight, down_weight
-        )
-        uu = w_zl(ordered(x_mine, *u_x, 0))
+        seg = jnp.stack(
+            [segments, swap(segments, ZL_BIT), swap(segments, X_BIT), swap(segments, X_BIT, ZL_BIT)]
+        )
+        u_x, c_own, seg, qkv_weight, out_weight, down_weight = sync(
+            u_x, c_own, seg, qkv_weight, out_weight, down_weight
+        )
+        uu = w_place(w_zl(ordered(x_mine, *u_x, 0)))
         n_got = swap(n_own, ZL_BIT)
-        seg = jnp.concatenate([seg, swap(seg, ZL_BIT)])
         qkv_piece = qkv_weight.reshape(share, 3, 4, att).swapaxes(1, 2).reshape(share, 4, 3 * att)
         out_piece = out_weight.T.reshape(share, 4, att)
         a_x = w_x(jnp.concatenate([qkv_piece, out_piece], axis=2).reshape(share, 16 * att))
         d_x = w_x(down_weight.T)
         uu, n_own, n_got, a_x, d_x, c_own, seg = sync(uu, n_own, n_got, a_x, d_x, c_own, seg)
-        uu = ordered(zl_mine, *uu, 0)
         u_rest = w_top(uu)
         u_far = swap(uu, Y_BIT)
         n_pair = jnp.concatenate([n_own, n_got])
         n_second = swap(n_pair, X_BIT)
         n_got_pair = swap_core(n_pair)
-        aa = w_zl(ordered(x_mine, *a_x, 0))
-        seg = jnp.concatenate([seg, swap(seg, X_BIT)])
+        aa = w_place(w_zl(ordered(x_mine, *a_x, 0)))
         dd = ordered(x_mine, *d_x, 0)
         u_rest, u_far, n_second, n_got_pair, aa, dd, c_own, seg = sync(
             u_rest, u_far, n_second, n_got_pair, aa, dd, c_own, seg
         )
-        aa = ordered(zl_mine, *aa, 0)
         a_rest = w_top(aa)
         a_far = swap(aa, Y_BIT)
         u_far_rest = g_swap_y(u_rest)
         n_got_second = swap_core(n_second)
-        dd = w_zl(dd)
+        dd = w_place(w_zl(dd))
         c_got = swap_mixed(c_own, (ZL_BIT, X_BIT))
         order = jnp.broadcast_to(jnp.arange(rows, dtype=jnp.int32), (4, rows))
         begins = jnp.concatenate([jnp.ones((4, 1), bool), seg[:, 1:] != seg[:, :-1]], axis=1)
@@ -709,7 +828,6 @@
         u_far_rest, a_rest, a_far, dd, c_own, c_got, n_got_second, tables, line, column = sync(
             u_far_rest, a_rest, a_far, dd, c_own, c_got, n_got_second, tables, line, column
         )
-        dd = ordered(zl_mine, *dd, 0)
         d_rest = w_top(dd)
         d_far = swap(dd, Y_BIT)
         a_far_rest = g_swap_y(a_rest)
@@ -726,7 +844,7 @@
         d_far_rest = g_swap_y(d_rest)
         c_got_second = swap_core(c_second)
         cot = join(crossed, c_pair, c_second, c_got_pair, c_got_second)
-        gd = weight_grads(unit, (cot, act))
+        gd = weight_grads(unit, (0, 1, 2), (cot, act))
         d_far_rest, cot, gd = sync(d_far_rest, cot, gd)
         d_a = g_swap_y(gd[0])
         my_qkv_bias = lax.dynamic_slice_in_dim(qkv_bias, block * att, att, 1).astype(F32)
@@ -738,74 +856,81 @@
         d_z1, d_z2 = top_send(gd[2], d_a)
         d_z1 = g_top(d_z1)
         d_b = swap(gd[1], Y_BIT)
-        ga = weight_grads(unit, (normed, qkv_g), (cot, attended))
-        d_z1, d_z2, d_b, ga, cot, slope = sync(d_z1, d_z2, d_b, ga, cot, slope)
+        ga = weight_grads(unit, (0, 1, 2), (normed, qkv_g), (cot, attended))
+        down_w = [w for w in (dd, d_rest, d_far, d_far_rest) if w is not None]
+        b_send = pair_dot(1, 1 - core, act, down_w, attended, att_w, 3 * att)
+        d_z1, d_z2, d_b, ga, b_send, cot, slope, act, attended = sync(
+            d_z1, d_z2, d_b, ga, b_send, cot, slope, act, attended
+        )
         d_z2 = g_top(d_z2)
         a_a = g_swap_y(ga[0])
-        down_w = [w for w in (dd, d_rest, d_far, d_far_rest) if w is not None]
+        b_got = swap_core(b_send)
         up_g, up_sums = up_gradient(cot, slope, down_w)
         n_send = pair_dot(1, 1 - core, up_g, up_w, qkv_g, att_w, 0)
-        d_z2, a_a, ga, up_g, n_send = sync(d_z2, a_a, ga, up_g, n_send)
-        d_l = g_zl(g_own(gd[3], d_b, d_z1, d_z2))
+        b_near, b_far = pair_dot(0, core, act, down_w, attended, att_w, 3 * att, b_got)
+        d_z2, a_a, ga, b_near, b_far, up_g, n_send = sync(
+            d_z2, a_a, ga, b_near, b_far, up_g, n_send
+        )
         a_z1, a_z2 = top_send(ga[2], a_a)
         a_z1 = g_top(a_z1)
         a_b = swap(ga[1], Y_BIT)
         n_got = swap_core(n_send)
-        gu = weight_grads(unit, (normed, up_g))
-        n_kept = pair_dot(0, core, up_g, up_w, qkv_g, att_w, 0)
-        d_l, a_z1, a_z2, a_b, gu, n_got, n_kept, act, attended = sync(
-            d_l, a_z1, a_z2, a_b, gu, n_got, n_kept, act, attended
-        )
-        n_second = swap_mixed(add(n_kept[2 * half :], n_got[2 * half :]).astype(BF), (X_BIT, ZL_BIT))
+        b_second = far_side(b_far)
+        gu = weight_grads(unit, (0,), (normed, up_g))
+        n_near, n_far = pair_dot(0, core, up_g, up_w, qkv_g, att_w, 0, n_got)
+        a_z1, a_z2, a_b, gu, n_near, n_far, b_second = sync(
+            a_z1, a_z2, a_b, gu, n_near, n_far, b_second
+        )
         a_z2 = g_top(a_z2)
         u_a = g_swap_y(gu[0])
-        d_x = g_x(ordered(zl_mine, *d_l, 1))
-        b_send = pair_dot(1, 1 - core, act, down_w, attended, att_w, 3 * att)
-        a_z2, u_a, gu, d_x, n_second, b_send, act, attended = sync(
-            a_z2, u_a, gu, d_x, n_second, b_send, act, attended
-        )
-        n_first = add(n_kept[half : 2 * half], n_got[half : 2 * half], n_second[half:])
-        n_first = swap_mixed(n_first.astype(BF), (ZL_BIT, X_BIT))
-        u_z1, u_z2 = top_send(gu[2], u_a)
+        n_second = far_side(n_far)
+        gu = weight_grads(unit, (1, 2), (normed, up_g))
+        (gd_own,) = weight_grads(unit, (3,), (cot, act))
+        d_l = g_split(gd_own, d_b, d_z1, d_z2)
+        a_z2, u_a, gu, d_l, n_second, b_near, b_second, up_g, qkv_g, attended, normed, cot = sync(
+            a_z2, u_a, gu, d_l, n_second, b_near, b_second, up_g, qkv_g, attended, normed, cot
+        )
+        u_z1, u_z2 = top_send(gu[1], u_a)
         u_z1 = g_top(u_z1)
-        u_b = swap(gu[1], Y_BIT)
-        a_l = g_zl(g_own(ga[3], a_b, a_z1, a_z2))
-        b_got = swap_core(b_send)
-        b_kept = pair_dot(0, core, act, down_w, attended, att_w, 3 * att)
-        n_keep = add(n_kept[:half], n_got[:half], n_second[:half])
-        u_z1, u_z2, u_b, a_l, n_first, n_keep, b_got, b_kept = sync(
-            u_z1, u_z2, u_b, a_l, n_first, n_keep, b_got, b_kept
-        )
-        b_second = swap_mixed(add(b_kept[2 * half :], b_got[2 * half :]).astype(BF), (X_BIT, ZL_BIT))
+        u_b = swap(gu[0], Y_BIT)
+        n_first = near_side(n_near, n_second)
+        b_first = near_side(b_near, b_second)
+        d_l = g_zl(d_l)
+        (ga_own,) = weight_grads(unit, (3,), (normed, qkv_g), (cot, attended))
+        a_l = g_split(ga_own, a_b, a_z1, a_z2)
+        (gu_own,) = weight_grads(unit, (3,), (normed, up_g))
+        u_z1, u_z2, u_b, n_first, b_first, d_l, a_l, gu_own = sync(
+            u_z1, u_z2, u_b, n_first, b_first, d_l, a_l, gu_own
+        )
         u_z2 = g_top(u_z2)
-        a_x = g_x(ordered(zl_mine, *a_l, 1))
-        input_grad, lines = norm_backward(n_keep, n_first)
+        a_l = g_zl(a_l)
+        d_x = g_x(g_cross(d_l))
+        input_grad = norm_backward(n_near, n_second, n_first)
+        result = finish(b_near, b_second, b_first)
+        biases = jnp.concatenate([qkv_sums[0], up_sums[0]])
+        spread = lax.dynamic_update_slice(
+            jnp.zeros((4, biases.shape[0]), F32), biases[None], (block, 0)
+        )
+        u_z2, a_l, d_x, input_grad, result, spread = sync(
+            u_z2, a_l, d_x, input_grad, result, spread
+        )
+        u_l = g_zl(g_split(gu_own, u_b, u_z1, u_z2))
+        a_x = g_x(g_cross(a_l))
         input_other = swap_core(input_grad)
-        lines = lines[:3].reshape(-1)
-        lines = lines + swap_core(lines)
-        biases = jnp.concatenate([qkv_sums[0], up_sums[0]])
-        spread = lax.dynamic_update_slice_in_dim(
-            jnp.zeros((4, biases.shape[0]), F32), biases[None], block, 0
-        )
-        lines = jnp.concatenate([lines, spread.reshape(-1)])
-        for bit in top_bits + [Y_BIT]:
+        result_other = swap_core(result)
+        lines = input_grad[half : half + 3] + input_other[half : half + 3]
+        lines = jnp.concatenate([lines.reshape(-1), spread.reshape(-1)])
+        for bit in [Y_BIT] + top_bits + [X_BIT]:
             lines = lines + swap(lines, bit)
-        u_z2, a_x, b_second, input_grad, input_other, lines = sync(
-            u_z2, a_x, b_second, input_grad, input_other, lines
-        )
-        b_first = add(b_kept[half : 2 * half], b_got[half : 2 * half], b_second[half:])
-        b_first = swap_mixed(b_first.astype(BF), (ZL_BIT, X_BIT))
-        u_l = g_zl(g_own(gu[3], u_b, u_z1, u_z2))
-        b_keep = add(b_kept[:half], b_got[:half], b_second[:half])
-        input_grad = place_halves(core, input_grad, input_other)
-        lines = lines + swap(lines, X_BIT)
+        u_l, a_x, input_other, result_other, lines = sync(
+            u_l, a_x, input_other, result_other, lines
+        )
+        gu = g_x(g_cross(u_l))
         lines = lines + swap(lines, ZL_BIT)
+        result = place_halves(core, result, result_other)
+        input_grad = place_halves(core, input_grad, input_other, rows=half)
         ga = ordered(x_mine, *a_x, 1)
         gd = ordered(x_mine, *d_x, 1)
-        u_l, b_first, b_keep, lines = sync(u_l, b_first, b_keep, lines)
-        gu = g_x(ordered(zl_mine, *u_l, 1))
-        result = finish(b_keep, b_first)
-        result = place_halves(core, result, swap_core(result))
         gu = ordered(x_mine, *gu, 1)
 
         gdown = gd.astype(F32).T

time: 593 us -> 579 us (0.976)
  Pallas kernels: 198 us -> 255 us
  other arithmetic: 60 us -> 21.5 us
  waiting for transfers between devices: 205 us -> 177 us
    pallas_call x14 -> x35, Pallas kernels: 191 us -> 246 us  [call(): pl.pallas_call(kernel, out_shape=outs, grid_spec=pltpu.PrefetchScalarGrid...]
    ppermute x41 -> x42, waiting for transfers between devices: 202 us -> 151 us  [swap(): return lax.ppermute(value, 'dp', [(i, i ^ flip) for i in range(dp_size)])]
    convert_element_type x8 -> x0, other arithmetic: 17.8 us -> none  [the longest x3 5.68 us: top_send(): add(kept[cut:], got[cut:]).astype(BF)]
    ppermute x6, waiting for transfers between devices: 0.02 us -> 17.6 us  [swap_mixed(): return lax.ppermute(value, ('dp', 'tensor'), pairs)]
    select_n x10 -> x4, other arithmetic: 16.3 us -> 5.67 us  [ordered(): jnp.where(bit == 0, jnp.concatenate([own, other], axis), jnp.concatenate(...]
    add x4 -> x1, other arithmetic: 9.87 us -> 0.88 us  [local(): lines = input_grad[half:half + 3] + input_other[half:half + 3]]
    unnamed x111 -> x90, local copies, waits for them, and re-layouts: 19.6 us -> 25.7 us
    dynamic_slice x12 -> x6, local copies, waits for them, and re-layouts: 13.9 us -> 8.95 us  [part_of(): return lax.dynamic_slice_in_dim(value, index * size, size, axis)]
  transfers between devices with their start and end apart: 56 -> 56, of which waited for: 17 -> 17; matrix products, arithmetic and copies ran while one was open for 15% -> 8% of each run, Pallas kernels for 33% -> 45%
where the time goes in v5:
time: 579 us; the launch traced here: 570 us
  Pallas kernels  255 us (44%)
  waiting for transfers between devices  177 us (31%)
  local copies, waits for them, and re-layouts  57.2 us (10%)
  starting transfers between devices  57 us (10%)
  other arithmetic  21.5 us (4%)
    pallas_call x35, Pallas kernels, call(): pl.pallas_call(kernel, out_shape=outs, grid_spec=pltpu.PrefetchScalarGrid...  246 us
    ppermute x42, waiting for transfers between devices, swap(): return lax.ppermute(value, 'dp', [(i, i ^ flip) for i in range(dp_size)])  151 us
    ppermute x42, starting transfers between devices, swap(): return lax.ppermute(value, 'dp', [(i, i ^ flip) for i in range(dp_size)])  49.4 us
    unnamed x90, local copies, waits for them, and re-layouts  25.7 us
    ppermute x6, waiting for transfers between devices, swap_mixed(): return lax.ppermute(value, ('dp', 'tensor'), pairs)  17.6 us
  transfers between devices with their start and end apart: 56, of which 17 were waited for; matrix products, arithmetic and copies ran while one was open for 8% of the time, Pallas kernels for 45%

profile of v5, /device:TPU:0, one launch (start us, length us, event | category | flops | bytes accessed | tf_op | source)
XLA Modules:
  0.0 569.7 jit_solution(4642774399642993759)
XLA Ops:
  38.6 10.9 %collective-permute-done.4.other_ref = bf16[256,1024]{1,0:T(8,128)(2,1)} collective-permute-done((bf16[256,1024]{1,0:T(8,128)(2,1)}, bf16[256,1024]{1,0:T(8,128)(2,1)}, u32[]{:S(2)}, u32[]{:S(2)}) %collective-permute-start.4) | collective-permute-done | bytes 524320 | tf_op jit(solution)/shard_map/ppermute | solution.py:589
  69.5 28.1 %collective-permute-done.12.other_ref = bf16[256,1024]{1,0:T(8,128)(2,1)} collective-permute-done((bf16[256,1024]{1,0:T(8,128)(2,1)}, bf16[256,1024]{1,0:T(8,128)(2,1)}, u32[]{:S(2)}, u32[]{:S(2)}) %collective-permute-start.12) | collective-permute-done | bytes 524320 | tf_op jit(solution)/shard_map/ppermute | solution.py:589
  99.8 9.6 %collective-permute-done.8.refs_1_ = bf16[512,1024]{1,0:T(8,128)(2,1)} collective-permute-done((bf16[512,1024]{1,0:T(8,128)(2,1)}, bf16[512,1024]{1,0:T(8,128)(2,1)}, u32[]{:S(2)}, u32[]{:S(2)}) %collective-permute-start.8) | collective-permute-done | bytes 1048608 | tf_op jit(solution)/shard_map/ppermute | solution.py:589
  117.9 26.2 %collective-permute-done.16.other_ref = bf16[256,1024]{1,0:T(8,128)(2,1)} collective-permute-done((bf16[256,1024]{1,0:T(8,128)(2,1)}, bf16[256,1024]{1,0:T(8,128)(2,1)}, u32[]{:S(2)}, u32[]{:S(2)}) %collective-permute-start.16) | collective-permute-done | bytes 524320 | tf_op jit(solution)/shard_map/ppermute | solution.py:589
  150.3 5.8 %fusion.2 = (f32[2048,128]{1,0:T(8,128)}, f32[2048,128]{1,0:T(8,128)}, f32[2048,128]{1,0:T(8,128)}) fusion(f32[128]{0:T(128)S(1)} %fusion.15, f32[2048]{0:T(1024)S(1)} %bitcast.103, pred[128]{0:T(512)(128)(4,1)S(1)} %get-tuple-element.416, pred[128]{0:T(512)(128)(4,1)S(1)} %broadcast_compare_fusion.2, pred[128]{0:T(512)(128)(4,1)S(1)} %get-tuple-element.417), kind=kLoop, calls=%fused_computation.6 | loop fusion | flops 1572864 | bytes 3154816 | tf_op jit(solution)/shard_map/jit(_where)/select_n | solution.py:488
  158.3 14.7 %collective-permute-done.17 = bf16[256,2048]{1,0:T(8,128)(2,1)} collective-permute-done((bf16[256,2048]{1,0:T(8,128)(2,1)S(1)}, bf16[256,2048]{1,0:T(8,128)(2,1)}, u32[]{:S(2)}, u32[]{:S(2)}) %collective-permute-start.17) | collective-permute-done | bytes 1048608 | tf_op jit(solution)/shard_map/ppermute | solution.py:596
  181.3 10.7 %shard_map.207.rows_ref.refs_0_ = bf16[2048,2048]{1,0:T(8,128)(2,1)} custom-call(s32[2]{0:T(128)} %broadcast_10_flags_ref.2.flags_ref, bf16[512,2048]{1,0:T(8,128)(2,1)} %constant_dynamic-update-slice_fusion.pair_ref, bf16[512,2048]{1,0:T(8,128)(2,1)} %collective-permute-done.10.second_ref, bf16[512,2048]{1,0:T(8,128)(2,1)} %collective-permute-done.11.got_pair_ref, ...), custom_call_target="tpu_custom_call" | custom-call | flops 1000 | bytes 1000 | tf_op jit(solution)/shard_map/pallas_call | solution.py:35
  192.0 17.3 %shard_map.208 = (bf16[2048,1024]{1,0:T(8,128)(2,1)}, bf16[2048,1024]{1,0:T(8,128)(2,1)}) custom-call(bf16[2048,2048]{1,0:T(8,128)(2,1)} %shard_map.207.rows_ref.refs_0_, f32[1,1024]{1,0:T(1,128)} %bitcast.108, bf16[512,1024]{1,0:T(8,128)(2,1)} %shard_map.204.refs_0_, bf16[512,1024]{1,0:T(8,128)(2,1)} %collective-permute-done.8.refs_1_, ...), custom_call_target="tpu_custom_call" | custom-call | flops 1000 | bytes 1000 | tf_op jit(solution)/shard_map/pallas_call | solution.py:35
  209.3 17.1 %collective-permute-done.19.refs_1_ = bf16[512,1024]{1,0:T(8,128)(2,1)} collective-permute-done((bf16[512,1024]{1,0:T(8,128)(2,1)}, bf16[512,1024]{1,0:T(8,128)(2,1)}, u32[]{:S(2)}, u32[]{:S(2)}) %collective-permute-start.19) | collective-permute-done | bytes 1048608 | tf_op jit(solution)/shard_map/ppermute | solution.py:589
  231.0 10.7 %shard_map.209.refs_0_.refs_2_.rows_ref = bf16[2048,2048]{1,0:T(8,128)(2,1)} custom-call(s32[2]{0:T(128)} %pad_add_fusion.3.flags_ref, bf16[512,2048]{1,0:T(8,128)(2,1)} %constant_dynamic-update-slice_fusion.2.pair_ref, bf16[512,2048]{1,0:T(8,128)(2,1)} %collective-permute-done.22.second_ref, bf16[512,2048]{1,0:T(8,128)(2,1)} %collective-permute-done.23.got_pair_ref, ...), custom_call_target="tpu_custom_call" | custom-call | flops 1000 | bytes 1000 | tf_op jit(solution)/shard_map/pallas_call | solution.py:35
  241.8 12.1 %shard_map.210 = (bf16[512,1024]{1,0:T(8,128)(2,1)}, bf16[512,1024]{1,0:T(8,128)(2,1)}, bf16[512,1024]{1,0:T(8,128)(2,1)}) custom-call(bf16[2048,2048]{1,0:T(8,128)(2,1)} %shard_map.209.refs_0_.refs_2_.rows_ref, bf16[2048,1024]{1,0:T(8,128)(2,1)} %get-tuple-element.235.refs_1_.a_ref), custom_call_target="tpu_custom_call" | custom-call | flops 1000 | bytes 1000 | tf_op jit(solution)/shard_map/pallas_call | solution.py:35
  256.8 33.9 %shard_map.211 = (bf16[2,4,256,256]{3,2,1,0:T(8,128)(2,1)}, bf16[2,4,256,768]{3,2,1,0:T(8,128)(2,1)}, f32[8,768]{1,0:T(8,128)}) custom-call(bf16[2,4,256,2048]{3,2,1,0:T(8,128)(2,1)} %bitcast.81, bf16[2,4,256,2048]{3,2,1,0:T(8,128)(2,1)} %bitcast.82, f32[1,768]{1,0:T(1,128)} %bitcast.112, f32[2,4,256,128]{3,2,1,0:T(8,128)} %bitcast.94, ...), custom_call_target="tpu_custom_call" | custom-call | flops 1000 | bytes 1000 | tf_op jit(solution)/shard_map/pallas_call | solution.py:35
  297.7 12.3 %shard_map.214 = (bf16[512,1024]{1,0:T(8,128)(2,1)}, bf16[512,1024]{1,0:T(8,128)(2,1)}, bf16[512,1024]{1,0:T(8,128)(2,1)}) custom-call(bf16[2048,2048]{1,0:T(8,128)(2,1)} %shard_map.207.rows_ref.refs_0_, bf16[2048,768]{1,0:T(8,128)(2,1)} %bitcast.83, bf16[2048,2048]{1,0:T(8,128)(2,1)} %shard_map.209.refs_0_.refs_2_.rows_ref, bf16[2048,256]{1,0:T(8,128)(2,1)} %bitcast.87), custom_call_target="tpu_custom_call" | custom-call | flops 1000 | bytes 1000 | tf_op jit(solution)/shard_map/pallas_call | solution.py:35
  310.0 10.4 %shard_map.215 = bf16[1024,2048]{1,0:T(8,128)(2,1)} custom-call(s32[1]{0:T(128)} %bitcast.22._, bf16[2048,1024]{1,0:T(8,128)(2,1)} %get-tuple-element.235.refs_1_.a_ref, bf16[2048,256]{1,0:T(8,128)(2,1)} %bitcast.88, bf16[512,1024]{1,0:T(8,128)(2,1)} %shard_map.206.refs_0_, bf16[512,1024]{1,0:T(8,128)(2,1)} %collective-permute-done.19.refs_1_, ...), custom_call_target="tpu_custom_call" | custom-call | flops 1000 | bytes 1000 | tf_op jit(solution)/shard_map/pallas_call | solution.py:35
  323.6 14.6 %shard_map.217 = (bf16[2048,1024]{1,0:T(8,128)(2,1)}, f32[8,1024]{1,0:T(8,128)}) custom-call(bf16[2048,2048]{1,0:T(8,128)(2,1)} %shard_map.209.refs_0_.refs_2_.rows_ref, bf16[2048,1024]{1,0:T(8,128)(2,1)} %get-tuple-element.241.slope_ref, bf16[512,1024]{1,0:T(8,128)(2,1)} %shard_map.206.refs_0_, bf16[512,1024]{1,0:T(8,128)(2,1)} %collective-permute-done.19.refs_1_, ...), custom_call_target="tpu_custom_call" | custom-call | flops 1000 | bytes 1000 | tf_op jit(solution)/shard_map/pallas_call | solution.py:35
  338.2 13.2 %shard_map.218 = bf16[1024,2048]{1,0:T(8,128)(2,1)} custom-call(s32[1]{0:T(128)} %bitcast.22._, bf16[2048,1024]{1,0:T(8,128)(2,1)} %get-tuple-element.281.a_ref.refs_1_, bf16[2048,768]{1,0:T(8,128)(2,1)} %bitcast.84, bf16[512,1024]{1,0:T(8,128)(2,1)} %shard_map.204.refs_0_, bf16[512,1024]{1,0:T(8,128)(2,1)} %collective-permute-done.8.refs_1_, ...), custom_call_target="tpu_custom_call" | custom-call | flops 1000 | bytes 1000 | tf_op jit(solution)/shard_map/pallas_call | solution.py:35
  353.5 11.3 %shard_map.216 = (bf16[512,2048]{1,0:T(8,128)(2,1)}, bf16[512,2048]{1,0:T(8,128)(2,1)}) custom-call(s32[1]{0:T(128)} %bitcast._.core_ref, bf16[2048,1024]{1,0:T(8,128)(2,1)} %get-tuple-element.235.refs_1_.a_ref, bf16[2048,256]{1,0:T(8,128)(2,1)} %bitcast.89, bf16[512,1024]{1,0:T(8,128)(2,1)} %shard_map.206.refs_0_, ...), custom_call_target="tpu_custom_call" | custom-call | flops 1000 | bytes 1000 | tf_op jit(solution)/shard_map/pallas_call | solution.py:35
  373.8 6.2 %shard_map.221 = bf16[512,1024]{1,0:T(8,128)(2,1)} custom-call(bf16[2048,2048]{1,0:T(8,128)(2,1)} %shard_map.207.rows_ref.refs_0_, bf16[2048,1024]{1,0:T(8,128)(2,1)} %get-tuple-element.281.a_ref.refs_1_), custom_call_target="tpu_custom_call" | custom-call | flops 1000 | bytes 1000 | tf_op jit(solution)/shard_map/pallas_call | solution.py:35
  382.0 14.1 %shard_map.222 = (bf16[512,2048]{1,0:T(8,128)(2,1)}, bf16[512,2048]{1,0:T(8,128)(2,1)}) custom-call(s32[1]{0:T(128)} %bitcast._.core_ref, bf16[2048,1024]{1,0:T(8,128)(2,1)} %get-tuple-element.281.a_ref.refs_1_, bf16[2048,768]{1,0:T(8,128)(2,1)} %bitcast.85, bf16[512,1024]{1,0:T(8,128)(2,1)} %shard_map.204.refs_0_, ...), custom_call_target="tpu_custom_call" | custom-call | flops 1000 | bytes 1000 | tf_op jit(solution)/shard_map/pallas_call | solution.py:35
  398.8 6.2 %shard_map.224.kept_ref = bf16[512,1024]{1,0:T(8,128)(2,1)} custom-call(bf16[2048,2048]{1,0:T(8,128)(2,1)} %shard_map.209.refs_0_.refs_2_.rows_ref, bf16[2048,1024]{1,0:T(8,128)(2,1)} %get-tuple-element.235.refs_1_.a_ref), custom_call_target="tpu_custom_call" | custom-call | flops 1000 | bytes 1000 | tf_op jit(solution)/shard_map/pallas_call | solution.py:35
  405.0 8.9 %shard_map.223 = (bf16[512,1024]{1,0:T(8,128)(2,1)}, bf16[512,1024]{1,0:T(8,128)(2,1)}) custom-call(bf16[2048,2048]{1,0:T(8,128)(2,1)} %shard_map.207.rows_ref.refs_0_, bf16[2048,1024]{1,0:T(8,128)(2,1)} %get-tuple-element.281.a_ref.refs_1_), custom_call_target="tpu_custom_call" | custom-call | flops 1000 | bytes 1000 | tf_op jit(solution)/shard_map/pallas_call | solution.py:35
  437.3 6.2 %shard_map.232.kept_ref = bf16[512,1024]{1,0:T(8,128)(2,1)} custom-call(bf16[2048,2048]{1,0:T(8,128)(2,1)} %shard_map.207.rows_ref.refs_0_, bf16[2048,1024]{1,0:T(8,128)(2,1)} %get-tuple-element.281.a_ref.refs_1_), custom_call_target="tpu_custom_call" | custom-call | flops 1000 | bytes 1000 | tf_op jit(solution)/shard_map/pallas_call | solution.py:35
  443.4 6.8 %shard_map.230.kept_ref = bf16[512,1024]{1,0:T(8,128)(2,1)} custom-call(bf16[2048,2048]{1,0:T(8,128)(2,1)} %shard_map.207.rows_ref.refs_0_, bf16[2048,768]{1,0:T(8,128)(2,1)} %bitcast.86, bf16[2048,2048]{1,0:T(8,128)(2,1)} %shard_map.209.refs_0_.refs_2_.rows_ref, bf16[2048,256]{1,0:T(8,128)(2,1)} %bitcast.90), custom_call_target="tpu_custom_call" | custom-call | flops 1000 | bytes 1000 | tf_op jit(solution)/shard_map/pallas_call | solution.py:35
  450.2 3.4 shard_map.231
  453.6 9.7 %collective-permute-done.39.one_ref = bf16[256,1024]{1,0:T(8,128)(2,1)S(1)} collective-permute-done((bf16[256,1024]{1,0:T(8,128)(2,1)}, bf16[256,1024]{1,0:T(8,128)(2,1)S(1)}, u32[]{:S(2)}, u32[]{:S(2)}) %collective-permute-start.39) | collective-permute-done | bytes 524320 | tf_op jit(solution)/shard_map/ppermute | solution.py:589
  463.2 20.9 %collective-permute-done.43.got_ref = bf16[256,1024]{1,0:T(8,128)(2,1)S(1)} collective-permute-done((bf16[256,1024]{1,0:T(8,128)(2,1)S(1)}, bf16[256,1024]{1,0:T(8,128)(2,1)S(1)}, u32[]{:S(2)}, u32[]{:S(2)}) %collective-permute-start.43) | collective-permute-done | bytes 524320 | tf_op jit(solution)/shard_map/ppermute | solution.py:589
  496.8 4.4 shard_map.234.own_ref
  502.6 9.8 %collective-permute-done.44.two_ref = bf16[256,1024]{1,0:T(8,128)(2,1)} collective-permute-done((bf16[256,1024]{1,0:T(8,128)(2,1)}, bf16[256,1024]{1,0:T(8,128)(2,1)}, u32[]{:S(2)}, u32[]{:S(2)}) %collective-permute-start.44) | collective-permute-done | bytes 524320 | tf_op jit(solution)/shard_map/ppermute | solution.py:589
  512.9 6.2 %collective-permute-done.49.other_ref = f32[320,2048]{1,0:T(8,128)} collective-permute-done((f32[320,2048]{1,0:T(8,128)}, f32[320,2048]{1,0:T(8,128)}, u32[]{:S(2)}, u32[]{:S(2)}) %collective-permute-start.49) | collective-permute-done | bytes 2621472 | tf_op jit(solution)/shard_map/ppermute | solution.py:592
  537.6 8.4 %collective-permute-done.53 = f32[13312]{0:T(1024)S(1)} collective-permute-done((f32[13312]{0:T(1024)S(1)}, f32[13312]{0:T(1024)S(1)}, u32[]{:S(2)}, u32[]{:S(2)}) %collective-permute-start.53) | collective-permute-done | bytes 53280 | tf_op jit(solution)/shard_map/ppermute | solution.py:589
  554.7 4.1 shard_map.238
  558.8 5.2 shard_map.239
  (295 shorter events, 188.4 us)
Async XLA Ops:
  14.2 37.6 %collective-permute-start.5 = (bf16[256,2048]{1,0:T(8,128)(2,1)}, bf16[256,2048]{1,0:T(8,128)(2,1)}, u32[]{:S(2)}, u32[]{:S(2)}) collective-permute-start(bf16[256,2048]{1,0:T(8,128)(2,1)} %get-tuple-element.174), channel_id=1, source_target_pairs={{0,8},{2,10},{4,12},{6,14},{8,0},{10,2},{12,4},{14,6},{16,24},{18,... | collective-permute-start | bytes 3145736 | tf_op jit(solution)/shard_map/ppermute | solution.py:589
  21.5 28.1 %collective-permute-start.4 = (bf16[256,1024]{1,0:T(8,128)(2,1)}, bf16[256,1024]{1,0:T(8,128)(2,1)}, u32[]{:S(2)}, u32[]{:S(2)}) collective-permute-start(bf16[256,1024]{1,0:T(8,128)(2,1)} %get-tuple-element.402), channel_id=1, source_target_pairs={{0,8},{2,10},{4,12},{6,14},{8,0},{10,2},{12,4},{14,6},{16,24},{18,... | collective-permute-start | bytes 1572872 | tf_op jit(solution)/shard_map/ppermute | solution.py:589
  58.7 50.8 %collective-permute-start.10 = (bf16[512,2048]{1,0:T(8,128)(2,1)}, bf16[512,2048]{1,0:T(8,128)(2,1)}, u32[]{:S(2)}, u32[]{:S(2)}) collective-permute-start(bf16[512,2048]{1,0:T(8,128)(2,1)} %constant_dynamic-update-slice_fusion.pair_ref), channel_id=1, source_target_pairs={{0,2},{2,0},{4,6},{6,4},{8,10},{10,8},{12,14},{14,12},{16,18},{18,... | collective-permute-start | bytes 6291464 | tf_op jit(solution)/shard_map/ppermute | solution.py:589
  60.2 49.3 %collective-permute-start.11 = (bf16[512,2048]{1,0:T(8,128)(2,1)}, bf16[512,2048]{1,0:T(8,128)(2,1)}, u32[]{:S(2)}, u32[]{:S(2)}) collective-permute-start(bf16[512,2048]{1,0:T(8,128)(2,1)} %constant_dynamic-update-slice_fusion.pair_ref), channel_id=1, source_target_pairs={{0,1},{1,0},{2,3},{3,2},{4,5},{5,4},{6,7},{7,6},{8,9},{9,8},{10,11... | collective-permute-start | bytes 6291464 | tf_op jit(solution)/shard_map/ppermute | solution.py:592
  60.3 49.2 %collective-permute-start.8 = (bf16[512,1024]{1,0:T(8,128)(2,1)}, bf16[512,1024]{1,0:T(8,128)(2,1)}, u32[]{:S(2)}, u32[]{:S(2)}) collective-permute-start(bf16[512,1024]{1,0:T(8,128)(2,1)} %shard_map.204.refs_0_), channel_id=1, source_target_pairs={{0,16},{2,18},{4,20},{6,22},{8,24},{10,26},{12,28},{14,30},{16,0},... | collective-permute-start | bytes 3145736 | tf_op jit(solution)/shard_map/ppermute | solution.py:589
  62.9 46.6 %collective-permute-start.9 = (bf16[512,1024]{1,0:T(8,128)(2,1)}, bf16[512,1024]{1,0:T(8,128)(2,1)}, u32[]{:S(2)}, u32[]{:S(2)}) collective-permute-start(bf16[512,1024]{1,0:T(8,128)(2,1)} %shard_map.204.refs_0_), channel_id=1, source_target_pairs={{0,4},{2,6},{4,0},{6,2},{8,12},{10,14},{12,8},{14,10},{16,20},{18,... | collective-permute-start | bytes 3145736 | tf_op jit(solution)/shard_map/ppermute | solution.py:589
  67.1 30.5 %collective-permute-start.12 = (bf16[256,1024]{1,0:T(8,128)(2,1)}, bf16[256,1024]{1,0:T(8,128)(2,1)}, u32[]{:S(2)}, u32[]{:S(2)}) collective-permute-start(bf16[256,1024]{1,0:T(8,128)(2,1)} %get-tuple-element.396), channel_id=1, source_target_pairs={{0,8},{2,10},{4,12},{6,14},{8,0},{10,2},{12,4},{14,6},{16,24},{18,... | collective-permute-start | bytes 1572872 | tf_op jit(solution)/shard_map/ppermute | solution.py:589
  109.5 48.8 %collective-permute-start.14 = (bf16[512,1024]{1,0:T(8,128)(2,1)}, bf16[512,1024]{1,0:T(8,128)(2,1)}, u32[]{:S(2)}, u32[]{:S(2)}) collective-permute-start(bf16[512,1024]{1,0:T(8,128)(2,1)} %shard_map.205.refs_0_.refs_4_), channel_id=1, source_target_pairs={{0,16},{2,18},{4,20},{6,22},{8,24},{10,26},{12,28},{14,30},{16,0},... | collective-permute-start | bytes 3145736 | tf_op jit(solution)/shard_map/ppermute | solution.py:589
  109.6 48.8 %collective-permute-start.15 = (bf16[512,1024]{1,0:T(8,128)(2,1)}, bf16[512,1024]{1,0:T(8,128)(2,1)}, u32[]{:S(2)}, u32[]{:S(2)}) collective-permute-start(bf16[512,1024]{1,0:T(8,128)(2,1)} %shard_map.205.refs_0_.refs_4_), channel_id=1, source_target_pairs={{0,4},{2,6},{4,0},{6,2},{8,12},{10,14},{12,8},{14,10},{16,20},{18,... | collective-permute-start | bytes 3145736 | tf_op jit(solution)/shard_map/ppermute | solution.py:589
  112.2 31.9 %collective-permute-start.16 = (bf16[256,1024]{1,0:T(8,128)(2,1)}, bf16[256,1024]{1,0:T(8,128)(2,1)}, u32[]{:S(2)}, u32[]{:S(2)}) collective-permute-start(bf16[256,1024]{1,0:T(8,128)(2,1)} %get-tuple-element.394), channel_id=1, source_target_pairs={{0,8},{2,10},{4,12},{6,14},{8,0},{10,2},{12,4},{14,6},{16,24},{18,... | collective-permute-start | bytes 1572872 | tf_op jit(solution)/shard_map/ppermute | solution.py:589
  115.3 57.8 %collective-permute-start.18 = (bf16[512,2048]{1,0:T(8,128)(2,1)}, bf16[512,2048]{1,0:T(8,128)(2,1)}, u32[]{:S(2)}, u32[]{:S(2)}) collective-permute-start(bf16[512,2048]{1,0:T(8,128)(2,1)} %collective-permute-done.10.second_ref), channel_id=1, source_target_pairs={{0,1},{1,0},{2,3},{3,2},{4,5},{5,4},{6,7},{7,6},{8,9},{9,8},{10,11... | collective-permute-start | bytes 6291464 | tf_op jit(solution)/shard_map/ppermute | solution.py:592
  117.2 41.1 %collective-permute-start.13 = (bf16[512,1024]{1,0:T(8,128)(2,1)}, bf16[512,1024]{1,0:T(8,128)(2,1)}, u32[]{:S(2)}, u32[]{:S(2)}) collective-permute-start(bf16[512,1024]{1,0:T(8,128)(2,1)} %collective-permute-done.8.refs_1_), channel_id=1, source_target_pairs={{0,4},{2,6},{4,0},{6,2},{8,12},{10,14},{12,8},{14,10},{16,20},{18,... | collective-permute-start | bytes 3145736 | tf_op jit(solution)/shard_map/ppermute | solution.py:589
  144.1 29.0 %collective-permute-start.17 = (bf16[256,2048]{1,0:T(8,128)(2,1)S(1)}, bf16[256,2048]{1,0:T(8,128)(2,1)}, u32[]{:S(2)}, u32[]{:S(2)}) collective-permute-start(bf16[256,2048]{1,0:T(8,128)(2,1)S(1)} %get-tuple-element.190), channel_id=1, source_target_pairs={{0,8},{1,3},{2,10},{3,1},{4,12},{5,7},{6,14},{7,5},{8,0},{9,11},{1... | collective-permute-start | bytes 3145736 | tf_op jit(solution)/shard_map/ppermute | solution.py:596
  177.0 49.4 %collective-permute-start.22 = (bf16[512,2048]{1,0:T(8,128)(2,1)}, bf16[512,2048]{1,0:T(8,128)(2,1)}, u32[]{:S(2)}, u32[]{:S(2)}) collective-permute-start(bf16[512,2048]{1,0:T(8,128)(2,1)} %constant_dynamic-update-slice_fusion.2.pair_ref), channel_id=1, source_target_pairs={{0,2},{1,9},{2,0},{3,11},{4,6},{5,13},{6,4},{7,15},{8,10},{9,1},{1... | collective-permute-start | bytes 6291464 | tf_op jit(solution)/shard_map/ppermute | solution.py:596
  177.5 49.0 %collective-permute-start.23 = (bf16[512,2048]{1,0:T(8,128)(2,1)}, bf16[512,2048]{1,0:T(8,128)(2,1)}, u32[]{:S(2)}, u32[]{:S(2)}) collective-permute-start(bf16[512,2048]{1,0:T(8,128)(2,1)} %constant_dynamic-update-slice_fusion.2.pair_ref), channel_id=1, source_target_pairs={{0,1},{1,0},{2,3},{3,2},{4,5},{5,4},{6,7},{7,6},{8,9},{9,8},{10,11... | collective-permute-start | bytes 6291464 | tf_op jit(solution)/shard_map/ppermute | solution.py:592
  177.5 49.0 %collective-permute-start.19 = (bf16[512,1024]{1,0:T(8,128)(2,1)}, bf16[512,1024]{1,0:T(8,128)(2,1)}, u32[]{:S(2)}, u32[]{:S(2)}) collective-permute-start(bf16[512,1024]{1,0:T(8,128)(2,1)} %shard_map.206.refs_0_), channel_id=1, source_target_pairs={{0,16},{2,18},{4,20},{6,22},{8,24},{10,26},{12,28},{14,30},{16,0},... | collective-permute-start | bytes 3145736 | tf_op jit(solution)/shard_map/ppermute | solution.py:589
  177.5 49.0 %collective-permute-start.20 = (bf16[512,1024]{1,0:T(8,128)(2,1)}, bf16[512,1024]{1,0:T(8,128)(2,1)}, u32[]{:S(2)}, u32[]{:S(2)}) collective-permute-start(bf16[512,1024]{1,0:T(8,128)(2,1)} %shard_map.206.refs_0_), channel_id=1, source_target_pairs={{0,4},{2,6},{4,0},{6,2},{8,12},{10,14},{12,8},{14,10},{16,20},{18,... | collective-permute-start | bytes 3145736 | tf_op jit(solution)/shard_map/ppermute | solution.py:589
  179.1 47.4 %collective-permute-start.21 = (bf16[512,1024]{1,0:T(8,128)(2,1)}, bf16[512,1024]{1,0:T(8,128)(2,1)S(1)}, u32[]{:S(2)}, u32[]{:S(2)}) collective-permute-start(bf16[512,1024]{1,0:T(8,128)(2,1)} %collective-permute-done.14.refs_1_.refs_5_), channel_id=1, source_target_pairs={{0,4},{2,6},{4,0},{6,2},{8,12},{10,14},{12,8},{14,10},{16,20},{18,... | collective-permute-start | bytes 3145736 | tf_op jit(solution)/shard_map/ppermute | solution.py:589
  226.5 27.4 %collective-permute-start.24 = (bf16[512,1024]{1,0:T(8,128)(2,1)}, bf16[512,1024]{1,0:T(8,128)(2,1)}, u32[]{:S(2)}, u32[]{:S(2)}) collective-permute-start(bf16[512,1024]{1,0:T(8,128)(2,1)} %collective-permute-done.19.refs_1_), channel_id=1, source_target_pairs={{0,4},{2,6},{4,0},{6,2},{8,12},{10,14},{12,8},{14,10},{16,20},{18,... | collective-permute-start | bytes 3145736 | tf_op jit(solution)/shard_map/ppermute | solution.py:589
  253.9 36.8 %collective-permute-start.26 = (bf16[512,1024]{1,0:T(8,128)(2,1)}, bf16[512,1024]{1,0:T(8,128)(2,1)S(1)}, u32[]{:S(2)}, u32[]{:S(2)}) collective-permute-start(bf16[512,1024]{1,0:T(8,128)(2,1)} %get-tuple-element.205), channel_id=1, source_target_pairs={{0,4},{2,6},{4,0},{6,2},{8,12},{10,14},{12,8},{14,10},{16,20},{18,... | collective-permute-start | bytes 3145736 | tf_op jit(solution)/shard_map/ppermute | solution.py:589
  290.7 29.6 %collective-permute-start.28 = (bf16[512,1024]{1,0:T(8,128)(2,1)S(1)}, bf16[512,1024]{1,0:T(8,128)(2,1)S(1)}, u32[]{:S(2)}, u32[]{:S(2)}) collective-permute-start(bf16[512,1024]{1,0:T(8,128)(2,1)S(1)} %copy-done.36), channel_id=1, source_target_pairs={{0,4},{2,6},{4,0},{6,2},{8,12},{10,14},{12,8},{14,10},{16,20},{18,... | collective-permute-start | bytes 3145736 | tf_op jit(solution)/shard_map/ppermute | solution.py:589
  321.5 29.9 %collective-permute-start.31 = (bf16[1024,2048]{1,0:T(8,128)(2,1)}, bf16[1024,2048]{1,0:T(8,128)(2,1)S(1)}, u32[]{:S(2)}, u32[]{:S(2)}) collective-permute-start(bf16[1024,2048]{1,0:T(8,128)(2,1)} %shard_map.215), channel_id=1, source_target_pairs={{0,1},{1,0},{2,3},{3,2},{4,5},{5,4},{6,7},{7,6},{8,9},{9,8},{10,11... | collective-permute-start | bytes 12582920 | tf_op jit(solution)/shard_map/ppermute | solution.py:592
  321.5 43.3 %collective-permute-start.30 = (bf16[512,1024]{1,0:T(8,128)(2,1)S(1)}, bf16[512,1024]{1,0:T(8,128)(2,1)S(1)}, u32[]{:S(2)}, u32[]{:S(2)}) collective-permute-start(bf16[512,1024]{1,0:T(8,128)(2,1)S(1)} %copy-done.37), channel_id=1, source_target_pairs={{0,4},{2,6},{4,0},{6,2},{8,12},{10,14},{12,8},{14,10},{16,20},{18,... | collective-permute-start | bytes 3145736 | tf_op jit(solution)/shard_map/ppermute | solution.py:589
  322.6 42.1 %collective-permute-start.29 = (bf16[256,1024]{1,0:T(8,128)(2,1)S(1)}, bf16[256,1024]{1,0:T(8,128)(2,1)S(1)}, u32[]{:S(2)}, u32[]{:S(2)}) collective-permute-start(bf16[256,1024]{1,0:T(8,128)(2,1)S(1)} %copy-done.23), channel_id=1, source_target_pairs={{0,16},{2,18},{4,20},{6,22},{8,24},{10,26},{12,28},{14,30},{16,0},... | collective-permute-start | bytes 1572872 | tf_op jit(solution)/shard_map/ppermute | solution.py:589
  365.6 30.5 %collective-permute-start.35 = (bf16[512,2048]{1,0:T(8,128)(2,1)}, bf16[512,2048]{1,0:T(8,128)(2,1)S(1)}, u32[]{:S(2)}, u32[]{:S(2)}) collective-permute-start(bf16[512,2048]{1,0:T(8,128)(2,1)} %get-tuple-element.250), channel_id=1, source_target_pairs={{0,2},{1,9},{2,0},{3,11},{4,6},{5,13},{6,4},{7,15},{8,10},{9,1},{1... | collective-permute-start | bytes 6291464 | tf_op jit(solution)/shard_map/ppermute | solution.py:596
  367.1 29.0 %collective-permute-start.33 = (bf16[512,1024]{1,0:T(8,128)(2,1)}, bf16[512,1024]{1,0:T(8,128)(2,1)}, u32[]{:S(2)}, u32[]{:S(2)}) collective-permute-start(bf16[512,1024]{1,0:T(8,128)(2,1)} %get-tuple-element.245), channel_id=1, source_target_pairs={{0,4},{2,6},{4,0},{6,2},{8,12},{10,14},{12,8},{14,10},{16,20},{18,... | collective-permute-start | bytes 3145736 | tf_op jit(solution)/shard_map/ppermute | solution.py:589
  422.4 61.7 %collective-permute-start.40 = (bf16[512,1024]{1,0:T(8,128)(2,1)}, bf16[512,1024]{1,0:T(8,128)(2,1)S(1)}, u32[]{:S(2)}, u32[]{:S(2)}) collective-permute-start(bf16[512,1024]{1,0:T(8,128)(2,1)} %get-tuple-element.265), channel_id=1, source_target_pairs={{0,4},{2,6},{4,0},{6,2},{8,12},{10,14},{12,8},{14,10},{16,20},{18,... | collective-permute-start | bytes 3145736 | tf_op jit(solution)/shard_map/ppermute | solution.py:589
  426.2 57.9 %collective-permute-start.41 = (bf16[256,2048]{1,0:T(8,128)(2,1)}, bf16[256,2048]{1,0:T(8,128)(2,1)S(1)}, u32[]{:S(2)}, u32[]{:S(2)}) collective-permute-start(bf16[256,2048]{1,0:T(8,128)(2,1)} %shard_map.228), channel_id=1, source_target_pairs={{0,8},{1,3},{2,10},{3,1},{4,12},{5,7},{6,14},{7,5},{8,0},{9,11},{1... | collective-permute-start | bytes 3145736 | tf_op jit(solution)/shard_map/ppermute | solution.py:596
  428.9 55.3 %collective-permute-start.42 = (bf16[256,2048]{1,0:T(8,128)(2,1)}, bf16[256,2048]{1,0:T(8,128)(2,1)S(1)}, u32[]{:S(2)}, u32[]{:S(2)}) collective-permute-start(bf16[256,2048]{1,0:T(8,128)(2,1)} %shard_map.229), channel_id=1, source_target_pairs={{0,8},{1,3},{2,10},{3,1},{4,12},{5,7},{6,14},{7,5},{8,0},{9,11},{1... | collective-permute-start | bytes 3145736 | tf_op jit(solution)/shard_map/ppermute | solution.py:596
  432.6 30.6 %collective-permute-start.39 = (bf16[256,1024]{1,0:T(8,128)(2,1)}, bf16[256,1024]{1,0:T(8,128)(2,1)S(1)}, u32[]{:S(2)}, u32[]{:S(2)}) collective-permute-start(bf16[256,1024]{1,0:T(8,128)(2,1)} %shard_map.226), channel_id=1, source_target_pairs={{0,16},{2,18},{4,20},{6,22},{8,24},{10,26},{12,28},{14,30},{16,0},... | collective-permute-start | bytes 1572872 | tf_op jit(solution)/shard_map/ppermute | solution.py:589
  433.6 50.5 %collective-permute-start.43 = (bf16[256,1024]{1,0:T(8,128)(2,1)S(1)}, bf16[256,1024]{1,0:T(8,128)(2,1)S(1)}, u32[]{:S(2)}, u32[]{:S(2)}) collective-permute-start(bf16[256,1024]{1,0:T(8,128)(2,1)S(1)} %copy-done.38), channel_id=1, source_target_pairs={{0,8},{2,10},{4,12},{6,14},{8,0},{10,2},{12,4},{14,6},{16,24},{18,... | collective-permute-start | bytes 1572872 | tf_op jit(solution)/shard_map/ppermute | solution.py:589
  512.4 33.6 %collective-permute-start.50 = (bf16[256,2048]{1,0:T(8,128)(2,1)S(1)}, bf16[256,2048]{1,0:T(8,128)(2,1)}, u32[]{:S(2)}, u32[]{:S(2)}) collective-permute-start(bf16[256,2048]{1,0:T(8,128)(2,1)S(1)} %shard_map.235.own_ref), channel_id=1, source_target_pairs={{0,1},{1,0},{2,3},{3,2},{4,5},{5,4},{6,7},{7,6},{8,9},{9,8},{10,11... | collective-permute-start | bytes 3145736 | tf_op jit(solution)/shard_map/ppermute | solution.py:592
  (63 other events, 740.3 us)

commit v6 on v5

--- a/solution.py
+++ b/solution.py
@@ -31,7 +31,7 @@
     return lax.dot_general(a, b, (((0,), (0,)), ((), ())), preferred_element_type=F32)
 
 
-def call(kernel, outs, grid, in_specs, out_specs, *operands, prefetch=0):
+def call(kernel, outs, grid, in_specs, out_specs, *operands, prefetch=0, cost=1000):
     return pl.pallas_call(
         kernel,
         out_shape=outs,
@@ -39,7 +39,7 @@
             num_scalar_prefetch=prefetch, grid=grid, in_specs=in_specs, out_specs=out_specs
         ),
         compiler_params=pltpu.CompilerParams(vmem_limit_bytes=54 * 1024 * 1024),
-        cost_estimate=pl.CostEstimate(flops=1000, bytes_accessed=1000, transcendentals=0),
+        cost_estimate=pl.CostEstimate(flops=1000, bytes_accessed=cost, transcendentals=0),
     )(*operands)
 
 
@@ -81,36 +81,24 @@
     )
 
 
-def split_kernel(flag_ref, kept_ref, got_ref, one_ref, two_ref, send_ref, own_ref):
-    sending = pl.program_id(0) == 0
-    upper = (flag_ref[0] == 1) != sending
-    total = kept_ref[...].astype(F32) + got_ref[...].astype(F32)
-    total = total + jnp.where(upper, two_ref[...], one_ref[...]).astype(F32)
-
-    @pl.when(sending)
-    def _():
-        send_ref[...] = total.astype(BF)
-
-    @pl.when(jnp.logical_not(sending))
-    def _():
-        own_ref[...] = total.astype(BF)
-
-
-def split_sum(flag, kept, got, one, two):
-    rows, cols = one.shape
-    out = jax.ShapeDtypeStruct((rows, cols), BF)
-    picked = pl.BlockSpec((rows, cols), lambda i, f: (jnp.where(i == 0, 1 - f[0], f[0]), 0))
+def half_kernel(_, *refs):
+    sum_kernel(*refs)
+
+
+def half_sum(which, wholes, halves=(), steps=2):
+    rows, cols = wholes[0].shape[0] // 2, wholes[0].shape[1]
+    tile = rows // steps
+    plain = pl.BlockSpec((tile, cols), lambda i, f: (i, 0))
+    picked = pl.BlockSpec((tile, cols), lambda i, f: (f[0] * steps + i, 0))
     return call(
-        split_kernel,
-        [out, out],
-        (2,),
-        [picked, picked, resident(one), resident(two)],
-        [pl.BlockSpec((rows, cols), lambda i, f: (0, 0))] * 2,
-        flag.reshape(1).astype(jnp.int32),
-        kept,
-        got,
-        one,
-        two,
+        half_kernel,
+        jax.ShapeDtypeStruct((rows, cols), BF),
+        (steps,),
+        [picked] * len(wholes) + [plain] * len(halves),
+        plain,
+        which.reshape(1).astype(jnp.int32),
+        *wholes,
+        *halves,
         prefetch=1,
     )
 
@@ -195,7 +183,7 @@
         out_ref[...] = other_ref[...]
 
 
-def place_halves(core, own, other, steps=2, rows=None):
+def place_halves(core, own, other, steps=2, rows=None, cost=1000):
     rows, width = rows or own.shape[0], own.shape[1]
     tile = rows // steps
     return call(
@@ -211,6 +199,7 @@
         own,
         other,
         prefetch=1,
+        cost=cost,
     )
 
 
@@ -324,56 +313,42 @@
 
 
 def pair_kernel(pieces, adding, _, a_ref, c_ref, *refs):
-    a, c = a_ref[...], c_ref[...]
-    outs = refs[2 * pieces + adding :]
-
-    def into(out_ref):
-        low = 0
-        for b_ref, d_ref in zip(refs[:pieces], refs[pieces : 2 * pieces]):
-            high = low + b_ref.shape[0]
-            total = dot_nt(a, b_ref[...]) + dot_nt(c, d_ref[...])
-            if adding:
-                total = total + refs[2 * pieces][:, low:high].astype(F32)
-            out_ref[:, low:high] = total.astype(BF)
-            low = high
-
-    steps = 4 // len(outs)
-    for n, out_ref in enumerate(outs):
-        pl.when(pl.program_id(0) // steps == n)(functools.partial(into, out_ref))
-
-
-def pair_dot(part, crossed, a, b, c, d, cut, got=None):
-    rows, width = a.shape[0] // 2, sum(piece.shape[0] for piece in b)
-    tile = rows // 4
-    adding = got is not None
+    a, c, out_ref = a_ref[...], c_ref[...], refs[-1]
+    low = 0
+    for b_ref, d_ref in zip(refs[:pieces], refs[pieces : 2 * pieces]):
+        high = low + b_ref.shape[0]
+        total = dot_nt(a, b_ref[...]) + dot_nt(c, d_ref[...])
+        if adding:
+            total = total + refs[2 * pieces][:, low:high].astype(F32)
+        out_ref[:, low:high] = total.astype(BF)
+        low = high
+
+
+def pair_dot(part, crossed, a, b, c, d, cut, got=None, begin=0, count=4):
+    tile, width = a.shape[0] // 8, sum(piece.shape[0] for piece in b)
+    extra = [] if got is None else [got]
 
     def row_block(i, f):
+        i = i + begin
         return part * 4 + jnp.where((f[0] == 1) & (i > 0) & (i < 3), 3 - i, i), 0
 
-    count = 2 if adding else 1
-    steps = 4 // count
-
-    def out_block(n):
-        return lambda i, f: (jnp.clip(i - n * steps, 0, steps - 1), 0)
-
-    outs = call(
-        functools.partial(pair_kernel, len(b), int(adding)),
-        [jax.ShapeDtypeStruct((rows // count, width), BF)] * count,
-        (4,),
+    return call(
+        functools.partial(pair_kernel, len(b), len(extra)),
+        jax.ShapeDtypeStruct((count * tile, width), BF),
+        (count,),
         [pl.BlockSpec((tile, a.shape[1]), row_block), pl.BlockSpec((tile, c.shape[1]), row_block)]
         + [resident(w) for w in b]
         + [pl.BlockSpec((w.shape[0], c.shape[1]), lambda i, f: (0, cut // c.shape[1])) for w in d]
-        + [pl.BlockSpec((tile, width), lambda i, f: (i, 0))] * int(adding),
-        [pl.BlockSpec((tile, width), out_block(n)) for n in range(count)],
+        + [pl.BlockSpec((tile, width), lambda i, f: (i + begin, 0))] * len(extra),
+        pl.BlockSpec((tile, width), lambda i, f: (i, 0)),
         crossed.reshape(1).astype(jnp.int32),
         a,
         c,
         *b,
         *d,
-        *([got] if adding else []),
+        *extra,
         prefetch=1,
     )
-    return outs if adding else outs[0]
 
 
 def attention_kernel(
@@ -736,12 +711,9 @@
             return total
 
         def top_send(kept, got):
-            if kept is None:
-                return None, None
             if tops > 2:
                 return add(kept, got).astype(BF), None
-            cut = kept.shape[0] // 2
-            return sum_rows(cut, (kept, 0), (got, 0)), sum_rows(cut, (kept, cut), (got, cut))
+            return half_sum(1 - zl_mine, (kept, got)), half_sum(zl_mine, (kept, got))
 
         def g_top(rest):
             if rest is None or tops == 2:
@@ -753,17 +725,18 @@
                 grad = add(grad[:cut], swap(grad[cut:], bit)).astype(BF)
             return grad
 
-        def g_split(kept, got, one, two):
-            if two is not None:
-                return split_sum(zl_mine, kept, got, one, two)
-            total = add(kept, got, one[:unit]).astype(BF)
-            return part_of(total, 1 - zl_mine, 0), part_of(total, zl_mine, 0)
-
-        def g_zl(split):
-            return split[1], swap(split[0], ZL_BIT)
-
-        def g_cross(pair):
-            return cross(zl_mine, x_mine, *pair)
+        def g_far(kept, got, one):
+            if tops > 2:
+                return part_of(add(kept, got, one[:unit]).astype(BF), 1 - zl_mine, 0)
+            return half_sum(1 - zl_mine, (kept, got), (one,))
+
+        def g_near(kept, got, one, two):
+            if tops > 2:
+                return part_of(add(kept, got, one[:unit]).astype(BF), zl_mine, 0)
+            return half_sum(zl_mine, (kept, got), (two,))
+
+        def g_cross(own, got):
+            return cross(zl_mine, x_mine, own, got)
 
         def g_x(split):
             return split[1], swap(split[0], X_BIT)
@@ -774,11 +747,18 @@
         straight = jnp.zeros((2,), jnp.int32)
         crossed = jnp.stack([core, 1 - core]).astype(jnp.int32)
 
-        def far_side(far):
-            return swap_mixed(far, (X_BIT, ZL_BIT))
-
-        def near_side(near, second):
-            return swap_mixed(sum_rows(half, (near, half), (second, half)), (ZL_BIT, X_BIT))
+        first_way, second_way = (ZL_BIT, X_BIT), (X_BIT, ZL_BIT)
+
+        def near_side(near, second, way):
+            return swap_mixed(sum_rows(half, (near, half), (second, half)), way)
+
+        def sum_over(value, bits):
+            if len(bits) == 2:
+                got = [swap(value, *way) for way in (bits[:1], bits[1:], bits)]
+                return value + got[0] + (got[1] + got[2])
+            for bit in bits:
+                value = value + swap(value, bit)
+            return value
 
         u_x = w_x(up_weight)
         n_own, c_own = norm_forward()
@@ -844,7 +824,7 @@
         d_far_rest = g_swap_y(d_rest)
         c_got_second = swap_core(c_second)
         cot = join(crossed, c_pair, c_second, c_got_pair, c_got_second)
-        gd = weight_grads(unit, (0, 1, 2), (cot, act))
+        gd = weight_grads(unit, (0, 1, 2, 3), (cot, act))
         d_far_rest, cot, gd = sync(d_far_rest, cot, gd)
         d_a = g_swap_y(gd[0])
         my_qkv_bias = lax.dynamic_slice_in_dim(qkv_bias, block * att, att, 1).astype(F32)
@@ -857,78 +837,79 @@
         d_z1 = g_top(d_z1)
         d_b = swap(gd[1], Y_BIT)
         ga = weight_grads(unit, (0, 1, 2), (normed, qkv_g), (cot, attended))
+        gd_own = gd[3]
         down_w = [w for w in (dd, d_rest, d_far, d_far_rest) if w is not None]
-        b_send = pair_dot(1, 1 - core, act, down_w, attended, att_w, 3 * att)
-        d_z1, d_z2, d_b, ga, b_send, cot, slope, act, attended = sync(
-            d_z1, d_z2, d_b, ga, b_send, cot, slope, act, attended
+        b_send = pair_dot(1, core, act, down_w, attended, att_w, 3 * att)
+        d_z1, d_z2, d_b, ga, gd_own, b_send, cot, slope, act, attended = sync(
+            d_z1, d_z2, d_b, ga, gd_own, b_send, cot, slope, act, attended
         )
         d_z2 = g_top(d_z2)
         a_a = g_swap_y(ga[0])
         b_got = swap_core(b_send)
+        d_l = swap(g_far(gd_own, d_b, d_z1), ZL_BIT)
         up_g, up_sums = up_gradient(cot, slope, down_w)
         n_send = pair_dot(1, 1 - core, up_g, up_w, qkv_g, att_w, 0)
-        b_near, b_far = pair_dot(0, core, act, down_w, attended, att_w, 3 * att, b_got)
-        d_z2, a_a, ga, b_near, b_far, up_g, n_send = sync(
-            d_z2, a_a, ga, b_near, b_far, up_g, n_send
+        b_far = pair_dot(0, 1 - core, act, down_w, attended, att_w, 3 * att, b_got, 2, 2)
+        d_z2, a_a, ga, b_got, b_far, d_l, up_g, n_send, act, attended = sync(
+            d_z2, a_a, ga, b_got, b_far, d_l, up_g, n_send, act, attended
         )
         a_z1, a_z2 = top_send(ga[2], a_a)
         a_z1 = g_top(a_z1)
         a_b = swap(ga[1], Y_BIT)
         n_got = swap_core(n_send)
-        b_second = far_side(b_far)
-        gu = weight_grads(unit, (0,), (normed, up_g))
-        n_near, n_far = pair_dot(0, core, up_g, up_w, qkv_g, att_w, 0, n_got)
-        a_z1, a_z2, a_b, gu, n_near, n_far, b_second = sync(
-            a_z1, a_z2, a_b, gu, n_near, n_far, b_second
+        b_second = swap_mixed(b_far, first_way)
+        (gu_a,) = weight_grads(unit, (0,), (normed, up_g))
+        n_far = pair_dot(0, core, up_g, up_w, qkv_g, att_w, 0, n_got, 2, 2)
+        b_near = pair_dot(0, 1 - core, act, down_w, attended, att_w, 3 * att, b_got, 0, 2)
+        a_z1, a_z2, a_b, gu_a, n_got, n_far, b_near, b_second, up_g, qkv_g = sync(
+            a_z1, a_z2, a_b, gu_a, n_got, n_far, b_near, b_second, up_g, qkv_g
         )
         a_z2 = g_top(a_z2)
-        u_a = g_swap_y(gu[0])
-        n_second = far_side(n_far)
+        u_a = g_swap_y(gu_a)
+        n_second = swap_mixed(n_far, second_way)
         gu = weight_grads(unit, (1, 2), (normed, up_g))
-        (gd_own,) = weight_grads(unit, (3,), (cot, act))
-        d_l = g_split(gd_own, d_b, d_z1, d_z2)
-        a_z2, u_a, gu, d_l, n_second, b_near, b_second, up_g, qkv_g, attended, normed, cot = sync(
-            a_z2, u_a, gu, d_l, n_second, b_near, b_second, up_g, qkv_g, attended, normed, cot
-        )
+        n_near = pair_dot(0, core, up_g, up_w, qkv_g, att_w, 0, n_got, 0, 2)
+        (ga_own,) = weight_grads(unit, (3,), (normed, qkv_g), (cot, attended))
+        a_l = g_far(ga_own, a_b, a_z1)
+        biases = jnp.concatenate([qkv_sums[0], up_sums[0]])
+        spread = lax.dynamic_update_slice(
+            jnp.zeros((4, biases.shape[0]), F32), biases[None], (block, 0)
+        )
+        a_z2, u_a, gu, ga_own, a_l, n_second, n_near, b_near, b_second, d_l, up_g, normed = sync(
+            a_z2, u_a, gu, ga_own, a_l, n_second, n_near, b_near, b_second, d_l, up_g, normed
+        )
+        spread = sync(spread, a_z2)[0]
         u_z1, u_z2 = top_send(gu[1], u_a)
         u_z1 = g_top(u_z1)
         u_b = swap(gu[0], Y_BIT)
-        n_first = near_side(n_near, n_second)
-        b_first = near_side(b_near, b_second)
-        d_l = g_zl(d_l)
-        (ga_own,) = weight_grads(unit, (3,), (normed, qkv_g), (cot, attended))
-        a_l = g_split(ga_own, a_b, a_z1, a_z2)
+        n_first = near_side(n_near, n_second, first_way)
+        b_first = near_side(b_near, b_second, second_way)
+        a_l = swap(a_l, ZL_BIT)
         (gu_own,) = weight_grads(unit, (3,), (normed, up_g))
-        u_z1, u_z2, u_b, n_first, b_first, d_l, a_l, gu_own = sync(
-            u_z1, u_z2, u_b, n_first, b_first, d_l, a_l, gu_own
+        d_x = g_cross(g_near(gd_own, d_b, d_z1, d_z2), d_l)
+        a_near = g_near(ga_own, a_b, a_z1, a_z2)
+        u_z1, u_z2, u_b, n_first, b_first, a_l, gu_own, d_x, a_near = sync(
+            u_z1, u_z2, u_b, n_first, b_first, a_l, gu_own, d_x, a_near
         )
         u_z2 = g_top(u_z2)
-        a_l = g_zl(a_l)
-        d_x = g_x(g_cross(d_l))
+        u_l = swap(g_far(gu_own, u_b, u_z1), ZL_BIT)
+        d_x = g_x(d_x)
+        a_x = g_x(g_cross(a_near, a_l))
         input_grad = norm_backward(n_near, n_second, n_first)
         result = finish(b_near, b_second, b_first)
-        biases = jnp.concatenate([qkv_sums[0], up_sums[0]])
-        spread = lax.dynamic_update_slice(
-            jnp.zeros((4, biases.shape[0]), F32), biases[None], (block, 0)
-        )
-        u_z2, a_l, d_x, input_grad, result, spread = sync(
-            u_z2, a_l, d_x, input_grad, result, spread
-        )
-        u_l = g_zl(g_split(gu_own, u_b, u_z1, u_z2))
-        a_x = g_x(g_cross(a_l))
+        u_z2, u_l, d_x, a_x, input_grad, result, spread = sync(
+            u_z2, u_l, d_x, a_x, input_grad, result, spread
+        )
+        gu = g_x(g_cross(g_near(gu_own, u_b, u_z1, u_z2), u_l))
         input_other = swap_core(input_grad)
         result_other = swap_core(result)
+        result = place_halves(core, result, result_other, cost=8 * result.size)
         lines = input_grad[half : half + 3] + input_other[half : half + 3]
         lines = jnp.concatenate([lines.reshape(-1), spread.reshape(-1)])
-        for bit in [Y_BIT] + top_bits + [X_BIT]:
-            lines = lines + swap(lines, bit)
-        u_l, a_x, input_other, result_other, lines = sync(
-            u_l, a_x, input_other, result_other, lines
-        )
-        gu = g_x(g_cross(u_l))
-        lines = lines + swap(lines, ZL_BIT)
-        result = place_halves(core, result, result_other)
-        input_grad = place_halves(core, input_grad, input_other, rows=half)
+        input_grad = place_halves(core, input_grad, input_other, rows=half, cost=16 * half * width)
+        lines = sum_over(lines, [Y_BIT] + top_bits)
+        lines, result, input_grad = sync(lines, result, input_grad)
+        lines = sum_over(lines, [X_BIT, ZL_BIT])
         ga = ordered(x_mine, *a_x, 1)
         gd = ordered(x_mine, *d_x, 1)
         gu = ordered(x_mine, *gu, 1)

time: 579 us -> 565 us (0.976)
  waiting for transfers between devices: 177 us -> 145 us
  Pallas kernels: 255 us -> 264 us
    ppermute x42 -> x44, waiting for transfers between devices: 151 us -> 132 us  [swap(): return lax.ppermute(value, 'dp', [(i, i ^ flip) for i in range(dp_size)])]
    pallas_call x35 -> x39, Pallas kernels: 246 us -> 255 us  [call(): pl.pallas_call(kernel, out_shape=outs, grid_spec=pltpu.PrefetchScalarGrid...]
    ppermute x6, waiting for transfers between devices: 17.6 us -> 10.3 us  [swap_mixed(): return lax.ppermute(value, ('dp', 'tensor'), pairs)]
    ppermute x42 -> x44, starting transfers between devices: 49.4 us -> 50.4 us  [swap(): return lax.ppermute(value, 'dp', [(i, i ^ flip) for i in range(dp_size)])]
    unnamed x90 -> x94, local copies, waits for them, and re-layouts: 25.7 us -> 26.4 us
  transfers between devices with their start and end apart: 56 -> 58, of which waited for: 17 -> 17; matrix products, arithmetic and copies ran while one was open for 8% -> 11% of each run, Pallas kernels for 45% -> 46%
where the time goes in v6:
time: 565 us; the launch traced here: 556 us
  Pallas kernels  264 us (47%)
  waiting for transfers between devices  145 us (26%)
  local copies, waits for them, and re-layouts  61.3 us (11%)
  starting transfers between devices  57.8 us (10%)
  other arithmetic  25.5 us (5%)
    pallas_call x39, Pallas kernels, call(): pl.pallas_call(kernel, out_shape=outs, grid_spec=pltpu.PrefetchScalarGrid...  255 us
    ppermute x44, waiting for transfers between devices, swap(): return lax.ppermute(value, 'dp', [(i, i ^ flip) for i in range(dp_size)])  132 us
    ppermute x44, starting transfers between devices, swap(): return lax.ppermute(value, 'dp', [(i, i ^ flip) for i in range(dp_size)])  50.4 us
    unnamed x94, local copies, waits for them, and re-layouts  26.4 us
  transfers between devices with their start and end apart: 58, of which 17 were waited for; matrix products, arithmetic and copies ran while one was open for 11% of the time, Pallas kernels for 46%

profile of v6, /device:TPU:0, one launch (start us, length us, event | category | flops | bytes accessed | tf_op | source)
XLA Modules:
  0.0 555.5 jit_solution(4296032517615391408)
XLA Ops:
  38.5 11.0 %collective-permute-done.4.other_ref = bf16[256,1024]{1,0:T(8,128)(2,1)} collective-permute-done((bf16[256,1024]{1,0:T(8,128)(2,1)}, bf16[256,1024]{1,0:T(8,128)(2,1)}, u32[]{:S(2)}, u32[]{:S(2)}) %collective-permute-start.4) | collective-permute-done | bytes 524320 | tf_op jit(solution)/shard_map/ppermute | solution.py:564
  70.3 28.2 %collective-permute-done.12.other_ref = bf16[256,1024]{1,0:T(8,128)(2,1)} collective-permute-done((bf16[256,1024]{1,0:T(8,128)(2,1)}, bf16[256,1024]{1,0:T(8,128)(2,1)}, u32[]{:S(2)}, u32[]{:S(2)}) %collective-permute-start.12) | collective-permute-done | bytes 524320 | tf_op jit(solution)/shard_map/ppermute | solution.py:564
  100.7 9.7 %collective-permute-done.8.refs_1_ = bf16[512,1024]{1,0:T(8,128)(2,1)} collective-permute-done((bf16[512,1024]{1,0:T(8,128)(2,1)}, bf16[512,1024]{1,0:T(8,128)(2,1)}, u32[]{:S(2)}, u32[]{:S(2)}) %collective-permute-start.8) | collective-permute-done | bytes 1048608 | tf_op jit(solution)/shard_map/ppermute | solution.py:564
  118.4 21.2 %collective-permute-done.16.other_ref = bf16[256,1024]{1,0:T(8,128)(2,1)} collective-permute-done((bf16[256,1024]{1,0:T(8,128)(2,1)}, bf16[256,1024]{1,0:T(8,128)(2,1)}, u32[]{:S(2)}, u32[]{:S(2)}) %collective-permute-start.16) | collective-permute-done | bytes 524320 | tf_op jit(solution)/shard_map/ppermute | solution.py:564
  143.3 5.8 %fusion.2 = (f32[2048,128]{1,0:T(8,128)}, f32[2048,128]{1,0:T(8,128)}, f32[2048,128]{1,0:T(8,128)}) fusion(f32[128]{0:T(128)S(1)} %fusion.15, f32[2048]{0:T(1024)S(1)} %bitcast.106, pred[128]{0:T(512)(128)(4,1)S(1)} %get-tuple-element.410, pred[128]{0:T(512)(128)(4,1)S(1)} %broadcast_compare_fusion.2, pred[128]{0:T(512)(128)(4,1)S(1)} %get-tuple-element.411), kind=kLoop, calls=%fused_computation.6 | loop fusion | flops 1572864 | bytes 3154816 | tf_op jit(solution)/shard_map/jit(_where)/select_n | solution.py:463
  151.3 9.1 %collective-permute-done.17 = bf16[256,2048]{1,0:T(8,128)(2,1)} collective-permute-done((bf16[256,2048]{1,0:T(8,128)(2,1)S(1)}, bf16[256,2048]{1,0:T(8,128)(2,1)}, u32[]{:S(2)}, u32[]{:S(2)}) %collective-permute-start.17) | collective-permute-done | bytes 1048608 | tf_op jit(solution)/shard_map/ppermute | solution.py:571
  160.5 4.2 collective-permute-done.13.refs_3_
  174.1 10.7 %shard_map.207.rows_ref.refs_0_ = bf16[2048,2048]{1,0:T(8,128)(2,1)} custom-call(s32[2]{0:T(128)} %broadcast_10_flags_ref.2.flags_ref, bf16[512,2048]{1,0:T(8,128)(2,1)} %constant_dynamic-update-slice_fusion.pair_ref, bf16[512,2048]{1,0:T(8,128)(2,1)} %collective-permute-done.10.second_ref, bf16[512,2048]{1,0:T(8,128)(2,1)} %collective-permute-done.11.got_pair_ref, ...), custom_call_target="tpu_custom_call" | custom-call | flops 1000 | bytes 1000 | tf_op jit(solution)/shard_map/pallas_call | solution.py:35
  184.8 17.3 %shard_map.208 = (bf16[2048,1024]{1,0:T(8,128)(2,1)}, bf16[2048,1024]{1,0:T(8,128)(2,1)}) custom-call(bf16[2048,2048]{1,0:T(8,128)(2,1)} %shard_map.207.rows_ref.refs_0_, f32[1,1024]{1,0:T(1,128)} %bitcast.111, bf16[512,1024]{1,0:T(8,128)(2,1)} %shard_map.204.refs_0_, bf16[512,1024]{1,0:T(8,128)(2,1)} %collective-permute-done.8.refs_1_, ...), custom_call_target="tpu_custom_call" | custom-call | flops 1000 | bytes 1000 | tf_op jit(solution)/shard_map/pallas_call | solution.py:35
  202.1 16.7 %collective-permute-done.19.refs_1_ = bf16[512,1024]{1,0:T(8,128)(2,1)} collective-permute-done((bf16[512,1024]{1,0:T(8,128)(2,1)}, bf16[512,1024]{1,0:T(8,128)(2,1)}, u32[]{:S(2)}, u32[]{:S(2)}) %collective-permute-start.19) | collective-permute-done | bytes 1048608 | tf_op jit(solution)/shard_map/ppermute | solution.py:564
  223.4 10.7 %shard_map.209.refs_0_.refs_2_.rows_ref = bf16[2048,2048]{1,0:T(8,128)(2,1)} custom-call(s32[2]{0:T(128)} %pad_add_fusion.3.flags_ref, bf16[512,2048]{1,0:T(8,128)(2,1)} %constant_dynamic-update-slice_fusion.2.pair_ref, bf16[512,2048]{1,0:T(8,128)(2,1)} %collective-permute-done.22.second_ref, bf16[512,2048]{1,0:T(8,128)(2,1)} %collective-permute-done.23.got_pair_ref, ...), custom_call_target="tpu_custom_call" | custom-call | flops 1000 | bytes 1000 | tf_op jit(solution)/shard_map/pallas_call | solution.py:35
  234.1 14.8 %shard_map.210 = (bf16[512,1024]{1,0:T(8,128)(2,1)}, bf16[512,1024]{1,0:T(8,128)(2,1)}, bf16[512,1024]{1,0:T(8,128)(2,1)}, bf16[512,1024]{1,0:T(8,128)(2,1)}) custom-call(bf16[2048,2048]{1,0:T(8,128)(2,1)} %shard_map.209.refs_0_.refs_2_.rows_ref, bf16[2048,1024]{1,0:T(8,128)(2,1)} %get-tuple-element.249.refs_1_.a_ref), custom_call_target="tpu_custom_call" | custom-call | flops 1000 | bytes 1000 | tf_op jit(solution)/shard_map/pallas_call | solution.py:35
  251.1 34.3 %shard_map.211 = (bf16[2,4,256,256]{3,2,1,0:T(8,128)(2,1)}, bf16[2,4,256,768]{3,2,1,0:T(8,128)(2,1)}, f32[8,768]{1,0:T(8,128)}) custom-call(bf16[2,4,256,2048]{3,2,1,0:T(8,128)(2,1)} %bitcast.82, bf16[2,4,256,2048]{3,2,1,0:T(8,128)(2,1)} %bitcast.83, f32[1,768]{1,0:T(1,128)} %bitcast.115, f32[2,4,256,128]{3,2,1,0:T(8,128)} %bitcast.97, ...), custom_call_target="tpu_custom_call" | custom-call | flops 1000 | bytes 1000 | tf_op jit(solution)/shard_map/pallas_call | solution.py:35
  290.6 12.5 %shard_map.214 = (bf16[512,1024]{1,0:T(8,128)(2,1)}, bf16[512,1024]{1,0:T(8,128)(2,1)}, bf16[512,1024]{1,0:T(8,128)(2,1)}) custom-call(bf16[2048,2048]{1,0:T(8,128)(2,1)} %shard_map.207.rows_ref.refs_0_, bf16[2048,768]{1,0:T(8,128)(2,1)} %bitcast.84, bf16[2048,2048]{1,0:T(8,128)(2,1)} %shard_map.209.refs_0_.refs_2_.rows_ref, bf16[2048,256]{1,0:T(8,128)(2,1)} %bitcast.89), custom_call_target="tpu_custom_call" | custom-call | flops 1000 | bytes 1000 | tf_op jit(solution)/shard_map/pallas_call | solution.py:35
  303.1 10.2 %shard_map.215 = bf16[1024,2048]{1,0:T(8,128)(2,1)} custom-call(s32[1]{0:T(128)} %bitcast.2._.core_ref, bf16[2048,1024]{1,0:T(8,128)(2,1)} %get-tuple-element.249.refs_1_.a_ref, bf16[2048,256]{1,0:T(8,128)(2,1)} %bitcast.90, bf16[512,1024]{1,0:T(8,128)(2,1)} %shard_map.206.refs_0_, bf16[512,1024]{1,0:T(8,128)(2,1)} %collective-permute-done.19.refs_1_, ...), custom_call_target="tpu_custom_call" | custom-call | flops 1000 | bytes 1000 | tf_op jit(solution)/shard_map/pallas_call | solution.py:35
  319.6 14.6 %shard_map.218 = (bf16[2048,1024]{1,0:T(8,128)(2,1)}, f32[8,1024]{1,0:T(8,128)}) custom-call(bf16[2048,2048]{1,0:T(8,128)(2,1)} %shard_map.209.refs_0_.refs_2_.rows_ref, bf16[2048,1024]{1,0:T(8,128)(2,1)} %get-tuple-element.242.slope_ref, bf16[512,1024]{1,0:T(8,128)(2,1)} %shard_map.206.refs_0_, bf16[512,1024]{1,0:T(8,128)(2,1)} %collective-permute-done.19.refs_1_, ...), custom_call_target="tpu_custom_call" | custom-call | flops 1000 | bytes 1000 | tf_op jit(solution)/shard_map/pallas_call | solution.py:35
  334.2 13.0 %shard_map.219 = bf16[1024,2048]{1,0:T(8,128)(2,1)} custom-call(s32[1]{0:T(128)} %bitcast.23._, bf16[2048,1024]{1,0:T(8,128)(2,1)} %get-tuple-element.275.a_ref.refs_1_, bf16[2048,768]{1,0:T(8,128)(2,1)} %bitcast.85, bf16[512,1024]{1,0:T(8,128)(2,1)} %shard_map.204.refs_0_, bf16[512,1024]{1,0:T(8,128)(2,1)} %collective-permute-done.8.refs_1_, ...), custom_call_target="tpu_custom_call" | custom-call | flops 1000 | bytes 1000 | tf_op jit(solution)/shard_map/pallas_call | solution.py:35
  349.2 7.2 %shard_map.216 = bf16[512,2048]{1,0:T(8,128)(2,1)} custom-call(s32[1]{0:T(128)} %bitcast.23._, bf16[2048,1024]{1,0:T(8,128)(2,1)} %get-tuple-element.249.refs_1_.a_ref, bf16[2048,256]{1,0:T(8,128)(2,1)} %bitcast.91, bf16[512,1024]{1,0:T(8,128)(2,1)} %shard_map.206.refs_0_, bf16[512,1024]{1,0:T(8,128)(2,1)} %collective-permute-done.19.refs_1_, ...), custom_call_target="tpu_custom_call" | custom-call | flops 1000 | bytes 1000 | tf_op jit(solution)/shard_map/pallas_call | solution.py:35
  366.1 6.2 %shard_map.222 = bf16[512,1024]{1,0:T(8,128)(2,1)} custom-call(bf16[2048,2048]{1,0:T(8,128)(2,1)} %shard_map.207.rows_ref.refs_0_, bf16[2048,1024]{1,0:T(8,128)(2,1)} %get-tuple-element.275.a_ref.refs_1_), custom_call_target="tpu_custom_call" | custom-call | flops 1000 | bytes 1000 | tf_op jit(solution)/shard_map/pallas_call | solution.py:35
  372.2 7.2 %shard_map.224.refs_0_ = bf16[512,2048]{1,0:T(8,128)(2,1)} custom-call(s32[1]{0:T(128)} %bitcast.23._, bf16[2048,1024]{1,0:T(8,128)(2,1)} %get-tuple-element.249.refs_1_.a_ref, bf16[2048,256]{1,0:T(8,128)(2,1)} %bitcast.92, bf16[512,1024]{1,0:T(8,128)(2,1)} %shard_map.206.refs_0_, bf16[512,1024]{1,0:T(8,128)(2,1)} %collective-permute-done.19.refs_1_, ...), custom_call_target="tpu_custom_call" | custom-call | flops 1000 | bytes 1000 | tf_op jit(solution)/shard_map/pallas_call | solution.py:35
  381.5 9.0 %shard_map.223 = bf16[512,2048]{1,0:T(8,128)(2,1)} custom-call(s32[1]{0:T(128)} %bitcast.2._.core_ref, bf16[2048,1024]{1,0:T(8,128)(2,1)} %get-tuple-element.275.a_ref.refs_1_, bf16[2048,768]{1,0:T(8,128)(2,1)} %bitcast.86, bf16[512,1024]{1,0:T(8,128)(2,1)} %shard_map.204.refs_0_, bf16[512,1024]{1,0:T(8,128)(2,1)} %collective-permute-done.8.refs_1_, ...), custom_call_target="tpu_custom_call" | custom-call | flops 1000 | bytes 1000 | tf_op jit(solution)/shard_map/pallas_call | solution.py:35
  390.5 8.1 %collective-permute-done.33.refs_2_ = bf16[256,1024]{1,0:T(8,128)(2,1)S(1)} collective-permute-done((bf16[256,1024]{1,0:T(8,128)(2,1)}, bf16[256,1024]{1,0:T(8,128)(2,1)S(1)}, u32[]{:S(2)}, u32[]{:S(2)}) %collective-permute-start.33) | collective-permute-done | bytes 524320 | tf_op jit(solution)/shard_map/ppermute | solution.py:564
  400.8 4.6 collective-permute-start.37
  405.4 6.8 %shard_map.226.refs_0_ = bf16[512,1024]{1,0:T(8,128)(2,1)} custom-call(bf16[2048,2048]{1,0:T(8,128)(2,1)} %shard_map.207.rows_ref.refs_0_, bf16[2048,768]{1,0:T(8,128)(2,1)} %bitcast.87, bf16[2048,2048]{1,0:T(8,128)(2,1)} %shard_map.209.refs_0_.refs_2_.rows_ref, bf16[2048,256]{1,0:T(8,128)(2,1)} %bitcast.93), custom_call_target="tpu_custom_call" | custom-call | flops 1000 | bytes 1000 | tf_op jit(solution)/shard_map/pallas_call | solution.py:35
  412.1 9.0 %shard_map.225 = (bf16[512,1024]{1,0:T(8,128)(2,1)}, bf16[512,1024]{1,0:T(8,128)(2,1)}) custom-call(bf16[2048,2048]{1,0:T(8,128)(2,1)} %shard_map.207.rows_ref.refs_0_, bf16[2048,1024]{1,0:T(8,128)(2,1)} %get-tuple-element.275.a_ref.refs_1_), custom_call_target="tpu_custom_call" | custom-call | flops 1000 | bytes 1000 | tf_op jit(solution)/shard_map/pallas_call | solution.py:35
  421.2 9.0 %shard_map.228.refs_0_ = bf16[512,2048]{1,0:T(8,128)(2,1)} custom-call(s32[1]{0:T(128)} %bitcast.2._.core_ref, bf16[2048,1024]{1,0:T(8,128)(2,1)} %get-tuple-element.275.a_ref.refs_1_, bf16[2048,768]{1,0:T(8,128)(2,1)} %bitcast.88, bf16[512,1024]{1,0:T(8,128)(2,1)} %shard_map.204.refs_0_, bf16[512,1024]{1,0:T(8,128)(2,1)} %collective-permute-done.8.refs_1_, ...), custom_call_target="tpu_custom_call" | custom-call | flops 1000 | bytes 1000 | tf_op jit(solution)/shard_map/pallas_call | solution.py:35
  453.5 6.2 %shard_map.233.refs_0_ = bf16[512,1024]{1,0:T(8,128)(2,1)} custom-call(bf16[2048,2048]{1,0:T(8,128)(2,1)} %shard_map.207.rows_ref.refs_0_, bf16[2048,1024]{1,0:T(8,128)(2,1)} %get-tuple-element.275.a_ref.refs_1_), custom_call_target="tpu_custom_call" | custom-call | flops 1000 | bytes 1000 | tf_op jit(solution)/shard_map/pallas_call | solution.py:35
  462.6 12.8 %collective-permute-done.40.refs_2_ = bf16[256,1024]{1,0:T(8,128)(2,1)S(1)} collective-permute-done((bf16[256,1024]{1,0:T(8,128)(2,1)}, bf16[256,1024]{1,0:T(8,128)(2,1)S(1)}, u32[]{:S(2)}, u32[]{:S(2)}) %collective-permute-start.40) | collective-permute-done | bytes 524320 | tf_op jit(solution)/shard_map/ppermute | solution.py:564
  475.4 14.1 %collective-permute-done.44.got_ref = bf16[256,1024]{1,0:T(8,128)(2,1)S(1)} collective-permute-done((bf16[256,1024]{1,0:T(8,128)(2,1)S(1)}, bf16[256,1024]{1,0:T(8,128)(2,1)S(1)}, u32[]{:S(2)}, u32[]{:S(2)}) %collective-permute-start.44) | collective-permute-done | bytes 524320 | tf_op jit(solution)/shard_map/ppermute | solution.py:564
  504.2 4.5 shard_map.239.own_ref
  536.0 4.1 shard_map.241
  540.1 5.3 shard_map.242
  (305 shorter events, 195.8 us)
Async XLA Ops:
  14.2 39.7 %collective-permute-start.5 = (bf16[256,2048]{1,0:T(8,128)(2,1)}, bf16[256,2048]{1,0:T(8,128)(2,1)}, u32[]{:S(2)}, u32[]{:S(2)}) collective-permute-start(bf16[256,2048]{1,0:T(8,128)(2,1)} %get-tuple-element.171), channel_id=1, source_target_pairs={{0,8},{2,10},{4,12},{6,14},{8,0},{10,2},{12,4},{14,6},{16,24},{18,... | collective-permute-start | bytes 3145736 | tf_op jit(solution)/shard_map/ppermute | solution.py:564
  58.6 51.7 %collective-permute-start.11 = (bf16[512,2048]{1,0:T(8,128)(2,1)}, bf16[512,2048]{1,0:T(8,128)(2,1)}, u32[]{:S(2)}, u32[]{:S(2)}) collective-permute-start(bf16[512,2048]{1,0:T(8,128)(2,1)} %constant_dynamic-update-slice_fusion.pair_ref), channel_id=1, source_target_pairs={{0,1},{1,0},{2,3},{3,2},{4,5},{5,4},{6,7},{7,6},{8,9},{9,8},{10,11... | collective-permute-start | bytes 6291464 | tf_op jit(solution)/shard_map/ppermute | solution.py:567
  58.6 51.7 %collective-permute-start.10 = (bf16[512,2048]{1,0:T(8,128)(2,1)}, bf16[512,2048]{1,0:T(8,128)(2,1)}, u32[]{:S(2)}, u32[]{:S(2)}) collective-permute-start(bf16[512,2048]{1,0:T(8,128)(2,1)} %constant_dynamic-update-slice_fusion.pair_ref), channel_id=1, source_target_pairs={{0,2},{2,0},{4,6},{6,4},{8,10},{10,8},{12,14},{14,12},{16,18},{18,... | collective-permute-start | bytes 6291464 | tf_op jit(solution)/shard_map/ppermute | solution.py:564
  60.2 40.5 %collective-permute-start.9 = (bf16[512,1024]{1,0:T(8,128)(2,1)}, bf16[512,1024]{1,0:T(8,128)(2,1)}, u32[]{:S(2)}, u32[]{:S(2)}) collective-permute-start(bf16[512,1024]{1,0:T(8,128)(2,1)} %shard_map.204.refs_0_), channel_id=1, source_target_pairs={{0,4},{2,6},{4,0},{6,2},{8,12},{10,14},{12,8},{14,10},{16,20},{18,... | collective-permute-start | bytes 3145736 | tf_op jit(solution)/shard_map/ppermute | solution.py:564
  61.7 48.6 %collective-permute-start.8 = (bf16[512,1024]{1,0:T(8,128)(2,1)}, bf16[512,1024]{1,0:T(8,128)(2,1)}, u32[]{:S(2)}, u32[]{:S(2)}) collective-permute-start(bf16[512,1024]{1,0:T(8,128)(2,1)} %shard_map.204.refs_0_), channel_id=1, source_target_pairs={{0,16},{2,18},{4,20},{6,22},{8,24},{10,26},{12,28},{14,30},{16,0},... | collective-permute-start | bytes 3145736 | tf_op jit(solution)/shard_map/ppermute | solution.py:564
  66.9 31.6 %collective-permute-start.12 = (bf16[256,1024]{1,0:T(8,128)(2,1)}, bf16[256,1024]{1,0:T(8,128)(2,1)}, u32[]{:S(2)}, u32[]{:S(2)}) collective-permute-start(bf16[256,1024]{1,0:T(8,128)(2,1)} %get-tuple-element.390), channel_id=1, source_target_pairs={{0,8},{2,10},{4,12},{6,14},{8,0},{10,2},{12,4},{14,6},{16,24},{18,... | collective-permute-start | bytes 1572872 | tf_op jit(solution)/shard_map/ppermute | solution.py:564
  110.4 54.3 %collective-permute-start.18 = (bf16[512,2048]{1,0:T(8,128)(2,1)}, bf16[512,2048]{1,0:T(8,128)(2,1)}, u32[]{:S(2)}, u32[]{:S(2)}) collective-permute-start(bf16[512,2048]{1,0:T(8,128)(2,1)} %collective-permute-done.10.second_ref), channel_id=1, source_target_pairs={{0,1},{1,0},{2,3},{3,2},{4,5},{5,4},{6,7},{7,6},{8,9},{9,8},{10,11... | collective-permute-start | bytes 6291464 | tf_op jit(solution)/shard_map/ppermute | solution.py:567
  114.5 50.2 %collective-permute-start.15 = (bf16[512,1024]{1,0:T(8,128)(2,1)}, bf16[512,1024]{1,0:T(8,128)(2,1)}, u32[]{:S(2)}, u32[]{:S(2)}) collective-permute-start(bf16[512,1024]{1,0:T(8,128)(2,1)} %shard_map.205.refs_0_.refs_4_), channel_id=1, source_target_pairs={{0,4},{2,6},{4,0},{6,2},{8,12},{10,14},{12,8},{14,10},{16,20},{18,... | collective-permute-start | bytes 3145736 | tf_op jit(solution)/shard_map/ppermute | solution.py:564
  115.1 49.6 %collective-permute-start.14 = (bf16[512,1024]{1,0:T(8,128)(2,1)}, bf16[512,1024]{1,0:T(8,128)(2,1)}, u32[]{:S(2)}, u32[]{:S(2)}) collective-permute-start(bf16[512,1024]{1,0:T(8,128)(2,1)} %shard_map.205.refs_0_.refs_4_), channel_id=1, source_target_pairs={{0,16},{2,18},{4,20},{6,22},{8,24},{10,26},{12,28},{14,30},{16,0},... | collective-permute-start | bytes 3145736 | tf_op jit(solution)/shard_map/ppermute | solution.py:564
  118.3 42.2 %collective-permute-start.17 = (bf16[256,2048]{1,0:T(8,128)(2,1)S(1)}, bf16[256,2048]{1,0:T(8,128)(2,1)}, u32[]{:S(2)}, u32[]{:S(2)}) collective-permute-start(bf16[256,2048]{1,0:T(8,128)(2,1)S(1)} %get-tuple-element.187), channel_id=1, source_target_pairs={{0,8},{1,3},{2,10},{3,1},{4,12},{5,7},{6,14},{7,5},{8,0},{9,11},{1... | collective-permute-start | bytes 3145736 | tf_op jit(solution)/shard_map/ppermute | solution.py:571
  168.7 50.1 %collective-permute-start.23 = (bf16[512,2048]{1,0:T(8,128)(2,1)}, bf16[512,2048]{1,0:T(8,128)(2,1)}, u32[]{:S(2)}, u32[]{:S(2)}) collective-permute-start(bf16[512,2048]{1,0:T(8,128)(2,1)} %constant_dynamic-update-slice_fusion.2.pair_ref), channel_id=1, source_target_pairs={{0,1},{1,0},{2,3},{3,2},{4,5},{5,4},{6,7},{7,6},{8,9},{9,8},{10,11... | collective-permute-start | bytes 6291464 | tf_op jit(solution)/shard_map/ppermute | solution.py:567
  168.7 50.1 %collective-permute-start.22 = (bf16[512,2048]{1,0:T(8,128)(2,1)}, bf16[512,2048]{1,0:T(8,128)(2,1)}, u32[]{:S(2)}, u32[]{:S(2)}) collective-permute-start(bf16[512,2048]{1,0:T(8,128)(2,1)} %constant_dynamic-update-slice_fusion.2.pair_ref), channel_id=1, source_target_pairs={{0,2},{1,9},{2,0},{3,11},{4,6},{5,13},{6,4},{7,15},{8,10},{9,1},{1... | collective-permute-start | bytes 6291464 | tf_op jit(solution)/shard_map/ppermute | solution.py:571
  169.2 32.9 %collective-permute-start.20 = (bf16[512,1024]{1,0:T(8,128)(2,1)}, bf16[512,1024]{1,0:T(8,128)(2,1)}, u32[]{:S(2)}, u32[]{:S(2)}) collective-permute-start(bf16[512,1024]{1,0:T(8,128)(2,1)} %shard_map.206.refs_0_), channel_id=1, source_target_pairs={{0,4},{2,6},{4,0},{6,2},{8,12},{10,14},{12,8},{14,10},{16,20},{18,... | collective-permute-start | bytes 3145736 | tf_op jit(solution)/shard_map/ppermute | solution.py:564
  170.4 48.4 %collective-permute-start.19 = (bf16[512,1024]{1,0:T(8,128)(2,1)}, bf16[512,1024]{1,0:T(8,128)(2,1)}, u32[]{:S(2)}, u32[]{:S(2)}) collective-permute-start(bf16[512,1024]{1,0:T(8,128)(2,1)} %shard_map.206.refs_0_), channel_id=1, source_target_pairs={{0,16},{2,18},{4,20},{6,22},{8,24},{10,26},{12,28},{14,30},{16,0},... | collective-permute-start | bytes 3145736 | tf_op jit(solution)/shard_map/ppermute | solution.py:564
  170.8 48.0 %collective-permute-start.21 = (bf16[512,1024]{1,0:T(8,128)(2,1)}, bf16[512,1024]{1,0:T(8,128)(2,1)S(1)}, u32[]{:S(2)}, u32[]{:S(2)}) collective-permute-start(bf16[512,1024]{1,0:T(8,128)(2,1)} %collective-permute-done.14.refs_1_.refs_5_), channel_id=1, source_target_pairs={{0,4},{2,6},{4,0},{6,2},{8,12},{10,14},{12,8},{14,10},{16,20},{18,... | collective-permute-start | bytes 3145736 | tf_op jit(solution)/shard_map/ppermute | solution.py:564
  218.9 30.0 %collective-permute-start.24 = (bf16[512,1024]{1,0:T(8,128)(2,1)}, bf16[512,1024]{1,0:T(8,128)(2,1)}, u32[]{:S(2)}, u32[]{:S(2)}) collective-permute-start(bf16[512,1024]{1,0:T(8,128)(2,1)} %collective-permute-done.19.refs_1_), channel_id=1, source_target_pairs={{0,4},{2,6},{4,0},{6,2},{8,12},{10,14},{12,8},{14,10},{16,20},{18,... | collective-permute-start | bytes 3145736 | tf_op jit(solution)/shard_map/ppermute | solution.py:564
  248.9 36.5 %collective-permute-start.26 = (bf16[512,1024]{1,0:T(8,128)(2,1)}, bf16[512,1024]{1,0:T(8,128)(2,1)S(1)}, u32[]{:S(2)}, u32[]{:S(2)}) collective-permute-start(bf16[512,1024]{1,0:T(8,128)(2,1)} %get-tuple-element.203), channel_id=1, source_target_pairs={{0,4},{2,6},{4,0},{6,2},{8,12},{10,14},{12,8},{14,10},{16,20},{18,... | collective-permute-start | bytes 3145736 | tf_op jit(solution)/shard_map/ppermute | solution.py:564
  314.1 33.1 %collective-permute-start.31 = (bf16[1024,2048]{1,0:T(8,128)(2,1)}, bf16[1024,2048]{1,0:T(8,128)(2,1)S(1)}, u32[]{:S(2)}, u32[]{:S(2)}) collective-permute-start(bf16[1024,2048]{1,0:T(8,128)(2,1)} %shard_map.215), channel_id=1, source_target_pairs={{0,1},{1,0},{2,3},{3,2},{4,5},{5,4},{6,7},{7,6},{8,9},{9,8},{10,11... | collective-permute-start | bytes 12582920 | tf_op jit(solution)/shard_map/ppermute | solution.py:567
  314.2 43.9 %collective-permute-start.30 = (bf16[512,1024]{1,0:T(8,128)(2,1)S(1)}, bf16[512,1024]{1,0:T(8,128)(2,1)}, u32[]{:S(2)}, u32[]{:S(2)}) collective-permute-start(bf16[512,1024]{1,0:T(8,128)(2,1)S(1)} %copy-done.40), channel_id=1, source_target_pairs={{0,4},{2,6},{4,0},{6,2},{8,12},{10,14},{12,8},{14,10},{16,20},{18,... | collective-permute-start | bytes 3145736 | tf_op jit(solution)/shard_map/ppermute | solution.py:564
  317.6 38.9 %collective-permute-start.32 = (bf16[256,1024]{1,0:T(8,128)(2,1)}, bf16[256,1024]{1,0:T(8,128)(2,1)S(1)}, u32[]{:S(2)}, u32[]{:S(2)}) collective-permute-start(bf16[256,1024]{1,0:T(8,128)(2,1)} %shard_map.217), channel_id=1, source_target_pairs={{0,8},{2,10},{4,12},{6,14},{8,0},{10,2},{12,4},{14,6},{16,24},{18,... | collective-permute-start | bytes 1572872 | tf_op jit(solution)/shard_map/ppermute | solution.py:564
  319.4 37.0 %collective-permute-start.29 = (bf16[256,1024]{1,0:T(8,128)(2,1)S(1)}, bf16[256,1024]{1,0:T(8,128)(2,1)S(1)}, u32[]{:S(2)}, u32[]{:S(2)}) collective-permute-start(bf16[256,1024]{1,0:T(8,128)(2,1)S(1)} %copy-done.30), channel_id=1, source_target_pairs={{0,16},{2,18},{4,20},{6,22},{8,24},{10,26},{12,28},{14,30},{16,0},... | collective-permute-start | bytes 1572872 | tf_op jit(solution)/shard_map/ppermute | solution.py:564
  358.1 41.7 %collective-permute-start.36 = (bf16[512,2048]{1,0:T(8,128)(2,1)}, bf16[512,2048]{1,0:T(8,128)(2,1)S(1)}, u32[]{:S(2)}, u32[]{:S(2)}) collective-permute-start(bf16[512,2048]{1,0:T(8,128)(2,1)} %shard_map.216), channel_id=1, source_target_pairs={{0,8},{1,3},{2,10},{3,1},{4,12},{5,7},{6,14},{7,5},{8,0},{9,11},{1... | collective-permute-start | bytes 6291464 | tf_op jit(solution)/shard_map/ppermute | solution.py:571
  359.9 38.6 %collective-permute-start.34 = (bf16[512,1024]{1,0:T(8,128)(2,1)}, bf16[512,1024]{1,0:T(8,128)(2,1)S(1)}, u32[]{:S(2)}, u32[]{:S(2)}) collective-permute-start(bf16[512,1024]{1,0:T(8,128)(2,1)} %get-tuple-element.246), channel_id=1, source_target_pairs={{0,4},{2,6},{4,0},{6,2},{8,12},{10,14},{12,8},{14,10},{16,20},{18,... | collective-permute-start | bytes 3145736 | tf_op jit(solution)/shard_map/ppermute | solution.py:564
  363.0 35.5 %collective-permute-start.33 = (bf16[256,1024]{1,0:T(8,128)(2,1)}, bf16[256,1024]{1,0:T(8,128)(2,1)S(1)}, u32[]{:S(2)}, u32[]{:S(2)}) collective-permute-start(bf16[256,1024]{1,0:T(8,128)(2,1)} %shard_map.220), channel_id=1, source_target_pairs={{0,16},{2,18},{4,20},{6,22},{8,24},{10,26},{12,28},{14,30},{16,0},... | collective-permute-start | bytes 1572872 | tf_op jit(solution)/shard_map/ppermute | solution.py:564
  399.7 32.7 %collective-permute-start.39 = (bf16[512,2048]{1,0:T(8,128)(2,1)}, bf16[512,2048]{1,0:T(8,128)(2,1)S(1)}, u32[]{:S(2)}, u32[]{:S(2)}) collective-permute-start(bf16[512,2048]{1,0:T(8,128)(2,1)} %shard_map.223), channel_id=1, source_target_pairs={{0,2},{1,9},{2,0},{3,11},{4,6},{5,13},{6,4},{7,15},{8,10},{9,1},{1... | collective-permute-start | bytes 6291464 | tf_op jit(solution)/shard_map/ppermute | solution.py:571
  399.7 32.6 %collective-permute-start.38 = (bf16[512,1024]{1,0:T(8,128)(2,1)}, bf16[512,1024]{1,0:T(8,128)(2,1)S(1)}, u32[]{:S(2)}, u32[]{:S(2)}) collective-permute-start(bf16[512,1024]{1,0:T(8,128)(2,1)} %shard_map.222), channel_id=1, source_target_pairs={{0,4},{2,6},{4,0},{6,2},{8,12},{10,14},{12,8},{14,10},{16,20},{18,... | collective-permute-start | bytes 3145736 | tf_op jit(solution)/shard_map/ppermute | solution.py:564
  400.8 31.6 %collective-permute-start.37 = (bf16[256,1024]{1,0:T(8,128)(2,1)}, bf16[256,1024]{1,0:T(8,128)(2,1)S(1)}, u32[]{:S(2)}, u32[]{:S(2)}) collective-permute-start(bf16[256,1024]{1,0:T(8,128)(2,1)} %shard_map.221), channel_id=1, source_target_pairs={{0,16},{2,18},{4,20},{6,22},{8,24},{10,26},{12,28},{14,30},{16,0},... | collective-permute-start | bytes 1572872 | tf_op jit(solution)/shard_map/ppermute | solution.py:564
  436.2 53.3 %collective-permute-start.43 = (bf16[256,2048]{1,0:T(8,128)(2,1)}, bf16[256,2048]{1,0:T(8,128)(2,1)S(1)}, u32[]{:S(2)}, u32[]{:S(2)}) collective-permute-start(bf16[256,2048]{1,0:T(8,128)(2,1)} %shard_map.232), channel_id=1, source_target_pairs={{0,2},{1,9},{2,0},{3,11},{4,6},{5,13},{6,4},{7,15},{8,10},{9,1},{1... | collective-permute-start | bytes 3145736 | tf_op jit(solution)/shard_map/ppermute | solution.py:571
  441.0 48.5 %collective-permute-start.42 = (bf16[256,2048]{1,0:T(8,128)(2,1)}, bf16[256,2048]{1,0:T(8,128)(2,1)S(1)}, u32[]{:S(2)}, u32[]{:S(2)}) collective-permute-start(bf16[256,2048]{1,0:T(8,128)(2,1)} %shard_map.231), channel_id=1, source_target_pairs={{0,8},{1,3},{2,10},{3,1},{4,12},{5,7},{6,14},{7,5},{8,0},{9,11},{1... | collective-permute-start | bytes 3145736 | tf_op jit(solution)/shard_map/ppermute | solution.py:571
  443.6 45.9 %collective-permute-start.41 = (bf16[512,1024]{1,0:T(8,128)(2,1)S(1)}, bf16[512,1024]{1,0:T(8,128)(2,1)S(1)}, u32[]{:S(2)}, u32[]{:S(2)}) collective-permute-start(bf16[512,1024]{1,0:T(8,128)(2,1)S(1)} %copy-done.38), channel_id=1, source_target_pairs={{0,4},{2,6},{4,0},{6,2},{8,12},{10,14},{12,8},{14,10},{16,20},{18,... | collective-permute-start | bytes 3145736 | tf_op jit(solution)/shard_map/ppermute | solution.py:564
  446.5 43.0 %collective-permute-start.44 = (bf16[256,1024]{1,0:T(8,128)(2,1)S(1)}, bf16[256,1024]{1,0:T(8,128)(2,1)S(1)}, u32[]{:S(2)}, u32[]{:S(2)}) collective-permute-start(bf16[256,1024]{1,0:T(8,128)(2,1)S(1)} %copy-done.28), channel_id=1, source_target_pairs={{0,8},{2,10},{4,12},{6,14},{8,0},{10,2},{12,4},{14,6},{16,24},{18,... | collective-permute-start | bytes 1572872 | tf_op jit(solution)/shard_map/ppermute | solution.py:564
  517.4 32.4 %collective-permute-start.57 = (bf16[128,2048]{1,0:T(8,128)(2,1)}, bf16[128,2048]{1,0:T(8,128)(2,1)}, u32[]{:S(2)}, u32[]{:S(2)}) collective-permute-start(bf16[128,2048]{1,0:T(8,128)(2,1)} %get-tuple-element.308), channel_id=1, source_target_pairs={{0,2},{2,0},{4,6},{6,4},{8,10},{10,8},{12,14},{14,12},{16,18},{18,... | collective-permute-start | bytes 1572872 | tf_op jit(solution)/shard_map/ppermute | solution.py:564
  (67 other events, 705.6 us)

commit v7 on v6

--- a/solution.py
+++ b/solution.py
@@ -130,44 +130,53 @@
     )
 
 
-def join_kernel(flags_ref, pair_ref, second_ref, got_pair_ref, got_second_ref, out_ref):
+def join_kernel(flags_ref, *refs):
     i = pl.program_id(0)
     place = lax.rem(i, 4)
-    for own, (p_ref, s_ref) in enumerate(
-        ((pair_ref, second_ref), (got_pair_ref, got_second_ref))
-    ):
-        here = (i // 4) == own
-        crossed = flags_ref[own] == 1
-        from_pair = (place == 0) | ((place == 1) & jnp.logical_not(crossed))
-        from_pair = from_pair | ((place == 2) & crossed)
-
-        @pl.when(here & from_pair)
-        def _(ref=p_ref):
-            out_ref[...] = ref[...]
-
-        @pl.when(here & jnp.logical_not(from_pair))
-        def _(ref=s_ref):
-            out_ref[...] = ref[...]
+    for own in range(2):
+        swapped = (flags_ref[own] == 1) & (place > 0) & (place < 3)
+        block = jnp.where(swapped, 3 - place, place)
+        for n in range(4):
+            ref = refs[2 * own + n // 2]
+            half = ref.shape[0] // 2
+
+            @pl.when((i // 4 == own) & (block == n))
+            def _(ref=ref, low=(n % 2) * half, half=half):
+                refs[-1][...] = ref[low : low + half, :]
 
 
 def join(flags, pair, second, got_pair, got_second):
     half, width = pair.shape[0] // 2, pair.shape[1]
-
-    def spec(low, edge):
-        return pl.BlockSpec((half, width), lambda i, f: (jnp.where(i - low > edge, 1, 0), 0))
-
+    arrays = (pair, second, got_pair, got_second)
     return call(
         join_kernel,
         jax.ShapeDtypeStruct((8 * half, width), pair.dtype),
         (8,),
-        [spec(0, 0), spec(0, 2), spec(4, 0), spec(4, 2)],
+        [resident(value) for value in arrays],
         pl.BlockSpec((half, width), lambda i, f: (i, 0)),
         flags,
-        pair,
-        second,
-        got_pair,
-        got_second,
+        *arrays,
         prefetch=1,
+    )
+
+
+def stack_kernel(*refs):
+    for n, ref in enumerate(refs[:-1]):
+
+        @pl.when(pl.program_id(0) == n)
+        def _(ref=ref):
+            refs[-1][...] = ref[...]
+
+
+def stack_rows(*blocks):
+    rows, width = blocks[0].shape
+    return call(
+        stack_kernel,
+        jax.ShapeDtypeStruct((len(blocks) * rows, width), blocks[0].dtype),
+        (len(blocks),),
+        [resident(value) for value in blocks],
+        pl.BlockSpec((rows, width), lambda i: (i, 0)),
+        *blocks,
     )
 
 
@@ -777,7 +786,7 @@
         uu, n_own, n_got, a_x, d_x, c_own, seg = sync(uu, n_own, n_got, a_x, d_x, c_own, seg)
         u_rest = w_top(uu)
         u_far = swap(uu, Y_BIT)
-        n_pair = jnp.concatenate([n_own, n_got])
+        n_pair = stack_rows(n_own, n_got)
         n_second = swap(n_pair, X_BIT)
         n_got_pair = swap_core(n_pair)
         aa = w_place(w_zl(ordered(x_mine, *a_x, 0)))
@@ -811,7 +820,7 @@
         d_rest = w_top(dd)
         d_far = swap(dd, Y_BIT)
         a_far_rest = g_swap_y(a_rest)
-        c_pair = jnp.concatenate([c_own, c_got])
+        c_pair = stack_rows(c_own, c_got)
         c_second = swap_mixed(c_pair, (X_BIT, ZL_BIT))
         c_got_pair = swap_core(c_pair)
         normed = join(straight, n_pair, n_second, n_got_pair, n_got_second)

time: 565 us -> 560 us (level)
  local copies, waits for them, and re-layouts: 61.3 us -> 53.3 us
    pallas_call x39 -> x41, Pallas kernels: 255 us -> 257 us  [call(): pl.pallas_call(kernel, out_shape=outs, grid_spec=pltpu.PrefetchScalarGrid...]
where the time goes in v7:
time: 560 us; the launch traced here: 551 us
  Pallas kernels  265 us (47%)
  waiting for transfers between devices  147 us (26%)
  starting transfers between devices  58 us (10%)
  local copies, waits for them, and re-layouts  53.3 us (10%)
  other arithmetic  25.6 us (5%)
    pallas_call x41, Pallas kernels, call(): pl.pallas_call(kernel, out_shape=outs, grid_spec=pltpu.PrefetchScalarGrid...  257 us
    ppermute x44, waiting for transfers between devices, swap(): return lax.ppermute(value, 'dp', [(i, i ^ flip) for i in range(dp_size)])  134 us
    ppermute x44, starting transfers between devices, swap(): return lax.ppermute(value, 'dp', [(i, i ^ flip) for i in range(dp_size)])  50.5 us
    unnamed x94, local copies, waits for them, and re-layouts  23 us
  transfers between devices with their start and end apart: 58, of which 17 were waited for; matrix products, arithmetic and copies ran while one was open for 11% of the time, Pallas kernels for 46%

profile of v7, /device:TPU:0, one launch (start us, length us, event | category | flops | bytes accessed | tf_op | source)
XLA Modules:
  0.0 551.0 jit_solution(7751532192783488036)
XLA Ops:
  38.5 11.1 %collective-permute-done.4.other_ref = bf16[256,1024]{1,0:T(8,128)(2,1)} collective-permute-done((bf16[256,1024]{1,0:T(8,128)(2,1)}, bf16[256,1024]{1,0:T(8,128)(2,1)}, u32[]{:S(2)}, u32[]{:S(2)}) %collective-permute-start.4) | collective-permute-done | bytes 524320 | tf_op jit(solution)/shard_map/ppermute | solution.py:573
  68.7 28.1 %collective-permute-done.12.other_ref = bf16[256,1024]{1,0:T(8,128)(2,1)} collective-permute-done((bf16[256,1024]{1,0:T(8,128)(2,1)}, bf16[256,1024]{1,0:T(8,128)(2,1)}, u32[]{:S(2)}, u32[]{:S(2)}) %collective-permute-start.12) | collective-permute-done | bytes 524320 | tf_op jit(solution)/shard_map/ppermute | solution.py:573
  99.1 9.6 %collective-permute-done.8.refs_1_ = bf16[512,1024]{1,0:T(8,128)(2,1)} collective-permute-done((bf16[512,1024]{1,0:T(8,128)(2,1)}, bf16[512,1024]{1,0:T(8,128)(2,1)}, u32[]{:S(2)}, u32[]{:S(2)}) %collective-permute-start.8) | collective-permute-done | bytes 1048608 | tf_op jit(solution)/shard_map/ppermute | solution.py:573
  116.8 21.2 %collective-permute-done.16.other_ref = bf16[256,1024]{1,0:T(8,128)(2,1)} collective-permute-done((bf16[256,1024]{1,0:T(8,128)(2,1)}, bf16[256,1024]{1,0:T(8,128)(2,1)}, u32[]{:S(2)}, u32[]{:S(2)}) %collective-permute-start.16) | collective-permute-done | bytes 524320 | tf_op jit(solution)/shard_map/ppermute | solution.py:573
  141.7 5.8 %fusion.2 = (f32[2048,128]{1,0:T(8,128)}, f32[2048,128]{1,0:T(8,128)}, f32[2048,128]{1,0:T(8,128)}) fusion(f32[128]{0:T(128)S(1)} %fusion.15, f32[2048]{0:T(1024)S(1)} %bitcast.106, pred[128]{0:T(512)(128)(4,1)S(1)} %get-tuple-element.410, pred[128]{0:T(512)(128)(4,1)S(1)} %broadcast_compare_fusion.2, pred[128]{0:T(512)(128)(4,1)S(1)} %get-tuple-element.411), kind=kLoop, calls=%fused_computation.6 | loop fusion | flops 1572864 | bytes 3154816 | tf_op jit(solution)/shard_map/jit(_where)/select_n | solution.py:472
  149.7 9.1 %collective-permute-done.17.refs_1_ = bf16[256,2048]{1,0:T(8,128)(2,1)} collective-permute-done((bf16[256,2048]{1,0:T(8,128)(2,1)S(1)}, bf16[256,2048]{1,0:T(8,128)(2,1)}, u32[]{:S(2)}, u32[]{:S(2)}) %collective-permute-start.17) | collective-permute-done | bytes 1048608 | tf_op jit(solution)/shard_map/ppermute | solution.py:580
  158.8 4.2 collective-permute-done.13.refs_3_
  172.1 8.8 %shard_map.209.rows_ref.refs_0_ = bf16[2048,2048]{1,0:T(8,128)(2,1)} custom-call(s32[2]{0:T(128)} %broadcast_10_flags_ref.2.flags_ref, bf16[512,2048]{1,0:T(8,128)(2,1)} %shard_map.205.refs_0_, bf16[512,2048]{1,0:T(8,128)(2,1)} %collective-permute-done.10.refs_1_, bf16[512,2048]{1,0:T(8,128)(2,1)} %collective-permute-done.11.refs_2_, ...), custom_call_target="tpu_custom_call" | custom-call | flops 1000 | bytes 1000 | tf_op jit(solution)/shard_map/pallas_call | solution.py:35
  180.9 17.3 %shard_map.210 = (bf16[2048,1024]{1,0:T(8,128)(2,1)}, bf16[2048,1024]{1,0:T(8,128)(2,1)}) custom-call(bf16[2048,2048]{1,0:T(8,128)(2,1)} %shard_map.209.rows_ref.refs_0_, f32[1,1024]{1,0:T(1,128)} %bitcast.111, bf16[512,1024]{1,0:T(8,128)(2,1)} %shard_map.204.refs_0_, bf16[512,1024]{1,0:T(8,128)(2,1)} %collective-permute-done.8.refs_1_, ...), custom_call_target="tpu_custom_call" | custom-call | flops 1000 | bytes 1000 | tf_op jit(solution)/shard_map/pallas_call | solution.py:35
  198.2 18.6 %collective-permute-done.19.refs_1_ = bf16[512,1024]{1,0:T(8,128)(2,1)} collective-permute-done((bf16[512,1024]{1,0:T(8,128)(2,1)}, bf16[512,1024]{1,0:T(8,128)(2,1)}, u32[]{:S(2)}, u32[]{:S(2)}) %collective-permute-start.19) | collective-permute-done | bytes 1048608 | tf_op jit(solution)/shard_map/ppermute | solution.py:573
  221.4 8.8 %shard_map.211.refs_0_.refs_2_.rows_ref = bf16[2048,2048]{1,0:T(8,128)(2,1)} custom-call(s32[2]{0:T(128)} %pad_add_fusion.3.flags_ref, bf16[512,2048]{1,0:T(8,128)(2,1)} %shard_map.208.refs_0_, bf16[512,2048]{1,0:T(8,128)(2,1)} %collective-permute-done.22.refs_1_, bf16[512,2048]{1,0:T(8,128)(2,1)} %collective-permute-done.23.refs_2_, ...), custom_call_target="tpu_custom_call" | custom-call | flops 1000 | bytes 1000 | tf_op jit(solution)/shard_map/pallas_call | solution.py:35
  230.2 14.7 %shard_map.212 = (bf16[512,1024]{1,0:T(8,128)(2,1)}, bf16[512,1024]{1,0:T(8,128)(2,1)}, bf16[512,1024]{1,0:T(8,128)(2,1)}, bf16[512,1024]{1,0:T(8,128)(2,1)}) custom-call(bf16[2048,2048]{1,0:T(8,128)(2,1)} %shard_map.211.refs_0_.refs_2_.rows_ref, bf16[2048,1024]{1,0:T(8,128)(2,1)} %get-tuple-element.249.refs_1_.a_ref), custom_call_target="tpu_custom_call" | custom-call | flops 1000 | bytes 1000 | tf_op jit(solution)/shard_map/pallas_call | solution.py:35
  247.0 33.9 %shard_map.213 = (bf16[2,4,256,256]{3,2,1,0:T(8,128)(2,1)}, bf16[2,4,256,768]{3,2,1,0:T(8,128)(2,1)}, f32[8,768]{1,0:T(8,128)}) custom-call(bf16[2,4,256,2048]{3,2,1,0:T(8,128)(2,1)} %bitcast.82, bf16[2,4,256,2048]{3,2,1,0:T(8,128)(2,1)} %bitcast.83, f32[1,768]{1,0:T(1,128)} %bitcast.115, f32[2,4,256,128]{3,2,1,0:T(8,128)} %bitcast.97, ...), custom_call_target="tpu_custom_call" | custom-call | flops 1000 | bytes 1000 | tf_op jit(solution)/shard_map/pallas_call | solution.py:35
  286.1 12.7 %shard_map.216 = (bf16[512,1024]{1,0:T(8,128)(2,1)}, bf16[512,1024]{1,0:T(8,128)(2,1)}, bf16[512,1024]{1,0:T(8,128)(2,1)}) custom-call(bf16[2048,2048]{1,0:T(8,128)(2,1)} %shard_map.209.rows_ref.refs_0_, bf16[2048,768]{1,0:T(8,128)(2,1)} %bitcast.84, bf16[2048,2048]{1,0:T(8,128)(2,1)} %shard_map.211.refs_0_.refs_2_.rows_ref, bf16[2048,256]{1,0:T(8,128)(2,1)} %bitcast.89), custom_call_target="tpu_custom_call" | custom-call | flops 1000 | bytes 1000 | tf_op jit(solution)/shard_map/pallas_call | solution.py:35
  298.8 10.2 %shard_map.217 = bf16[1024,2048]{1,0:T(8,128)(2,1)} custom-call(s32[1]{0:T(128)} %bitcast.2._.core_ref, bf16[2048,1024]{1,0:T(8,128)(2,1)} %get-tuple-element.249.refs_1_.a_ref, bf16[2048,256]{1,0:T(8,128)(2,1)} %bitcast.90, bf16[512,1024]{1,0:T(8,128)(2,1)} %shard_map.207.refs_0_, bf16[512,1024]{1,0:T(8,128)(2,1)} %collective-permute-done.19.refs_1_, ...), custom_call_target="tpu_custom_call" | custom-call | flops 1000 | bytes 1000 | tf_op jit(solution)/shard_map/pallas_call | solution.py:35
  315.2 14.6 %shard_map.220 = (bf16[2048,1024]{1,0:T(8,128)(2,1)}, f32[8,1024]{1,0:T(8,128)}) custom-call(bf16[2048,2048]{1,0:T(8,128)(2,1)} %shard_map.211.refs_0_.refs_2_.rows_ref, bf16[2048,1024]{1,0:T(8,128)(2,1)} %get-tuple-element.242.slope_ref, bf16[512,1024]{1,0:T(8,128)(2,1)} %shard_map.207.refs_0_, bf16[512,1024]{1,0:T(8,128)(2,1)} %collective-permute-done.19.refs_1_, ...), custom_call_target="tpu_custom_call" | custom-call | flops 1000 | bytes 1000 | tf_op jit(solution)/shard_map/pallas_call | solution.py:35
  329.8 13.0 %shard_map.221 = bf16[1024,2048]{1,0:T(8,128)(2,1)} custom-call(s32[1]{0:T(128)} %bitcast.23._, bf16[2048,1024]{1,0:T(8,128)(2,1)} %get-tuple-element.275.a_ref.refs_1_, bf16[2048,768]{1,0:T(8,128)(2,1)} %bitcast.85, bf16[512,1024]{1,0:T(8,128)(2,1)} %shard_map.204.refs_0_, bf16[512,1024]{1,0:T(8,128)(2,1)} %collective-permute-done.8.refs_1_, ...), custom_call_target="tpu_custom_call" | custom-call | flops 1000 | bytes 1000 | tf_op jit(solution)/shard_map/pallas_call | solution.py:35
  344.9 7.2 %shard_map.218 = bf16[512,2048]{1,0:T(8,128)(2,1)} custom-call(s32[1]{0:T(128)} %bitcast.23._, bf16[2048,1024]{1,0:T(8,128)(2,1)} %get-tuple-element.249.refs_1_.a_ref, bf16[2048,256]{1,0:T(8,128)(2,1)} %bitcast.91, bf16[512,1024]{1,0:T(8,128)(2,1)} %shard_map.207.refs_0_, bf16[512,1024]{1,0:T(8,128)(2,1)} %collective-permute-done.19.refs_1_, ...), custom_call_target="tpu_custom_call" | custom-call | flops 1000 | bytes 1000 | tf_op jit(solution)/shard_map/pallas_call | solution.py:35
  361.8 6.2 %shard_map.224 = bf16[512,1024]{1,0:T(8,128)(2,1)} custom-call(bf16[2048,2048]{1,0:T(8,128)(2,1)} %shard_map.209.rows_ref.refs_0_, bf16[2048,1024]{1,0:T(8,128)(2,1)} %get-tuple-element.275.a_ref.refs_1_), custom_call_target="tpu_custom_call" | custom-call | flops 1000 | bytes 1000 | tf_op jit(solution)/shard_map/pallas_call | solution.py:35
  367.9 7.2 %shard_map.226.refs_0_ = bf16[512,2048]{1,0:T(8,128)(2,1)} custom-call(s32[1]{0:T(128)} %bitcast.23._, bf16[2048,1024]{1,0:T(8,128)(2,1)} %get-tuple-element.249.refs_1_.a_ref, bf16[2048,256]{1,0:T(8,128)(2,1)} %bitcast.92, bf16[512,1024]{1,0:T(8,128)(2,1)} %shard_map.207.refs_0_, bf16[512,1024]{1,0:T(8,128)(2,1)} %collective-permute-done.19.refs_1_, ...), custom_call_target="tpu_custom_call" | custom-call | flops 1000 | bytes 1000 | tf_op jit(solution)/shard_map/pallas_call | solution.py:35
  377.1 9.0 %shard_map.225 = bf16[512,2048]{1,0:T(8,128)(2,1)} custom-call(s32[1]{0:T(128)} %bitcast.2._.core_ref, bf16[2048,1024]{1,0:T(8,128)(2,1)} %get-tuple-element.275.a_ref.refs_1_, bf16[2048,768]{1,0:T(8,128)(2,1)} %bitcast.86, bf16[512,1024]{1,0:T(8,128)(2,1)} %shard_map.204.refs_0_, bf16[512,1024]{1,0:T(8,128)(2,1)} %collective-permute-done.8.refs_1_, ...), custom_call_target="tpu_custom_call" | custom-call | flops 1000 | bytes 1000 | tf_op jit(solution)/shard_map/pallas_call | solution.py:35
  386.1 8.2 %collective-permute-done.33.refs_2_ = bf16[256,1024]{1,0:T(8,128)(2,1)S(1)} collective-permute-done((bf16[256,1024]{1,0:T(8,128)(2,1)}, bf16[256,1024]{1,0:T(8,128)(2,1)S(1)}, u32[]{:S(2)}, u32[]{:S(2)}) %collective-permute-start.33) | collective-permute-done | bytes 524320 | tf_op jit(solution)/shard_map/ppermute | solution.py:573
  396.7 4.5 collective-permute-start.37
  401.2 6.8 %shard_map.228.refs_0_ = bf16[512,1024]{1,0:T(8,128)(2,1)} custom-call(bf16[2048,2048]{1,0:T(8,128)(2,1)} %shard_map.209.rows_ref.refs_0_, bf16[2048,768]{1,0:T(8,128)(2,1)} %bitcast.87, bf16[2048,2048]{1,0:T(8,128)(2,1)} %shard_map.211.refs_0_.refs_2_.rows_ref, bf16[2048,256]{1,0:T(8,128)(2,1)} %bitcast.93), custom_call_target="tpu_custom_call" | custom-call | flops 1000 | bytes 1000 | tf_op jit(solution)/shard_map/pallas_call | solution.py:35
  408.0 8.9 %shard_map.227 = (bf16[512,1024]{1,0:T(8,128)(2,1)}, bf16[512,1024]{1,0:T(8,128)(2,1)}) custom-call(bf16[2048,2048]{1,0:T(8,128)(2,1)} %shard_map.209.rows_ref.refs_0_, bf16[2048,1024]{1,0:T(8,128)(2,1)} %get-tuple-element.275.a_ref.refs_1_), custom_call_target="tpu_custom_call" | custom-call | flops 1000 | bytes 1000 | tf_op jit(solution)/shard_map/pallas_call | solution.py:35
  416.9 9.0 %shard_map.230.refs_0_ = bf16[512,2048]{1,0:T(8,128)(2,1)} custom-call(s32[1]{0:T(128)} %bitcast.2._.core_ref, bf16[2048,1024]{1,0:T(8,128)(2,1)} %get-tuple-element.275.a_ref.refs_1_, bf16[2048,768]{1,0:T(8,128)(2,1)} %bitcast.88, bf16[512,1024]{1,0:T(8,128)(2,1)} %shard_map.204.refs_0_, bf16[512,1024]{1,0:T(8,128)(2,1)} %collective-permute-done.8.refs_1_, ...), custom_call_target="tpu_custom_call" | custom-call | flops 1000 | bytes 1000 | tf_op jit(solution)/shard_map/pallas_call | solution.py:35
  449.0 6.2 %shard_map.235.refs_0_ = bf16[512,1024]{1,0:T(8,128)(2,1)} custom-call(bf16[2048,2048]{1,0:T(8,128)(2,1)} %shard_map.209.rows_ref.refs_0_, bf16[2048,1024]{1,0:T(8,128)(2,1)} %get-tuple-element.275.a_ref.refs_1_), custom_call_target="tpu_custom_call" | custom-call | flops 1000 | bytes 1000 | tf_op jit(solution)/shard_map/pallas_call | solution.py:35
  458.1 13.1 %collective-permute-done.40.refs_2_ = bf16[256,1024]{1,0:T(8,128)(2,1)S(1)} collective-permute-done((bf16[256,1024]{1,0:T(8,128)(2,1)}, bf16[256,1024]{1,0:T(8,128)(2,1)S(1)}, u32[]{:S(2)}, u32[]{:S(2)}) %collective-permute-start.40) | collective-permute-done | bytes 524320 | tf_op jit(solution)/shard_map/ppermute | solution.py:573
  471.2 14.0 %collective-permute-done.44.got_ref = bf16[256,1024]{1,0:T(8,128)(2,1)S(1)} collective-permute-done((bf16[256,1024]{1,0:T(8,128)(2,1)S(1)}, bf16[256,1024]{1,0:T(8,128)(2,1)S(1)}, u32[]{:S(2)}, u32[]{:S(2)}) %collective-permute-start.44) | collective-permute-done | bytes 524320 | tf_op jit(solution)/shard_map/ppermute | solution.py:573
  499.9 4.4 shard_map.241.own_ref
  531.7 4.1 shard_map.243
  535.8 5.3 shard_map.244
  (305 shorter events, 193.6 us)
Async XLA Ops:
  14.3 39.7 %collective-permute-start.5 = (bf16[256,2048]{1,0:T(8,128)(2,1)}, bf16[256,2048]{1,0:T(8,128)(2,1)}, u32[]{:S(2)}, u32[]{:S(2)}) collective-permute-start(bf16[256,2048]{1,0:T(8,128)(2,1)} %get-tuple-element.171.refs_0_), channel_id=1, source_target_pairs={{0,8},{2,10},{4,12},{6,14},{8,0},{10,2},{12,4},{14,6},{16,24},{18,... | collective-permute-start | bytes 3145736 | tf_op jit(solution)/shard_map/ppermute | solution.py:573
  57.0 51.7 %collective-permute-start.11 = (bf16[512,2048]{1,0:T(8,128)(2,1)}, bf16[512,2048]{1,0:T(8,128)(2,1)}, u32[]{:S(2)}, u32[]{:S(2)}) collective-permute-start(bf16[512,2048]{1,0:T(8,128)(2,1)} %shard_map.205.refs_0_), channel_id=1, source_target_pairs={{0,1},{1,0},{2,3},{3,2},{4,5},{5,4},{6,7},{7,6},{8,9},{9,8},{10,11... | collective-permute-start | bytes 6291464 | tf_op jit(solution)/shard_map/ppermute | solution.py:576
  57.0 51.7 %collective-permute-start.10 = (bf16[512,2048]{1,0:T(8,128)(2,1)}, bf16[512,2048]{1,0:T(8,128)(2,1)}, u32[]{:S(2)}, u32[]{:S(2)}) collective-permute-start(bf16[512,2048]{1,0:T(8,128)(2,1)} %shard_map.205.refs_0_), channel_id=1, source_target_pairs={{0,2},{2,0},{4,6},{6,4},{8,10},{10,8},{12,14},{14,12},{16,18},{18,... | collective-permute-start | bytes 6291464 | tf_op jit(solution)/shard_map/ppermute | solution.py:573
  58.5 40.5 %collective-permute-start.9 = (bf16[512,1024]{1,0:T(8,128)(2,1)}, bf16[512,1024]{1,0:T(8,128)(2,1)}, u32[]{:S(2)}, u32[]{:S(2)}) collective-permute-start(bf16[512,1024]{1,0:T(8,128)(2,1)} %shard_map.204.refs_0_), channel_id=1, source_target_pairs={{0,4},{2,6},{4,0},{6,2},{8,12},{10,14},{12,8},{14,10},{16,20},{18,... | collective-permute-start | bytes 3145736 | tf_op jit(solution)/shard_map/ppermute | solution.py:573
  60.1 48.6 %collective-permute-start.8 = (bf16[512,1024]{1,0:T(8,128)(2,1)}, bf16[512,1024]{1,0:T(8,128)(2,1)}, u32[]{:S(2)}, u32[]{:S(2)}) collective-permute-start(bf16[512,1024]{1,0:T(8,128)(2,1)} %shard_map.204.refs_0_), channel_id=1, source_target_pairs={{0,16},{2,18},{4,20},{6,22},{8,24},{10,26},{12,28},{14,30},{16,0},... | collective-permute-start | bytes 3145736 | tf_op jit(solution)/shard_map/ppermute | solution.py:573
  65.3 31.5 %collective-permute-start.12 = (bf16[256,1024]{1,0:T(8,128)(2,1)}, bf16[256,1024]{1,0:T(8,128)(2,1)}, u32[]{:S(2)}, u32[]{:S(2)}) collective-permute-start(bf16[256,1024]{1,0:T(8,128)(2,1)} %get-tuple-element.390), channel_id=1, source_target_pairs={{0,8},{2,10},{4,12},{6,14},{8,0},{10,2},{12,4},{14,6},{16,24},{18,... | collective-permute-start | bytes 1572872 | tf_op jit(solution)/shard_map/ppermute | solution.py:573
  108.8 54.3 %collective-permute-start.18 = (bf16[512,2048]{1,0:T(8,128)(2,1)}, bf16[512,2048]{1,0:T(8,128)(2,1)}, u32[]{:S(2)}, u32[]{:S(2)}) collective-permute-start(bf16[512,2048]{1,0:T(8,128)(2,1)} %collective-permute-done.10.refs_1_), channel_id=1, source_target_pairs={{0,1},{1,0},{2,3},{3,2},{4,5},{5,4},{6,7},{7,6},{8,9},{9,8},{10,11... | collective-permute-start | bytes 6291464 | tf_op jit(solution)/shard_map/ppermute | solution.py:576
  112.9 50.2 %collective-permute-start.15 = (bf16[512,1024]{1,0:T(8,128)(2,1)}, bf16[512,1024]{1,0:T(8,128)(2,1)}, u32[]{:S(2)}, u32[]{:S(2)}) collective-permute-start(bf16[512,1024]{1,0:T(8,128)(2,1)} %shard_map.206.refs_0_.refs_4_), channel_id=1, source_target_pairs={{0,4},{2,6},{4,0},{6,2},{8,12},{10,14},{12,8},{14,10},{16,20},{18,... | collective-permute-start | bytes 3145736 | tf_op jit(solution)/shard_map/ppermute | solution.py:573
  113.4 49.6 %collective-permute-start.14 = (bf16[512,1024]{1,0:T(8,128)(2,1)}, bf16[512,1024]{1,0:T(8,128)(2,1)}, u32[]{:S(2)}, u32[]{:S(2)}) collective-permute-start(bf16[512,1024]{1,0:T(8,128)(2,1)} %shard_map.206.refs_0_.refs_4_), channel_id=1, source_target_pairs={{0,16},{2,18},{4,20},{6,22},{8,24},{10,26},{12,28},{14,30},{16,0},... | collective-permute-start | bytes 3145736 | tf_op jit(solution)/shard_map/ppermute | solution.py:573
  116.7 42.2 %collective-permute-start.17 = (bf16[256,2048]{1,0:T(8,128)(2,1)S(1)}, bf16[256,2048]{1,0:T(8,128)(2,1)}, u32[]{:S(2)}, u32[]{:S(2)}) collective-permute-start(bf16[256,2048]{1,0:T(8,128)(2,1)S(1)} %get-tuple-element.187.refs_0_), channel_id=1, source_target_pairs={{0,8},{1,3},{2,10},{3,1},{4,12},{5,7},{6,14},{7,5},{8,0},{9,11},{1... | collective-permute-start | bytes 3145736 | tf_op jit(solution)/shard_map/ppermute | solution.py:580
  166.7 50.1 %collective-permute-start.23 = (bf16[512,2048]{1,0:T(8,128)(2,1)}, bf16[512,2048]{1,0:T(8,128)(2,1)}, u32[]{:S(2)}, u32[]{:S(2)}) collective-permute-start(bf16[512,2048]{1,0:T(8,128)(2,1)} %shard_map.208.refs_0_), channel_id=1, source_target_pairs={{0,1},{1,0},{2,3},{3,2},{4,5},{5,4},{6,7},{7,6},{8,9},{9,8},{10,11... | collective-permute-start | bytes 6291464 | tf_op jit(solution)/shard_map/ppermute | solution.py:576
  166.7 50.1 %collective-permute-start.22 = (bf16[512,2048]{1,0:T(8,128)(2,1)}, bf16[512,2048]{1,0:T(8,128)(2,1)}, u32[]{:S(2)}, u32[]{:S(2)}) collective-permute-start(bf16[512,2048]{1,0:T(8,128)(2,1)} %shard_map.208.refs_0_), channel_id=1, source_target_pairs={{0,2},{1,9},{2,0},{3,11},{4,6},{5,13},{6,4},{7,15},{8,10},{9,1},{1... | collective-permute-start | bytes 6291464 | tf_op jit(solution)/shard_map/ppermute | solution.py:580
  167.2 31.0 %collective-permute-start.20 = (bf16[512,1024]{1,0:T(8,128)(2,1)}, bf16[512,1024]{1,0:T(8,128)(2,1)}, u32[]{:S(2)}, u32[]{:S(2)}) collective-permute-start(bf16[512,1024]{1,0:T(8,128)(2,1)} %shard_map.207.refs_0_), channel_id=1, source_target_pairs={{0,4},{2,6},{4,0},{6,2},{8,12},{10,14},{12,8},{14,10},{16,20},{18,... | collective-permute-start | bytes 3145736 | tf_op jit(solution)/shard_map/ppermute | solution.py:573
  168.3 48.4 %collective-permute-start.19 = (bf16[512,1024]{1,0:T(8,128)(2,1)}, bf16[512,1024]{1,0:T(8,128)(2,1)}, u32[]{:S(2)}, u32[]{:S(2)}) collective-permute-start(bf16[512,1024]{1,0:T(8,128)(2,1)} %shard_map.207.refs_0_), channel_id=1, source_target_pairs={{0,16},{2,18},{4,20},{6,22},{8,24},{10,26},{12,28},{14,30},{16,0},... | collective-permute-start | bytes 3145736 | tf_op jit(solution)/shard_map/ppermute | solution.py:573
  168.8 48.0 %collective-permute-start.21 = (bf16[512,1024]{1,0:T(8,128)(2,1)}, bf16[512,1024]{1,0:T(8,128)(2,1)S(1)}, u32[]{:S(2)}, u32[]{:S(2)}) collective-permute-start(bf16[512,1024]{1,0:T(8,128)(2,1)} %collective-permute-done.14.refs_1_.refs_5_), channel_id=1, source_target_pairs={{0,4},{2,6},{4,0},{6,2},{8,12},{10,14},{12,8},{14,10},{16,20},{18,... | collective-permute-start | bytes 3145736 | tf_op jit(solution)/shard_map/ppermute | solution.py:573
  244.9 36.1 %collective-permute-start.26 = (bf16[512,1024]{1,0:T(8,128)(2,1)}, bf16[512,1024]{1,0:T(8,128)(2,1)S(1)}, u32[]{:S(2)}, u32[]{:S(2)}) collective-permute-start(bf16[512,1024]{1,0:T(8,128)(2,1)} %get-tuple-element.203), channel_id=1, source_target_pairs={{0,4},{2,6},{4,0},{6,2},{8,12},{10,14},{12,8},{14,10},{16,20},{18,... | collective-permute-start | bytes 3145736 | tf_op jit(solution)/shard_map/ppermute | solution.py:573
  309.6 33.2 %collective-permute-start.31 = (bf16[1024,2048]{1,0:T(8,128)(2,1)}, bf16[1024,2048]{1,0:T(8,128)(2,1)S(1)}, u32[]{:S(2)}, u32[]{:S(2)}) collective-permute-start(bf16[1024,2048]{1,0:T(8,128)(2,1)} %shard_map.217), channel_id=1, source_target_pairs={{0,1},{1,0},{2,3},{3,2},{4,5},{5,4},{6,7},{7,6},{8,9},{9,8},{10,11... | collective-permute-start | bytes 12582920 | tf_op jit(solution)/shard_map/ppermute | solution.py:576
  309.7 44.1 %collective-permute-start.30 = (bf16[512,1024]{1,0:T(8,128)(2,1)S(1)}, bf16[512,1024]{1,0:T(8,128)(2,1)}, u32[]{:S(2)}, u32[]{:S(2)}) collective-permute-start(bf16[512,1024]{1,0:T(8,128)(2,1)S(1)} %copy-done.41), channel_id=1, source_target_pairs={{0,4},{2,6},{4,0},{6,2},{8,12},{10,14},{12,8},{14,10},{16,20},{18,... | collective-permute-start | bytes 3145736 | tf_op jit(solution)/shard_map/ppermute | solution.py:573
  313.1 39.0 %collective-permute-start.32 = (bf16[256,1024]{1,0:T(8,128)(2,1)}, bf16[256,1024]{1,0:T(8,128)(2,1)S(1)}, u32[]{:S(2)}, u32[]{:S(2)}) collective-permute-start(bf16[256,1024]{1,0:T(8,128)(2,1)} %shard_map.219), channel_id=1, source_target_pairs={{0,8},{2,10},{4,12},{6,14},{8,0},{10,2},{12,4},{14,6},{16,24},{18,... | collective-permute-start | bytes 1572872 | tf_op jit(solution)/shard_map/ppermute | solution.py:573
  315.1 37.0 %collective-permute-start.29 = (bf16[256,1024]{1,0:T(8,128)(2,1)S(1)}, bf16[256,1024]{1,0:T(8,128)(2,1)S(1)}, u32[]{:S(2)}, u32[]{:S(2)}) collective-permute-start(bf16[256,1024]{1,0:T(8,128)(2,1)S(1)} %copy-done.31), channel_id=1, source_target_pairs={{0,16},{2,18},{4,20},{6,22},{8,24},{10,26},{12,28},{14,30},{16,0},... | collective-permute-start | bytes 1572872 | tf_op jit(solution)/shard_map/ppermute | solution.py:573
  353.7 41.6 %collective-permute-start.36 = (bf16[512,2048]{1,0:T(8,128)(2,1)}, bf16[512,2048]{1,0:T(8,128)(2,1)S(1)}, u32[]{:S(2)}, u32[]{:S(2)}) collective-permute-start(bf16[512,2048]{1,0:T(8,128)(2,1)} %shard_map.218), channel_id=1, source_target_pairs={{0,8},{1,3},{2,10},{3,1},{4,12},{5,7},{6,14},{7,5},{8,0},{9,11},{1... | collective-permute-start | bytes 6291464 | tf_op jit(solution)/shard_map/ppermute | solution.py:580
  355.7 38.7 %collective-permute-start.34 = (bf16[512,1024]{1,0:T(8,128)(2,1)}, bf16[512,1024]{1,0:T(8,128)(2,1)S(1)}, u32[]{:S(2)}, u32[]{:S(2)}) collective-permute-start(bf16[512,1024]{1,0:T(8,128)(2,1)} %get-tuple-element.246), channel_id=1, source_target_pairs={{0,4},{2,6},{4,0},{6,2},{8,12},{10,14},{12,8},{14,10},{16,20},{18,... | collective-permute-start | bytes 3145736 | tf_op jit(solution)/shard_map/ppermute | solution.py:573
  358.7 35.6 %collective-permute-start.33 = (bf16[256,1024]{1,0:T(8,128)(2,1)}, bf16[256,1024]{1,0:T(8,128)(2,1)S(1)}, u32[]{:S(2)}, u32[]{:S(2)}) collective-permute-start(bf16[256,1024]{1,0:T(8,128)(2,1)} %shard_map.222), channel_id=1, source_target_pairs={{0,16},{2,18},{4,20},{6,22},{8,24},{10,26},{12,28},{14,30},{16,0},... | collective-permute-start | bytes 1572872 | tf_op jit(solution)/shard_map/ppermute | solution.py:573
  395.3 32.8 %collective-permute-start.39 = (bf16[512,2048]{1,0:T(8,128)(2,1)}, bf16[512,2048]{1,0:T(8,128)(2,1)S(1)}, u32[]{:S(2)}, u32[]{:S(2)}) collective-permute-start(bf16[512,2048]{1,0:T(8,128)(2,1)} %shard_map.225), channel_id=1, source_target_pairs={{0,2},{1,9},{2,0},{3,11},{4,6},{5,13},{6,4},{7,15},{8,10},{9,1},{1... | collective-permute-start | bytes 6291464 | tf_op jit(solution)/shard_map/ppermute | solution.py:580
  395.3 32.8 %collective-permute-start.38 = (bf16[512,1024]{1,0:T(8,128)(2,1)}, bf16[512,1024]{1,0:T(8,128)(2,1)S(1)}, u32[]{:S(2)}, u32[]{:S(2)}) collective-permute-start(bf16[512,1024]{1,0:T(8,128)(2,1)} %shard_map.224), channel_id=1, source_target_pairs={{0,4},{2,6},{4,0},{6,2},{8,12},{10,14},{12,8},{14,10},{16,20},{18,... | collective-permute-start | bytes 3145736 | tf_op jit(solution)/shard_map/ppermute | solution.py:573
  396.7 31.4 %collective-permute-start.37 = (bf16[256,1024]{1,0:T(8,128)(2,1)}, bf16[256,1024]{1,0:T(8,128)(2,1)S(1)}, u32[]{:S(2)}, u32[]{:S(2)}) collective-permute-start(bf16[256,1024]{1,0:T(8,128)(2,1)} %shard_map.223), channel_id=1, source_target_pairs={{0,16},{2,18},{4,20},{6,22},{8,24},{10,26},{12,28},{14,30},{16,0},... | collective-permute-start | bytes 1572872 | tf_op jit(solution)/shard_map/ppermute | solution.py:573
  431.9 53.3 %collective-permute-start.43 = (bf16[256,2048]{1,0:T(8,128)(2,1)}, bf16[256,2048]{1,0:T(8,128)(2,1)S(1)}, u32[]{:S(2)}, u32[]{:S(2)}) collective-permute-start(bf16[256,2048]{1,0:T(8,128)(2,1)} %shard_map.234), channel_id=1, source_target_pairs={{0,2},{1,9},{2,0},{3,11},{4,6},{5,13},{6,4},{7,15},{8,10},{9,1},{1... | collective-permute-start | bytes 3145736 | tf_op jit(solution)/shard_map/ppermute | solution.py:580
  436.6 48.6 %collective-permute-start.42 = (bf16[256,2048]{1,0:T(8,128)(2,1)}, bf16[256,2048]{1,0:T(8,128)(2,1)S(1)}, u32[]{:S(2)}, u32[]{:S(2)}) collective-permute-start(bf16[256,2048]{1,0:T(8,128)(2,1)} %shard_map.233), channel_id=1, source_target_pairs={{0,8},{1,3},{2,10},{3,1},{4,12},{5,7},{6,14},{7,5},{8,0},{9,11},{1... | collective-permute-start | bytes 3145736 | tf_op jit(solution)/shard_map/ppermute | solution.py:580
  439.2 46.0 %collective-permute-start.41 = (bf16[512,1024]{1,0:T(8,128)(2,1)S(1)}, bf16[512,1024]{1,0:T(8,128)(2,1)S(1)}, u32[]{:S(2)}, u32[]{:S(2)}) collective-permute-start(bf16[512,1024]{1,0:T(8,128)(2,1)S(1)} %copy-done.39), channel_id=1, source_target_pairs={{0,4},{2,6},{4,0},{6,2},{8,12},{10,14},{12,8},{14,10},{16,20},{18,... | collective-permute-start | bytes 3145736 | tf_op jit(solution)/shard_map/ppermute | solution.py:573
  442.0 29.2 %collective-permute-start.40 = (bf16[256,1024]{1,0:T(8,128)(2,1)}, bf16[256,1024]{1,0:T(8,128)(2,1)S(1)}, u32[]{:S(2)}, u32[]{:S(2)}) collective-permute-start(bf16[256,1024]{1,0:T(8,128)(2,1)} %shard_map.231), channel_id=1, source_target_pairs={{0,16},{2,18},{4,20},{6,22},{8,24},{10,26},{12,28},{14,30},{16,0},... | collective-permute-start | bytes 1572872 | tf_op jit(solution)/shard_map/ppermute | solution.py:573
  442.0 43.2 %collective-permute-start.44 = (bf16[256,1024]{1,0:T(8,128)(2,1)S(1)}, bf16[256,1024]{1,0:T(8,128)(2,1)S(1)}, u32[]{:S(2)}, u32[]{:S(2)}) collective-permute-start(bf16[256,1024]{1,0:T(8,128)(2,1)S(1)} %copy-done.29), channel_id=1, source_target_pairs={{0,8},{2,10},{4,12},{6,14},{8,0},{10,2},{12,4},{14,6},{16,24},{18,... | collective-permute-start | bytes 1572872 | tf_op jit(solution)/shard_map/ppermute | solution.py:573
  513.1 32.4 %collective-permute-start.57 = (bf16[128,2048]{1,0:T(8,128)(2,1)}, bf16[128,2048]{1,0:T(8,128)(2,1)}, u32[]{:S(2)}, u32[]{:S(2)}) collective-permute-start(bf16[128,2048]{1,0:T(8,128)(2,1)} %get-tuple-element.308), channel_id=1, source_target_pairs={{0,2},{2,0},{4,6},{6,4},{8,10},{10,8},{12,14},{14,12},{16,18},{18,... | collective-permute-start | bytes 1572872 | tf_op jit(solution)/shard_map/ppermute | solution.py:573
  (68 other events, 802.9 us)
